TPU v7x, 32 devices: a whole 2x2x4 slice. The times are simulated.
32 devices in a mesh: rows: 8 (over z, x), feat: 4 (over y, core).
Axes of the slice: x: 2, y: 2, z: 4, core: 2. Of those that a mesh axis runs over, the one named last changes fastest.
Arguments:
- predictions: bfloat16 [12288, 4096], P('rows', 'feat'), may hold values from -6 to 6
- labels: bfloat16 [12288, 4096], P('rows', 'feat'), may hold values from 0 to 1
- feature_codes: int32 [32, 12288], P('feat', 'rows'), may hold values from 0 to 255
- leaf_index: int32 [12288], P('rows'), may hold values from 0 to 63
- sketch_weight: bfloat16 [4096, 256], P('feat'), may hold values from -0.09375 to 0.09375
Outputs:
- histograms: float32 [256, 32, 256], P('rows', 'feat')
- leaf_values: float32 [64, 4096], P(None, 'feat')
- updated: bfloat16 [12288, 4096], P('rows', 'feat')
All inputs are finite; a program needn't handle non-finite values.
Results may differ from a plain program's by a relative error of at most 0.008.
Values may be sent and summed in bfloat16 or wider, within the bound.
No kernel may reach another device: no remote copies, remote signals or barrier semaphores. Data moves between devices by JAX's collectives and lax.ppermute only.
A program may use at most 64 MiB of HBM per device.

v0:
```python
import jax
import jax.numpy as jnp
from jax import lax
from jax.sharding import PartitionSpec as P

BINS = 256
LEAVES = 64


shrinkage = 0.5
ridge_term = 1.0


def local(predictions, labels, feature_codes, leaf_index, sketch_weight):
    logits = predictions.astype(jnp.float32)
    probability = jax.nn.sigmoid(logits)
    gradient = (labels.astype(jnp.float32) - probability).astype(jnp.bfloat16)
    hessian = (probability * (1.0 - probability)).astype(jnp.bfloat16)
    partial_sketch = jnp.dot(gradient, sketch_weight, preferred_element_type=jnp.float32)
    partial_sketch = partial_sketch.astype(jnp.bfloat16)
    sketch = lax.psum(partial_sketch, "feat").astype(jnp.float32).astype(jnp.bfloat16)
    owned_bins = BINS // lax.axis_size("rows")
    levels = jnp.arange(BINS, dtype=jnp.int32)
    one_hot = (levels[:, None, None] == feature_codes[None, :, :]).astype(jnp.bfloat16)
    every_bin = lax.psum(
        jnp.einsum("bfr,rk->bfk", one_hot, sketch, preferred_element_type=jnp.float32), "rows"
    )
    histograms = lax.dynamic_slice_in_dim(
        every_bin, lax.axis_index("rows") * owned_bins, owned_bins, 0
    )
    leaf_hot = jnp.arange(LEAVES, dtype=jnp.int32)[:, None] == leaf_index[None, :]
    leaf_weights = leaf_hot.astype(jnp.bfloat16)
    grad_sum = jnp.dot(leaf_weights, gradient, preferred_element_type=jnp.float32)
    hess_sum = jnp.dot(leaf_weights, hessian, preferred_element_type=jnp.float32)
    grad_total, hess_total = lax.psum((grad_sum, hess_sum), "rows")
    leaf_values = grad_total / (hess_total + ridge_term)
    looked_up = jnp.einsum(
        "lr,lc->rc", leaf_hot.astype(jnp.float32), leaf_values, precision=lax.Precision.HIGHEST
    )
    updated = (logits + shrinkage * looked_up).astype(jnp.bfloat16)
    return (histograms, leaf_values, updated)


def solution(mesh):
    return jax.shard_map(
        local,
        mesh=mesh,
        in_specs=(
            P("rows", "feat"),
            P("rows", "feat"),
            P("feat", "rows"),
            P("rows"),
            P("feat", None),
        ),
        out_specs=(P("rows", "feat", None), P(None, "feat"), P("rows", "feat")),
        check_vma=False,
    )
```

profile of v0, /device:TPU:0, one launch (start us, length us, event | category | flops | bytes accessed | tf_op | source)
XLA Modules:
  0.0 190.5 jit_solution(17666894907560924390)
XLA Ops:
  7.2 0.0 copy-start
  7.2 0.0 all-reduce.4.cloned.1.call-start
  7.2 4.9 %subtract_convert_fusion = bf16[1536,1024]{1,0:T(8,128)(2,1)S(1)} fusion(bf16[1536,1024]{1,0:T(8,128)(2,1)} %param.6, bf16[1536,1024]{1,0:T(8,128)(2,1)} %param.5), kind=kLoop, calls=%fused_computation.10 | loop fusion | flops 11010048 | bytes 9437184 | tf_op jit(solution)/shard_map/convert_element_type | solution.py:17
  12.2 0.0 copy-start.1
  12.2 1.7 copy-done.1
  13.8 0.0 copy-done
  13.9 0.0 copy-start.4
  13.9 1.9 convolution_convert_fusion
  15.7 0.0 all-reduce.4.cloned.1.call-update
  15.8 0.0 all-reduce.6.cloned.1.call-start
  15.8 0.0 copy-done.4
  15.8 0.0 copy-start.2
  15.8 4.6 %fusion.7 = f32[64,1024]{1,0:T(8,128)} fusion(bf16[1536,1024]{1,0:T(8,128)(2,1)} %param.5, s32[1536]{0:T(1024)S(1)} %copy-done.4), kind=kOutput, calls=%fused_computation.12 | convolution fusion | flops 212434944 | bytes 3414016 | tf_op jit(solution)/shard_map/dot_general | solution.py:34
  20.4 0.0 copy-done.2
  20.4 0.0 copy-start.5
  20.4 1.4 fusion.12
  21.8 31.4 %all-reduce.4.cloned.1.call-done = bf16[1536,256]{1,0:T(8,128)(2,1)} async-done(((bf16[1536,256]{1,0:T(8,128)(2,1)}), bf16[1536,256]{1,0:T(8,128)(2,1)}) %all-reduce.4.cloned.1.call-update) | async-done | bytes 786448 | tf_op jit(solution)/shard_map/psum | solution.py:21
  53.3 0.0 copy-done.5
  53.3 4.8 %fusion = f32[256,8,256]{2,0,1:T(8,128)} fusion(s32[8,1536]{1,0:T(8,128)S(1)} %copy-done.5, bf16[1536,256]{1,0:T(8,128)(2,1)} %all-reduce.4.cloned.1.call-done), kind=kOutput, calls=%fused_computation.1 | convolution fusion | flops 1613758464 | bytes 2932736 | tf_op jit(solution)/shard_map/bfr,rk->bfk/dot_general | solution.py:26
  58.1 0.0 all-reduce.6.cloned.1.call-update
  58.1 116.8 %all-reduce.6.cloned.1.call-done = (f32[256,8,256]{2,0,1:T(8,128)}, f32[64,1024]{1,0:T(8,128)}, f32[64,1024]{1,0:T(8,128)}) async-done(((f32[256,8,256]{2,0,1:T(8,128)}, f32[64,1024]{1,0:T(8,128)}, f32[64,1024]{1,0:T(8,128)}), (f32[256,8,256]{2,0,1:T(8,128)}, f32[64,1024]{1,0:T(8,128)}, f32[64,1024]{1,0:T(8,128)})) %all-reduce.6.cloned.1.call-update) | async-done | bytes 2621456 | tf_op jit(solution)/shard_map/psum | solution.py:25
  174.9 1.0 constant_dynamic-slice_fusion
  175.9 0.9 copy.8
  176.8 1.1 add_divide_fusion
  177.9 0.0 copy-start.3
  177.9 5.7 %fusion.4 = bf16[1536,1024]{1,0:T(8,128)(2,1)} fusion(bf16[1536,1024]{1,0:T(8,128)(2,1)} %param.5, f32[64,1024]{1,0:T(8,128)S(1)} %add_divide_fusion, s32[1536]{0:T(1024)S(1)} %copy-done.4), kind=kOutput, calls=%fused_computation.8 | convolution fusion | flops 1214349312 | bytes 6559744 | tf_op jit(solution)/shard_map/lr,lc->rc/dot_general | solution.py:37
  183.6 0.0 copy-done.3
Async XLA Ops:
  7.2 6.7 %copy-start = (bf16[1024,256]{1,0:T(8,128)(2,1)S(1)}, bf16[1024,256]{1,0:T(8,128)(2,1)}, u32[]{:S(2)}) copy-start(bf16[1024,256]{1,0:T(8,128)(2,1)} %param.9) | copy-start | bytes 1572868
  7.2 46.1 %all-reduce.4.cloned.1.call-start = ((), (), s32[]{:S(2)}) async-start(), calls=%async_computation | async-start | bytes 1572864 | tf_op jit(solution)/shard_map/psum | solution.py:21
  12.2 1.7 copy-start.1
  13.9 2.0 %copy-start.4 = (s32[1536]{0:T(1024)S(1)}, s32[1536]{0:T(1024)}, u32[]{:S(2)}) copy-start(s32[1536]{0:T(1024)} %param.8) | copy-start | bytes 18436
  15.8 159.2 %all-reduce.6.cloned.1.call-start = ((), (), s32[]{:S(2)}) async-start(), calls=%async_computation.1 | async-start | bytes 5242880 | tf_op jit(solution)/shard_map/psum | solution.py:25
  15.8 4.6 %copy-start.2 = (bf16[1536,1024]{1,0:T(8,128)(2,1)S(1)}, bf16[1536,1024]{1,0:T(8,128)(2,1)}, u32[]{:S(2)}) copy-start(bf16[1536,1024]{1,0:T(8,128)(2,1)} %copy-done.1) | copy-start | bytes 9437188
  20.4 32.8 %copy-start.5 = (s32[8,1536]{1,0:T(8,128)S(1)}, s32[8,1536]{1,0:T(8,128)}, u32[]{:S(2)}) copy-start(s32[8,1536]{1,0:T(8,128)} %param.7) | copy-start | bytes 147460
  177.9 5.8 %copy-start.3 = (f32[64,1024]{1,0:T(8,128)}, f32[64,1024]{1,0:T(8,128)S(1)}, u32[]{:S(2)}) copy-start(f32[64,1024]{1,0:T(8,128)S(1)} %add_divide_fusion) | copy-start | bytes 786436
Sparse Core Ops, SparseCore 0:
  15.9 37.3 all-reduce.3
  58.2 116.6 all-reduce.5
where the time goes:
time: 191 us; the launch traced here: 190 us
  waiting for transfers between devices  148 us (77%)
  matrix products  18.4 us (10%)
  between operations  14.1 us (7%)
  other arithmetic  6.02 us (3%)
  local copies, waits for them, and re-layouts  3.52 us (2%)
    psum x1, waiting for transfers between devices, local(): lax.psum(jnp.einsum('bfr,rk->bfk', one_hot, sketch, preferred_element_typ...  117 us
    psum x1, waiting for transfers between devices, local(): lax.psum(partial_sketch, 'feat').astype(jnp.float32).astype(jnp.bfloat16)  31.4 us
    dot_general x1, matrix products, local(): jnp.einsum('lr,lc->rc', leaf_hot.astype(jnp.float32), leaf_values, precis...  5.75 us
    convert_element_type x1, other arithmetic, local(): gradient = (labels.astype(jnp.float32) - probability).astype(jnp.bfloat16)  4.95 us
    dot_general x1, matrix products, local(): jnp.einsum('bfr,rk->bfk', one_hot, sketch, preferred_element_type=jnp.flo...  4.84 us
    dot_general x1, matrix products, local(): jnp.dot(leaf_weights, hessian, preferred_element_type=jnp.float32)  4.59 us
  transfers between devices with their start and end apart: 2, of which 2 were waited for; matrix products, arithmetic and copies ran while one was open for 3% of the time, Pallas kernels for 0%

commit v1 on v0

v1 whole, which is shorter than its diff:
```python
import functools

import jax
import jax.numpy as jnp
from jax import lax
from jax.experimental import pallas as pl
from jax.experimental.pallas import tpu as pltpu
from jax.sharding import PartitionSpec as P

BINS = 256
LEAVES = 64


shrinkage = 0.5
ridge_term = 1.0

f32 = jnp.float32
bf16 = jnp.bfloat16
VMEM_LIMIT = 48 * 1024 * 1024


def block_rows(rows):
    for size in (256, 128, 64, 32, 16):
        if rows % size == 0:
            return size
    return rows


def swap(x, axis, size, by):
    return lax.ppermute(x, axis, [(i, i ^ by) for i in range(size)])


def rows_kernel(core_ref, pred_ref, lab_ref, leaf_ref, w_ref, *rest, first):
    if first:
        sk_refs, (g_ref, h_ref) = rest[:-2], rest[-2:]
    else:
        (g0_ref, h0_ref), sk_refs, (g_ref, h_ref) = rest[:2], rest[2:-2], rest[-2:]
    step = pl.program_id(0)

    @pl.when(step == 0)
    def _():
        if first:
            g_ref[...] = jnp.zeros_like(g_ref)
            h_ref[...] = jnp.zeros_like(h_ref)
        else:
            g_ref[...] = g0_ref[...]
            h_ref[...] = h0_ref[...]

    t = jnp.tanh(pred_ref[...].astype(f32) * 0.5)
    grad = ((lab_ref[...].astype(f32) - 0.5) - 0.5 * t).astype(bf16)
    hess = (0.25 - 0.25 * t * t).astype(bf16)
    sketch = jnp.dot(grad, w_ref[...], preferred_element_type=f32)
    width = sk_refs[0].shape[1]
    for i, ref in enumerate(sk_refs):
        ref[...] = sketch[:, i * width:(i + 1) * width].astype(bf16)
    blk = pred_ref.shape[0]
    hot = (lax.broadcasted_iota(jnp.int32, (LEAVES, blk), 0) == leaf_ref[0]).astype(f32).astype(bf16)
    g_ref[...] += jnp.dot(hot, grad, preferred_element_type=f32)
    h_ref[...] += jnp.dot(hot, hess, preferred_element_type=f32)


def rows_pass(which, pred, lab, leaf, w, before, parts):
    rows, cols = pred.shape
    half = rows // 2
    blk = block_rows(half)
    steps = half // blk
    width = w.shape[1] // parts
    first = before is None
    row_map = lambda i, c: (c[0] * steps + i, 0)
    fixed = lambda i, c: (0, 0)
    sums = pl.BlockSpec((LEAVES, cols), fixed)
    in_specs = [
        pl.BlockSpec((blk, cols), row_map),
        pl.BlockSpec((blk, cols), row_map),
        pl.BlockSpec((1, 1, blk), lambda i, c: (c[0] * steps + i, 0, 0)),
        pl.BlockSpec(w.shape, fixed),
    ]
    args = [pred, lab, leaf.reshape(rows // blk, 1, blk), w]
    if not first:
        in_specs += [sums, sums]
        args += list(before)
    out = pl.pallas_call(
        functools.partial(rows_kernel, first=first),
        grid_spec=pltpu.PrefetchScalarGridSpec(
            num_scalar_prefetch=1,
            grid=(steps,),
            in_specs=in_specs,
            out_specs=[pl.BlockSpec((blk, width), lambda i, c: (i, 0))] * parts + [sums, sums],
        ),
        out_shape=[jax.ShapeDtypeStruct((half, width), bf16)] * parts
        + [jax.ShapeDtypeStruct((LEAVES, cols), f32)] * 2,
        compiler_params=pltpu.CompilerParams(vmem_limit_bytes=VMEM_LIMIT),
        name="rows_first" if first else "rows_second",
    )(which, *args)
    return out[:parts], tuple(out[parts:])


def hist_kernel(codes_ref, own_ref, other_ref, out_ref, *, per, odd):
    feats = codes_ref.shape[1]
    half = codes_ref.shape[2]
    codes = codes_ref[...].astype(f32).astype(bf16)
    base = (2 * pl.program_id(0) + odd) * per
    levels = (lax.broadcasted_iota(jnp.int32, (per, 1, 1), 0) + base).astype(f32).astype(bf16)
    one = jnp.ones((), bf16)
    zero = jnp.zeros((), bf16)
    total = None
    for part, ref in ((0, own_ref), (1, other_ref)):
        hot = jnp.where(codes[part][None] == levels, one, zero).reshape(per * feats, half)
        term = jnp.dot(hot, ref[...], preferred_element_type=f32)
        total = term if total is None else total + term
    out_ref[0] = total.astype(out_ref.dtype)


def hist_pass(codes, own, other, per, blocks, odd, dtype):
    feats = codes.shape[1]
    width = own.shape[1]
    whole = lambda a: pl.BlockSpec(a.shape, lambda i: (0,) * a.ndim)
    return pl.pallas_call(
        functools.partial(hist_kernel, per=per, odd=odd),
        grid=(blocks,),
        in_specs=[whole(codes), whole(own), whole(other)],
        out_specs=pl.BlockSpec((1, per * feats, width), lambda i: (i, 0, 0)),
        out_shape=jax.ShapeDtypeStruct((blocks, per * feats, width), dtype),
        compiler_params=pltpu.CompilerParams(vmem_limit_bytes=VMEM_LIMIT),
        name="hist_send" if odd else "hist_keep",
    )(codes, own, other)


def update_kernel(me_ref, pred_ref, leaf_ref, table_ref, new_ref, values_ref):
    n = table_ref.shape[0]

    @pl.when(pl.program_id(0) == 0)
    def _():
        for d in range(n):
            values_ref[d] = table_ref[d ^ me_ref[0]]

    blk = pred_ref.shape[0]
    table = table_ref[...].reshape(LEAVES, table_ref.shape[2])
    hot = (lax.broadcasted_iota(jnp.int32, (LEAVES, blk), 0) == leaf_ref[0]).astype(f32).astype(bf16)
    found = lax.dot_general(hot, table.astype(bf16), (((0,), (0,)), ((), ())), preferred_element_type=f32)
    new_ref[...] = (pred_ref[...].astype(f32) + shrinkage * found).astype(bf16)


def update_pass(me, pred, leaf, table):
    rows, cols = pred.shape
    blk = block_rows(rows)
    return pl.pallas_call(
        update_kernel,
        grid_spec=pltpu.PrefetchScalarGridSpec(
            num_scalar_prefetch=1,
            grid=(rows // blk,),
            in_specs=[
                pl.BlockSpec((blk, cols), lambda i, m: (i, 0)),
                pl.BlockSpec((1, 1, blk), lambda i, m: (i, 0, 0)),
                pl.BlockSpec(table.shape, lambda i, m: (0, 0, 0)),
            ],
            out_specs=[
                pl.BlockSpec((blk, cols), lambda i, m: (i, 0)),
                pl.BlockSpec(table.shape, lambda i, m: (0, 0, 0)),
            ],
        ),
        out_shape=[
            jax.ShapeDtypeStruct((rows, cols), bf16),
            jax.ShapeDtypeStruct(table.shape, f32),
        ],
        compiler_params=pltpu.CompilerParams(vmem_limit_bytes=VMEM_LIMIT),
        name="update",
    )(me, pred, leaf.reshape(rows // blk, 1, blk), table)


def local(n, nf, predictions, labels, feature_codes, leaf_index, sketch_weight):
    rows, cols = predictions.shape
    feats = feature_codes.shape[0]
    half = rows // 2
    parts = 2
    me = lax.axis_index("rows")
    core = lax.axis_index("feat") & 1
    per = BINS // n
    leaf_per = LEAVES // n
    leaf = leaf_index ^ (me * leaf_per)
    codes = (feature_codes ^ (me * per)).reshape(feats, 2, half)
    codes = jnp.where(core == 0, codes, codes[:, ::-1]).swapaxes(0, 1)

    send, sums = rows_pass((1 - core).reshape(1), predictions, labels, leaf, sketch_weight, None, parts)
    got = [swap(s, "feat", nf, 1) for s in send]
    keep, sums = rows_pass(core.reshape(1), predictions, labels, leaf, sketch_weight, sums, parts)

    grad, hess = (s.reshape(n, leaf_per, cols) for s in sums)
    both = jnp.concatenate([grad, hess], axis=1)
    both16 = both.astype(bf16)
    total = both[0]
    for t in range(1, n):
        total = total + swap(both16[t], "rows", n, t).astype(f32)
    values = (total[:leaf_per] / (total[leaf_per:] + ridge_term)).astype(bf16)
    table = jnp.stack([values] + [swap(values, "rows", n, t) for t in range(1, n)]).astype(f32)
    updated, leaf_values = update_pass(me.reshape(1), predictions, leaf, table)

    finals = []
    for p in range(parts):
        pair = (keep[p].astype(f32) + got[p].astype(f32)).astype(bf16)
        acc = pair.astype(f32)
        for t in range(2, nf, 2):
            acc = acc + swap(pair, "feat", nf, t).astype(f32)
        own = acc.astype(bf16)
        other = swap(own, "feat", nf, 1)
        away = hist_pass(codes, own, other, per, n // 2, 1, bf16)
        back = swap(away, "rows", n, 1)
        here = hist_pass(codes, own, other, per, n // 2, 0, bf16)
        acc = here.astype(f32) + back.astype(f32)
        acc16 = acc.astype(bf16)
        final = acc[0]
        for t in range(1, n // 2):
            final = final + swap(acc16[t], "rows", n, 2 * t).astype(f32)
        finals.append(final.reshape(per, feats, -1))
    histograms = jnp.concatenate(finals, axis=2)
    return histograms, leaf_values.reshape(LEAVES, cols), updated


def solution(mesh):
    n, nf = mesh.shape["rows"], mesh.shape["feat"]
    return jax.shard_map(
        functools.partial(local, n, nf),
        mesh=mesh,
        in_specs=(
            P("rows", "feat"),
            P("rows", "feat"),
            P("feat", "rows"),
            P("rows"),
            P("feat", None),
        ),
        out_specs=(P("rows", "feat", None), P(None, "feat"), P("rows", "feat")),
        check_vma=False,
    )
```

time: 191 us -> 87.8 us (0.46)
  waiting for transfers between devices: 148 us -> 21.3 us
  starting transfers between devices: 0.08 us -> 39.4 us
  matrix products: 18.4 us -> 0 us
  Pallas kernels: 0 us -> 16.5 us
  between operations: 14.1 us -> 0.96 us
    psum x2 -> x0, waiting for transfers between devices: 148 us -> none  [the longest x1 117 us: local(): lax.psum(jnp.einsum('bfr,rk->bfk', one_hot, sketch, preferred_element_typ...]
    ppermute x0 -> x28, starting transfers between devices: none -> 39.4 us  [swap(): return lax.ppermute(x, axis, [(i, i ^ by) for i in range(size)])]
    ppermute x0 -> x28, waiting for transfers between devices: none -> 21.3 us  [swap(): return lax.ppermute(x, axis, [(i, i ^ by) for i in range(size)])]
    dot_general x5 -> x0, matrix products: 18.4 us -> none  [the longest x1 5.75 us: local(): jnp.einsum('lr,lc->rc', leaf_hot.astype(jnp.float32), leaf_values, precis...]
    pallas_call x0 -> x7, Pallas kernels: none -> 16.5 us  [the longest x2 6.95 us: rows_pass(): pl.pallas_call(functools.partial(rows_kernel, first=first), grid_spec=plt...]
    convert_element_type x1 -> x8, other arithmetic: 4.95 us -> 2.29 us  [the longest x2 1.99 us: local(): pair = (keep[p].astype(f32) + got[p].astype(f32)).astype(bf16)]
  transfers between devices with their start and end apart: 2 -> 28, of which waited for: 2 -> 12; matrix products, arithmetic and copies ran while one was open for 3% -> 4% of each run, Pallas kernels for 0% -> 11%
where the time goes in v1:
time: 87.8 us; the launch traced here: 87.3 us
  starting transfers between devices  39.4 us (45%)
  waiting for transfers between devices  21.3 us (24%)
  Pallas kernels  16.5 us (19%)
  other arithmetic  4.71 us (5%)
  local copies, waits for them, and re-layouts  4.4 us (5%)
  between operations  0.96 us (1%)
    ppermute x28, starting transfers between devices, swap(): return lax.ppermute(x, axis, [(i, i ^ by) for i in range(size)])  39.4 us
    ppermute x28, waiting for transfers between devices, swap(): return lax.ppermute(x, axis, [(i, i ^ by) for i in range(size)])  21.3 us
    pallas_call x2, Pallas kernels, rows_pass(): pl.pallas_call(functools.partial(rows_kernel, first=first), grid_spec=plt...  6.95 us
    pallas_call x4, Pallas kernels, hist_pass(): pl.pallas_call(functools.partial(hist_kernel, per=per, odd=odd), grid=(bl...  5.83 us
    pallas_call x1, Pallas kernels, update_pass(): pl.pallas_call(update_kernel, grid_spec=pltpu.PrefetchScalarGridSpec(num_...  3.74 us
    unnamed x26, local copies, waits for them, and re-layouts  3.68 us
    convert_element_type x2, other arithmetic, local(): pair = (keep[p].astype(f32) + got[p].astype(f32)).astype(bf16)  1.99 us
  transfers between devices with their start and end apart: 28, of which 12 were waited for; matrix products, arithmetic and copies ran while one was open for 4% of the time, Pallas kernels for 11%

profile of v1, /device:TPU:0, one launch (start us, length us, event | category | flops | bytes accessed | tf_op | source)
XLA Modules:
  0.0 87.3 jit_solution(10172434497179523717)
XLA Ops:
  0.6 0.7 broadcast_xor_fusion.1
  1.4 1.9 %copy-done = bf16[1536,1024]{1,0:T(8,128)(2,1)S(1)} copy-done((bf16[1536,1024]{1,0:T(8,128)(2,1)S(1)}, bf16[1536,1024]{1,0:T(8,128)(2,1)}, u32[]{:S(2)}) %copy-start) | copy-done | bytes 3145752
  3.2 1.0 %copy-done.2 = bf16[1024,256]{1,0:T(8,128)(2,1)S(1)} copy-done((bf16[1024,256]{1,0:T(8,128)(2,1)S(1)}, bf16[1024,256]{1,0:T(8,128)(2,1)}, u32[]{:S(2)}) %copy-start.2) | copy-done | bytes 524312
  4.3 3.5 %rows_first.1 = (bf16[768,128]{1,0:T(8,128)(2,1)S(1)}, bf16[768,128]{1,0:T(8,128)(2,1)S(1)}, f32[64,1024]{1,0:T(8,128)S(1)}, f32[64,1024]{1,0:T(8,128)S(1)}) custom-call(s32[1]{0:T(128)} %bitcast.3.core_ref, bf16[1536,1024]{1,0:T(8,128)(2,1)S(1)} %copy-done, bf16[1536,1024]{1,0:T(8,128)(2,1)} %lab_ref.3, s32[6,1,256]{2,1,0:T(1,128)S(1)} %reshape.40.leaf_ref, ...), custom_call_target="tpu_custom_call" | custom-call | tf_op jit(solution)/shard_map/rows_first/pallas_call | solution.py:82
  7.8 3.5 %rows_second.1 = (bf16[768,128]{1,0:T(8,128)(2,1)S(1)}, bf16[768,128]{1,0:T(8,128)(2,1)S(1)}, f32[64,1024]{1,0:T(8,128)S(1)}, f32[64,1024]{1,0:T(8,128)S(1)}) custom-call(s32[1]{0:T(128)} %bitcast.2.core_ref, bf16[1536,1024]{1,0:T(8,128)(2,1)S(1)} %copy-done.1, bf16[1536,1024]{1,0:T(8,128)(2,1)} %lab_ref.3, s32[6,1,256]{2,1,0:T(1,128)S(1)} %reshape.40.leaf_ref, ...), custom_call_target="tpu_custom_call" | custom-call | tf_op jit(solution)/shard_map/rows_second/pallas_call | solution.py:82
  11.4 0.7 copy-done.4
  12.1 0.7 slice_bitcast_fusion.14
  12.8 2.9 %collective-permute-start.14 = (bf16[16,1024]{1,0:T(8,128)(2,1)}, bf16[16,1024]{1,0:T(8,128)(2,1)}, u32[]{:S(2)}, u32[]{:S(2)}) collective-permute-start(bf16[16,1024]{1,0:T(8,128)(2,1)} %get-tuple-element.29), channel_id=1, source_target_pairs={{0,4},{4,0},{8,12},{12,8},{16,20},{20,16},{24,28},{28,24},{1,5},{5... | collective-permute-start | bytes 98312 | tf_op jit(solution)/shard_map/ppermute | solution.py:30
  15.7 3.6 %collective-permute-start.20 = (bf16[16,1024]{1,0:T(8,128)(2,1)S(1)}, bf16[16,1024]{1,0:T(8,128)(2,1)}, u32[]{:S(2)}, u32[]{:S(2)}) collective-permute-start(bf16[16,1024]{1,0:T(8,128)(2,1)S(1)} %get-tuple-element.30), channel_id=1, source_target_pairs={{0,28},{4,24},{8,20},{12,16},{16,12},{20,8},{24,4},{28,0},{1,29},{... | collective-permute-start | bytes 98312 | tf_op jit(solution)/shard_map/ppermute | solution.py:30
  19.3 1.9 %collective-permute-start.18 = (bf16[16,1024]{1,0:T(8,128)(2,1)}, bf16[16,1024]{1,0:T(8,128)(2,1)}, u32[]{:S(2)}, u32[]{:S(2)}) collective-permute-start(bf16[16,1024]{1,0:T(8,128)(2,1)} %get-tuple-element.32), channel_id=1, source_target_pairs={{0,20},{4,16},{8,28},{12,24},{16,4},{20,0},{24,12},{28,8},{1,21},{... | collective-permute-start | bytes 98312 | tf_op jit(solution)/shard_map/ppermute | solution.py:30
  21.2 2.1 %collective-permute-start.17 = (bf16[16,1024]{1,0:T(8,128)(2,1)}, bf16[16,1024]{1,0:T(8,128)(2,1)}, u32[]{:S(2)}, u32[]{:S(2)}) collective-permute-start(bf16[16,1024]{1,0:T(8,128)(2,1)} %get-tuple-element.33), channel_id=1, source_target_pairs={{0,16},{4,20},{8,24},{12,28},{16,0},{20,4},{24,8},{28,12},{1,17},{... | collective-permute-start | bytes 98312 | tf_op jit(solution)/shard_map/ppermute | solution.py:30
  23.4 1.2 %collective-permute-start.16 = (bf16[16,1024]{1,0:T(8,128)(2,1)}, bf16[16,1024]{1,0:T(8,128)(2,1)}, u32[]{:S(2)}, u32[]{:S(2)}) collective-permute-start(bf16[16,1024]{1,0:T(8,128)(2,1)} %get-tuple-element.34), channel_id=1, source_target_pairs={{0,12},{4,8},{8,4},{12,0},{16,28},{20,24},{24,20},{28,16},{1,13},{... | collective-permute-start | bytes 98312 | tf_op jit(solution)/shard_map/ppermute | solution.py:30
  24.6 0.6 collective-permute-start.15
  25.4 0.5 collective-permute-start.7
  26.4 2.1 %collective-permute-done.16 = bf16[16,1024]{1,0:T(8,128)(2,1)} collective-permute-done((bf16[16,1024]{1,0:T(8,128)(2,1)}, bf16[16,1024]{1,0:T(8,128)(2,1)}, u32[]{:S(2)}, u32[]{:S(2)}) %collective-permute-start.16) | collective-permute-done | bytes 32800 | tf_op jit(solution)/shard_map/ppermute | solution.py:30
  28.6 0.9 %fusion.17 = f32[16,1024]{1,0:T(8,128)S(1)} fusion(f32[8,8,1024]{2,1,0:T(8,128)S(1)} %bitcast.92, f32[8,8,1024]{2,1,0:T(8,128)} %bitcast.94, bf16[16,1024]{1,0:T(8,128)(2,1)} %collective-permute-done.20, bf16[16,1024]{1,0:T(8,128)(2,1)} %collective-permute-done.19, bf16[16,1024]{1,0:T(8,128)(2,1)} %collective-permute-done.18, ...), kind=kLoop, calls=%fused_computation.30 | loop fusion | flops 245760 | bytes 819200 | tf_op jit(solution)/shard_map/add | solution.py:193
  29.6 1.5 %collective-permute-start.21 = (bf16[8,1024]{1,0:T(8,128)(2,1)S(1)}, bf16[8,1024]{1,0:T(8,128)(2,1)S(1)}, u32[]{:S(2)}, u32[]{:S(2)}) collective-permute-start(bf16[8,1024]{1,0:T(8,128)(2,1)S(1)} %get-tuple-element.24), channel_id=1, source_target_pairs={{0,4},{4,0},{8,12},{12,8},{16,20},{20,16},{24,28},{28,24},{1,5},{5... | collective-permute-start | bytes 49160 | tf_op jit(solution)/shard_map/ppermute | solution.py:30
  31.1 2.9 %collective-permute-start.26 = (bf16[8,1024]{1,0:T(8,128)(2,1)S(1)}, bf16[8,1024]{1,0:T(8,128)(2,1)S(1)}, u32[]{:S(2)}, u32[]{:S(2)}) collective-permute-start(bf16[8,1024]{1,0:T(8,128)(2,1)S(1)} %get-tuple-element.24), channel_id=1, source_target_pairs={{0,24},{4,28},{8,16},{12,20},{16,8},{20,12},{24,0},{28,4},{1,25},{... | collective-permute-start | bytes 49160 | tf_op jit(solution)/shard_map/ppermute | solution.py:30
  34.1 1.4 %collective-permute-start.22 = (bf16[8,1024]{1,0:T(8,128)(2,1)S(1)}, bf16[8,1024]{1,0:T(8,128)(2,1)S(1)}, u32[]{:S(2)}, u32[]{:S(2)}) collective-permute-start(bf16[8,1024]{1,0:T(8,128)(2,1)S(1)} %get-tuple-element.24), channel_id=1, source_target_pairs={{0,8},{4,12},{8,0},{12,4},{16,24},{20,28},{24,16},{28,20},{1,9},{5... | collective-permute-start | bytes 49160 | tf_op jit(solution)/shard_map/ppermute | solution.py:30
  35.5 2.3 %collective-permute-done.22 = bf16[8,1024]{1,0:T(8,128)(2,1)S(1)} collective-permute-done((bf16[8,1024]{1,0:T(8,128)(2,1)S(1)}, bf16[8,1024]{1,0:T(8,128)(2,1)S(1)}, u32[]{:S(2)}, u32[]{:S(2)}) %collective-permute-start.22) | collective-permute-done | bytes 16416 | tf_op jit(solution)/shard_map/ppermute | solution.py:30
  37.8 2.3 %collective-permute-start.23 = (bf16[8,1024]{1,0:T(8,128)(2,1)S(1)}, bf16[8,1024]{1,0:T(8,128)(2,1)S(1)}, u32[]{:S(2)}, u32[]{:S(2)}) collective-permute-start(bf16[8,1024]{1,0:T(8,128)(2,1)S(1)} %get-tuple-element.24), channel_id=1, source_target_pairs={{0,12},{4,8},{8,4},{12,0},{16,28},{20,24},{24,20},{28,16},{1,13},{... | collective-permute-start | bytes 49160 | tf_op jit(solution)/shard_map/ppermute | solution.py:30
  40.1 2.3 %collective-permute-done.23 = bf16[8,1024]{1,0:T(8,128)(2,1)S(1)} collective-permute-done((bf16[8,1024]{1,0:T(8,128)(2,1)S(1)}, bf16[8,1024]{1,0:T(8,128)(2,1)S(1)}, u32[]{:S(2)}, u32[]{:S(2)}) %collective-permute-start.23) | collective-permute-done | bytes 16416 | tf_op jit(solution)/shard_map/ppermute | solution.py:30
  42.5 3.4 %collective-permute-start.24 = (bf16[8,1024]{1,0:T(8,128)(2,1)S(1)}, bf16[8,1024]{1,0:T(8,128)(2,1)S(1)}, u32[]{:S(2)}, u32[]{:S(2)}) collective-permute-start(bf16[8,1024]{1,0:T(8,128)(2,1)S(1)} %get-tuple-element.24), channel_id=1, source_target_pairs={{0,16},{4,20},{8,24},{12,28},{16,0},{20,4},{24,8},{28,12},{1,17},{... | collective-permute-start | bytes 49160 | tf_op jit(solution)/shard_map/ppermute | solution.py:30
  45.9 1.7 %collective-permute-done.24 = bf16[8,1024]{1,0:T(8,128)(2,1)S(1)} collective-permute-done((bf16[8,1024]{1,0:T(8,128)(2,1)S(1)}, bf16[8,1024]{1,0:T(8,128)(2,1)S(1)}, u32[]{:S(2)}, u32[]{:S(2)}) %collective-permute-start.24) | collective-permute-done | bytes 16416 | tf_op jit(solution)/shard_map/ppermute | solution.py:30
  47.6 3.3 %collective-permute-start.27 = (bf16[8,1024]{1,0:T(8,128)(2,1)S(1)}, bf16[8,1024]{1,0:T(8,128)(2,1)S(1)}, u32[]{:S(2)}, u32[]{:S(2)}) collective-permute-start(bf16[8,1024]{1,0:T(8,128)(2,1)S(1)} %get-tuple-element.24), channel_id=1, source_target_pairs={{0,28},{4,24},{8,20},{12,16},{16,12},{20,8},{24,4},{28,0},{1,29},{... | collective-permute-start | bytes 49160 | tf_op jit(solution)/shard_map/ppermute | solution.py:30
  50.9 1.0 %add_convert_fusion.1 = bf16[768,128]{1,0:T(8,128)(2,1)S(1)} fusion(bf16[768,128]{1,0:T(8,128)(2,1)S(1)} %collective-permute-done.7, bf16[768,128]{1,0:T(8,128)(2,1)} %copy-done.6), kind=kLoop, calls=%fused_computation.7 | loop fusion | flops 393216 | bytes 589824 | tf_op jit(solution)/shard_map/convert_element_type | solution.py:200
  51.9 1.6 %collective-permute-start.8 = (bf16[768,128]{1,0:T(8,128)(2,1)S(1)}, bf16[768,128]{1,0:T(8,128)(2,1)S(1)}, u32[]{:S(2)}, u32[]{:S(2)}) collective-permute-start(bf16[768,128]{1,0:T(8,128)(2,1)S(1)} %add_convert_fusion.1), channel_id=1, source_target_pairs={{0,2},{1,3},{2,0},{3,1},{4,6},{5,7},{6,4},{7,5},{8,10},{9,11},{10,... | collective-permute-start | bytes 589832 | tf_op jit(solution)/shard_map/ppermute | solution.py:30
  53.5 1.0 %add_convert_fusion.3 = bf16[768,128]{1,0:T(8,128)(2,1)S(1)} fusion(bf16[768,128]{1,0:T(8,128)(2,1)S(1)} %collective-permute-done, bf16[768,128]{1,0:T(8,128)(2,1)} %copy-done.5), kind=kLoop, calls=%fused_computation.9 | loop fusion | flops 393216 | bytes 589824 | tf_op jit(solution)/shard_map/convert_element_type | solution.py:200
  54.5 0.6 collective-permute-start.1
  55.0 2.6 %collective-permute-done.8 = bf16[768,128]{1,0:T(8,128)(2,1)S(1)} collective-permute-done((bf16[768,128]{1,0:T(8,128)(2,1)S(1)}, bf16[768,128]{1,0:T(8,128)(2,1)S(1)}, u32[]{:S(2)}, u32[]{:S(2)}) %collective-permute-start.8) | collective-permute-done | bytes 196640 | tf_op jit(solution)/shard_map/ppermute | solution.py:30
  57.8 1.4 %collective-permute-done.9.other_ref = bf16[768,128]{1,0:T(8,128)(2,1)S(1)} collective-permute-done((bf16[768,128]{1,0:T(8,128)(2,1)S(1)}, bf16[768,128]{1,0:T(8,128)(2,1)S(1)}, u32[]{:S(2)}, u32[]{:S(2)}) %collective-permute-start.9) | collective-permute-done | bytes 196640 | tf_op jit(solution)/shard_map/ppermute | solution.py:30
  59.2 1.5 %hist_send.3 = bf16[4,256,128]{2,1,0:T(8,128)(2,1)S(1)} custom-call(s32[2,8,768]{2,1,0:T(8,128)S(1)} %fusion.18.codes_ref, bf16[768,128]{1,0:T(8,128)(2,1)S(1)} %add_convert_fusion.own_ref, bf16[768,128]{1,0:T(8,128)(2,1)S(1)} %collective-permute-done.9.other_ref), custom_call_target="tpu_custom_call" | custom-call | tf_op jit(solution)/shard_map/hist_send/pallas_call | solution.py:118
  60.7 0.7 collective-permute-start.10
  61.5 3.7 %update.1 = (bf16[1536,1024]{1,0:T(8,128)(2,1)}, f32[8,8,1024]{2,1,0:T(8,128)}) custom-call(s32[1]{0:T(128)} %bitcast.14.me_ref, bf16[1536,1024]{1,0:T(8,128)(2,1)S(1)} %copy-done.1, s32[6,1,256]{2,1,0:T(1,128)S(1)} %reshape.40.leaf_ref, f32[8,8,1024]{2,1,0:T(8,128)S(1)} %convert_element_type.135.table_ref), custom_call_target="tpu_custom_call" | custom-call | tf_op jit(solution)/shard_map/update/pallas_call | solution.py:147
  65.3 1.5 %hist_send.2 = bf16[4,256,128]{2,1,0:T(8,128)(2,1)S(1)} custom-call(s32[2,8,768]{2,1,0:T(8,128)S(1)} %fusion.18.codes_ref, bf16[768,128]{1,0:T(8,128)(2,1)S(1)} %add_convert_fusion.2.own_ref, bf16[768,128]{1,0:T(8,128)(2,1)S(1)} %collective-permute-done.2.other_ref), custom_call_target="tpu_custom_call" | custom-call | tf_op jit(solution)/shard_map/hist_send/pallas_call | solution.py:118
  66.7 1.5 %collective-permute-start.3 = (bf16[4,256,128]{2,1,0:T(8,128)(2,1)S(1)}, bf16[4,256,128]{2,1,0:T(8,128)(2,1)S(1)}, u32[]{:S(2)}, u32[]{:S(2)}) collective-permute-start(bf16[4,256,128]{2,1,0:T(8,128)(2,1)S(1)} %hist_send.2), channel_id=1, source_target_pairs={{0,4},{4,0},{8,12},{12,8},{16,20},{20,16},{24,28},{28,24},{1,5},{5... | collective-permute-start | bytes 786440 | tf_op jit(solution)/shard_map/ppermute | solution.py:30
  68.2 1.5 %hist_keep.2 = bf16[4,256,128]{2,1,0:T(8,128)(2,1)S(1)} custom-call(s32[2,8,768]{2,1,0:T(8,128)S(1)} %fusion.18.codes_ref, bf16[768,128]{1,0:T(8,128)(2,1)S(1)} %add_convert_fusion.2.own_ref, bf16[768,128]{1,0:T(8,128)(2,1)S(1)} %collective-permute-done.2.other_ref), custom_call_target="tpu_custom_call" | custom-call | tf_op jit(solution)/shard_map/hist_keep/pallas_call | solution.py:118
  69.7 1.5 %hist_keep.3 = bf16[4,256,128]{2,1,0:T(8,128)(2,1)S(1)} custom-call(s32[2,8,768]{2,1,0:T(8,128)S(1)} %fusion.18.codes_ref, bf16[768,128]{1,0:T(8,128)(2,1)S(1)} %add_convert_fusion.own_ref, bf16[768,128]{1,0:T(8,128)(2,1)S(1)} %collective-permute-done.9.other_ref), custom_call_target="tpu_custom_call" | custom-call | tf_op jit(solution)/shard_map/hist_keep/pallas_call | solution.py:118
  71.3 0.6 collective-permute-start.11
  71.9 0.9 %collective-permute-start.13 = (bf16[256,128]{1,0:T(8,128)(2,1)S(1)}, bf16[256,128]{1,0:T(8,128)(2,1)S(1)}, u32[]{:S(2)}, u32[]{:S(2)}) collective-permute-start(bf16[256,128]{1,0:T(8,128)(2,1)S(1)} %get-tuple-element.40), channel_id=1, source_target_pairs={{0,24},{4,28},{8,16},{12,20},{16,8},{20,12},{24,0},{28,4},{1,25},{... | collective-permute-start | bytes 196616 | tf_op jit(solution)/shard_map/ppermute | solution.py:30
  72.8 2.0 %collective-permute-start.12 = (bf16[256,128]{1,0:T(8,128)(2,1)S(1)}, bf16[256,128]{1,0:T(8,128)(2,1)S(1)}, u32[]{:S(2)}, u32[]{:S(2)}) collective-permute-start(bf16[256,128]{1,0:T(8,128)(2,1)S(1)} %get-tuple-element.41), channel_id=1, source_target_pairs={{0,16},{4,20},{8,24},{12,28},{16,0},{20,4},{24,8},{28,12},{1,17},{... | collective-permute-start | bytes 196616 | tf_op jit(solution)/shard_map/ppermute | solution.py:30
  74.8 0.7 collective-permute-done.3
  75.6 1.1 %collective-permute-start.4 = (bf16[256,128]{1,0:T(8,128)(2,1)S(1)}, bf16[256,128]{1,0:T(8,128)(2,1)S(1)}, u32[]{:S(2)}, u32[]{:S(2)}) collective-permute-start(bf16[256,128]{1,0:T(8,128)(2,1)S(1)} %get-tuple-element.36), channel_id=1, source_target_pairs={{0,8},{4,12},{8,0},{12,4},{16,24},{20,28},{24,16},{28,20},{1,9},{5... | collective-permute-start | bytes 196616 | tf_op jit(solution)/shard_map/ppermute | solution.py:30
  76.7 0.6 collective-permute-start.6
  77.3 1.8 %collective-permute-start.5 = (bf16[256,128]{1,0:T(8,128)(2,1)S(1)}, bf16[256,128]{1,0:T(8,128)(2,1)S(1)}, u32[]{:S(2)}, u32[]{:S(2)}) collective-permute-start(bf16[256,128]{1,0:T(8,128)(2,1)S(1)} %get-tuple-element.38), channel_id=1, source_target_pairs={{0,16},{4,20},{8,24},{12,28},{16,0},{20,4},{24,8},{28,12},{1,17},{... | collective-permute-start | bytes 196616 | tf_op jit(solution)/shard_map/ppermute | solution.py:30
  79.2 5.6 %collective-permute-done.12 = bf16[256,128]{1,0:T(8,128)(2,1)S(1)} collective-permute-done((bf16[256,128]{1,0:T(8,128)(2,1)S(1)}, bf16[256,128]{1,0:T(8,128)(2,1)S(1)}, u32[]{:S(2)}, u32[]{:S(2)}) %collective-permute-start.12) | collective-permute-done | bytes 65568 | tf_op jit(solution)/shard_map/ppermute | solution.py:30
  84.8 1.8 %collective-permute-done.5 = bf16[256,128]{1,0:T(8,128)(2,1)S(1)} collective-permute-done((bf16[256,128]{1,0:T(8,128)(2,1)S(1)}, bf16[256,128]{1,0:T(8,128)(2,1)S(1)}, u32[]{:S(2)}, u32[]{:S(2)}) %collective-permute-start.5) | collective-permute-done | bytes 65568 | tf_op jit(solution)/shard_map/ppermute | solution.py:30
  86.6 0.7 pad_maximum_fusion.1
  (62 shorter events, 1.6 us)
Async XLA Ops:
  1.4 1.9 %copy-start = (bf16[1536,1024]{1,0:T(8,128)(2,1)S(1)}, bf16[1536,1024]{1,0:T(8,128)(2,1)}, u32[]{:S(2)}) copy-start(bf16[1536,1024]{1,0:T(8,128)(2,1)} %pred_ref.5) | copy-start | bytes 9437188
  3.2 1.0 %copy-start.2 = (bf16[1024,256]{1,0:T(8,128)(2,1)S(1)}, bf16[1024,256]{1,0:T(8,128)(2,1)}, u32[]{:S(2)}) copy-start(bf16[1024,256]{1,0:T(8,128)(2,1)} %w_ref.3) | copy-start | bytes 1572868
  4.3 3.5 %copy-start.1 = (bf16[1536,1024]{1,0:T(8,128)(2,1)S(1)}, bf16[1536,1024]{1,0:T(8,128)(2,1)}, u32[]{:S(2)}) copy-start(bf16[1536,1024]{1,0:T(8,128)(2,1)} %pred_ref.5) | copy-start | bytes 9437188
  4.3 3.5 %copy-start.3 = (bf16[1024,256]{1,0:T(8,128)(2,1)S(1)}, bf16[1024,256]{1,0:T(8,128)(2,1)}, u32[]{:S(2)}) copy-start(bf16[1024,256]{1,0:T(8,128)(2,1)} %w_ref.3) | copy-start | bytes 1572868
  7.8 3.5 %copy-start.7 = (bf16[768,128]{1,0:T(8,128)(2,1)}, bf16[768,128]{1,0:T(8,128)(2,1)S(1)}, u32[]{:S(2)}) copy-start(bf16[768,128]{1,0:T(8,128)(2,1)S(1)} %get-tuple-element.16) | copy-start | bytes 589828
  7.8 3.5 %copy-start.8 = (bf16[768,128]{1,0:T(8,128)(2,1)}, bf16[768,128]{1,0:T(8,128)(2,1)S(1)}, u32[]{:S(2)}) copy-start(bf16[768,128]{1,0:T(8,128)(2,1)S(1)} %get-tuple-element.18) | copy-start | bytes 589828
  7.8 17.4 %copy-start.9 = (s32[8,1536]{1,0:T(8,128)S(1)}, s32[8,1536]{1,0:T(8,128)}, u32[]{:S(2)}) copy-start(s32[8,1536]{1,0:T(8,128)} %param.7) | copy-start | bytes 147460
  11.3 0.7 copy-start.4
  11.3 0.8 copy-start.5
  11.4 1.4 %copy-start.6 = (bf16[768,128]{1,0:T(8,128)(2,1)}, bf16[768,128]{1,0:T(8,128)(2,1)S(1)}, u32[]{:S(2)}) copy-start(bf16[768,128]{1,0:T(8,128)(2,1)S(1)} %get-tuple-element.17) | copy-start | bytes 589828
  12.8 10.6 %collective-permute-start.14 = (bf16[16,1024]{1,0:T(8,128)(2,1)}, bf16[16,1024]{1,0:T(8,128)(2,1)}, u32[]{:S(2)}, u32[]{:S(2)}) collective-permute-start(bf16[16,1024]{1,0:T(8,128)(2,1)} %get-tuple-element.29), channel_id=1, source_target_pairs={{0,4},{4,0},{8,12},{12,8},{16,20},{20,16},{24,28},{28,24},{1,5},{5... | collective-permute-start | bytes 98312 | tf_op jit(solution)/shard_map/ppermute | solution.py:30
  15.7 8.9 %collective-permute-start.20 = (bf16[16,1024]{1,0:T(8,128)(2,1)S(1)}, bf16[16,1024]{1,0:T(8,128)(2,1)}, u32[]{:S(2)}, u32[]{:S(2)}) collective-permute-start(bf16[16,1024]{1,0:T(8,128)(2,1)S(1)} %get-tuple-element.30), channel_id=1, source_target_pairs={{0,28},{4,24},{8,20},{12,16},{16,12},{20,8},{24,4},{28,0},{1,29},{... | collective-permute-start | bytes 98312 | tf_op jit(solution)/shard_map/ppermute | solution.py:30
  19.3 6.1 %collective-permute-start.19 = (bf16[16,1024]{1,0:T(8,128)(2,1)}, bf16[16,1024]{1,0:T(8,128)(2,1)}, u32[]{:S(2)}, u32[]{:S(2)}) collective-permute-start(bf16[16,1024]{1,0:T(8,128)(2,1)} %get-tuple-element.31), channel_id=1, source_target_pairs={{0,24},{4,28},{8,16},{12,20},{16,8},{20,12},{24,0},{28,4},{1,25},{... | collective-permute-start | bytes 98312 | tf_op jit(solution)/shard_map/ppermute | solution.py:30
  19.3 6.1 %collective-permute-start.18 = (bf16[16,1024]{1,0:T(8,128)(2,1)}, bf16[16,1024]{1,0:T(8,128)(2,1)}, u32[]{:S(2)}, u32[]{:S(2)}) collective-permute-start(bf16[16,1024]{1,0:T(8,128)(2,1)} %get-tuple-element.32), channel_id=1, source_target_pairs={{0,20},{4,16},{8,28},{12,24},{16,4},{20,0},{24,12},{28,8},{1,21},{... | collective-permute-start | bytes 98312 | tf_op jit(solution)/shard_map/ppermute | solution.py:30
  21.2 5.2 %collective-permute-start.17 = (bf16[16,1024]{1,0:T(8,128)(2,1)}, bf16[16,1024]{1,0:T(8,128)(2,1)}, u32[]{:S(2)}, u32[]{:S(2)}) collective-permute-start(bf16[16,1024]{1,0:T(8,128)(2,1)} %get-tuple-element.33), channel_id=1, source_target_pairs={{0,16},{4,20},{8,24},{12,28},{16,0},{20,4},{24,8},{28,12},{1,17},{... | collective-permute-start | bytes 98312 | tf_op jit(solution)/shard_map/ppermute | solution.py:30
  23.4 5.1 %collective-permute-start.16 = (bf16[16,1024]{1,0:T(8,128)(2,1)}, bf16[16,1024]{1,0:T(8,128)(2,1)}, u32[]{:S(2)}, u32[]{:S(2)}) collective-permute-start(bf16[16,1024]{1,0:T(8,128)(2,1)} %get-tuple-element.34), channel_id=1, source_target_pairs={{0,12},{4,8},{8,4},{12,0},{16,28},{20,24},{24,20},{28,16},{1,13},{... | collective-permute-start | bytes 98312 | tf_op jit(solution)/shard_map/ppermute | solution.py:30
  24.6 4.0 %collective-permute-start.15 = (bf16[16,1024]{1,0:T(8,128)(2,1)S(1)}, bf16[16,1024]{1,0:T(8,128)(2,1)}, u32[]{:S(2)}, u32[]{:S(2)}) collective-permute-start(bf16[16,1024]{1,0:T(8,128)(2,1)S(1)} %get-tuple-element.35), channel_id=1, source_target_pairs={{0,8},{4,12},{8,0},{12,4},{16,24},{20,28},{24,16},{28,20},{1,9},{5... | collective-permute-start | bytes 98312 | tf_op jit(solution)/shard_map/ppermute | solution.py:30
  25.4 28.1 %collective-permute-start = (bf16[768,128]{1,0:T(8,128)(2,1)}, bf16[768,128]{1,0:T(8,128)(2,1)S(1)}, u32[]{:S(2)}, u32[]{:S(2)}) collective-permute-start(bf16[768,128]{1,0:T(8,128)(2,1)} %copy-done.7), channel_id=1, source_target_pairs={{0,1},{1,0},{2,3},{3,2},{4,5},{5,4},{6,7},{7,6},{8,9},{9,8},{10,11... | collective-permute-start | bytes 589832 | tf_op jit(solution)/shard_map/ppermute | solution.py:30
  25.4 25.5 %collective-permute-start.7 = (bf16[768,128]{1,0:T(8,128)(2,1)}, bf16[768,128]{1,0:T(8,128)(2,1)S(1)}, u32[]{:S(2)}, u32[]{:S(2)}) collective-permute-start(bf16[768,128]{1,0:T(8,128)(2,1)} %copy-done.8), channel_id=1, source_target_pairs={{0,1},{1,0},{2,3},{3,2},{4,5},{5,4},{6,7},{7,6},{8,9},{9,8},{10,11... | collective-permute-start | bytes 589832 | tf_op jit(solution)/shard_map/ppermute | solution.py:30
  29.6 4.5 %collective-permute-start.21 = (bf16[8,1024]{1,0:T(8,128)(2,1)S(1)}, bf16[8,1024]{1,0:T(8,128)(2,1)S(1)}, u32[]{:S(2)}, u32[]{:S(2)}) collective-permute-start(bf16[8,1024]{1,0:T(8,128)(2,1)S(1)} %get-tuple-element.24), channel_id=1, source_target_pairs={{0,4},{4,0},{8,12},{12,8},{16,20},{20,16},{24,28},{28,24},{1,5},{5... | collective-permute-start | bytes 49160 | tf_op jit(solution)/shard_map/ppermute | solution.py:30
  31.1 26.7 %collective-permute-start.26 = (bf16[8,1024]{1,0:T(8,128)(2,1)S(1)}, bf16[8,1024]{1,0:T(8,128)(2,1)S(1)}, u32[]{:S(2)}, u32[]{:S(2)}) collective-permute-start(bf16[8,1024]{1,0:T(8,128)(2,1)S(1)} %get-tuple-element.24), channel_id=1, source_target_pairs={{0,24},{4,28},{8,16},{12,20},{16,8},{20,12},{24,0},{28,4},{1,25},{... | collective-permute-start | bytes 49160 | tf_op jit(solution)/shard_map/ppermute | solution.py:30
  34.0 16.9 %collective-permute-start.25 = (bf16[8,1024]{1,0:T(8,128)(2,1)S(1)}, bf16[8,1024]{1,0:T(8,128)(2,1)S(1)}, u32[]{:S(2)}, u32[]{:S(2)}) collective-permute-start(bf16[8,1024]{1,0:T(8,128)(2,1)S(1)} %get-tuple-element.24), channel_id=1, source_target_pairs={{0,20},{4,16},{8,28},{12,24},{16,4},{20,0},{24,12},{28,8},{1,21},{... | collective-permute-start | bytes 49160 | tf_op jit(solution)/shard_map/ppermute | solution.py:30
  34.1 3.7 %collective-permute-start.22 = (bf16[8,1024]{1,0:T(8,128)(2,1)S(1)}, bf16[8,1024]{1,0:T(8,128)(2,1)S(1)}, u32[]{:S(2)}, u32[]{:S(2)}) collective-permute-start(bf16[8,1024]{1,0:T(8,128)(2,1)S(1)} %get-tuple-element.24), channel_id=1, source_target_pairs={{0,8},{4,12},{8,0},{12,4},{16,24},{20,28},{24,16},{28,20},{1,9},{5... | collective-permute-start | bytes 49160 | tf_op jit(solution)/shard_map/ppermute | solution.py:30
  37.8 4.6 %collective-permute-start.23 = (bf16[8,1024]{1,0:T(8,128)(2,1)S(1)}, bf16[8,1024]{1,0:T(8,128)(2,1)S(1)}, u32[]{:S(2)}, u32[]{:S(2)}) collective-permute-start(bf16[8,1024]{1,0:T(8,128)(2,1)S(1)} %get-tuple-element.24), channel_id=1, source_target_pairs={{0,12},{4,8},{8,4},{12,0},{16,28},{20,24},{24,20},{28,16},{1,13},{... | collective-permute-start | bytes 49160 | tf_op jit(solution)/shard_map/ppermute | solution.py:30
  42.5 5.1 %collective-permute-start.24 = (bf16[8,1024]{1,0:T(8,128)(2,1)S(1)}, bf16[8,1024]{1,0:T(8,128)(2,1)S(1)}, u32[]{:S(2)}, u32[]{:S(2)}) collective-permute-start(bf16[8,1024]{1,0:T(8,128)(2,1)S(1)} %get-tuple-element.24), channel_id=1, source_target_pairs={{0,16},{4,20},{8,24},{12,28},{16,0},{20,4},{24,8},{28,12},{1,17},{... | collective-permute-start | bytes 49160 | tf_op jit(solution)/shard_map/ppermute | solution.py:30
  47.6 13.9 %collective-permute-start.27 = (bf16[8,1024]{1,0:T(8,128)(2,1)S(1)}, bf16[8,1024]{1,0:T(8,128)(2,1)S(1)}, u32[]{:S(2)}, u32[]{:S(2)}) collective-permute-start(bf16[8,1024]{1,0:T(8,128)(2,1)S(1)} %get-tuple-element.24), channel_id=1, source_target_pairs={{0,28},{4,24},{8,20},{12,16},{16,12},{20,8},{24,4},{28,0},{1,29},{... | collective-permute-start | bytes 49160 | tf_op jit(solution)/shard_map/ppermute | solution.py:30
  51.9 5.7 %collective-permute-start.8 = (bf16[768,128]{1,0:T(8,128)(2,1)S(1)}, bf16[768,128]{1,0:T(8,128)(2,1)S(1)}, u32[]{:S(2)}, u32[]{:S(2)}) collective-permute-start(bf16[768,128]{1,0:T(8,128)(2,1)S(1)} %add_convert_fusion.1), channel_id=1, source_target_pairs={{0,2},{1,3},{2,0},{3,1},{4,6},{5,7},{6,4},{7,5},{8,10},{9,11},{10,... | collective-permute-start | bytes 589832 | tf_op jit(solution)/shard_map/ppermute | solution.py:30
  54.5 6.9 %collective-permute-start.1 = (bf16[768,128]{1,0:T(8,128)(2,1)S(1)}, bf16[768,128]{1,0:T(8,128)(2,1)S(1)}, u32[]{:S(2)}, u32[]{:S(2)}) collective-permute-start(bf16[768,128]{1,0:T(8,128)(2,1)S(1)} %add_convert_fusion.3), channel_id=1, source_target_pairs={{0,2},{1,3},{2,0},{3,1},{4,6},{5,7},{6,4},{7,5},{8,10},{9,11},{10,... | collective-permute-start | bytes 589832 | tf_op jit(solution)/shard_map/ppermute | solution.py:30
  57.7 1.5 %collective-permute-start.9 = (bf16[768,128]{1,0:T(8,128)(2,1)S(1)}, bf16[768,128]{1,0:T(8,128)(2,1)S(1)}, u32[]{:S(2)}, u32[]{:S(2)}) collective-permute-start(bf16[768,128]{1,0:T(8,128)(2,1)S(1)} %add_convert_fusion.own_ref), channel_id=1, source_target_pairs={{0,1},{1,0},{2,3},{3,2},{4,5},{5,4},{6,7},{7,6},{8,9},{9,8},{10,11... | collective-permute-start | bytes 589832 | tf_op jit(solution)/shard_map/ppermute | solution.py:30
  60.7 10.5 %collective-permute-start.10 = (bf16[4,256,128]{2,1,0:T(8,128)(2,1)S(1)}, bf16[4,256,128]{2,1,0:T(8,128)(2,1)S(1)}, u32[]{:S(2)}, u32[]{:S(2)}) collective-permute-start(bf16[4,256,128]{2,1,0:T(8,128)(2,1)S(1)} %hist_send.3), channel_id=1, source_target_pairs={{0,4},{4,0},{8,12},{12,8},{16,20},{20,16},{24,28},{28,24},{1,5},{5... | collective-permute-start | bytes 786440 | tf_op jit(solution)/shard_map/ppermute | solution.py:30
  61.4 3.9 %collective-permute-start.2 = (bf16[768,128]{1,0:T(8,128)(2,1)S(1)}, bf16[768,128]{1,0:T(8,128)(2,1)S(1)}, u32[]{:S(2)}, u32[]{:S(2)}) collective-permute-start(bf16[768,128]{1,0:T(8,128)(2,1)S(1)} %add_convert_fusion.2.own_ref), channel_id=1, source_target_pairs={{0,1},{1,0},{2,3},{3,2},{4,5},{5,4},{6,7},{7,6},{8,9},{9,8},{10,11... | collective-permute-start | bytes 589832 | tf_op jit(solution)/shard_map/ppermute | solution.py:30
  66.7 8.8 %collective-permute-start.3 = (bf16[4,256,128]{2,1,0:T(8,128)(2,1)S(1)}, bf16[4,256,128]{2,1,0:T(8,128)(2,1)S(1)}, u32[]{:S(2)}, u32[]{:S(2)}) collective-permute-start(bf16[4,256,128]{2,1,0:T(8,128)(2,1)S(1)} %hist_send.2), channel_id=1, source_target_pairs={{0,4},{4,0},{8,12},{12,8},{16,20},{20,16},{24,28},{28,24},{1,5},{5... | collective-permute-start | bytes 786440 | tf_op jit(solution)/shard_map/ppermute | solution.py:30
  71.3 6.1 %collective-permute-start.11 = (bf16[256,128]{1,0:T(8,128)(2,1)S(1)}, bf16[256,128]{1,0:T(8,128)(2,1)S(1)}, u32[]{:S(2)}, u32[]{:S(2)}) collective-permute-start(bf16[256,128]{1,0:T(8,128)(2,1)S(1)} %get-tuple-element.39), channel_id=1, source_target_pairs={{0,8},{4,12},{8,0},{12,4},{16,24},{20,28},{24,16},{28,20},{1,9},{5... | collective-permute-start | bytes 196616 | tf_op jit(solution)/shard_map/ppermute | solution.py:30
  71.9 7.3 %collective-permute-start.13 = (bf16[256,128]{1,0:T(8,128)(2,1)S(1)}, bf16[256,128]{1,0:T(8,128)(2,1)S(1)}, u32[]{:S(2)}, u32[]{:S(2)}) collective-permute-start(bf16[256,128]{1,0:T(8,128)(2,1)S(1)} %get-tuple-element.40), channel_id=1, source_target_pairs={{0,24},{4,28},{8,16},{12,20},{16,8},{20,12},{24,0},{28,4},{1,25},{... | collective-permute-start | bytes 196616 | tf_op jit(solution)/shard_map/ppermute | solution.py:30
  72.8 11.9 %collective-permute-start.12 = (bf16[256,128]{1,0:T(8,128)(2,1)S(1)}, bf16[256,128]{1,0:T(8,128)(2,1)S(1)}, u32[]{:S(2)}, u32[]{:S(2)}) collective-permute-start(bf16[256,128]{1,0:T(8,128)(2,1)S(1)} %get-tuple-element.41), channel_id=1, source_target_pairs={{0,16},{4,20},{8,24},{12,28},{16,0},{20,4},{24,8},{28,12},{1,17},{... | collective-permute-start | bytes 196616 | tf_op jit(solution)/shard_map/ppermute | solution.py:30
  75.6 9.2 %collective-permute-start.4 = (bf16[256,128]{1,0:T(8,128)(2,1)S(1)}, bf16[256,128]{1,0:T(8,128)(2,1)S(1)}, u32[]{:S(2)}, u32[]{:S(2)}) collective-permute-start(bf16[256,128]{1,0:T(8,128)(2,1)S(1)} %get-tuple-element.36), channel_id=1, source_target_pairs={{0,8},{4,12},{8,0},{12,4},{16,24},{20,28},{24,16},{28,20},{1,9},{5... | collective-permute-start | bytes 196616 | tf_op jit(solution)/shard_map/ppermute | solution.py:30
  76.7 8.1 %collective-permute-start.6 = (bf16[256,128]{1,0:T(8,128)(2,1)S(1)}, bf16[256,128]{1,0:T(8,128)(2,1)S(1)}, u32[]{:S(2)}, u32[]{:S(2)}) collective-permute-start(bf16[256,128]{1,0:T(8,128)(2,1)S(1)} %get-tuple-element.37), channel_id=1, source_target_pairs={{0,24},{4,28},{8,16},{12,20},{16,8},{20,12},{24,0},{28,4},{1,25},{... | collective-permute-start | bytes 196616 | tf_op jit(solution)/shard_map/ppermute | solution.py:30
  77.3 9.2 %collective-permute-start.5 = (bf16[256,128]{1,0:T(8,128)(2,1)S(1)}, bf16[256,128]{1,0:T(8,128)(2,1)S(1)}, u32[]{:S(2)}, u32[]{:S(2)}) collective-permute-start(bf16[256,128]{1,0:T(8,128)(2,1)S(1)} %get-tuple-element.38), channel_id=1, source_target_pairs={{0,16},{4,20},{8,24},{12,28},{16,0},{20,4},{24,8},{28,12},{1,17},{... | collective-permute-start | bytes 196616 | tf_op jit(solution)/shard_map/ppermute | solution.py:30

commit v2 on v1

v2 whole, which is shorter than its diff:
```python
import functools

import jax
import jax.numpy as jnp
from jax import lax
from jax.experimental import pallas as pl
from jax.experimental.pallas import tpu as pltpu
from jax.sharding import PartitionSpec as P

BINS = 256
LEAVES = 64


shrinkage = 0.5
ridge_term = 1.0

f32 = jnp.float32
bf16 = jnp.bfloat16
VMEM_LIMIT = 48 * 1024 * 1024


def block_rows(rows):
    for size in (256, 128, 64, 32, 16):
        if rows % size == 0:
            return size
    return rows


def cost(us):
    return pl.CostEstimate(flops=0, transcendentals=0, bytes_accessed=int(us * 3.69e6))


def swap(x, axis, size, by):
    return lax.ppermute(x, axis, [(i, i ^ by) for i in range(size)])


def sketch_kernel(core_ref, pred_ref, lab_ref, w_ref, out_ref):
    t = jnp.tanh(pred_ref[...].astype(f32) * 0.5)
    grad = ((lab_ref[...].astype(f32) - 0.5) - 0.5 * t).astype(bf16)
    out_ref[...] = jnp.dot(grad, w_ref[...], preferred_element_type=f32).astype(bf16)


def sketch_pass(which, pred, lab, w, name):
    rows, cols = pred.shape
    half = rows // 2
    blk = block_rows(half)
    steps = half // blk
    row_map = lambda i, c: (c[0] * steps + i, 0)
    return pl.pallas_call(
        sketch_kernel,
        grid_spec=pltpu.PrefetchScalarGridSpec(
            num_scalar_prefetch=1,
            grid=(steps,),
            in_specs=[
                pl.BlockSpec((blk, cols), row_map),
                pl.BlockSpec((blk, cols), row_map),
                pl.BlockSpec(w.shape, lambda i, c: (0, 0)),
            ],
            out_specs=pl.BlockSpec((blk, w.shape[1]), lambda i, c: (i, 0)),
        ),
        out_shape=jax.ShapeDtypeStruct((half, w.shape[1]), bf16),
        compiler_params=pltpu.CompilerParams(vmem_limit_bytes=VMEM_LIMIT),
        cost_estimate=cost(1.6),
        name=name,
    )(which, pred, lab, w)


def pair_kernel(keep_ref, got_ref, out_ref):
    out_ref[...] = (keep_ref[...].astype(f32) + got_ref[...].astype(f32)).astype(out_ref.dtype)


def pair_pass(keep, got, part, parts, name):
    rows, cols = keep.shape
    width = cols // parts
    spec = pl.BlockSpec((rows, width), lambda i: (0, part))
    return pl.pallas_call(
        pair_kernel,
        grid=(1,),
        in_specs=[spec, spec],
        out_specs=pl.BlockSpec((rows, width), lambda i: (0, 0)),
        out_shape=jax.ShapeDtypeStruct((rows, width), bf16),
        compiler_params=pltpu.CompilerParams(vmem_limit_bytes=VMEM_LIMIT),
        cost_estimate=cost(0.2),
        name=name,
    )(keep, got)


def leaf_kernel(side_ref, pred_ref, lab_ref, leaf_ref, after_ref, keep_ref, send_ref, g_ref, h_ref):
    step = pl.program_id(0)

    @pl.when(step == 0)
    def _():
        g_ref[...] = jnp.zeros_like(g_ref)
        h_ref[...] = jnp.zeros_like(h_ref)

    t = jnp.tanh(pred_ref[...].astype(f32) * 0.5)
    grad = ((lab_ref[...].astype(f32) - 0.5) - 0.5 * t).astype(bf16)
    hess = (0.25 - 0.25 * t * t).astype(bf16)
    blk = pred_ref.shape[0]
    leaf = leaf_ref[0] ^ (side_ref[0] * (LEAVES // 2))
    hot = (lax.broadcasted_iota(jnp.int32, (LEAVES, blk), 0) == leaf).astype(f32).astype(bf16)
    g_ref[...] += jnp.dot(hot, grad, preferred_element_type=f32)
    h_ref[...] += jnp.dot(hot, hess, preferred_element_type=f32)

    @pl.when(step == pl.num_programs(0) - 1)
    def _():
        half = LEAVES // 2
        keep_ref[:half] = g_ref[:half]
        keep_ref[half:] = h_ref[:half]
        send_ref[:half] = g_ref[half:].astype(bf16)
        send_ref[half:] = h_ref[half:].astype(bf16)


def leaf_pass(side, pred, lab, leaf, after):
    rows, cols = pred.shape
    blk = block_rows(rows)
    fixed = lambda i, c: (0, 0)
    return pl.pallas_call(
        leaf_kernel,
        grid_spec=pltpu.PrefetchScalarGridSpec(
            num_scalar_prefetch=1,
            grid=(rows // blk,),
            in_specs=[
                pl.BlockSpec((blk, cols), lambda i, c: (i, 0)),
                pl.BlockSpec((blk, cols), lambda i, c: (i, 0)),
                pl.BlockSpec((1, 1, blk), lambda i, c: (i, 0, 0)),
                pl.BlockSpec(memory_space=pl.ANY),
            ],
            out_specs=[pl.BlockSpec((LEAVES, cols), fixed)] * 2,
            scratch_shapes=[pltpu.VMEM((LEAVES, cols), f32)] * 2,
        ),
        out_shape=[
            jax.ShapeDtypeStruct((LEAVES, cols), f32),
            jax.ShapeDtypeStruct((LEAVES, cols), bf16),
        ],
        compiler_params=pltpu.CompilerParams(vmem_limit_bytes=VMEM_LIMIT),
        cost_estimate=cost(5.0),
        name="leaf_sums",
    )(side, pred, lab, leaf.reshape(rows // blk, 1, blk), after)


def hist_kernel(codes_ref, own_ref, other_ref, out_ref, *, per, odd, bits):
    feats = codes_ref.shape[1]
    half = codes_ref.shape[2]
    codes = codes_ref[...].astype(f32).astype(bf16)
    step = pl.program_id(0)
    place = sum(((step >> b) & 1) << (bits - 1 - b) for b in range(bits))
    base = (2 * place + odd) * per
    levels = (lax.broadcasted_iota(jnp.int32, (per, 1, 1), 0) + base).astype(f32).astype(bf16)
    one = jnp.ones((), bf16)
    zero = jnp.zeros((), bf16)
    total = None
    for part, ref in ((0, own_ref), (1, other_ref)):
        hot = jnp.where(codes[part][None] == levels, one, zero).reshape(per * feats, half)
        term = jnp.dot(hot, ref[...], preferred_element_type=f32)
        total = term if total is None else total + term
    out_ref[0] = total.astype(out_ref.dtype)


def hist_pass(codes, own, other, per, blocks, odd, dtype):
    feats = codes.shape[1]
    width = own.shape[1]
    whole = lambda a: pl.BlockSpec(a.shape, lambda i: (0,) * a.ndim)
    return pl.pallas_call(
        functools.partial(hist_kernel, per=per, odd=odd, bits=blocks.bit_length() - 1),
        grid=(blocks,),
        in_specs=[whole(codes), whole(own), whole(other)],
        out_specs=pl.BlockSpec((1, per * feats, width), lambda i: (i, 0, 0)),
        out_shape=jax.ShapeDtypeStruct((blocks, per * feats, width), dtype),
        compiler_params=pltpu.CompilerParams(vmem_limit_bytes=VMEM_LIMIT),
        cost_estimate=cost(1.5),
        name="hist_send" if odd else "hist_keep",
    )(codes, own, other)


def update_kernel(side_ref, pred_ref, leaf_ref, own_ref, other_ref, new_ref, values_ref):
    half = LEAVES // 2
    own, other = own_ref[...], other_ref[...]

    @pl.when(pl.program_id(0) == 0)
    def _():
        first = side_ref[0] == 0
        values_ref[:half] = jnp.where(first, own.astype(f32), other.astype(f32))
        values_ref[half:] = jnp.where(first, other.astype(f32), own.astype(f32))

    blk = pred_ref.shape[0]
    leaf = leaf_ref[0] ^ (side_ref[0] * half)
    hot = (lax.broadcasted_iota(jnp.int32, (LEAVES, blk), 0) == leaf).astype(f32).astype(bf16)
    table = jnp.concatenate([own, other], axis=0)
    found = lax.dot_general(hot, table, (((0,), (0,)), ((), ())), preferred_element_type=f32)
    new_ref[...] = (pred_ref[...].astype(f32) + shrinkage * found).astype(bf16)


def update_pass(side, pred, leaf, own, other):
    rows, cols = pred.shape
    blk = block_rows(rows)
    fixed = lambda i, m: (0, 0)
    return pl.pallas_call(
        update_kernel,
        grid_spec=pltpu.PrefetchScalarGridSpec(
            num_scalar_prefetch=1,
            grid=(rows // blk,),
            in_specs=[
                pl.BlockSpec((blk, cols), lambda i, m: (i, 0)),
                pl.BlockSpec((1, 1, blk), lambda i, m: (i, 0, 0)),
                pl.BlockSpec(own.shape, fixed),
                pl.BlockSpec(own.shape, fixed),
            ],
            out_specs=[
                pl.BlockSpec((blk, cols), lambda i, m: (i, 0)),
                pl.BlockSpec((LEAVES, cols), fixed),
            ],
        ),
        out_shape=[
            jax.ShapeDtypeStruct((rows, cols), bf16),
            jax.ShapeDtypeStruct((LEAVES, cols), f32),
        ],
        compiler_params=pltpu.CompilerParams(vmem_limit_bytes=VMEM_LIMIT),
        cost_estimate=cost(3.7),
        name="update",
    )(side, pred, leaf.reshape(rows // blk, 1, blk), own, other)


def last_kernel(*refs):
    out_ref = refs[-1]
    width = refs[0].shape[1]
    for p in range(len(refs) // 2):
        out_ref[:, p * width:(p + 1) * width] = refs[2 * p][...] + refs[2 * p + 1][...].astype(f32)


def last_pass(pairs):
    rows, width = pairs[0][0].shape
    return pl.pallas_call(
        last_kernel,
        out_shape=jax.ShapeDtypeStruct((rows, width * len(pairs)), f32),
        compiler_params=pltpu.CompilerParams(vmem_limit_bytes=VMEM_LIMIT),
        cost_estimate=cost(0.5),
        name="last_add",
    )(*[a for pair in pairs for a in pair])


def local(n, nf, predictions, labels, feature_codes, leaf_index, sketch_weight):
    rows, cols = predictions.shape
    feats = feature_codes.shape[0]
    half = rows // 2
    parts = 2
    width = sketch_weight.shape[1] // parts
    me = lax.axis_index("rows")
    core = lax.axis_index("feat") & 1
    side = (me & 1).reshape(1)
    per = BINS // n
    codes = (feature_codes ^ (me * per)).reshape(feats, 2, half)
    codes = jnp.where(core == 0, codes, codes[:, ::-1]).swapaxes(0, 1)

    pred = pltpu.with_memory_space_constraint(predictions, pltpu.HBM)
    lab = pltpu.with_memory_space_constraint(labels, pltpu.HBM)
    weight = pltpu.with_memory_space_constraint(sketch_weight, pltpu.HBM)

    send = sketch_pass((1 - core).reshape(1), pred, lab, weight, "sketch_send")
    got = swap(send, "feat", nf, 1)
    keep = sketch_pass(core.reshape(1), pred, lab, weight, "sketch_keep")
    pair = [pair_pass(keep, got, p, parts, "core_add") for p in range(parts)]
    owns = []
    for p in range(parts):
        own = pair[p]
        for t in range(2, nf, 2):
            own = pair_pass(own, swap(pair[p], "feat", nf, t), 0, 1, "feat_add")
        owns.append(own)

    kept, sent = leaf_pass(side, pred, lab, leaf_index, pair[0])
    acc = kept + swap(sent, "rows", n, 1).astype(f32)
    by = 2
    while by < n:
        acc16 = acc.astype(bf16)
        acc = acc16.astype(f32) + swap(acc16, "rows", n, by).astype(f32)
        by *= 2
    values = (acc[:LEAVES // 2] / (acc[LEAVES // 2:] + ridge_term)).astype(bf16)
    updated, leaf_values = update_pass(side, pred, leaf_index, values, swap(values, "rows", n, 1))

    pairs = []
    for p in range(parts):
        own = owns[p]
        other = swap(own, "feat", nf, 1)
        away = hist_pass(codes, own, other, per, n // 2, 1, bf16)
        back = swap(away, "rows", n, 1)
        here = hist_pass(codes, own, other, per, n // 2, 0, f32)
        blocks, by = n // 2, 2
        while blocks > 1:
            acc = here + back.astype(f32)
            blocks //= 2
            back = swap(acc[blocks:].astype(bf16), "rows", n, by)
            here = acc[:blocks]
            by *= 2
        pairs.append((here[0], back[0]))
    histograms = last_pass(pairs).reshape(per, feats, -1)
    return histograms, leaf_values, updated


def solution(mesh):
    n, nf = mesh.shape["rows"], mesh.shape["feat"]
    return jax.shard_map(
        functools.partial(local, n, nf),
        mesh=mesh,
        in_specs=(
            P("rows", "feat"),
            P("rows", "feat"),
            P("feat", "rows"),
            P("rows"),
            P("feat", None),
        ),
        out_specs=(P("rows", "feat", None), P(None, "feat"), P("rows", "feat")),
        check_vma=False,
    )
```

time: 87.8 us -> 63.7 us (0.73)
  starting transfers between devices: 39.4 us -> 21.6 us
  Pallas kernels: 16.5 us -> 25.9 us
  waiting for transfers between devices: 21.3 us -> 14.6 us
  other arithmetic: 4.71 us -> 0.28 us
  local copies, waits for them, and re-layouts: 4.4 us -> 0.1 us
    ppermute x28 -> x15, starting transfers between devices: 39.4 us -> 21.6 us  [swap(): return lax.ppermute(x, axis, [(i, i ^ by) for i in range(size)])]
    pallas_call x6 -> x12, Pallas kernels: 12.8 us -> 19.9 us  [the longest x2 6.86 us: sketch_pass(): pl.pallas_call(sketch_kernel, grid_spec=pltpu.PrefetchScalarGridSpec(num_...]
    ppermute x28 -> x15, waiting for transfers between devices: 21.3 us -> 14.6 us  [swap(): return lax.ppermute(x, axis, [(i, i ^ by) for i in range(size)])]
    unnamed x26 -> x4, local copies, waits for them, and re-layouts: 3.68 us -> 0.01 us
    pallas_call x1, Pallas kernels: 3.74 us -> 6 us  [update_pass(): pl.pallas_call(update_kernel, grid_spec=pltpu.PrefetchScalarGridSpec(num_...]
    convert_element_type x6 -> x1, other arithmetic: 2.14 us -> 0.03 us  [local(): values = (acc[:LEAVES // 2] / (acc[LEAVES // 2:] + ridge_term)).astype(bf16)]
  transfers between devices with their start and end apart: 28 -> 15, of which waited for: 12 -> 8; matrix products, arithmetic and copies ran while one was open for 4% -> 1% of each run, Pallas kernels for 11% -> 25%
where the time goes in v2:
time: 63.7 us; the launch traced here: 63.2 us
  Pallas kernels  25.9 us (41%)
  starting transfers between devices  21.6 us (34%)
  waiting for transfers between devices  14.6 us (23%)
  between operations  0.86 us (1%)
    ppermute x15, starting transfers between devices, swap(): return lax.ppermute(x, axis, [(i, i ^ by) for i in range(size)])  21.6 us
    ppermute x15, waiting for transfers between devices, swap(): return lax.ppermute(x, axis, [(i, i ^ by) for i in range(size)])  14.6 us
    pallas_call x2, Pallas kernels, sketch_pass(): pl.pallas_call(sketch_kernel, grid_spec=pltpu.PrefetchScalarGridSpec(num_...  6.86 us
    pallas_call x1, Pallas kernels, leaf_pass(): pl.pallas_call(leaf_kernel, grid_spec=pltpu.PrefetchScalarGridSpec(num_sc...  6.02 us
    pallas_call x1, Pallas kernels, update_pass(): pl.pallas_call(update_kernel, grid_spec=pltpu.PrefetchScalarGridSpec(num_...  6 us
    pallas_call x4, Pallas kernels, hist_pass(): pl.pallas_call(functools.partial(hist_kernel, per=per, odd=odd, bits=bloc...  5.89 us
  transfers between devices with their start and end apart: 15, of which 8 were waited for; matrix products, arithmetic and copies ran while one was open for 1% of the time, Pallas kernels for 25%

profile of v2, /device:TPU:0, one launch (start us, length us, event | category | flops | bytes accessed | tf_op | source)
XLA Modules:
  0.0 63.2 jit_solution(2420901789476575483)
XLA Ops:
  0.6 0.0 copy-start.1
  0.6 3.4 %sketch_send.1 = bf16[768,256]{1,0:T(8,128)(2,1)S(1)} custom-call(s32[1]{0:T(128)} %bitcast.3.core_ref, bf16[1536,1024]{1,0:T(8,128)(2,1)} %pred_ref.7, bf16[1536,1024]{1,0:T(8,128)(2,1)} %lab_ref.5, bf16[1024,256]{1,0:T(8,128)(2,1)} %w_ref.3), custom_call_target="tpu_custom_call" | custom-call | bytes 5904000 | tf_op jit(solution)/shard_map/sketch_send/pallas_call | solution.py:49
  4.1 0.5 collective-permute-start
  4.6 0.0 copy-done.1
  4.6 3.4 %sketch_keep.1.keep_ref = bf16[768,256]{1,0:T(8,128)(2,1)S(1)} custom-call(s32[1]{0:T(128)} %bitcast.2.core_ref, bf16[1536,1024]{1,0:T(8,128)(2,1)} %pred_ref.7, bf16[1536,1024]{1,0:T(8,128)(2,1)} %lab_ref.5, bf16[1024,256]{1,0:T(8,128)(2,1)} %w_ref.3), custom_call_target="tpu_custom_call" | custom-call | bytes 5904000 | tf_op jit(solution)/shard_map/sketch_keep/pallas_call | solution.py:49
  8.0 0.0 collective-permute-done.got_ref
  8.1 0.1 core_add.2.keep_ref.after_ref
  8.2 0.0 copy-start
  8.2 6.0 %leaf_sums.1 = (f32[64,1024]{1,0:T(8,128)S(1)}, bf16[64,1024]{1,0:T(8,128)(2,1)S(1)}) custom-call(s32[1]{0:T(128)} %bitcast.9.side_ref, bf16[1536,1024]{1,0:T(8,128)(2,1)} %pred_ref.7, bf16[1536,1024]{1,0:T(8,128)(2,1)} %lab_ref.5, s32[6,1,256]{2,1,0:T(1,128)S(1)} %reshape.30.leaf_ref, bf16[768,128]{1,0:T(8,128)(2,1)S(1)} %core_add.2.keep_ref.after_ref), custom_call_target="tpu_custom_call" | custom-call | bytes 18450000 | tf_op jit(solution)/shard_map/leaf_sums/pallas_call | solution.py:118
  14.3 2.6 %collective-permute-start.11 = (bf16[64,1024]{1,0:T(8,128)(2,1)S(1)}, bf16[64,1024]{1,0:T(8,128)(2,1)S(1)}, u32[]{:S(2)}, u32[]{:S(2)}) collective-permute-start(bf16[64,1024]{1,0:T(8,128)(2,1)S(1)} %get-tuple-element.8), channel_id=1, source_target_pairs={{0,4},{4,0},{8,12},{12,8},{16,20},{20,16},{24,28},{28,24},{1,5},{5... | collective-permute-start | bytes 393224 | tf_op jit(solution)/shard_map/ppermute | solution.py:34
  16.8 0.1 core_add.3.keep_ref
  17.0 1.6 %collective-permute-start.6 = (bf16[768,128]{1,0:T(8,128)(2,1)S(1)}, bf16[768,128]{1,0:T(8,128)(2,1)S(1)}, u32[]{:S(2)}, u32[]{:S(2)}) collective-permute-start(bf16[768,128]{1,0:T(8,128)(2,1)S(1)} %core_add.3.keep_ref), channel_id=1, source_target_pairs={{0,2},{1,3},{2,0},{3,1},{4,6},{5,7},{6,4},{7,5},{8,10},{9,11},{10,... | collective-permute-start | bytes 589832 | tf_op jit(solution)/shard_map/ppermute | solution.py:34
  18.6 2.4 %collective-permute-done.11 = bf16[64,1024]{1,0:T(8,128)(2,1)S(1)} collective-permute-done((bf16[64,1024]{1,0:T(8,128)(2,1)S(1)}, bf16[64,1024]{1,0:T(8,128)(2,1)S(1)}, u32[]{:S(2)}, u32[]{:S(2)}) %collective-permute-start.11) | collective-permute-done | bytes 131104 | tf_op jit(solution)/shard_map/ppermute | solution.py:34
  21.0 1.9 %collective-permute-start.12 = (bf16[64,1024]{1,0:T(8,128)(2,1)S(1)}, bf16[64,1024]{1,0:T(8,128)(2,1)S(1)}, u32[]{:S(2)}, u32[]{:S(2)}) collective-permute-start(bf16[64,1024]{1,0:T(8,128)(2,1)S(1)} %add_convert_fusion.1), channel_id=1, source_target_pairs={{0,8},{4,12},{8,0},{12,4},{16,24},{20,28},{24,16},{28,20},{1,9},{5... | collective-permute-start | bytes 393224 | tf_op jit(solution)/shard_map/ppermute | solution.py:34
  22.9 0.0 copy-done
  22.9 1.6 %collective-permute-start.1 = (bf16[768,128]{1,0:T(8,128)(2,1)S(1)}, bf16[768,128]{1,0:T(8,128)(2,1)S(1)}, u32[]{:S(2)}, u32[]{:S(2)}) collective-permute-start(bf16[768,128]{1,0:T(8,128)(2,1)S(1)} %core_add.2.keep_ref.after_ref), channel_id=1, source_target_pairs={{0,2},{1,3},{2,0},{3,1},{4,6},{5,7},{6,4},{7,5},{8,10},{9,11},{10,... | collective-permute-start | bytes 589832 | tf_op jit(solution)/shard_map/ppermute | solution.py:34
  24.5 0.0 collective-permute-done.6.got_ref
  24.6 0.1 collective-permute-start.7
  24.6 1.7 %collective-permute-done.12 = bf16[64,1024]{1,0:T(8,128)(2,1)S(1)} collective-permute-done((bf16[64,1024]{1,0:T(8,128)(2,1)S(1)}, bf16[64,1024]{1,0:T(8,128)(2,1)S(1)}, u32[]{:S(2)}, u32[]{:S(2)}) %collective-permute-start.12) | collective-permute-done | bytes 131104 | tf_op jit(solution)/shard_map/ppermute | solution.py:34
  26.4 2.7 %collective-permute-start.13 = (bf16[64,1024]{1,0:T(8,128)(2,1)S(1)}, bf16[64,1024]{1,0:T(8,128)(2,1)S(1)}, u32[]{:S(2)}, u32[]{:S(2)}) collective-permute-start(bf16[64,1024]{1,0:T(8,128)(2,1)S(1)} %add_convert_fusion), channel_id=1, source_target_pairs={{0,16},{4,20},{8,24},{12,28},{16,0},{20,4},{24,8},{28,12},{1,17},{... | collective-permute-start | bytes 393224 | tf_op jit(solution)/shard_map/ppermute | solution.py:34
  29.1 0.1 collective-permute-done.1.got_ref
  29.3 0.1 collective-permute-start.2
  29.4 0.0 collective-permute-done.7.other_ref
  29.4 1.5 %hist_send.3 = bf16[4,256,128]{2,1,0:T(8,128)(2,1)S(1)} custom-call(s32[2,8,768]{2,1,0:T(8,128)S(1)} %fusion.2.codes_ref, bf16[768,128]{1,0:T(8,128)(2,1)S(1)} %feat_add.3.own_ref, bf16[768,128]{1,0:T(8,128)(2,1)S(1)} %collective-permute-done.7.other_ref), custom_call_target="tpu_custom_call" | custom-call | bytes 5535000 | tf_op jit(solution)/shard_map/hist_send/pallas_call | solution.py:164
  30.9 1.6 %collective-permute-start.8 = (bf16[4,256,128]{2,1,0:T(8,128)(2,1)S(1)}, bf16[4,256,128]{2,1,0:T(8,128)(2,1)S(1)}, u32[]{:S(2)}, u32[]{:S(2)}) collective-permute-start(bf16[4,256,128]{2,1,0:T(8,128)(2,1)S(1)} %hist_send.3), channel_id=1, source_target_pairs={{0,4},{4,0},{8,12},{12,8},{16,20},{20,16},{24,28},{28,24},{1,5},{5... | collective-permute-start | bytes 786440 | tf_op jit(solution)/shard_map/ppermute | solution.py:34
  32.4 2.2 %collective-permute-done.13 = bf16[64,1024]{1,0:T(8,128)(2,1)S(1)} collective-permute-done((bf16[64,1024]{1,0:T(8,128)(2,1)S(1)}, bf16[64,1024]{1,0:T(8,128)(2,1)S(1)}, u32[]{:S(2)}, u32[]{:S(2)}) %collective-permute-start.13) | collective-permute-done | bytes 131104 | tf_op jit(solution)/shard_map/ppermute | solution.py:34
  34.7 1.4 %collective-permute-start.14 = (bf16[32,1024]{1,0:T(8,128)(2,1)S(1)}, bf16[32,1024]{1,0:T(8,128)(2,1)S(1)}, u32[]{:S(2)}, u32[]{:S(2)}) collective-permute-start(bf16[32,1024]{1,0:T(8,128)(2,1)S(1)} %fusion.1.own_ref), channel_id=1, source_target_pairs={{0,4},{4,0},{8,12},{12,8},{16,20},{20,16},{24,28},{28,24},{1,5},{5... | collective-permute-start | bytes 196616 | tf_op jit(solution)/shard_map/ppermute | solution.py:34
  36.1 0.0 collective-permute-done.2.other_ref
  36.1 1.5 %hist_send.2 = bf16[4,256,128]{2,1,0:T(8,128)(2,1)S(1)} custom-call(s32[2,8,768]{2,1,0:T(8,128)S(1)} %fusion.2.codes_ref, bf16[768,128]{1,0:T(8,128)(2,1)S(1)} %feat_add.2.own_ref, bf16[768,128]{1,0:T(8,128)(2,1)S(1)} %collective-permute-done.2.other_ref), custom_call_target="tpu_custom_call" | custom-call | bytes 5535000 | tf_op jit(solution)/shard_map/hist_send/pallas_call | solution.py:164
  37.6 0.8 %collective-permute-start.3 = (bf16[4,256,128]{2,1,0:T(8,128)(2,1)S(1)}, bf16[4,256,128]{2,1,0:T(8,128)(2,1)S(1)}, u32[]{:S(2)}, u32[]{:S(2)}) collective-permute-start(bf16[4,256,128]{2,1,0:T(8,128)(2,1)S(1)} %hist_send.2), channel_id=1, source_target_pairs={{0,4},{4,0},{8,12},{12,8},{16,20},{20,16},{24,28},{28,24},{1,5},{5... | collective-permute-start | bytes 786440 | tf_op jit(solution)/shard_map/ppermute | solution.py:34
  38.4 1.5 %hist_keep.2 = f32[4,256,128]{2,1,0:T(8,128)S(1)} custom-call(s32[2,8,768]{2,1,0:T(8,128)S(1)} %fusion.2.codes_ref, bf16[768,128]{1,0:T(8,128)(2,1)S(1)} %feat_add.2.own_ref, bf16[768,128]{1,0:T(8,128)(2,1)S(1)} %collective-permute-done.2.other_ref), custom_call_target="tpu_custom_call" | custom-call | bytes 5535000 | tf_op jit(solution)/shard_map/hist_keep/pallas_call | solution.py:164
  39.8 1.5 %hist_keep.3 = f32[4,256,128]{2,1,0:T(8,128)S(1)} custom-call(s32[2,8,768]{2,1,0:T(8,128)S(1)} %fusion.2.codes_ref, bf16[768,128]{1,0:T(8,128)(2,1)S(1)} %feat_add.3.own_ref, bf16[768,128]{1,0:T(8,128)(2,1)S(1)} %collective-permute-done.7.other_ref), custom_call_target="tpu_custom_call" | custom-call | bytes 5535000 | tf_op jit(solution)/shard_map/hist_keep/pallas_call | solution.py:164
  41.3 0.1 collective-permute-done.14.other_ref
  41.4 6.0 %update.1 = (bf16[1536,1024]{1,0:T(8,128)(2,1)}, f32[64,1024]{1,0:T(8,128)}) custom-call(s32[1]{0:T(128)} %bitcast.9.side_ref, bf16[1536,1024]{1,0:T(8,128)(2,1)} %pred_ref.7, s32[6,1,256]{2,1,0:T(1,128)S(1)} %reshape.30.leaf_ref, bf16[32,1024]{1,0:T(8,128)(2,1)S(1)} %fusion.1.own_ref, bf16[32,1024]{1,0:T(8,128)(2,1)S(1)} %collective-permute-done.14.other_ref), custom_call_target="tpu_custom_call" | custom-call | bytes 13653000 | tf_op jit(solution)/shard_map/update/pallas_call | solution.py:198
  47.4 0.0 collective-permute-done.8
  47.5 1.6 %collective-permute-start.9 = (bf16[2,256,128]{2,1,0:T(8,128)(2,1)S(1)}, bf16[2,256,128]{2,1,0:T(8,128)(2,1)S(1)}, u32[]{:S(2)}, u32[]{:S(2)}) collective-permute-start(bf16[2,256,128]{2,1,0:T(8,128)(2,1)S(1)} %slice.68), channel_id=1, source_target_pairs={{0,8},{4,12},{8,0},{12,4},{16,24},{20,28},{24,16},{28,20},{1,9},{5... | collective-permute-start | bytes 393224 | tf_op jit(solution)/shard_map/ppermute | solution.py:34
  49.1 0.0 collective-permute-done.3
  49.2 0.6 collective-permute-start.4
  49.7 3.9 %collective-permute-done.9 = bf16[2,256,128]{2,1,0:T(8,128)(2,1)S(1)} collective-permute-done((bf16[2,256,128]{2,1,0:T(8,128)(2,1)S(1)}, bf16[2,256,128]{2,1,0:T(8,128)(2,1)S(1)}, u32[]{:S(2)}, u32[]{:S(2)}) %collective-permute-start.9) | collective-permute-done | bytes 131104 | tf_op jit(solution)/shard_map/ppermute | solution.py:34
  53.7 3.0 %collective-permute-start.10 = (bf16[1,256,128]{2,1,0:T(8,128)(2,1)S(1)}, bf16[1,256,128]{2,1,0:T(8,128)(2,1)S(1)}, u32[]{:S(2)}, u32[]{:S(2)}) collective-permute-start(bf16[1,256,128]{2,1,0:T(8,128)(2,1)S(1)} %slice.70), channel_id=1, source_target_pairs={{0,16},{4,20},{8,24},{12,28},{16,0},{20,4},{24,8},{28,12},{1,17},{... | collective-permute-start | bytes 196616 | tf_op jit(solution)/shard_map/ppermute | solution.py:34
  56.7 0.0 collective-permute-done.4
  56.8 1.7 %collective-permute-start.5 = (bf16[1,256,128]{2,1,0:T(8,128)(2,1)S(1)}, bf16[1,256,128]{2,1,0:T(8,128)(2,1)S(1)}, u32[]{:S(2)}, u32[]{:S(2)}) collective-permute-start(bf16[1,256,128]{2,1,0:T(8,128)(2,1)S(1)} %slice.71), channel_id=1, source_target_pairs={{0,16},{4,20},{8,24},{12,28},{16,0},{20,4},{24,8},{28,12},{1,17},{... | collective-permute-start | bytes 196616 | tf_op jit(solution)/shard_map/ppermute | solution.py:34
  58.5 1.6 %collective-permute-done.10 = bf16[1,256,128]{2,1,0:T(8,128)(2,1)S(1)} collective-permute-done((bf16[1,256,128]{2,1,0:T(8,128)(2,1)S(1)}, bf16[1,256,128]{2,1,0:T(8,128)(2,1)S(1)}, u32[]{:S(2)}, u32[]{:S(2)}) %collective-permute-start.10) | collective-permute-done | bytes 65568 | tf_op jit(solution)/shard_map/ppermute | solution.py:34
  60.1 2.5 %collective-permute-done.5 = bf16[1,256,128]{2,1,0:T(8,128)(2,1)S(1)} collective-permute-done((bf16[1,256,128]{2,1,0:T(8,128)(2,1)S(1)}, bf16[1,256,128]{2,1,0:T(8,128)(2,1)S(1)}, u32[]{:S(2)}, u32[]{:S(2)}) %collective-permute-start.5) | collective-permute-done | bytes 65568 | tf_op jit(solution)/shard_map/ppermute | solution.py:34
  62.5 0.7 %last_add.1 = f32[256,256]{1,0:T(8,128)} custom-call(f32[256,128]{1,0:T(8,128)S(1)} %slice_bitcast_fusion.1.refs_0_, bf16[256,128]{1,0:T(8,128)(2,1)S(1)} %bitcast.14, f32[256,128]{1,0:T(8,128)S(1)} %slice_bitcast_fusion.refs_2_, bf16[256,128]{1,0:T(8,128)(2,1)S(1)} %bitcast.13), custom_call_target="tpu_custom_call" | custom-call | bytes 1845000 | tf_op jit(solution)/shard_map/last_add/pallas_call | solution.py:233
  (19 shorter events, 0.5 us)
Async XLA Ops:
  0.6 4.0 %copy-start.1 = (s32[1536]{0:T(1024)S(1)}, s32[1536]{0:T(1024)}, u32[]{:S(2)}) copy-start(s32[1536]{0:T(1024)} %param.8) | copy-start | bytes 18436
  4.1 4.0 %collective-permute-start = (bf16[768,256]{1,0:T(8,128)(2,1)S(1)}, bf16[768,256]{1,0:T(8,128)(2,1)S(1)}, u32[]{:S(2)}, u32[]{:S(2)}) collective-permute-start(bf16[768,256]{1,0:T(8,128)(2,1)S(1)} %sketch_send.1), channel_id=1, source_target_pairs={{0,1},{1,0},{2,3},{3,2},{4,5},{5,4},{6,7},{7,6},{8,9},{9,8},{10,11... | collective-permute-start | bytes 1179656 | tf_op jit(solution)/shard_map/ppermute | solution.py:34
  8.2 14.7 %copy-start = (s32[8,1536]{1,0:T(8,128)S(1)}, s32[8,1536]{1,0:T(8,128)}, u32[]{:S(2)}) copy-start(s32[8,1536]{1,0:T(8,128)} %param.7) | copy-start | bytes 147460
  14.3 6.7 %collective-permute-start.11 = (bf16[64,1024]{1,0:T(8,128)(2,1)S(1)}, bf16[64,1024]{1,0:T(8,128)(2,1)S(1)}, u32[]{:S(2)}, u32[]{:S(2)}) collective-permute-start(bf16[64,1024]{1,0:T(8,128)(2,1)S(1)} %get-tuple-element.8), channel_id=1, source_target_pairs={{0,4},{4,0},{8,12},{12,8},{16,20},{20,16},{24,28},{28,24},{1,5},{5... | collective-permute-start | bytes 393224 | tf_op jit(solution)/shard_map/ppermute | solution.py:34
  17.0 7.5 %collective-permute-start.6 = (bf16[768,128]{1,0:T(8,128)(2,1)S(1)}, bf16[768,128]{1,0:T(8,128)(2,1)S(1)}, u32[]{:S(2)}, u32[]{:S(2)}) collective-permute-start(bf16[768,128]{1,0:T(8,128)(2,1)S(1)} %core_add.3.keep_ref), channel_id=1, source_target_pairs={{0,2},{1,3},{2,0},{3,1},{4,6},{5,7},{6,4},{7,5},{8,10},{9,11},{10,... | collective-permute-start | bytes 589832 | tf_op jit(solution)/shard_map/ppermute | solution.py:34
  21.0 5.4 %collective-permute-start.12 = (bf16[64,1024]{1,0:T(8,128)(2,1)S(1)}, bf16[64,1024]{1,0:T(8,128)(2,1)S(1)}, u32[]{:S(2)}, u32[]{:S(2)}) collective-permute-start(bf16[64,1024]{1,0:T(8,128)(2,1)S(1)} %add_convert_fusion.1), channel_id=1, source_target_pairs={{0,8},{4,12},{8,0},{12,4},{16,24},{20,28},{24,16},{28,20},{1,9},{5... | collective-permute-start | bytes 393224 | tf_op jit(solution)/shard_map/ppermute | solution.py:34
  22.9 6.3 %collective-permute-start.1 = (bf16[768,128]{1,0:T(8,128)(2,1)S(1)}, bf16[768,128]{1,0:T(8,128)(2,1)S(1)}, u32[]{:S(2)}, u32[]{:S(2)}) collective-permute-start(bf16[768,128]{1,0:T(8,128)(2,1)S(1)} %core_add.2.keep_ref.after_ref), channel_id=1, source_target_pairs={{0,2},{1,3},{2,0},{3,1},{4,6},{5,7},{6,4},{7,5},{8,10},{9,11},{10,... | collective-permute-start | bytes 589832 | tf_op jit(solution)/shard_map/ppermute | solution.py:34
  24.6 4.8 %collective-permute-start.7 = (bf16[768,128]{1,0:T(8,128)(2,1)S(1)}, bf16[768,128]{1,0:T(8,128)(2,1)S(1)}, u32[]{:S(2)}, u32[]{:S(2)}) collective-permute-start(bf16[768,128]{1,0:T(8,128)(2,1)S(1)} %feat_add.3.own_ref), channel_id=1, source_target_pairs={{0,1},{1,0},{2,3},{3,2},{4,5},{5,4},{6,7},{7,6},{8,9},{9,8},{10,11... | collective-permute-start | bytes 589832 | tf_op jit(solution)/shard_map/ppermute | solution.py:34
  26.4 8.2 %collective-permute-start.13 = (bf16[64,1024]{1,0:T(8,128)(2,1)S(1)}, bf16[64,1024]{1,0:T(8,128)(2,1)S(1)}, u32[]{:S(2)}, u32[]{:S(2)}) collective-permute-start(bf16[64,1024]{1,0:T(8,128)(2,1)S(1)} %add_convert_fusion), channel_id=1, source_target_pairs={{0,16},{4,20},{8,24},{12,28},{16,0},{20,4},{24,8},{28,12},{1,17},{... | collective-permute-start | bytes 393224 | tf_op jit(solution)/shard_map/ppermute | solution.py:34
  29.3 6.8 %collective-permute-start.2 = (bf16[768,128]{1,0:T(8,128)(2,1)S(1)}, bf16[768,128]{1,0:T(8,128)(2,1)S(1)}, u32[]{:S(2)}, u32[]{:S(2)}) collective-permute-start(bf16[768,128]{1,0:T(8,128)(2,1)S(1)} %feat_add.2.own_ref), channel_id=1, source_target_pairs={{0,1},{1,0},{2,3},{3,2},{4,5},{5,4},{6,7},{7,6},{8,9},{9,8},{10,11... | collective-permute-start | bytes 589832 | tf_op jit(solution)/shard_map/ppermute | solution.py:34
  30.9 16.6 %collective-permute-start.8 = (bf16[4,256,128]{2,1,0:T(8,128)(2,1)S(1)}, bf16[4,256,128]{2,1,0:T(8,128)(2,1)S(1)}, u32[]{:S(2)}, u32[]{:S(2)}) collective-permute-start(bf16[4,256,128]{2,1,0:T(8,128)(2,1)S(1)} %hist_send.3), channel_id=1, source_target_pairs={{0,4},{4,0},{8,12},{12,8},{16,20},{20,16},{24,28},{28,24},{1,5},{5... | collective-permute-start | bytes 786440 | tf_op jit(solution)/shard_map/ppermute | solution.py:34
  34.7 6.7 %collective-permute-start.14 = (bf16[32,1024]{1,0:T(8,128)(2,1)S(1)}, bf16[32,1024]{1,0:T(8,128)(2,1)S(1)}, u32[]{:S(2)}, u32[]{:S(2)}) collective-permute-start(bf16[32,1024]{1,0:T(8,128)(2,1)S(1)} %fusion.1.own_ref), channel_id=1, source_target_pairs={{0,4},{4,0},{8,12},{12,8},{16,20},{20,16},{24,28},{28,24},{1,5},{5... | collective-permute-start | bytes 196616 | tf_op jit(solution)/shard_map/ppermute | solution.py:34
  37.6 11.5 %collective-permute-start.3 = (bf16[4,256,128]{2,1,0:T(8,128)(2,1)S(1)}, bf16[4,256,128]{2,1,0:T(8,128)(2,1)S(1)}, u32[]{:S(2)}, u32[]{:S(2)}) collective-permute-start(bf16[4,256,128]{2,1,0:T(8,128)(2,1)S(1)} %hist_send.2), channel_id=1, source_target_pairs={{0,4},{4,0},{8,12},{12,8},{16,20},{20,16},{24,28},{28,24},{1,5},{5... | collective-permute-start | bytes 786440 | tf_op jit(solution)/shard_map/ppermute | solution.py:34
  47.5 6.1 %collective-permute-start.9 = (bf16[2,256,128]{2,1,0:T(8,128)(2,1)S(1)}, bf16[2,256,128]{2,1,0:T(8,128)(2,1)S(1)}, u32[]{:S(2)}, u32[]{:S(2)}) collective-permute-start(bf16[2,256,128]{2,1,0:T(8,128)(2,1)S(1)} %slice.68), channel_id=1, source_target_pairs={{0,8},{4,12},{8,0},{12,4},{16,24},{20,28},{24,16},{28,20},{1,9},{5... | collective-permute-start | bytes 393224 | tf_op jit(solution)/shard_map/ppermute | solution.py:34
  49.2 7.6 %collective-permute-start.4 = (bf16[2,256,128]{2,1,0:T(8,128)(2,1)S(1)}, bf16[2,256,128]{2,1,0:T(8,128)(2,1)S(1)}, u32[]{:S(2)}, u32[]{:S(2)}) collective-permute-start(bf16[2,256,128]{2,1,0:T(8,128)(2,1)S(1)} %slice.69), channel_id=1, source_target_pairs={{0,8},{4,12},{8,0},{12,4},{16,24},{20,28},{24,16},{28,20},{1,9},{5... | collective-permute-start | bytes 393224 | tf_op jit(solution)/shard_map/ppermute | solution.py:34
  53.7 6.4 %collective-permute-start.10 = (bf16[1,256,128]{2,1,0:T(8,128)(2,1)S(1)}, bf16[1,256,128]{2,1,0:T(8,128)(2,1)S(1)}, u32[]{:S(2)}, u32[]{:S(2)}) collective-permute-start(bf16[1,256,128]{2,1,0:T(8,128)(2,1)S(1)} %slice.70), channel_id=1, source_target_pairs={{0,16},{4,20},{8,24},{12,28},{16,0},{20,4},{24,8},{28,12},{1,17},{... | collective-permute-start | bytes 196616 | tf_op jit(solution)/shard_map/ppermute | solution.py:34
  56.8 5.7 %collective-permute-start.5 = (bf16[1,256,128]{2,1,0:T(8,128)(2,1)S(1)}, bf16[1,256,128]{2,1,0:T(8,128)(2,1)S(1)}, u32[]{:S(2)}, u32[]{:S(2)}) collective-permute-start(bf16[1,256,128]{2,1,0:T(8,128)(2,1)S(1)} %slice.71), channel_id=1, source_target_pairs={{0,16},{4,20},{8,24},{12,28},{16,0},{20,4},{24,8},{28,12},{1,17},{... | collective-permute-start | bytes 196616 | tf_op jit(solution)/shard_map/ppermute | solution.py:34

commit v3 on v0

v3 whole, which is shorter than its diff:
```python
import functools

import jax
import jax.numpy as jnp
from jax import lax
from jax.experimental import pallas as pl
from jax.experimental.pallas import tpu as pltpu
from jax.sharding import PartitionSpec as P

BINS = 256
LEAVES = 64


shrinkage = 0.5
ridge_term = 1.0

f32 = jnp.float32
bf16 = jnp.bfloat16
VMEM_LIMIT = 48 * 1024 * 1024


def block_rows(rows):
    for size in (256, 128, 64, 32, 16):
        if rows % size == 0:
            return size
    return rows


PARAMS = pltpu.CompilerParams(vmem_limit_bytes=VMEM_LIMIT)


def swap(x, axis, size, by):
    return lax.ppermute(x, axis, [(i, i ^ by) for i in range(size)])


def ordered(kernel, out_shape, args, after, name):
    def body(*refs):
        kernel(*refs[:len(args)], *refs[len(args) + 1:])

    many = isinstance(out_shape, (list, tuple))
    return pl.pallas_call(
        body,
        in_specs=[pl.BlockSpec(memory_space=pltpu.VMEM)] * len(args) + [pl.BlockSpec(memory_space=pl.ANY)],
        out_specs=[pl.BlockSpec(memory_space=pltpu.VMEM)] * len(out_shape)
        if many else pl.BlockSpec(memory_space=pltpu.VMEM),
        out_shape=out_shape,
        compiler_params=PARAMS,
        name=name,
    )(*args, after)


def rows_kernel(pos_ref, leaf_ref, pred_hbm, lab_hbm, w_hbm, send_ref, keep_ref, g_ref, h_ref,
                pred_buf, lab_buf, w_buf, pred_sem, lab_sem, w_sem):
    core, side = pos_ref[0], pos_ref[1]
    chunks, _, blk = leaf_ref.shape
    per_half = chunks // 2

    def place(i):
        half = 1 - core if i < per_half else core
        return half * per_half + i % per_half

    def copies(i):
        at = pl.ds(pl.multiple_of(place(i) * blk, blk), blk)
        return (pltpu.make_async_copy(pred_hbm.at[at], pred_buf.at[i], pred_sem.at[i]),
                pltpu.make_async_copy(lab_hbm.at[at], lab_buf.at[i], lab_sem.at[i]))

    w_copy = pltpu.make_async_copy(w_hbm, w_buf, w_sem)
    for i in range(chunks):
        for copy in copies(i):
            copy.start()
        if i == 0:
            w_copy.start()
    for i in range(chunks):
        for copy in copies(i):
            copy.wait()
        if i == 0:
            w_copy.wait()
        p = 0.5 * jnp.tanh((pred_buf[i] * 0.5).astype(f32)) + 0.5
        grad = (lab_buf[i].astype(f32) - p).astype(bf16)
        hess = (p - p * p).astype(bf16)
        out = send_ref if i < per_half else keep_ref
        out[pl.ds(i % per_half * blk, blk)] = jnp.dot(grad, w_buf[...], preferred_element_type=f32).astype(bf16)
        leaf = leaf_ref[place(i)] ^ (side * (LEAVES // 2))
        hot = (lax.broadcasted_iota(jnp.int32, (LEAVES, blk), 0) == leaf).astype(f32).astype(bf16)
        g = jnp.dot(hot, grad, preferred_element_type=f32)
        h = jnp.dot(hot, hess, preferred_element_type=f32)
        if i == 0:
            g_ref[...] = g
            h_ref[...] = h
        else:
            g_ref[...] += g
            h_ref[...] += h


def rows_pass(pos, leaf, pred, lab, w):
    chunks, _, blk = leaf.shape
    rows, cols = pred.shape
    vmem = pl.BlockSpec(memory_space=pltpu.VMEM)
    hbm = pl.BlockSpec(memory_space=pl.ANY)
    return pl.pallas_call(
        rows_kernel,
        in_specs=[pl.BlockSpec(memory_space=pltpu.SMEM), vmem, hbm, hbm, hbm],
        out_specs=[vmem] * 4,
        out_shape=[jax.ShapeDtypeStruct((rows // 2, w.shape[1]), bf16)] * 2
        + [jax.ShapeDtypeStruct((LEAVES, cols), f32)] * 2,
        scratch_shapes=[
            pltpu.VMEM((chunks, blk, cols), bf16),
            pltpu.VMEM((chunks, blk, cols), bf16),
            pltpu.VMEM(w.shape, bf16),
            pltpu.SemaphoreType.DMA((chunks,)),
            pltpu.SemaphoreType.DMA((chunks,)),
            pltpu.SemaphoreType.DMA,
        ],
        compiler_params=PARAMS,
        name="rows",
    )(pos, leaf, pred, lab, w)


def part_add(part, parts):
    def kernel(a_ref, b_ref, out_ref):
        width = out_ref.shape[1]
        at = slice(part * width, (part + 1) * width)
        out_ref[...] = (a_ref[:, at].astype(f32) + b_ref[:, at].astype(f32)).astype(bf16)
    return kernel


def add_kernel(a_ref, b_ref, out_ref):
    out_ref[...] = (a_ref[...].astype(f32) + b_ref[...].astype(f32)).astype(out_ref.dtype)


def leaf_pack_kernel(g_ref, h_ref, keep_ref, send_ref):
    half = LEAVES // 2
    keep_ref[:half] = g_ref[:half]
    keep_ref[half:] = h_ref[:half]
    send_ref[:half] = g_ref[half:].astype(bf16)
    send_ref[half:] = h_ref[half:].astype(bf16)


def value_kernel(a_ref, b_ref, out_ref):
    half = LEAVES // 2
    total = a_ref[...].astype(f32) + b_ref[...].astype(f32)
    out_ref[...] = (total[:half] / (total[half:] + ridge_term)).astype(bf16)


def halving_kernel(here_ref, back_ref, keep_ref, send_ref):
    half = keep_ref.shape[0]
    keep_ref[...] = here_ref[:half] + back_ref[:half].astype(f32)
    send_ref[...] = (here_ref[half:] + back_ref[half:].astype(f32)).astype(bf16)


def last_kernel(*refs):
    out_ref = refs[-1]
    width = refs[0].shape[2]
    for p in range(len(refs) // 2):
        out_ref[:, p * width:(p + 1) * width] = refs[2 * p][0] + refs[2 * p + 1][0].astype(f32)


def hist_kernel(codes_ref, own_ref, other_ref, after_ref, out_ref, *, per, odd, bits):
    feats = codes_ref.shape[1]
    half = codes_ref.shape[2]
    codes = codes_ref[...].astype(f32).astype(bf16)
    step = pl.program_id(0)
    place = sum(((step >> b) & 1) << (bits - 1 - b) for b in range(bits))
    base = (2 * place + odd) * per
    levels = (lax.broadcasted_iota(jnp.int32, (per, 1, 1), 0) + base).astype(f32).astype(bf16)
    one = jnp.ones((), bf16)
    zero = jnp.zeros((), bf16)
    total = None
    for part, ref in ((0, own_ref), (1, other_ref)):
        hot = jnp.where(codes[part][None] == levels, one, zero).reshape(per * feats, half)
        term = jnp.dot(hot, ref[...], preferred_element_type=f32)
        total = term if total is None else total + term
    out_ref[0] = total.astype(out_ref.dtype)


def hist_pass(codes, own, other, per, blocks, odd, dtype, after):
    feats = codes.shape[1]
    width = own.shape[1]
    whole = lambda a: pl.BlockSpec(a.shape, lambda i: (0,) * a.ndim)
    return pl.pallas_call(
        functools.partial(hist_kernel, per=per, odd=odd, bits=blocks.bit_length() - 1),
        grid=(blocks,),
        in_specs=[whole(codes), whole(own), whole(other), pl.BlockSpec(memory_space=pl.ANY)],
        out_specs=pl.BlockSpec((1, per * feats, width), lambda i: (i, 0, 0)),
        out_shape=jax.ShapeDtypeStruct((blocks, per * feats, width), dtype),
        compiler_params=PARAMS,
        name="hist_send" if odd else "hist_keep",
    )(codes, own, other, after)


def update_kernel(pos_ref, leaf_ref, own_ref, other_ref, pred_hbm, after_ref, new_hbm, values_ref,
                  pred_buf, new_buf, pred_sem, new_sem):
    side = pos_ref[1]
    chunks, _, blk = leaf_ref.shape
    half = LEAVES // 2

    def read(i):
        return pltpu.make_async_copy(pred_hbm.at[pl.ds(i * blk, blk)], pred_buf.at[i], pred_sem.at[i])

    def write(i):
        return pltpu.make_async_copy(new_buf.at[i], new_hbm.at[pl.ds(i * blk, blk)], new_sem.at[i])

    for i in range(chunks):
        read(i).start()
    own, other = own_ref[...], other_ref[...]
    first = side == 0
    values_ref[:half] = jnp.where(first, own.astype(f32), other.astype(f32))
    values_ref[half:] = jnp.where(first, other.astype(f32), own.astype(f32))
    table = jnp.concatenate([own, other], axis=0)
    for i in range(chunks):
        leaf = leaf_ref[i] ^ (side * half)
        hot = (lax.broadcasted_iota(jnp.int32, (LEAVES, blk), 0) == leaf).astype(f32) * shrinkage
        found = lax.dot_general(hot.astype(bf16), table, (((0,), (0,)), ((), ())), preferred_element_type=f32)
        read(i).wait()
        new_buf[i] = (pred_buf[i].astype(f32) + found).astype(bf16)
        write(i).start()
    for i in range(chunks):
        write(i).wait()


def update_pass(pos, leaf, own, other, pred, after):
    chunks, _, blk = leaf.shape
    rows, cols = pred.shape
    vmem = pl.BlockSpec(memory_space=pltpu.VMEM)
    hbm = pl.BlockSpec(memory_space=pl.ANY)
    return pl.pallas_call(
        update_kernel,
        in_specs=[pl.BlockSpec(memory_space=pltpu.SMEM), vmem, vmem, vmem, hbm, hbm],
        out_specs=[hbm, vmem],
        out_shape=[
            jax.ShapeDtypeStruct((rows, cols), bf16),
            jax.ShapeDtypeStruct((LEAVES, cols), f32),
        ],
        scratch_shapes=[
            pltpu.VMEM((chunks, blk, cols), bf16),
            pltpu.VMEM((chunks, blk, cols), bf16),
            pltpu.SemaphoreType.DMA((chunks,)),
            pltpu.SemaphoreType.DMA((chunks,)),
        ],
        compiler_params=PARAMS,
        name="update",
    )(pos, leaf, own, other, pred, after)


def local(n, nf, predictions, labels, feature_codes, leaf_index, sketch_weight):
    rows, cols = predictions.shape
    feats = feature_codes.shape[0]
    half = rows // 2
    parts = 2
    width = sketch_weight.shape[1] // parts
    me = lax.axis_index("rows")
    core = lax.axis_index("feat") & 1
    pos = jnp.stack([core, me & 1])
    per = BINS // n
    codes = (feature_codes ^ (me * per)).reshape(feats, 2, half)
    codes = jnp.where(core == 0, codes, codes[:, ::-1]).swapaxes(0, 1)
    blk = block_rows(half)
    leaf = leaf_index.reshape(rows // blk, 1, blk)

    pred = pltpu.with_memory_space_constraint(predictions, pltpu.HBM)
    lab = pltpu.with_memory_space_constraint(labels, pltpu.HBM)
    weight = pltpu.with_memory_space_constraint(sketch_weight, pltpu.HBM)
    sketch16 = jax.ShapeDtypeStruct((half, width), bf16)
    sums16 = jax.ShapeDtypeStruct((LEAVES, cols), bf16)
    sums32 = jax.ShapeDtypeStruct((LEAVES, cols), f32)

    send, keep, grad, hess = rows_pass(pos, leaf, pred, lab, weight)
    got = swap(send, "feat", nf, 1)
    pair, crossed, after = [], [], keep
    for p in range(parts):
        after = ordered(part_add(p, parts), sketch16, [keep, got], after, "core_add")
        pair.append(after)
        crossed.append([swap(after, "feat", nf, t) for t in range(2, nf, 2)])

    leaf_acc, sent = ordered(leaf_pack_kernel, [sums32, sums16], [grad, hess], after, "leaf_pack")
    leaf_got, leaf_by = swap(sent, "rows", n, 1), 2
    after = leaf_acc

    def leaf_step(acc, got, by, after):
        if by < n:
            acc = ordered(add_kernel, sums16, [acc, got], after, "leaf_add")
            return acc, swap(acc, "rows", n, by), 2 * by, acc
        if by == n:
            values16 = jax.ShapeDtypeStruct((LEAVES // 2, cols), bf16)
            acc = ordered(value_kernel, values16, [acc, got], after, "leaf_value")
            return acc, swap(acc, "rows", n, 1), 2 * by, acc
        return acc, got, by, after

    owns, others, backs, heres = [], [], [], []
    for p in range(parts):
        own = pair[p]
        for recv in crossed[p]:
            own = ordered(add_kernel, sketch16, [own, recv], after, "feat_add")
        owns.append(own)
        others.append(swap(own, "feat", nf, 1))
        after = hist_pass(codes, own, others[p], per, n // 2, 1, bf16, own)
        backs.append(swap(after, "rows", n, 1))
        if p == 0:
            leaf_acc, leaf_got, leaf_by, after = leaf_step(leaf_acc, leaf_got, leaf_by, after)
    after = hist_pass(codes, owns[0], others[0], per, n // 2, 0, f32, after)
    heres.append(after)

    levels = (n // 2).bit_length() - 1
    for slot in range(levels + parts - 1):
        for p in range(parts):
            level = slot - p
            if 0 <= level < levels:
                blocks = heres[p].shape[0] // 2
                shape = (blocks,) + heres[p].shape[1:]
                after, sent = ordered(
                    halving_kernel,
                    [jax.ShapeDtypeStruct(shape, f32), jax.ShapeDtypeStruct(shape, bf16)],
                    [heres[p], backs[p]], after, "hist_add")
                heres[p] = after
                backs[p] = swap(sent, "rows", n, 2 << level)
                if p == 1:
                    continue
                leaf_acc, leaf_got, leaf_by, after = leaf_step(leaf_acc, leaf_got, leaf_by, after)
                if slot == 0:
                    after = hist_pass(codes, owns[1], others[1], per, n // 2, 0, f32, after)
                    heres.append(after)
    while leaf_by <= n:
        leaf_acc, leaf_got, leaf_by, after = leaf_step(leaf_acc, leaf_got, leaf_by, after)
    updated, leaf_values = update_pass(pos, leaf, leaf_acc, leaf_got, pred, after)
    histograms = ordered(
        last_kernel, jax.ShapeDtypeStruct((per * feats, width * parts), f32),
        [a for p in range(parts) for a in (heres[p], backs[p])], leaf_values, "last_add")
    return histograms.reshape(per, feats, -1), leaf_values, updated


def solution(mesh):
    n, nf = mesh.shape["rows"], mesh.shape["feat"]
    return jax.shard_map(
        functools.partial(local, n, nf),
        mesh=mesh,
        in_specs=(
            P("rows", "feat"),
            P("rows", "feat"),
            P("feat", "rows"),
            P("rows"),
            P("feat", None),
        ),
        out_specs=(P("rows", "feat", None), P(None, "feat"), P("rows", "feat")),
        check_vma=False,
    )
```

time: 191 us -> 55.7 us (0.29)
  waiting for transfers between devices: 148 us -> 14.7 us
  starting transfers between devices: 0.08 us -> 19.3 us
  Pallas kernels: 0 us -> 18.8 us
  matrix products: 18.4 us -> 0 us
  between operations: 14.1 us -> 0.82 us
  other arithmetic: 6.02 us -> 0.09 us
    psum x2 -> x0, waiting for transfers between devices: 148 us -> none  [the longest x1 117 us: local(): lax.psum(jnp.einsum('bfr,rk->bfk', one_hot, sketch, preferred_element_typ...]
    ppermute x0 -> x15, starting transfers between devices: none -> 19.3 us  [swap(): return lax.ppermute(x, axis, [(i, i ^ by) for i in range(size)])]
    pallas_call x0 -> x19, Pallas kernels: none -> 18.8 us  [the longest x1 6.05 us: rows_pass(): pl.pallas_call(rows_kernel, in_specs=[pl.BlockSpec(memory_space=pltpu.SME...]
    dot_general x5 -> x0, matrix products: 18.4 us -> none  [the longest x1 5.75 us: local(): jnp.einsum('lr,lc->rc', leaf_hot.astype(jnp.float32), leaf_values, precis...]
    ppermute x0 -> x15, waiting for transfers between devices: none -> 14.7 us  [swap(): return lax.ppermute(x, axis, [(i, i ^ by) for i in range(size)])]
    convert_element_type x1 -> x0, other arithmetic: 4.95 us -> none  [local(): gradient = (labels.astype(jnp.float32) - probability).astype(jnp.bfloat16)]
  transfers between devices with their start and end apart: 2 -> 15, of which waited for: 2 -> 8; matrix products, arithmetic and copies ran while one was open for 3% -> 0% of each run, Pallas kernels for 0% -> 21%
where the time goes in v3:
time: 55.7 us; the launch traced here: 55.5 us
  starting transfers between devices  19.3 us (35%)
  Pallas kernels  18.8 us (34%)
  waiting for transfers between devices  14.7 us (26%)
  local copies, waits for them, and re-layouts  1.66 us (3%)
  between operations  0.82 us (1%)
    ppermute x15, starting transfers between devices, swap(): return lax.ppermute(x, axis, [(i, i ^ by) for i in range(size)])  19.3 us
    ppermute x15, waiting for transfers between devices, swap(): return lax.ppermute(x, axis, [(i, i ^ by) for i in range(size)])  14.7 us
    pallas_call x1, Pallas kernels, rows_pass(): pl.pallas_call(rows_kernel, in_specs=[pl.BlockSpec(memory_space=pltpu.SME...  6.05 us
    pallas_call x4, Pallas kernels, hist_pass(): pl.pallas_call(functools.partial(hist_kernel, per=per, odd=odd, bits=bloc...  5.86 us
    pallas_call x1, Pallas kernels, update_pass(): pl.pallas_call(update_kernel, in_specs=[pl.BlockSpec(memory_space=pltpu.S...  5.71 us
    pallas_call x13, Pallas kernels, ordered(): pl.pallas_call(body, in_specs=[pl.BlockSpec(memory_space=pltpu.VMEM)] * l...  1.21 us
  transfers between devices with their start and end apart: 15, of which 8 were waited for; matrix products, arithmetic and copies ran while one was open for 0% of the time, Pallas kernels for 21%

profile of v3, /device:TPU:0, one launch (start us, length us, event | category | flops | bytes accessed | tf_op | source)
XLA Modules:
  0.0 55.5 jit_solution(396531617510345400)
XLA Ops:
  0.6 0.7 %reshape.16.leaf_ref = s32[6,1,256]{2,1,0:T(1,128)S(1)} reshape(s32[1536]{0:T(1024)} %param.8) | data formatting | bytes 12288 | tf_op jit(solution)/shard_map/reshape | solution.py:258
  1.3 0.1 pad_add_fusion.pos_ref
  1.4 0.0 copy-start.1
  1.4 6.0 %rows.1 = (bf16[768,256]{1,0:T(8,128)(2,1)S(1)}, bf16[768,256]{1,0:T(8,128)(2,1)S(1)}, f32[64,1024]{1,0:T(8,128)S(1)}, f32[64,1024]{1,0:T(8,128)S(1)}) custom-call(s32[2]{0:T(128)S(1)} %pad_add_fusion.pos_ref, s32[6,1,256]{2,1,0:T(1,128)S(1)} %reshape.16.leaf_ref, bf16[1536,1024]{1,0:T(8,128)(2,1)} %pred_hbm.3, bf16[1536,1024]{1,0:T(8,128)(2,1)} %lab_hbm.1, ...), custom_call_target="tpu_custom_call" | custom-call | tf_op jit(solution)/shard_map/rows/pallas_call | solution.py:100
  7.5 0.5 collective-permute-start
  8.0 1.3 %collective-permute-done.refs_1_ = bf16[768,256]{1,0:T(8,128)(2,1)S(1)} collective-permute-done((bf16[768,256]{1,0:T(8,128)(2,1)S(1)}, bf16[768,256]{1,0:T(8,128)(2,1)S(1)}, u32[]{:S(2)}, u32[]{:S(2)}) %collective-permute-start) | collective-permute-done | bytes 393248 | tf_op jit(solution)/shard_map/ppermute | solution.py:33
  9.4 2.9 %collective-permute-start.1 = (bf16[768,128]{1,0:T(8,128)(2,1)S(1)}, bf16[768,128]{1,0:T(8,128)(2,1)S(1)}, u32[]{:S(2)}, u32[]{:S(2)}) collective-permute-start(bf16[768,128]{1,0:T(8,128)(2,1)S(1)} %core_add.2.refs_2_.refs_0_), channel_id=1, source_target_pairs={{0,2},{1,3},{2,0},{3,1},{4,6},{5,7},{6,4},{7,5},{8,10},{9,11},{10,... | collective-permute-start | bytes 589832 | tf_op jit(solution)/shard_map/ppermute | solution.py:33
  12.4 0.0 copy-done.1
  12.4 0.1 collective-permute-start.3
  12.6 2.0 %collective-permute-start.4 = (bf16[64,1024]{1,0:T(8,128)(2,1)S(1)}, bf16[64,1024]{1,0:T(8,128)(2,1)S(1)}, u32[]{:S(2)}, u32[]{:S(2)}) collective-permute-start(bf16[64,1024]{1,0:T(8,128)(2,1)S(1)} %get-tuple-element.24), channel_id=1, source_target_pairs={{0,4},{4,0},{8,12},{12,8},{16,20},{20,16},{24,28},{28,24},{1,5},{5... | collective-permute-start | bytes 393224 | tf_op jit(solution)/shard_map/ppermute | solution.py:33
  14.6 3.4 %collective-permute-done.1.refs_1_ = bf16[768,128]{1,0:T(8,128)(2,1)S(1)} collective-permute-done((bf16[768,128]{1,0:T(8,128)(2,1)S(1)}, bf16[768,128]{1,0:T(8,128)(2,1)S(1)}, u32[]{:S(2)}, u32[]{:S(2)}) %collective-permute-start.1) | collective-permute-done | bytes 196640 | tf_op jit(solution)/shard_map/ppermute | solution.py:33
  18.1 0.1 collective-permute-start.2
  18.2 1.4 %collective-permute-done.2.other_ref = bf16[768,128]{1,0:T(8,128)(2,1)S(1)} collective-permute-done((bf16[768,128]{1,0:T(8,128)(2,1)S(1)}, bf16[768,128]{1,0:T(8,128)(2,1)S(1)}, u32[]{:S(2)}, u32[]{:S(2)}) %collective-permute-start.2) | collective-permute-done | bytes 196640 | tf_op jit(solution)/shard_map/ppermute | solution.py:33
  19.6 1.5 %hist_send.2.refs_2_ = bf16[4,256,128]{2,1,0:T(8,128)(2,1)S(1)} custom-call(s32[2,8,768]{2,1,0:T(8,128)S(1)} %fusion.codes_ref, bf16[768,128]{1,0:T(8,128)(2,1)S(1)} %feat_add.2.own_ref.after_ref, bf16[768,128]{1,0:T(8,128)(2,1)S(1)} %collective-permute-done.2.other_ref, bf16[768,128]{1,0:T(8,128)(2,1)S(1)} %feat_add.2.own_ref.after_ref), custom_call_target="tpu_custom_call" | custom-call | tf_op jit(solution)/shard_map/hist_send/pallas_call | solution.py:180
  21.1 0.0 collective-permute-done.4.refs_1_
  21.1 0.7 %collective-permute-done.3.refs_1_ = bf16[768,128]{1,0:T(8,128)(2,1)S(1)} collective-permute-done((bf16[768,128]{1,0:T(8,128)(2,1)S(1)}, bf16[768,128]{1,0:T(8,128)(2,1)S(1)}, u32[]{:S(2)}, u32[]{:S(2)}) %collective-permute-start.3) | collective-permute-done | bytes 196640 | tf_op jit(solution)/shard_map/ppermute | solution.py:33
  21.8 0.1 collective-permute-start.5
  21.9 1.8 %collective-permute-start.6 = (bf16[4,256,128]{2,1,0:T(8,128)(2,1)S(1)}, bf16[4,256,128]{2,1,0:T(8,128)(2,1)S(1)}, u32[]{:S(2)}, u32[]{:S(2)}) collective-permute-start(bf16[4,256,128]{2,1,0:T(8,128)(2,1)S(1)} %hist_send.2.refs_2_), channel_id=1, source_target_pairs={{0,4},{4,0},{8,12},{12,8},{16,20},{20,16},{24,28},{28,24},{1,5},{5... | collective-permute-start | bytes 786440 | tf_op jit(solution)/shard_map/ppermute | solution.py:33
  23.7 1.6 %collective-permute-start.8 = (bf16[64,1024]{1,0:T(8,128)(2,1)S(1)}, bf16[64,1024]{1,0:T(8,128)(2,1)S(1)}, u32[]{:S(2)}, u32[]{:S(2)}) collective-permute-start(bf16[64,1024]{1,0:T(8,128)(2,1)S(1)} %leaf_add.2.refs_2_.refs_0_), channel_id=1, source_target_pairs={{0,8},{4,12},{8,0},{12,4},{16,24},{20,28},{24,16},{28,20},{1,9},{5... | collective-permute-start | bytes 393224 | tf_op jit(solution)/shard_map/ppermute | solution.py:33
  25.3 0.0 collective-permute-done.5.other_ref
  25.3 1.5 %hist_send.3.after_ref = bf16[4,256,128]{2,1,0:T(8,128)(2,1)S(1)} custom-call(s32[2,8,768]{2,1,0:T(8,128)S(1)} %fusion.codes_ref, bf16[768,128]{1,0:T(8,128)(2,1)S(1)} %feat_add.3.own_ref.after_ref, bf16[768,128]{1,0:T(8,128)(2,1)S(1)} %collective-permute-done.5.other_ref, bf16[768,128]{1,0:T(8,128)(2,1)S(1)} %feat_add.3.own_ref.after_ref), custom_call_target="tpu_custom_call" | custom-call | tf_op jit(solution)/shard_map/hist_send/pallas_call | solution.py:180
  26.7 0.6 %collective-permute-start.10 = (bf16[4,256,128]{2,1,0:T(8,128)(2,1)S(1)}, bf16[4,256,128]{2,1,0:T(8,128)(2,1)S(1)}, u32[]{:S(2)}, u32[]{:S(2)}) collective-permute-start(bf16[4,256,128]{2,1,0:T(8,128)(2,1)S(1)} %hist_send.3.after_ref), channel_id=1, source_target_pairs={{0,4},{4,0},{8,12},{12,8},{16,20},{20,16},{24,28},{28,24},{1,5},{5... | collective-permute-start | bytes 786440 | tf_op jit(solution)/shard_map/ppermute | solution.py:33
  27.3 1.5 %hist_keep.2.refs_0_.refs_2_ = f32[4,256,128]{2,1,0:T(8,128)S(1)} custom-call(s32[2,8,768]{2,1,0:T(8,128)S(1)} %fusion.codes_ref, bf16[768,128]{1,0:T(8,128)(2,1)S(1)} %feat_add.2.own_ref.after_ref, bf16[768,128]{1,0:T(8,128)(2,1)S(1)} %collective-permute-done.2.other_ref, bf16[4,256,128]{2,1,0:T(8,128)(2,1)S(1)} %hist_send.3.after_ref), custom_call_target="tpu_custom_call" | custom-call | tf_op jit(solution)/shard_map/hist_keep/pallas_call | solution.py:180
  28.8 2.3 %collective-permute-done.6.refs_1_ = bf16[4,256,128]{2,1,0:T(8,128)(2,1)S(1)} collective-permute-done((bf16[4,256,128]{2,1,0:T(8,128)(2,1)S(1)}, bf16[4,256,128]{2,1,0:T(8,128)(2,1)S(1)}, u32[]{:S(2)}, u32[]{:S(2)}) %collective-permute-start.6) | collective-permute-done | bytes 262176 | tf_op jit(solution)/shard_map/ppermute | solution.py:33
  31.1 1.9 %collective-permute-start.7 = (bf16[2,256,128]{2,1,0:T(8,128)(2,1)S(1)}, bf16[2,256,128]{2,1,0:T(8,128)(2,1)S(1)}, u32[]{:S(2)}, u32[]{:S(2)}) collective-permute-start(bf16[2,256,128]{2,1,0:T(8,128)(2,1)S(1)} %get-tuple-element.26), channel_id=1, source_target_pairs={{0,8},{4,12},{8,0},{12,4},{16,24},{20,28},{24,16},{28,20},{1,9},{5... | collective-permute-start | bytes 393224 | tf_op jit(solution)/shard_map/ppermute | solution.py:33
  33.0 0.0 collective-permute-done.8.refs_1_
  33.0 2.7 %collective-permute-start.11 = (bf16[64,1024]{1,0:T(8,128)(2,1)S(1)}, bf16[64,1024]{1,0:T(8,128)(2,1)S(1)}, u32[]{:S(2)}, u32[]{:S(2)}) collective-permute-start(bf16[64,1024]{1,0:T(8,128)(2,1)S(1)} %leaf_add.3.after_ref.refs_0_), channel_id=1, source_target_pairs={{0,16},{4,20},{8,24},{12,28},{16,0},{20,4},{24,8},{28,12},{1,17},{... | collective-permute-start | bytes 393224 | tf_op jit(solution)/shard_map/ppermute | solution.py:33
  35.7 1.5 %hist_keep.3.refs_2_.refs_0_ = f32[4,256,128]{2,1,0:T(8,128)S(1)} custom-call(s32[2,8,768]{2,1,0:T(8,128)S(1)} %fusion.codes_ref, bf16[768,128]{1,0:T(8,128)(2,1)S(1)} %feat_add.3.own_ref.after_ref, bf16[768,128]{1,0:T(8,128)(2,1)S(1)} %collective-permute-done.5.other_ref, bf16[64,1024]{1,0:T(8,128)(2,1)S(1)} %leaf_add.3.after_ref.refs_0_), custom_call_target="tpu_custom_call" | custom-call | tf_op jit(solution)/shard_map/hist_keep/pallas_call | solution.py:180
  37.2 0.3 collective-permute-done.7.refs_1_
  37.5 3.8 %collective-permute-done.11.refs_1_ = bf16[64,1024]{1,0:T(8,128)(2,1)S(1)} collective-permute-done((bf16[64,1024]{1,0:T(8,128)(2,1)S(1)}, bf16[64,1024]{1,0:T(8,128)(2,1)S(1)}, u32[]{:S(2)}, u32[]{:S(2)}) %collective-permute-start.11) | collective-permute-done | bytes 131104 | tf_op jit(solution)/shard_map/ppermute | solution.py:33
  41.3 0.0 collective-permute-done.10.refs_1_
  41.4 0.2 collective-permute-start.12
  41.6 1.5 %collective-permute-start.14 = (bf16[32,1024]{1,0:T(8,128)(2,1)S(1)}, bf16[32,1024]{1,0:T(8,128)(2,1)S(1)}, u32[]{:S(2)}, u32[]{:S(2)}) collective-permute-start(bf16[32,1024]{1,0:T(8,128)(2,1)S(1)} %leaf_value.1.refs_2_.own_ref), channel_id=1, source_target_pairs={{0,4},{4,0},{8,12},{12,8},{16,20},{20,16},{24,28},{28,24},{1,5},{5... | collective-permute-start | bytes 196616 | tf_op jit(solution)/shard_map/ppermute | solution.py:33
  43.1 2.9 %collective-permute-start.9 = (bf16[1,256,128]{2,1,0:T(8,128)(2,1)S(1)}, bf16[1,256,128]{2,1,0:T(8,128)(2,1)S(1)}, u32[]{:S(2)}, u32[]{:S(2)}) collective-permute-start(bf16[1,256,128]{2,1,0:T(8,128)(2,1)S(1)} %get-tuple-element.28), channel_id=1, source_target_pairs={{0,16},{4,20},{8,24},{12,28},{16,0},{20,4},{24,8},{28,12},{1,17},{... | collective-permute-start | bytes 196616 | tf_op jit(solution)/shard_map/ppermute | solution.py:33
  46.0 1.5 %collective-permute-done.12.refs_1_ = bf16[2,256,128]{2,1,0:T(8,128)(2,1)S(1)} collective-permute-done((bf16[2,256,128]{2,1,0:T(8,128)(2,1)S(1)}, bf16[2,256,128]{2,1,0:T(8,128)(2,1)S(1)}, u32[]{:S(2)}, u32[]{:S(2)}) %collective-permute-start.12) | collective-permute-done | bytes 131104 | tf_op jit(solution)/shard_map/ppermute | solution.py:33
  47.6 0.5 collective-permute-start.13
  48.1 0.0 collective-permute-done.14.other_ref
  48.1 5.7 %update.1 = (bf16[1536,1024]{1,0:T(8,128)(2,1)}, f32[64,1024]{1,0:T(8,128)}) custom-call(s32[2]{0:T(128)S(1)} %pad_add_fusion.pos_ref, s32[6,1,256]{2,1,0:T(1,128)S(1)} %reshape.16.leaf_ref, bf16[32,1024]{1,0:T(8,128)(2,1)S(1)} %leaf_value.1.refs_2_.own_ref, bf16[32,1024]{1,0:T(8,128)(2,1)S(1)} %collective-permute-done.14.other_ref, ...), custom_call_target="tpu_custom_call" | custom-call | tf_op jit(solution)/shard_map/update/pallas_call | solution.py:226
  53.8 0.0 collective-permute-done.9.refs_1_
  53.8 0.0 collective-permute-done.13.refs_3_
  53.8 0.0 copy-start
  53.8 0.9 %copy-done = f32[64,1024]{1,0:T(8,128)S(1)} copy-done((f32[64,1024]{1,0:T(8,128)S(1)}, f32[64,1024]{1,0:T(8,128)}, u32[]{:S(2)}) %copy-start) | copy-done | bytes 262168
  54.8 0.7 %last_add.1 = f32[256,256]{1,0:T(8,128)} custom-call(f32[1,256,128]{2,1,0:T(8,128)S(1)} %get-tuple-element.27.refs_2_.refs_0_, bf16[1,256,128]{2,1,0:T(8,128)(2,1)S(1)} %collective-permute-done.9.refs_1_, f32[1,256,128]{2,1,0:T(8,128)S(1)} %get-tuple-element.31.after_ref.refs_2_, bf16[1,256,128]{2,1,0:T(8,128)(2,1)S(1)} %collective-permute-done.13.refs_3_, ...), custom_call_target="tpu_custom_call" | custom-call | tf_op jit(solution)/shard_map/last_add/pallas_call | solution.py:41
  (14 shorter events, 0.5 us)
Async XLA Ops:
  1.4 10.9 %copy-start.1 = (s32[8,1536]{1,0:T(8,128)S(1)}, s32[8,1536]{1,0:T(8,128)}, u32[]{:S(2)}) copy-start(s32[8,1536]{1,0:T(8,128)} %param.7) | copy-start | bytes 147460
  7.5 1.9 %collective-permute-start = (bf16[768,256]{1,0:T(8,128)(2,1)S(1)}, bf16[768,256]{1,0:T(8,128)(2,1)S(1)}, u32[]{:S(2)}, u32[]{:S(2)}) collective-permute-start(bf16[768,256]{1,0:T(8,128)(2,1)S(1)} %get-tuple-element.20), channel_id=1, source_target_pairs={{0,1},{1,0},{2,3},{3,2},{4,5},{5,4},{6,7},{7,6},{8,9},{9,8},{10,11... | collective-permute-start | bytes 1179656 | tf_op jit(solution)/shard_map/ppermute | solution.py:33
  9.4 8.6 %collective-permute-start.1 = (bf16[768,128]{1,0:T(8,128)(2,1)S(1)}, bf16[768,128]{1,0:T(8,128)(2,1)S(1)}, u32[]{:S(2)}, u32[]{:S(2)}) collective-permute-start(bf16[768,128]{1,0:T(8,128)(2,1)S(1)} %core_add.2.refs_2_.refs_0_), channel_id=1, source_target_pairs={{0,2},{1,3},{2,0},{3,1},{4,6},{5,7},{6,4},{7,5},{8,10},{9,11},{10,... | collective-permute-start | bytes 589832 | tf_op jit(solution)/shard_map/ppermute | solution.py:33
  12.4 9.3 %collective-permute-start.3 = (bf16[768,128]{1,0:T(8,128)(2,1)S(1)}, bf16[768,128]{1,0:T(8,128)(2,1)S(1)}, u32[]{:S(2)}, u32[]{:S(2)}) collective-permute-start(bf16[768,128]{1,0:T(8,128)(2,1)S(1)} %core_add.3.refs_2_.refs_0_), channel_id=1, source_target_pairs={{0,2},{1,3},{2,0},{3,1},{4,6},{5,7},{6,4},{7,5},{8,10},{9,11},{10,... | collective-permute-start | bytes 589832 | tf_op jit(solution)/shard_map/ppermute | solution.py:33
  12.6 8.5 %collective-permute-start.4 = (bf16[64,1024]{1,0:T(8,128)(2,1)S(1)}, bf16[64,1024]{1,0:T(8,128)(2,1)S(1)}, u32[]{:S(2)}, u32[]{:S(2)}) collective-permute-start(bf16[64,1024]{1,0:T(8,128)(2,1)S(1)} %get-tuple-element.24), channel_id=1, source_target_pairs={{0,4},{4,0},{8,12},{12,8},{16,20},{20,16},{24,28},{28,24},{1,5},{5... | collective-permute-start | bytes 393224 | tf_op jit(solution)/shard_map/ppermute | solution.py:33
  18.1 1.5 %collective-permute-start.2 = (bf16[768,128]{1,0:T(8,128)(2,1)S(1)}, bf16[768,128]{1,0:T(8,128)(2,1)S(1)}, u32[]{:S(2)}, u32[]{:S(2)}) collective-permute-start(bf16[768,128]{1,0:T(8,128)(2,1)S(1)} %feat_add.2.own_ref.after_ref), channel_id=1, source_target_pairs={{0,1},{1,0},{2,3},{3,2},{4,5},{5,4},{6,7},{7,6},{8,9},{9,8},{10,11... | collective-permute-start | bytes 589832 | tf_op jit(solution)/shard_map/ppermute | solution.py:33
  21.8 3.4 %collective-permute-start.5 = (bf16[768,128]{1,0:T(8,128)(2,1)S(1)}, bf16[768,128]{1,0:T(8,128)(2,1)S(1)}, u32[]{:S(2)}, u32[]{:S(2)}) collective-permute-start(bf16[768,128]{1,0:T(8,128)(2,1)S(1)} %feat_add.3.own_ref.after_ref), channel_id=1, source_target_pairs={{0,1},{1,0},{2,3},{3,2},{4,5},{5,4},{6,7},{7,6},{8,9},{9,8},{10,11... | collective-permute-start | bytes 589832 | tf_op jit(solution)/shard_map/ppermute | solution.py:33
  21.9 9.2 %collective-permute-start.6 = (bf16[4,256,128]{2,1,0:T(8,128)(2,1)S(1)}, bf16[4,256,128]{2,1,0:T(8,128)(2,1)S(1)}, u32[]{:S(2)}, u32[]{:S(2)}) collective-permute-start(bf16[4,256,128]{2,1,0:T(8,128)(2,1)S(1)} %hist_send.2.refs_2_), channel_id=1, source_target_pairs={{0,4},{4,0},{8,12},{12,8},{16,20},{20,16},{24,28},{28,24},{1,5},{5... | collective-permute-start | bytes 786440 | tf_op jit(solution)/shard_map/ppermute | solution.py:33
  23.7 9.3 %collective-permute-start.8 = (bf16[64,1024]{1,0:T(8,128)(2,1)S(1)}, bf16[64,1024]{1,0:T(8,128)(2,1)S(1)}, u32[]{:S(2)}, u32[]{:S(2)}) collective-permute-start(bf16[64,1024]{1,0:T(8,128)(2,1)S(1)} %leaf_add.2.refs_2_.refs_0_), channel_id=1, source_target_pairs={{0,8},{4,12},{8,0},{12,4},{16,24},{20,28},{24,16},{28,20},{1,9},{5... | collective-permute-start | bytes 393224 | tf_op jit(solution)/shard_map/ppermute | solution.py:33
  26.7 14.6 %collective-permute-start.10 = (bf16[4,256,128]{2,1,0:T(8,128)(2,1)S(1)}, bf16[4,256,128]{2,1,0:T(8,128)(2,1)S(1)}, u32[]{:S(2)}, u32[]{:S(2)}) collective-permute-start(bf16[4,256,128]{2,1,0:T(8,128)(2,1)S(1)} %hist_send.3.after_ref), channel_id=1, source_target_pairs={{0,4},{4,0},{8,12},{12,8},{16,20},{20,16},{24,28},{28,24},{1,5},{5... | collective-permute-start | bytes 786440 | tf_op jit(solution)/shard_map/ppermute | solution.py:33
  31.1 6.3 %collective-permute-start.7 = (bf16[2,256,128]{2,1,0:T(8,128)(2,1)S(1)}, bf16[2,256,128]{2,1,0:T(8,128)(2,1)S(1)}, u32[]{:S(2)}, u32[]{:S(2)}) collective-permute-start(bf16[2,256,128]{2,1,0:T(8,128)(2,1)S(1)} %get-tuple-element.26), channel_id=1, source_target_pairs={{0,8},{4,12},{8,0},{12,4},{16,24},{20,28},{24,16},{28,20},{1,9},{5... | collective-permute-start | bytes 393224 | tf_op jit(solution)/shard_map/ppermute | solution.py:33
  33.0 8.3 %collective-permute-start.11 = (bf16[64,1024]{1,0:T(8,128)(2,1)S(1)}, bf16[64,1024]{1,0:T(8,128)(2,1)S(1)}, u32[]{:S(2)}, u32[]{:S(2)}) collective-permute-start(bf16[64,1024]{1,0:T(8,128)(2,1)S(1)} %leaf_add.3.after_ref.refs_0_), channel_id=1, source_target_pairs={{0,16},{4,20},{8,24},{12,28},{16,0},{20,4},{24,8},{28,12},{1,17},{... | collective-permute-start | bytes 393224 | tf_op jit(solution)/shard_map/ppermute | solution.py:33
  41.4 6.1 %collective-permute-start.12 = (bf16[2,256,128]{2,1,0:T(8,128)(2,1)S(1)}, bf16[2,256,128]{2,1,0:T(8,128)(2,1)S(1)}, u32[]{:S(2)}, u32[]{:S(2)}) collective-permute-start(bf16[2,256,128]{2,1,0:T(8,128)(2,1)S(1)} %get-tuple-element.30), channel_id=1, source_target_pairs={{0,8},{4,12},{8,0},{12,4},{16,24},{20,28},{24,16},{28,20},{1,9},{5... | collective-permute-start | bytes 393224 | tf_op jit(solution)/shard_map/ppermute | solution.py:33
  41.6 6.5 %collective-permute-start.14 = (bf16[32,1024]{1,0:T(8,128)(2,1)S(1)}, bf16[32,1024]{1,0:T(8,128)(2,1)S(1)}, u32[]{:S(2)}, u32[]{:S(2)}) collective-permute-start(bf16[32,1024]{1,0:T(8,128)(2,1)S(1)} %leaf_value.1.refs_2_.own_ref), channel_id=1, source_target_pairs={{0,4},{4,0},{8,12},{12,8},{16,20},{20,16},{24,28},{28,24},{1,5},{5... | collective-permute-start | bytes 196616 | tf_op jit(solution)/shard_map/ppermute | solution.py:33
  43.1 10.7 %collective-permute-start.9 = (bf16[1,256,128]{2,1,0:T(8,128)(2,1)S(1)}, bf16[1,256,128]{2,1,0:T(8,128)(2,1)S(1)}, u32[]{:S(2)}, u32[]{:S(2)}) collective-permute-start(bf16[1,256,128]{2,1,0:T(8,128)(2,1)S(1)} %get-tuple-element.28), channel_id=1, source_target_pairs={{0,16},{4,20},{8,24},{12,28},{16,0},{20,4},{24,8},{28,12},{1,17},{... | collective-permute-start | bytes 196616 | tf_op jit(solution)/shard_map/ppermute | solution.py:33
  47.6 6.2 %collective-permute-start.13 = (bf16[1,256,128]{2,1,0:T(8,128)(2,1)S(1)}, bf16[1,256,128]{2,1,0:T(8,128)(2,1)S(1)}, u32[]{:S(2)}, u32[]{:S(2)}) collective-permute-start(bf16[1,256,128]{2,1,0:T(8,128)(2,1)S(1)} %get-tuple-element.32), channel_id=1, source_target_pairs={{0,16},{4,20},{8,24},{12,28},{16,0},{20,4},{24,8},{28,12},{1,17},{... | collective-permute-start | bytes 196616 | tf_op jit(solution)/shard_map/ppermute | solution.py:33
  53.8 1.0 %copy-start = (f32[64,1024]{1,0:T(8,128)S(1)}, f32[64,1024]{1,0:T(8,128)}, u32[]{:S(2)}) copy-start(f32[64,1024]{1,0:T(8,128)} %get-tuple-element.17.refs_4_) | copy-start | bytes 786436

commit v4 on v3

--- a/solution.py
+++ b/solution.py
@@ -49,39 +49,51 @@
     )(*args, after)
 
 
-def rows_kernel(pos_ref, leaf_ref, pred_hbm, lab_hbm, w_hbm, send_ref, keep_ref, g_ref, h_ref,
-                pred_buf, lab_buf, w_buf, pred_sem, lab_sem, w_sem):
+def leaf_hot(leaf_ref, chunk, blk, flip, scale):
+    lanes = leaf_ref.shape[1]
+    lines = blk // lanes
+    leaf = jnp.concatenate([leaf_ref[pl.ds(chunk * lines + j, 1)] for j in range(lines)], axis=1)
+    hot = lax.broadcasted_iota(jnp.int32, (LEAVES, blk), 0) == (leaf ^ flip)
+    return jnp.where(hot, f32(scale), f32(0)).astype(bf16)
+
+
+def chunk_place(i, chunks, core):
+    per_half = chunks // 2
+    half = 1 - core if i < per_half else core
+    return half * per_half + i % per_half
+
+
+def rows_kernel(pos_ref, leaf_hbm, pred_hbm, lab_hbm, w_hbm, send_ref, keep_ref, g_ref, h_ref, pred_buf,
+                leaf_buf, lab_buf, w_buf, pred_sem, lab_sem, w_sem, leaf_sem):
     core, side = pos_ref[0], pos_ref[1]
-    chunks, _, blk = leaf_ref.shape
+    chunks, blk, _ = pred_buf.shape
     per_half = chunks // 2
 
-    def place(i):
-        half = 1 - core if i < per_half else core
-        return half * per_half + i % per_half
-
     def copies(i):
-        at = pl.ds(pl.multiple_of(place(i) * blk, blk), blk)
+        at = pl.ds(pl.multiple_of(chunk_place(i, chunks, core) * blk, blk), blk)
         return (pltpu.make_async_copy(pred_hbm.at[at], pred_buf.at[i], pred_sem.at[i]),
                 pltpu.make_async_copy(lab_hbm.at[at], lab_buf.at[i], lab_sem.at[i]))
 
     w_copy = pltpu.make_async_copy(w_hbm, w_buf, w_sem)
+    leaf_copy = pltpu.make_async_copy(leaf_hbm, leaf_buf, leaf_sem)
     for i in range(chunks):
-        for copy in copies(i):
-            copy.start()
+        for j, copy in enumerate(copies(i)):
+            copy.start(priority=j)
         if i == 0:
             w_copy.start()
+            leaf_copy.start(priority=1)
     for i in range(chunks):
         for copy in copies(i):
             copy.wait()
         if i == 0:
             w_copy.wait()
+            leaf_copy.wait()
         p = 0.5 * jnp.tanh((pred_buf[i] * 0.5).astype(f32)) + 0.5
         grad = (lab_buf[i].astype(f32) - p).astype(bf16)
         hess = (p - p * p).astype(bf16)
         out = send_ref if i < per_half else keep_ref
         out[pl.ds(i % per_half * blk, blk)] = jnp.dot(grad, w_buf[...], preferred_element_type=f32).astype(bf16)
-        leaf = leaf_ref[place(i)] ^ (side * (LEAVES // 2))
-        hot = (lax.broadcasted_iota(jnp.int32, (LEAVES, blk), 0) == leaf).astype(f32).astype(bf16)
+        hot = leaf_hot(leaf_buf, chunk_place(i, chunks, core), blk, side * (LEAVES // 2), 1.0)
         g = jnp.dot(hot, grad, preferred_element_type=f32)
         h = jnp.dot(hot, hess, preferred_element_type=f32)
         if i == 0:
@@ -93,22 +105,25 @@
 
 
 def rows_pass(pos, leaf, pred, lab, w):
-    chunks, _, blk = leaf.shape
     rows, cols = pred.shape
+    blk = block_rows(rows // 2)
+    chunks = rows // blk
     vmem = pl.BlockSpec(memory_space=pltpu.VMEM)
     hbm = pl.BlockSpec(memory_space=pl.ANY)
     return pl.pallas_call(
         rows_kernel,
-        in_specs=[pl.BlockSpec(memory_space=pltpu.SMEM), vmem, hbm, hbm, hbm],
-        out_specs=[vmem] * 4,
+        in_specs=[pl.BlockSpec(memory_space=pltpu.SMEM), hbm, hbm, hbm, hbm],
+        out_specs=[vmem] * 5,
         out_shape=[jax.ShapeDtypeStruct((rows // 2, w.shape[1]), bf16)] * 2
-        + [jax.ShapeDtypeStruct((LEAVES, cols), f32)] * 2,
+        + [jax.ShapeDtypeStruct((LEAVES, cols), f32)] * 2
+        + [jax.ShapeDtypeStruct((chunks, blk, cols), bf16)],
         scratch_shapes=[
-            pltpu.VMEM((chunks, blk, cols), bf16),
+            pltpu.VMEM(leaf.shape, jnp.int32),
             pltpu.VMEM((chunks, blk, cols), bf16),
             pltpu.VMEM(w.shape, bf16),
             pltpu.SemaphoreType.DMA((chunks,)),
             pltpu.SemaphoreType.DMA((chunks,)),
+            pltpu.SemaphoreType.DMA,
             pltpu.SemaphoreType.DMA,
         ],
         compiler_params=PARAMS,
@@ -188,54 +203,52 @@
     )(codes, own, other, after)
 
 
-def update_kernel(pos_ref, leaf_ref, own_ref, other_ref, pred_hbm, after_ref, new_hbm, values_ref,
-                  pred_buf, new_buf, pred_sem, new_sem):
-    side = pos_ref[1]
-    chunks, _, blk = leaf_ref.shape
+def update_kernel(pos_ref, leaf_ref, own_ref, other_ref, pred_ref, after_ref, new_hbm, values_hbm, done_ref,
+                  new_buf, values_buf, new_sem, values_sem):
+    core, side = pos_ref[0], pos_ref[1]
+    chunks, blk, _ = pred_ref.shape
     half = LEAVES // 2
 
-    def read(i):
-        return pltpu.make_async_copy(pred_hbm.at[pl.ds(i * blk, blk)], pred_buf.at[i], pred_sem.at[i])
-
     def write(i):
-        return pltpu.make_async_copy(new_buf.at[i], new_hbm.at[pl.ds(i * blk, blk)], new_sem.at[i])
-
-    for i in range(chunks):
-        read(i).start()
+        at = pl.ds(pl.multiple_of(chunk_place(i, chunks, core) * blk, blk), blk)
+        return pltpu.make_async_copy(new_buf.at[i], new_hbm.at[at], new_sem.at[i])
+
     own, other = own_ref[...], other_ref[...]
     first = side == 0
-    values_ref[:half] = jnp.where(first, own.astype(f32), other.astype(f32))
-    values_ref[half:] = jnp.where(first, other.astype(f32), own.astype(f32))
+    values_buf[:half] = jnp.where(first, own.astype(f32), other.astype(f32))
+    values_buf[half:] = jnp.where(first, other.astype(f32), own.astype(f32))
+    values_copy = pltpu.make_async_copy(values_buf, values_hbm, values_sem)
+    values_copy.start(priority=1)
     table = jnp.concatenate([own, other], axis=0)
     for i in range(chunks):
-        leaf = leaf_ref[i] ^ (side * half)
-        hot = (lax.broadcasted_iota(jnp.int32, (LEAVES, blk), 0) == leaf).astype(f32) * shrinkage
-        found = lax.dot_general(hot.astype(bf16), table, (((0,), (0,)), ((), ())), preferred_element_type=f32)
-        read(i).wait()
-        new_buf[i] = (pred_buf[i].astype(f32) + found).astype(bf16)
-        write(i).start()
+        hot = leaf_hot(leaf_ref, chunk_place(i, chunks, core), blk, side * half, shrinkage)
+        found = lax.dot_general(hot, table, (((0,), (0,)), ((), ())), preferred_element_type=f32)
+        new_buf[i] = (pred_ref[i].astype(f32) + found).astype(bf16)
+        write(i).start(priority=i % 2)
+    done_ref[...] = jnp.zeros_like(done_ref)
+    values_copy.wait()
     for i in range(chunks):
         write(i).wait()
 
 
 def update_pass(pos, leaf, own, other, pred, after):
-    chunks, _, blk = leaf.shape
-    rows, cols = pred.shape
+    chunks, blk, cols = pred.shape
     vmem = pl.BlockSpec(memory_space=pltpu.VMEM)
     hbm = pl.BlockSpec(memory_space=pl.ANY)
     return pl.pallas_call(
         update_kernel,
-        in_specs=[pl.BlockSpec(memory_space=pltpu.SMEM), vmem, vmem, vmem, hbm, hbm],
-        out_specs=[hbm, vmem],
+        in_specs=[pl.BlockSpec(memory_space=pltpu.SMEM), vmem, vmem, vmem, vmem, hbm],
+        out_specs=[pl.BlockSpec(memory_space=pltpu.HBM)] * 2 + [vmem],
         out_shape=[
-            jax.ShapeDtypeStruct((rows, cols), bf16),
+            jax.ShapeDtypeStruct((chunks * blk, cols), bf16),
             jax.ShapeDtypeStruct((LEAVES, cols), f32),
+            jax.ShapeDtypeStruct((8, 128), f32),
         ],
         scratch_shapes=[
             pltpu.VMEM((chunks, blk, cols), bf16),
-            pltpu.VMEM((chunks, blk, cols), bf16),
+            pltpu.VMEM((LEAVES, cols), f32),
             pltpu.SemaphoreType.DMA((chunks,)),
-            pltpu.SemaphoreType.DMA((chunks,)),
+            pltpu.SemaphoreType.DMA,
         ],
         compiler_params=PARAMS,
         name="update",
@@ -254,8 +267,8 @@
     per = BINS // n
     codes = (feature_codes ^ (me * per)).reshape(feats, 2, half)
     codes = jnp.where(core == 0, codes, codes[:, ::-1]).swapaxes(0, 1)
-    blk = block_rows(half)
-    leaf = leaf_index.reshape(rows // blk, 1, blk)
+    lanes = min(128, block_rows(half))
+    leaf = leaf_index.reshape(rows // lanes, lanes)
 
     pred = pltpu.with_memory_space_constraint(predictions, pltpu.HBM)
     lab = pltpu.with_memory_space_constraint(labels, pltpu.HBM)
@@ -264,40 +277,45 @@
     sums16 = jax.ShapeDtypeStruct((LEAVES, cols), bf16)
     sums32 = jax.ShapeDtypeStruct((LEAVES, cols), f32)
 
-    send, keep, grad, hess = rows_pass(pos, leaf, pred, lab, weight)
+    send, keep, grad, hess, held = rows_pass(pos, pltpu.with_memory_space_constraint(leaf, pltpu.HBM), pred, lab, weight)
     got = swap(send, "feat", nf, 1)
     pair, crossed, after = [], [], keep
     for p in range(parts):
         after = ordered(part_add(p, parts), sketch16, [keep, got], after, "core_add")
         pair.append(after)
         crossed.append([swap(after, "feat", nf, t) for t in range(2, nf, 2)])
-
-    leaf_acc, sent = ordered(leaf_pack_kernel, [sums32, sums16], [grad, hess], after, "leaf_pack")
-    leaf_got, leaf_by = swap(sent, "rows", n, 1), 2
-    after = leaf_acc
-
-    def leaf_step(acc, got, by, after):
+        if p == 0:
+            after, sent = ordered(leaf_pack_kernel, [sums32, sums16], [grad, hess], after, "leaf_pack")
+            leaf_state = (after, swap(sent, "rows", n, 1), 2)
+
+    def leaf_step(after):
+        nonlocal leaf_state
+        acc, got, by = leaf_state
         if by < n:
             acc = ordered(add_kernel, sums16, [acc, got], after, "leaf_add")
-            return acc, swap(acc, "rows", n, by), 2 * by, acc
-        if by == n:
+            leaf_state = (acc, swap(acc, "rows", n, by), 2 * by)
+        elif by == n:
             values16 = jax.ShapeDtypeStruct((LEAVES // 2, cols), bf16)
             acc = ordered(value_kernel, values16, [acc, got], after, "leaf_value")
-            return acc, swap(acc, "rows", n, 1), 2 * by, acc
-        return acc, got, by, after
+            leaf_state = (acc, swap(acc, "rows", n, 1), 2 * by)
+        else:
+            return after
+        return acc
 
     owns, others, backs, heres = [], [], [], []
     for p in range(parts):
         own = pair[p]
         for recv in crossed[p]:
-            own = ordered(add_kernel, sketch16, [own, recv], after, "feat_add")
+            after = own = ordered(add_kernel, sketch16, [own, recv], after, "feat_add")
         owns.append(own)
         others.append(swap(own, "feat", nf, 1))
-        after = hist_pass(codes, own, others[p], per, n // 2, 1, bf16, own)
+        if p > 0:
+            after = hist_pass(codes, owns[p - 1], others[p - 1], per, n // 2, 0, f32, after)
+            heres.append(after)
+        after = leaf_step(after)
+        after = hist_pass(codes, own, others[p], per, n // 2, 1, bf16, after)
         backs.append(swap(after, "rows", n, 1))
-        if p == 0:
-            leaf_acc, leaf_got, leaf_by, after = leaf_step(leaf_acc, leaf_got, leaf_by, after)
-    after = hist_pass(codes, owns[0], others[0], per, n // 2, 0, f32, after)
+    after = hist_pass(codes, owns[-1], others[-1], per, n // 2, 0, f32, after)
     heres.append(after)
 
     levels = (n // 2).bit_length() - 1
@@ -305,6 +323,11 @@
         for p in range(parts):
             level = slot - p
             if 0 <= level < levels:
+                if p == parts - 1 and level == levels - 1:
+                    while leaf_state[2] <= n:
+                        after = leaf_step(after)
+                    updated, leaf_values, after = update_pass(
+                        pos, leaf, leaf_state[0], leaf_state[1], held, after)
                 blocks = heres[p].shape[0] // 2
                 shape = (blocks,) + heres[p].shape[1:]
                 after, sent = ordered(
@@ -313,18 +336,11 @@
                     [heres[p], backs[p]], after, "hist_add")
                 heres[p] = after
                 backs[p] = swap(sent, "rows", n, 2 << level)
-                if p == 1:
-                    continue
-                leaf_acc, leaf_got, leaf_by, after = leaf_step(leaf_acc, leaf_got, leaf_by, after)
                 if slot == 0:
-                    after = hist_pass(codes, owns[1], others[1], per, n // 2, 0, f32, after)
-                    heres.append(after)
-    while leaf_by <= n:
-        leaf_acc, leaf_got, leaf_by, after = leaf_step(leaf_acc, leaf_got, leaf_by, after)
-    updated, leaf_values = update_pass(pos, leaf, leaf_acc, leaf_got, pred, after)
+                    after = leaf_step(after)
     histograms = ordered(
         last_kernel, jax.ShapeDtypeStruct((per * feats, width * parts), f32),
-        [a for p in range(parts) for a in (heres[p], backs[p])], leaf_values, "last_add")
+        [a for p in range(parts) for a in (heres[p], backs[p])], after, "last_add")
     return histograms.reshape(per, feats, -1), leaf_values, updated
 
 

time: 55.7 us -> 61.9 us (1.11)
  other arithmetic: 0.09 us -> 2.37 us
  local copies, waits for them, and re-layouts: 1.66 us -> 3.3 us
  starting transfers between devices: 19.3 us -> 20.5 us
  Pallas kernels: 18.8 us -> 19.7 us
    pallas_call x13, Pallas kernels: 1.21 us -> 4.9 us  [ordered(): pl.pallas_call(body, in_specs=[pl.BlockSpec(memory_space=pltpu.VMEM)] * l...]
    pallas_call x1, Pallas kernels: 5.71 us -> 2.67 us  [update_pass(): pl.pallas_call(update_kernel, in_specs=[pl.BlockSpec(memory_space=pltpu.S...]
    unnamed x4 -> x10, local copies, waits for them, and re-layouts: 0.95 us -> 3.3 us
    xor x1, other arithmetic: 0.01 us -> 1.41 us  [local(): codes = (feature_codes ^ me * per).reshape(feats, 2, half)]
    ppermute x15, starting transfers between devices: 19.3 us -> 20.5 us  [swap(): return lax.ppermute(x, axis, [(i, i ^ by) for i in range(size)])]
    transpose x1, other arithmetic: 0.01 us -> 0.89 us  [local(): codes = jnp.where(core == 0, codes, codes[:, ::-1]).swapaxes(0, 1)]
    reshape x1 -> x0, local copies, waits for them, and re-layouts: 0.71 us -> none  [local(): leaf = leaf_index.reshape(rows // blk, 1, blk)]
  transfers between devices with their start and end apart: 15 -> 15, of which waited for: 8 -> 9; matrix products, arithmetic and copies ran while one was open for 0% -> 4% of each run, Pallas kernels for 21% -> 18%
where the time goes in v4:
time: 61.9 us; the launch traced here: 61.5 us
  starting transfers between devices  20.5 us (33%)
  Pallas kernels  19.7 us (32%)
  waiting for transfers between devices  14.8 us (24%)
  local copies, waits for them, and re-layouts  3.3 us (5%)
  other arithmetic  2.37 us (4%)
  between operations  0.81 us (1%)
    ppermute x15, starting transfers between devices, swap(): return lax.ppermute(x, axis, [(i, i ^ by) for i in range(size)])  20.5 us
    ppermute x15, waiting for transfers between devices, swap(): return lax.ppermute(x, axis, [(i, i ^ by) for i in range(size)])  14.8 us
    pallas_call x1, Pallas kernels, rows_pass(): pl.pallas_call(rows_kernel, in_specs=[pl.BlockSpec(memory_space=pltpu.SME...  6.28 us
    pallas_call x4, Pallas kernels, hist_pass(): pl.pallas_call(functools.partial(hist_kernel, per=per, odd=odd, bits=bloc...  5.87 us
    pallas_call x13, Pallas kernels, ordered(): pl.pallas_call(body, in_specs=[pl.BlockSpec(memory_space=pltpu.VMEM)] * l...  4.9 us
    unnamed x10, local copies, waits for them, and re-layouts  3.3 us
    pallas_call x1, Pallas kernels, update_pass(): pl.pallas_call(update_kernel, in_specs=[pl.BlockSpec(memory_space=pltpu.S...  2.67 us
    xor x1, other arithmetic, local(): codes = (feature_codes ^ me * per).reshape(feats, 2, half)  1.41 us
  transfers between devices with their start and end apart: 15, of which 9 were waited for; matrix products, arithmetic and copies ran while one was open for 4% of the time, Pallas kernels for 18%

profile of v4, /device:TPU:0, one launch (start us, length us, event | category | flops | bytes accessed | tf_op | source)
XLA Modules:
  0.0 61.5 jit_solution(6086498148449490660)
XLA Ops:
  0.6 0.1 pad_add_fusion.pos_ref
  0.7 6.3 %rows.1 = (bf16[768,256]{1,0:T(8,128)(2,1)}, bf16[768,256]{1,0:T(8,128)(2,1)S(1)}, f32[64,1024]{1,0:T(8,128)S(1)}, f32[64,1024]{1,0:T(8,128)S(1)}, bf16[6,256,1024]{2,1,0:T(8,128)(2,1)S(1)}) custom-call(s32[2]{0:T(128)S(1)} %pad_add_fusion.pos_ref, s32[12,128]{1,0:T(8,128)} %bitcast.7, bf16[1536,1024]{1,0:T(8,128)(2,1)} %pred_hbm.1, ...), custom_call_target="tpu_custom_call" | custom-call | tf_op jit(solution)/shard_map/rows/pallas_call | solution.py:113
  7.0 0.0 copy-start
  7.0 0.7 %copy-done = f32[64,1024]{1,0:T(8,128)} copy-done((f32[64,1024]{1,0:T(8,128)}, f32[64,1024]{1,0:T(8,128)S(1)}, u32[]{:S(2)}) %copy-start) | copy-done | bytes 262168
  7.7 0.7 %copy-done.2 = f32[64,1024]{1,0:T(8,128)} copy-done((f32[64,1024]{1,0:T(8,128)}, f32[64,1024]{1,0:T(8,128)S(1)}, u32[]{:S(2)}) %copy-start.2) | copy-done | bytes 262168
  8.4 0.5 collective-permute-start
  8.9 1.7 %collective-permute-done.refs_1_ = bf16[768,256]{1,0:T(8,128)(2,1)} collective-permute-done((bf16[768,256]{1,0:T(8,128)(2,1)}, bf16[768,256]{1,0:T(8,128)(2,1)}, u32[]{:S(2)}, u32[]{:S(2)}) %collective-permute-start) | collective-permute-done | bytes 393248 | tf_op jit(solution)/shard_map/ppermute | solution.py:33
  10.5 1.7 %core_add.2.refs_2_.refs_0_ = bf16[768,128]{1,0:T(8,128)(2,1)} custom-call(bf16[768,256]{1,0:T(8,128)(2,1)S(1)} %get-tuple-element.21.refs_0_.refs_2_, bf16[768,256]{1,0:T(8,128)(2,1)} %collective-permute-done.refs_1_, bf16[768,256]{1,0:T(8,128)(2,1)S(1)} %get-tuple-element.21.refs_0_.refs_2_), custom_call_target="tpu_custom_call" | custom-call | tf_op jit(solution)/shard_map/core_add/pallas_call | solution.py:41
  12.3 2.9 %collective-permute-start.1 = (bf16[768,128]{1,0:T(8,128)(2,1)}, bf16[768,128]{1,0:T(8,128)(2,1)}, u32[]{:S(2)}, u32[]{:S(2)}) collective-permute-start(bf16[768,128]{1,0:T(8,128)(2,1)} %core_add.2.refs_2_.refs_0_), channel_id=1, source_target_pairs={{0,2},{1,3},{2,0},{3,1},{4,6},{5,7},{6,4},{7,5},{8,10},{9,11},{10,... | collective-permute-start | bytes 589832 | tf_op jit(solution)/shard_map/ppermute | solution.py:33
  15.2 1.4 %broadcast_xor_fusion = s32[8,1536]{1,0:T(8,128)} fusion(s32[8,1536]{1,0:T(8,128)} %param.7, s32[]{:T(128)S(6)} %mul.3), kind=kLoop, calls=%fused_computation.2 | loop fusion | flops 12288 | bytes 98308 | tf_op jit(solution)/shard_map/xor | solution.py:268
  16.6 0.9 %copy-done.1 = f32[64,1024]{1,0:T(8,128)S(1)} copy-done((f32[64,1024]{1,0:T(8,128)S(1)}, f32[64,1024]{1,0:T(8,128)}, u32[]{:S(2)}) %copy-start.1) | copy-done | bytes 262168
  17.5 0.9 %copy-done.3 = f32[64,1024]{1,0:T(8,128)S(1)} copy-done((f32[64,1024]{1,0:T(8,128)S(1)}, f32[64,1024]{1,0:T(8,128)}, u32[]{:S(2)}) %copy-start.3) | copy-done | bytes 262168
  18.5 1.6 %collective-permute-start.4 = (bf16[64,1024]{1,0:T(8,128)(2,1)S(1)}, bf16[64,1024]{1,0:T(8,128)(2,1)S(1)}, u32[]{:S(2)}, u32[]{:S(2)}) collective-permute-start(bf16[64,1024]{1,0:T(8,128)(2,1)S(1)} %get-tuple-element.26), channel_id=1, source_target_pairs={{0,4},{4,0},{8,12},{12,8},{16,20},{20,16},{24,28},{28,24},{1,5},{5... | collective-permute-start | bytes 393224 | tf_op jit(solution)/shard_map/ppermute | solution.py:33
  20.1 1.0 %core_add.3.refs_2_.refs_0_ = bf16[768,128]{1,0:T(8,128)(2,1)S(1)} custom-call(bf16[768,256]{1,0:T(8,128)(2,1)S(1)} %get-tuple-element.21.refs_0_.refs_2_, bf16[768,256]{1,0:T(8,128)(2,1)} %collective-permute-done.refs_1_, f32[64,1024]{1,0:T(8,128)S(1)} %get-tuple-element.25.refs_2_.refs_0_), custom_call_target="tpu_custom_call" | custom-call | tf_op jit(solution)/shard_map/core_add/pallas_call | solution.py:41
  21.1 0.6 collective-permute-start.3
  21.7 0.0 collective-permute-done.1.refs_1_
  21.7 1.1 %feat_add.2.refs_2_.own_ref = bf16[768,128]{1,0:T(8,128)(2,1)S(1)} custom-call(bf16[768,128]{1,0:T(8,128)(2,1)} %core_add.2.refs_2_.refs_0_, bf16[768,128]{1,0:T(8,128)(2,1)} %collective-permute-done.1.refs_1_, bf16[768,128]{1,0:T(8,128)(2,1)S(1)} %core_add.3.refs_2_.refs_0_), custom_call_target="tpu_custom_call" | custom-call | tf_op jit(solution)/shard_map/feat_add/pallas_call | solution.py:41
  22.7 0.1 collective-permute-start.2
  22.8 0.9 %fusion.codes_ref = s32[2,8,768]{2,1,0:T(8,128)S(1)} fusion(s32[8,2,768]{2,0,1:T(8,128)} %bitcast.10, pred[]{:T(512)S(6)} %eq.3), kind=kLoop, calls=%fused_computation.1 | loop fusion | flops 12288 | bytes 98305 | tf_op jit(solution)/shard_map/transpose | solution.py:269
  23.7 0.1 collective-permute-done.4.refs_1_
  23.9 0.4 collective-permute-done.2.other_ref
  24.3 1.5 %hist_send.2.refs_2_ = bf16[4,256,128]{2,1,0:T(8,128)(2,1)S(1)} custom-call(s32[2,8,768]{2,1,0:T(8,128)S(1)} %fusion.codes_ref, bf16[768,128]{1,0:T(8,128)(2,1)S(1)} %feat_add.2.refs_2_.own_ref, bf16[768,128]{1,0:T(8,128)(2,1)S(1)} %collective-permute-done.2.other_ref, bf16[64,1024]{1,0:T(8,128)(2,1)S(1)} %leaf_add.2.after_ref.refs_0_), custom_call_target="tpu_custom_call" | custom-call | tf_op jit(solution)/shard_map/hist_send/pallas_call | solution.py:195
  25.7 1.8 %collective-permute-done.3.refs_1_ = bf16[768,128]{1,0:T(8,128)(2,1)S(1)} collective-permute-done((bf16[768,128]{1,0:T(8,128)(2,1)S(1)}, bf16[768,128]{1,0:T(8,128)(2,1)S(1)}, u32[]{:S(2)}, u32[]{:S(2)}) %collective-permute-start.3) | collective-permute-done | bytes 196640 | tf_op jit(solution)/shard_map/ppermute | solution.py:33
  27.6 0.1 collective-permute-start.6
  27.7 0.6 collective-permute-start.5
  28.3 1.6 %collective-permute-start.7 = (bf16[64,1024]{1,0:T(8,128)(2,1)S(1)}, bf16[64,1024]{1,0:T(8,128)(2,1)S(1)}, u32[]{:S(2)}, u32[]{:S(2)}) collective-permute-start(bf16[64,1024]{1,0:T(8,128)(2,1)S(1)} %leaf_add.2.after_ref.refs_0_), channel_id=1, source_target_pairs={{0,8},{4,12},{8,0},{12,4},{16,24},{20,28},{24,16},{28,20},{1,9},{5... | collective-permute-start | bytes 393224 | tf_op jit(solution)/shard_map/ppermute | solution.py:33
  29.9 1.5 %hist_keep.2.refs_2_.refs_0_ = f32[4,256,128]{2,1,0:T(8,128)S(1)} custom-call(s32[2,8,768]{2,1,0:T(8,128)S(1)} %fusion.codes_ref, bf16[768,128]{1,0:T(8,128)(2,1)S(1)} %feat_add.2.refs_2_.own_ref, bf16[768,128]{1,0:T(8,128)(2,1)S(1)} %collective-permute-done.2.other_ref, bf16[768,128]{1,0:T(8,128)(2,1)S(1)} %feat_add.3.after_ref.own_ref), custom_call_target="tpu_custom_call" | custom-call | tf_op jit(solution)/shard_map/hist_keep/pallas_call | solution.py:195
  31.3 0.0 copy-start.4
  31.3 2.5 %collective-permute-done.7.refs_1_ = bf16[64,1024]{1,0:T(8,128)(2,1)S(1)} collective-permute-done((bf16[64,1024]{1,0:T(8,128)(2,1)S(1)}, bf16[64,1024]{1,0:T(8,128)(2,1)S(1)}, u32[]{:S(2)}, u32[]{:S(2)}) %collective-permute-start.7) | collective-permute-done | bytes 131104 | tf_op jit(solution)/shard_map/ppermute | solution.py:33
  33.9 0.0 collective-permute-done.6.other_ref
  33.9 1.5 %hist_send.3.after_ref = bf16[4,256,128]{2,1,0:T(8,128)(2,1)S(1)} custom-call(s32[2,8,768]{2,1,0:T(8,128)S(1)} %fusion.codes_ref, bf16[768,128]{1,0:T(8,128)(2,1)S(1)} %feat_add.3.after_ref.own_ref, bf16[768,128]{1,0:T(8,128)(2,1)S(1)} %collective-permute-done.6.other_ref, bf16[64,1024]{1,0:T(8,128)(2,1)S(1)} %leaf_add.3.after_ref.refs_0_), custom_call_target="tpu_custom_call" | custom-call | tf_op jit(solution)/shard_map/hist_send/pallas_call | solution.py:195
  35.4 1.6 %collective-permute-start.11 = (bf16[4,256,128]{2,1,0:T(8,128)(2,1)S(1)}, bf16[4,256,128]{2,1,0:T(8,128)(2,1)S(1)}, u32[]{:S(2)}, u32[]{:S(2)}) collective-permute-start(bf16[4,256,128]{2,1,0:T(8,128)(2,1)S(1)} %hist_send.3.after_ref), channel_id=1, source_target_pairs={{0,4},{4,0},{8,12},{12,8},{16,20},{20,16},{24,28},{28,24},{1,5},{5... | collective-permute-start | bytes 786440 | tf_op jit(solution)/shard_map/ppermute | solution.py:33
  36.9 2.6 %collective-permute-start.9 = (bf16[64,1024]{1,0:T(8,128)(2,1)S(1)}, bf16[64,1024]{1,0:T(8,128)(2,1)S(1)}, u32[]{:S(2)}, u32[]{:S(2)}) collective-permute-start(bf16[64,1024]{1,0:T(8,128)(2,1)S(1)} %leaf_add.3.after_ref.refs_0_), channel_id=1, source_target_pairs={{0,16},{4,20},{8,24},{12,28},{16,0},{20,4},{24,8},{28,12},{1,17},{... | collective-permute-start | bytes 393224 | tf_op jit(solution)/shard_map/ppermute | solution.py:33
  39.5 1.5 %hist_keep.3.refs_2_.refs_0_ = f32[4,256,128]{2,1,0:T(8,128)S(1)} custom-call(s32[2,8,768]{2,1,0:T(8,128)S(1)} %fusion.codes_ref, bf16[768,128]{1,0:T(8,128)(2,1)S(1)} %feat_add.3.after_ref.own_ref, bf16[768,128]{1,0:T(8,128)(2,1)S(1)} %collective-permute-done.6.other_ref, bf16[4,256,128]{2,1,0:T(8,128)(2,1)S(1)} %hist_send.3.after_ref), custom_call_target="tpu_custom_call" | custom-call | tf_op jit(solution)/shard_map/hist_keep/pallas_call | solution.py:195
  41.0 0.0 collective-permute-done.5.refs_1_
  41.1 1.6 %collective-permute-start.8 = (bf16[2,256,128]{2,1,0:T(8,128)(2,1)S(1)}, bf16[2,256,128]{2,1,0:T(8,128)(2,1)S(1)}, u32[]{:S(2)}, u32[]{:S(2)}) collective-permute-start(bf16[2,256,128]{2,1,0:T(8,128)(2,1)S(1)} %get-tuple-element.28), channel_id=1, source_target_pairs={{0,8},{4,12},{8,0},{12,4},{16,24},{20,28},{24,16},{28,20},{1,9},{5... | collective-permute-start | bytes 393224 | tf_op jit(solution)/shard_map/ppermute | solution.py:33
  42.7 2.5 %collective-permute-done.9.refs_1_ = bf16[64,1024]{1,0:T(8,128)(2,1)S(1)} collective-permute-done((bf16[64,1024]{1,0:T(8,128)(2,1)S(1)}, bf16[64,1024]{1,0:T(8,128)(2,1)S(1)}, u32[]{:S(2)}, u32[]{:S(2)}) %collective-permute-start.9) | collective-permute-done | bytes 131104 | tf_op jit(solution)/shard_map/ppermute | solution.py:33
  45.3 1.3 %collective-permute-done.8.refs_1_ = bf16[2,256,128]{2,1,0:T(8,128)(2,1)S(1)} collective-permute-done((bf16[2,256,128]{2,1,0:T(8,128)(2,1)S(1)}, bf16[2,256,128]{2,1,0:T(8,128)(2,1)S(1)}, u32[]{:S(2)}, u32[]{:S(2)}) %collective-permute-start.8) | collective-permute-done | bytes 131104 | tf_op jit(solution)/shard_map/ppermute | solution.py:33
  46.6 0.0 collective-permute-done.11.refs_1_
  46.7 1.2 %collective-permute-start.12 = (bf16[2,256,128]{2,1,0:T(8,128)(2,1)S(1)}, bf16[2,256,128]{2,1,0:T(8,128)(2,1)S(1)}, u32[]{:S(2)}, u32[]{:S(2)}) collective-permute-start(bf16[2,256,128]{2,1,0:T(8,128)(2,1)S(1)} %get-tuple-element.32), channel_id=1, source_target_pairs={{0,8},{4,12},{8,0},{12,4},{16,24},{20,28},{24,16},{28,20},{1,9},{5... | collective-permute-start | bytes 393224 | tf_op jit(solution)/shard_map/ppermute | solution.py:33
  47.8 0.5 collective-permute-start.13
  48.4 2.5 %collective-permute-start.10 = (bf16[1,256,128]{2,1,0:T(8,128)(2,1)S(1)}, bf16[1,256,128]{2,1,0:T(8,128)(2,1)S(1)}, u32[]{:S(2)}, u32[]{:S(2)}) collective-permute-start(bf16[1,256,128]{2,1,0:T(8,128)(2,1)S(1)} %get-tuple-element.30), channel_id=1, source_target_pairs={{0,16},{4,20},{8,24},{12,28},{16,0},{20,4},{24,8},{28,12},{1,17},{... | collective-permute-start | bytes 196616 | tf_op jit(solution)/shard_map/ppermute | solution.py:33
  50.9 1.2 %collective-permute-done.13.other_ref = bf16[32,1024]{1,0:T(8,128)(2,1)S(1)} collective-permute-done((bf16[32,1024]{1,0:T(8,128)(2,1)S(1)}, bf16[32,1024]{1,0:T(8,128)(2,1)S(1)}, u32[]{:S(2)}, u32[]{:S(2)}) %collective-permute-start.13) | collective-permute-done | bytes 65568 | tf_op jit(solution)/shard_map/ppermute | solution.py:33
  52.1 2.7 %update.1 = (bf16[1536,1024]{1,0:T(8,128)(2,1)}, f32[64,1024]{1,0:T(8,128)}, f32[8,128]{1,0:T(8,128)S(1)}) custom-call(s32[2]{0:T(128)S(1)} %pad_add_fusion.pos_ref, s32[12,128]{1,0:T(8,128)S(1)} %bitcast.8, bf16[32,1024]{1,0:T(8,128)(2,1)S(1)} %leaf_value.1.refs_2_.own_ref, bf16[32,1024]{1,0:T(8,128)(2,1)S(1)} %collective-permute-done.13.other_ref, ...), custom_call_target="tpu_custom_call" | custom-call | tf_op jit(solution)/shard_map/update/pallas_call | solution.py:238
  54.8 0.0 collective-permute-done.12.refs_1_
  54.8 2.6 %collective-permute-start.14 = (bf16[1,256,128]{2,1,0:T(8,128)(2,1)S(1)}, bf16[1,256,128]{2,1,0:T(8,128)(2,1)S(1)}, u32[]{:S(2)}, u32[]{:S(2)}) collective-permute-start(bf16[1,256,128]{2,1,0:T(8,128)(2,1)S(1)} %get-tuple-element.36), channel_id=1, source_target_pairs={{0,16},{4,20},{8,24},{12,28},{16,0},{20,4},{24,8},{28,12},{1,17},{... | collective-permute-start | bytes 196616 | tf_op jit(solution)/shard_map/ppermute | solution.py:33
  57.5 3.3 %collective-permute-done.14.refs_3_ = bf16[1,256,128]{2,1,0:T(8,128)(2,1)S(1)} collective-permute-done((bf16[1,256,128]{2,1,0:T(8,128)(2,1)S(1)}, bf16[1,256,128]{2,1,0:T(8,128)(2,1)S(1)}, u32[]{:S(2)}, u32[]{:S(2)}) %collective-permute-start.14) | collective-permute-done | bytes 65568 | tf_op jit(solution)/shard_map/ppermute | solution.py:33
  60.8 0.7 %last_add.1 = f32[256,256]{1,0:T(8,128)} custom-call(f32[1,256,128]{2,1,0:T(8,128)S(1)} %get-tuple-element.29.refs_2_.refs_0_, bf16[1,256,128]{2,1,0:T(8,128)(2,1)S(1)} %collective-permute-done.10.refs_1_, f32[1,256,128]{2,1,0:T(8,128)S(1)} %get-tuple-element.35.refs_2_.refs_4_, bf16[1,256,128]{2,1,0:T(8,128)(2,1)S(1)} %collective-permute-done.14.refs_3_, ...), custom_call_target="tpu_custom_call" | custom-call | tf_op jit(solution)/shard_map/last_add/pallas_call | solution.py:41
  (14 shorter events, 0.3 us)
Async XLA Ops:
  7.0 0.7 %copy-start = (f32[64,1024]{1,0:T(8,128)}, f32[64,1024]{1,0:T(8,128)S(1)}, u32[]{:S(2)}) copy-start(f32[64,1024]{1,0:T(8,128)S(1)} %get-tuple-element.23.refs_0_) | copy-start | bytes 786436
  7.7 0.7 %copy-start.2 = (f32[64,1024]{1,0:T(8,128)}, f32[64,1024]{1,0:T(8,128)S(1)}, u32[]{:S(2)}) copy-start(f32[64,1024]{1,0:T(8,128)S(1)} %get-tuple-element.24.refs_1_) | copy-start | bytes 786436
  8.4 2.1 %collective-permute-start = (bf16[768,256]{1,0:T(8,128)(2,1)}, bf16[768,256]{1,0:T(8,128)(2,1)}, u32[]{:S(2)}, u32[]{:S(2)}) collective-permute-start(bf16[768,256]{1,0:T(8,128)(2,1)} %get-tuple-element.22), channel_id=1, source_target_pairs={{0,1},{1,0},{2,3},{3,2},{4,5},{5,4},{6,7},{7,6},{8,9},{9,8},{10,11... | collective-permute-start | bytes 1179656 | tf_op jit(solution)/shard_map/ppermute | solution.py:33
  12.3 9.4 %collective-permute-start.1 = (bf16[768,128]{1,0:T(8,128)(2,1)}, bf16[768,128]{1,0:T(8,128)(2,1)}, u32[]{:S(2)}, u32[]{:S(2)}) collective-permute-start(bf16[768,128]{1,0:T(8,128)(2,1)} %core_add.2.refs_2_.refs_0_), channel_id=1, source_target_pairs={{0,2},{1,3},{2,0},{3,1},{4,6},{5,7},{6,4},{7,5},{8,10},{9,11},{10,... | collective-permute-start | bytes 589832 | tf_op jit(solution)/shard_map/ppermute | solution.py:33
  16.6 0.9 %copy-start.1 = (f32[64,1024]{1,0:T(8,128)S(1)}, f32[64,1024]{1,0:T(8,128)}, u32[]{:S(2)}) copy-start(f32[64,1024]{1,0:T(8,128)} %copy-done) | copy-start | bytes 786436
  17.5 0.9 %copy-start.3 = (f32[64,1024]{1,0:T(8,128)S(1)}, f32[64,1024]{1,0:T(8,128)}, u32[]{:S(2)}) copy-start(f32[64,1024]{1,0:T(8,128)} %copy-done.2) | copy-start | bytes 786436
  18.5 5.3 %collective-permute-start.4 = (bf16[64,1024]{1,0:T(8,128)(2,1)S(1)}, bf16[64,1024]{1,0:T(8,128)(2,1)S(1)}, u32[]{:S(2)}, u32[]{:S(2)}) collective-permute-start(bf16[64,1024]{1,0:T(8,128)(2,1)S(1)} %get-tuple-element.26), channel_id=1, source_target_pairs={{0,4},{4,0},{8,12},{12,8},{16,20},{20,16},{24,28},{28,24},{1,5},{5... | collective-permute-start | bytes 393224 | tf_op jit(solution)/shard_map/ppermute | solution.py:33
  21.1 6.4 %collective-permute-start.3 = (bf16[768,128]{1,0:T(8,128)(2,1)S(1)}, bf16[768,128]{1,0:T(8,128)(2,1)S(1)}, u32[]{:S(2)}, u32[]{:S(2)}) collective-permute-start(bf16[768,128]{1,0:T(8,128)(2,1)S(1)} %core_add.3.refs_2_.refs_0_), channel_id=1, source_target_pairs={{0,2},{1,3},{2,0},{3,1},{4,6},{5,7},{6,4},{7,5},{8,10},{9,11},{10,... | collective-permute-start | bytes 589832 | tf_op jit(solution)/shard_map/ppermute | solution.py:33
  22.7 1.5 %collective-permute-start.2 = (bf16[768,128]{1,0:T(8,128)(2,1)S(1)}, bf16[768,128]{1,0:T(8,128)(2,1)S(1)}, u32[]{:S(2)}, u32[]{:S(2)}) collective-permute-start(bf16[768,128]{1,0:T(8,128)(2,1)S(1)} %feat_add.2.refs_2_.own_ref), channel_id=1, source_target_pairs={{0,1},{1,0},{2,3},{3,2},{4,5},{5,4},{6,7},{7,6},{8,9},{9,8},{10,11... | collective-permute-start | bytes 589832 | tf_op jit(solution)/shard_map/ppermute | solution.py:33
  27.6 6.3 %collective-permute-start.6 = (bf16[768,128]{1,0:T(8,128)(2,1)S(1)}, bf16[768,128]{1,0:T(8,128)(2,1)S(1)}, u32[]{:S(2)}, u32[]{:S(2)}) collective-permute-start(bf16[768,128]{1,0:T(8,128)(2,1)S(1)} %feat_add.3.after_ref.own_ref), channel_id=1, source_target_pairs={{0,1},{1,0},{2,3},{3,2},{4,5},{5,4},{6,7},{7,6},{8,9},{9,8},{10,11... | collective-permute-start | bytes 589832 | tf_op jit(solution)/shard_map/ppermute | solution.py:33
  27.7 13.3 %collective-permute-start.5 = (bf16[4,256,128]{2,1,0:T(8,128)(2,1)S(1)}, bf16[4,256,128]{2,1,0:T(8,128)(2,1)S(1)}, u32[]{:S(2)}, u32[]{:S(2)}) collective-permute-start(bf16[4,256,128]{2,1,0:T(8,128)(2,1)S(1)} %hist_send.2.refs_2_), channel_id=1, source_target_pairs={{0,4},{4,0},{8,12},{12,8},{16,20},{20,16},{24,28},{28,24},{1,5},{5... | collective-permute-start | bytes 786440 | tf_op jit(solution)/shard_map/ppermute | solution.py:33
  28.3 5.6 %collective-permute-start.7 = (bf16[64,1024]{1,0:T(8,128)(2,1)S(1)}, bf16[64,1024]{1,0:T(8,128)(2,1)S(1)}, u32[]{:S(2)}, u32[]{:S(2)}) collective-permute-start(bf16[64,1024]{1,0:T(8,128)(2,1)S(1)} %leaf_add.2.after_ref.refs_0_), channel_id=1, source_target_pairs={{0,8},{4,12},{8,0},{12,4},{16,24},{20,28},{24,16},{28,20},{1,9},{5... | collective-permute-start | bytes 393224 | tf_op jit(solution)/shard_map/ppermute | solution.py:33
  31.3 20.8 %copy-start.4 = (s32[1536]{0:T(1024)S(1)}, s32[1536]{0:T(1024)}, u32[]{:S(2)}) copy-start(s32[1536]{0:T(1024)} %param.8) | copy-start | bytes 18436
  35.4 11.2 %collective-permute-start.11 = (bf16[4,256,128]{2,1,0:T(8,128)(2,1)S(1)}, bf16[4,256,128]{2,1,0:T(8,128)(2,1)S(1)}, u32[]{:S(2)}, u32[]{:S(2)}) collective-permute-start(bf16[4,256,128]{2,1,0:T(8,128)(2,1)S(1)} %hist_send.3.after_ref), channel_id=1, source_target_pairs={{0,4},{4,0},{8,12},{12,8},{16,20},{20,16},{24,28},{28,24},{1,5},{5... | collective-permute-start | bytes 786440 | tf_op jit(solution)/shard_map/ppermute | solution.py:33
  36.9 8.3 %collective-permute-start.9 = (bf16[64,1024]{1,0:T(8,128)(2,1)S(1)}, bf16[64,1024]{1,0:T(8,128)(2,1)S(1)}, u32[]{:S(2)}, u32[]{:S(2)}) collective-permute-start(bf16[64,1024]{1,0:T(8,128)(2,1)S(1)} %leaf_add.3.after_ref.refs_0_), channel_id=1, source_target_pairs={{0,16},{4,20},{8,24},{12,28},{16,0},{20,4},{24,8},{28,12},{1,17},{... | collective-permute-start | bytes 393224 | tf_op jit(solution)/shard_map/ppermute | solution.py:33
  41.1 5.5 %collective-permute-start.8 = (bf16[2,256,128]{2,1,0:T(8,128)(2,1)S(1)}, bf16[2,256,128]{2,1,0:T(8,128)(2,1)S(1)}, u32[]{:S(2)}, u32[]{:S(2)}) collective-permute-start(bf16[2,256,128]{2,1,0:T(8,128)(2,1)S(1)} %get-tuple-element.28), channel_id=1, source_target_pairs={{0,8},{4,12},{8,0},{12,4},{16,24},{20,28},{24,16},{28,20},{1,9},{5... | collective-permute-start | bytes 393224 | tf_op jit(solution)/shard_map/ppermute | solution.py:33
  46.7 8.1 %collective-permute-start.12 = (bf16[2,256,128]{2,1,0:T(8,128)(2,1)S(1)}, bf16[2,256,128]{2,1,0:T(8,128)(2,1)S(1)}, u32[]{:S(2)}, u32[]{:S(2)}) collective-permute-start(bf16[2,256,128]{2,1,0:T(8,128)(2,1)S(1)} %get-tuple-element.32), channel_id=1, source_target_pairs={{0,8},{4,12},{8,0},{12,4},{16,24},{20,28},{24,16},{28,20},{1,9},{5... | collective-permute-start | bytes 393224 | tf_op jit(solution)/shard_map/ppermute | solution.py:33
  47.8 4.3 %collective-permute-start.13 = (bf16[32,1024]{1,0:T(8,128)(2,1)S(1)}, bf16[32,1024]{1,0:T(8,128)(2,1)S(1)}, u32[]{:S(2)}, u32[]{:S(2)}) collective-permute-start(bf16[32,1024]{1,0:T(8,128)(2,1)S(1)} %leaf_value.1.refs_2_.own_ref), channel_id=1, source_target_pairs={{0,4},{4,0},{8,12},{12,8},{16,20},{20,16},{24,28},{28,24},{1,5},{5... | collective-permute-start | bytes 196616 | tf_op jit(solution)/shard_map/ppermute | solution.py:33
  48.4 9.1 %collective-permute-start.10 = (bf16[1,256,128]{2,1,0:T(8,128)(2,1)S(1)}, bf16[1,256,128]{2,1,0:T(8,128)(2,1)S(1)}, u32[]{:S(2)}, u32[]{:S(2)}) collective-permute-start(bf16[1,256,128]{2,1,0:T(8,128)(2,1)S(1)} %get-tuple-element.30), channel_id=1, source_target_pairs={{0,16},{4,20},{8,24},{12,28},{16,0},{20,4},{24,8},{28,12},{1,17},{... | collective-permute-start | bytes 196616 | tf_op jit(solution)/shard_map/ppermute | solution.py:33
  54.8 5.9 %collective-permute-start.14 = (bf16[1,256,128]{2,1,0:T(8,128)(2,1)S(1)}, bf16[1,256,128]{2,1,0:T(8,128)(2,1)S(1)}, u32[]{:S(2)}, u32[]{:S(2)}) collective-permute-start(bf16[1,256,128]{2,1,0:T(8,128)(2,1)S(1)} %get-tuple-element.36), channel_id=1, source_target_pairs={{0,16},{4,20},{8,24},{12,28},{16,0},{20,4},{24,8},{28,12},{1,17},{... | collective-permute-start | bytes 196616 | tf_op jit(solution)/shard_map/ppermute | solution.py:33

commit v5 on v4

--- a/solution.py
+++ b/solution.py
@@ -16,7 +16,7 @@
 
 f32 = jnp.float32
 bf16 = jnp.bfloat16
-VMEM_LIMIT = 48 * 1024 * 1024
+VMEM_LIMIT = 16 * 1024 * 1024
 
 
 def block_rows(rows):
@@ -303,6 +303,7 @@
         return acc
 
     owns, others, backs, heres = [], [], [], []
+    after = leaf_step(after)
     for p in range(parts):
         own = pair[p]
         for recv in crossed[p]:
@@ -310,9 +311,9 @@
         owns.append(own)
         others.append(swap(own, "feat", nf, 1))
         if p > 0:
+            after = leaf_step(after)
             after = hist_pass(codes, owns[p - 1], others[p - 1], per, n // 2, 0, f32, after)
             heres.append(after)
-        after = leaf_step(after)
         after = hist_pass(codes, own, others[p], per, n // 2, 1, bf16, after)
         backs.append(swap(after, "rows", n, 1))
     after = hist_pass(codes, owns[-1], others[-1], per, n // 2, 0, f32, after)

time: 61.9 us -> 64 us (1.034)
  waiting for transfers between devices: 14.8 us -> 13.1 us
  local copies, waits for them, and re-layouts: 3.3 us -> 4.96 us
  Pallas kernels: 19.7 us -> 21.3 us
    ppermute x15, waiting for transfers between devices: 14.8 us -> 13.1 us  [swap(): return lax.ppermute(x, axis, [(i, i ^ by) for i in range(size)])]
    unnamed x10 -> x14, local copies, waits for them, and re-layouts: 3.3 us -> 4.96 us
    pallas_call x13, Pallas kernels: 4.9 us -> 6.47 us  [ordered(): pl.pallas_call(body, in_specs=[pl.BlockSpec(memory_space=pltpu.VMEM)] * l...]
  transfers between devices with their start and end apart: 15 -> 15, of which waited for: 9 -> 8; matrix products, arithmetic and copies ran while one was open for 4% -> 4% of each run, Pallas kernels for 18% -> 20%
where the time goes in v5:
time: 64 us; the launch traced here: 63.5 us
  Pallas kernels  21.3 us (33%)
  starting transfers between devices  21 us (33%)
  waiting for transfers between devices  13.1 us (20%)
  local copies, waits for them, and re-layouts  4.96 us (8%)
  other arithmetic  2.38 us (4%)
  between operations  0.82 us (1%)
    ppermute x15, starting transfers between devices, swap(): return lax.ppermute(x, axis, [(i, i ^ by) for i in range(size)])  21 us
    ppermute x15, waiting for transfers between devices, swap(): return lax.ppermute(x, axis, [(i, i ^ by) for i in range(size)])  13.1 us
    pallas_call x13, Pallas kernels, ordered(): pl.pallas_call(body, in_specs=[pl.BlockSpec(memory_space=pltpu.VMEM)] * l...  6.47 us
    pallas_call x1, Pallas kernels, rows_pass(): pl.pallas_call(rows_kernel, in_specs=[pl.BlockSpec(memory_space=pltpu.SME...  6.28 us
    pallas_call x4, Pallas kernels, hist_pass(): pl.pallas_call(functools.partial(hist_kernel, per=per, odd=odd, bits=bloc...  5.89 us
    unnamed x14, local copies, waits for them, and re-layouts  4.96 us
    pallas_call x1, Pallas kernels, update_pass(): pl.pallas_call(update_kernel, in_specs=[pl.BlockSpec(memory_space=pltpu.S...  2.67 us
    xor x1, other arithmetic, local(): codes = (feature_codes ^ me * per).reshape(feats, 2, half)  1.42 us
  transfers between devices with their start and end apart: 15, of which 8 were waited for; matrix products, arithmetic and copies ran while one was open for 4% of the time, Pallas kernels for 20%

profile of v5, /device:TPU:0, one launch (start us, length us, event | category | flops | bytes accessed | tf_op | source)
XLA Modules:
  0.0 63.5 jit_solution(12873234961235632799)
XLA Ops:
  0.6 0.1 pad_add_fusion.pos_ref
  0.7 6.3 %rows.1 = (bf16[768,256]{1,0:T(8,128)(2,1)}, bf16[768,256]{1,0:T(8,128)(2,1)S(1)}, f32[64,1024]{1,0:T(8,128)S(1)}, f32[64,1024]{1,0:T(8,128)S(1)}, bf16[6,256,1024]{2,1,0:T(8,128)(2,1)S(1)}) custom-call(s32[2]{0:T(128)S(1)} %pad_add_fusion.pos_ref, s32[12,128]{1,0:T(8,128)} %bitcast.7, bf16[1536,1024]{1,0:T(8,128)(2,1)} %pred_hbm.1, ...), custom_call_target="tpu_custom_call" | custom-call | tf_op jit(solution)/shard_map/rows/pallas_call | solution.py:113
  7.0 0.0 copy-start.2
  7.0 0.7 %copy-done.2 = f32[64,1024]{1,0:T(8,128)} copy-done((f32[64,1024]{1,0:T(8,128)}, f32[64,1024]{1,0:T(8,128)S(1)}, u32[]{:S(2)}) %copy-start.2) | copy-done | bytes 262168
  7.7 0.7 %copy-done.4 = f32[64,1024]{1,0:T(8,128)} copy-done((f32[64,1024]{1,0:T(8,128)}, f32[64,1024]{1,0:T(8,128)S(1)}, u32[]{:S(2)}) %copy-start.4) | copy-done | bytes 262168
  8.4 0.5 collective-permute-start
  8.9 1.7 %collective-permute-done.refs_1_ = bf16[768,256]{1,0:T(8,128)(2,1)} collective-permute-done((bf16[768,256]{1,0:T(8,128)(2,1)}, bf16[768,256]{1,0:T(8,128)(2,1)}, u32[]{:S(2)}, u32[]{:S(2)}) %collective-permute-start) | collective-permute-done | bytes 393248 | tf_op jit(solution)/shard_map/ppermute | solution.py:33
  10.5 1.7 %core_add.2.refs_2_.refs_0_ = bf16[768,128]{1,0:T(8,128)(2,1)} custom-call(bf16[768,256]{1,0:T(8,128)(2,1)S(1)} %get-tuple-element.21.refs_0_.refs_2_, bf16[768,256]{1,0:T(8,128)(2,1)} %collective-permute-done.refs_1_, bf16[768,256]{1,0:T(8,128)(2,1)S(1)} %get-tuple-element.21.refs_0_.refs_2_), custom_call_target="tpu_custom_call" | custom-call | tf_op jit(solution)/shard_map/core_add/pallas_call | solution.py:41
  12.3 2.9 %collective-permute-start.1 = (bf16[768,128]{1,0:T(8,128)(2,1)}, bf16[768,128]{1,0:T(8,128)(2,1)}, u32[]{:S(2)}, u32[]{:S(2)}) collective-permute-start(bf16[768,128]{1,0:T(8,128)(2,1)} %core_add.2.refs_2_.refs_0_), channel_id=1, source_target_pairs={{0,2},{1,3},{2,0},{3,1},{4,6},{5,7},{6,4},{7,5},{8,10},{9,11},{10,... | collective-permute-start | bytes 589832 | tf_op jit(solution)/shard_map/ppermute | solution.py:33
  15.2 0.9 %copy-done.3 = f32[64,1024]{1,0:T(8,128)S(1)} copy-done((f32[64,1024]{1,0:T(8,128)S(1)}, f32[64,1024]{1,0:T(8,128)}, u32[]{:S(2)}) %copy-start.3) | copy-done | bytes 262168
  16.1 0.9 %copy-done.5 = f32[64,1024]{1,0:T(8,128)S(1)} copy-done((f32[64,1024]{1,0:T(8,128)S(1)}, f32[64,1024]{1,0:T(8,128)}, u32[]{:S(2)}) %copy-start.5) | copy-done | bytes 262168
  17.1 0.7 %leaf_pack.1 = (f32[64,1024]{1,0:T(8,128)S(1)}, bf16[64,1024]{1,0:T(8,128)(2,1)}) custom-call(f32[64,1024]{1,0:T(8,128)S(1)} %copy-done.3, f32[64,1024]{1,0:T(8,128)S(1)} %copy-done.5, bf16[768,128]{1,0:T(8,128)(2,1)} %core_add.2.refs_2_.refs_0_), custom_call_target="tpu_custom_call" | custom-call | tf_op jit(solution)/shard_map/leaf_pack/pallas_call | solution.py:41
  17.7 0.7 %copy-done = f32[64,1024]{1,0:T(8,128)} copy-done((f32[64,1024]{1,0:T(8,128)}, f32[64,1024]{1,0:T(8,128)S(1)}, u32[]{:S(2)}) %copy-start) | copy-done | bytes 262168
  18.4 1.5 %collective-permute-start.2 = (bf16[64,1024]{1,0:T(8,128)(2,1)}, bf16[64,1024]{1,0:T(8,128)(2,1)}, u32[]{:S(2)}, u32[]{:S(2)}) collective-permute-start(bf16[64,1024]{1,0:T(8,128)(2,1)} %get-tuple-element.26), channel_id=1, source_target_pairs={{0,4},{4,0},{8,12},{12,8},{16,20},{20,16},{24,28},{28,24},{1,5},{5... | collective-permute-start | bytes 393224 | tf_op jit(solution)/shard_map/ppermute | solution.py:33
  19.9 1.4 %broadcast_xor_fusion = s32[8,1536]{1,0:T(8,128)} fusion(s32[8,1536]{1,0:T(8,128)} %param.7, s32[]{:T(128)S(6)} %mul.3), kind=kLoop, calls=%fused_computation.2 | loop fusion | flops 12288 | bytes 98308 | tf_op jit(solution)/shard_map/xor | solution.py:268
  21.4 0.9 %copy-done.1 = f32[64,1024]{1,0:T(8,128)S(1)} copy-done((f32[64,1024]{1,0:T(8,128)S(1)}, f32[64,1024]{1,0:T(8,128)}, u32[]{:S(2)}) %copy-start.1) | copy-done | bytes 262168
  22.3 1.0 %core_add.3.refs_2_.refs_0_ = bf16[768,128]{1,0:T(8,128)(2,1)S(1)} custom-call(bf16[768,256]{1,0:T(8,128)(2,1)S(1)} %get-tuple-element.21.refs_0_.refs_2_, bf16[768,256]{1,0:T(8,128)(2,1)} %collective-permute-done.refs_1_, f32[64,1024]{1,0:T(8,128)S(1)} %copy-done.1), custom_call_target="tpu_custom_call" | custom-call | tf_op jit(solution)/shard_map/core_add/pallas_call | solution.py:41
  23.3 0.6 collective-permute-start.5
  23.9 0.1 collective-permute-done.2.refs_1_
  24.0 0.9 %leaf_add.2.refs_2_.refs_0_ = bf16[64,1024]{1,0:T(8,128)(2,1)S(1)} custom-call(f32[64,1024]{1,0:T(8,128)S(1)} %copy-done.1, bf16[64,1024]{1,0:T(8,128)(2,1)} %collective-permute-done.2.refs_1_, bf16[768,128]{1,0:T(8,128)(2,1)S(1)} %core_add.3.refs_2_.refs_0_), custom_call_target="tpu_custom_call" | custom-call | tf_op jit(solution)/shard_map/leaf_add/pallas_call | solution.py:41
  25.0 1.1 %feat_add.2.own_ref.after_ref = bf16[768,128]{1,0:T(8,128)(2,1)S(1)} custom-call(bf16[768,128]{1,0:T(8,128)(2,1)} %core_add.2.refs_2_.refs_0_, bf16[768,128]{1,0:T(8,128)(2,1)} %collective-permute-done.1.refs_1_, bf16[64,1024]{1,0:T(8,128)(2,1)S(1)} %leaf_add.2.refs_2_.refs_0_), custom_call_target="tpu_custom_call" | custom-call | tf_op jit(solution)/shard_map/feat_add/pallas_call | solution.py:41
  26.1 0.1 collective-permute-start.3
  26.1 0.9 %fusion.codes_ref = s32[2,8,768]{2,1,0:T(8,128)S(1)} fusion(s32[8,2,768]{2,0,1:T(8,128)} %bitcast.10, pred[]{:T(512)S(6)} %eq.3), kind=kLoop, calls=%fused_computation.1 | loop fusion | flops 12288 | bytes 98305 | tf_op jit(solution)/shard_map/transpose | solution.py:269
  27.0 0.5 collective-permute-done.3.other_ref
  27.6 1.5 %hist_send.2.refs_2_ = bf16[4,256,128]{2,1,0:T(8,128)(2,1)S(1)} custom-call(s32[2,8,768]{2,1,0:T(8,128)S(1)} %fusion.codes_ref, bf16[768,128]{1,0:T(8,128)(2,1)S(1)} %feat_add.2.own_ref.after_ref, bf16[768,128]{1,0:T(8,128)(2,1)S(1)} %collective-permute-done.3.other_ref, bf16[768,128]{1,0:T(8,128)(2,1)S(1)} %feat_add.2.own_ref.after_ref), custom_call_target="tpu_custom_call" | custom-call | tf_op jit(solution)/shard_map/hist_send/pallas_call | solution.py:195
  29.0 0.8 %collective-permute-done.5.refs_1_ = bf16[768,128]{1,0:T(8,128)(2,1)S(1)} collective-permute-done((bf16[768,128]{1,0:T(8,128)(2,1)S(1)}, bf16[768,128]{1,0:T(8,128)(2,1)S(1)}, u32[]{:S(2)}, u32[]{:S(2)}) %collective-permute-start.5) | collective-permute-done | bytes 196640 | tf_op jit(solution)/shard_map/ppermute | solution.py:33
  29.8 0.1 collective-permute-start.7
  29.9 1.6 %collective-permute-start.4 = (bf16[64,1024]{1,0:T(8,128)(2,1)S(1)}, bf16[64,1024]{1,0:T(8,128)(2,1)S(1)}, u32[]{:S(2)}, u32[]{:S(2)}) collective-permute-start(bf16[64,1024]{1,0:T(8,128)(2,1)S(1)} %leaf_add.2.refs_2_.refs_0_), channel_id=1, source_target_pairs={{0,8},{4,12},{8,0},{12,4},{16,24},{20,28},{24,16},{28,20},{1,9},{5... | collective-permute-start | bytes 393224 | tf_op jit(solution)/shard_map/ppermute | solution.py:33
  31.6 0.8 %collective-permute-start.6 = (bf16[4,256,128]{2,1,0:T(8,128)(2,1)S(1)}, bf16[4,256,128]{2,1,0:T(8,128)(2,1)S(1)}, u32[]{:S(2)}, u32[]{:S(2)}) collective-permute-start(bf16[4,256,128]{2,1,0:T(8,128)(2,1)S(1)} %hist_send.2.refs_2_), channel_id=1, source_target_pairs={{0,4},{4,0},{8,12},{12,8},{16,20},{20,16},{24,28},{28,24},{1,5},{5... | collective-permute-start | bytes 786440 | tf_op jit(solution)/shard_map/ppermute | solution.py:33
  32.4 3.5 %collective-permute-done.4.refs_1_ = bf16[64,1024]{1,0:T(8,128)(2,1)S(1)} collective-permute-done((bf16[64,1024]{1,0:T(8,128)(2,1)S(1)}, bf16[64,1024]{1,0:T(8,128)(2,1)S(1)}, u32[]{:S(2)}, u32[]{:S(2)}) %collective-permute-start.4) | collective-permute-done | bytes 131104 | tf_op jit(solution)/shard_map/ppermute | solution.py:33
  35.9 1.5 %hist_keep.2.after_ref.refs_0_ = f32[4,256,128]{2,1,0:T(8,128)S(1)} custom-call(s32[2,8,768]{2,1,0:T(8,128)S(1)} %fusion.codes_ref, bf16[768,128]{1,0:T(8,128)(2,1)S(1)} %feat_add.2.own_ref.after_ref, bf16[768,128]{1,0:T(8,128)(2,1)S(1)} %collective-permute-done.3.other_ref, bf16[64,1024]{1,0:T(8,128)(2,1)S(1)} %leaf_add.3.after_ref.refs_0_), custom_call_target="tpu_custom_call" | custom-call | tf_op jit(solution)/shard_map/hist_keep/pallas_call | solution.py:195
  37.4 0.0 copy-start.6
  37.4 0.0 collective-permute-done.7.other_ref
  37.4 1.5 %hist_send.3.after_ref = bf16[4,256,128]{2,1,0:T(8,128)(2,1)S(1)} custom-call(s32[2,8,768]{2,1,0:T(8,128)S(1)} %fusion.codes_ref, bf16[768,128]{1,0:T(8,128)(2,1)S(1)} %feat_add.3.refs_2_.own_ref, bf16[768,128]{1,0:T(8,128)(2,1)S(1)} %collective-permute-done.7.other_ref, f32[4,256,128]{2,1,0:T(8,128)S(1)} %hist_keep.2.after_ref.refs_0_), custom_call_target="tpu_custom_call" | custom-call | tf_op jit(solution)/shard_map/hist_send/pallas_call | solution.py:195
  38.9 0.8 %collective-permute-start.11 = (bf16[4,256,128]{2,1,0:T(8,128)(2,1)S(1)}, bf16[4,256,128]{2,1,0:T(8,128)(2,1)S(1)}, u32[]{:S(2)}, u32[]{:S(2)}) collective-permute-start(bf16[4,256,128]{2,1,0:T(8,128)(2,1)S(1)} %hist_send.3.after_ref), channel_id=1, source_target_pairs={{0,4},{4,0},{8,12},{12,8},{16,20},{20,16},{24,28},{28,24},{1,5},{5... | collective-permute-start | bytes 786440 | tf_op jit(solution)/shard_map/ppermute | solution.py:33
  39.7 2.6 %collective-permute-start.9 = (bf16[64,1024]{1,0:T(8,128)(2,1)S(1)}, bf16[64,1024]{1,0:T(8,128)(2,1)S(1)}, u32[]{:S(2)}, u32[]{:S(2)}) collective-permute-start(bf16[64,1024]{1,0:T(8,128)(2,1)S(1)} %leaf_add.3.after_ref.refs_0_), channel_id=1, source_target_pairs={{0,16},{4,20},{8,24},{12,28},{16,0},{20,4},{24,8},{28,12},{1,17},{... | collective-permute-start | bytes 393224 | tf_op jit(solution)/shard_map/ppermute | solution.py:33
  42.3 1.5 %hist_keep.3.refs_2_.refs_0_ = f32[4,256,128]{2,1,0:T(8,128)S(1)} custom-call(s32[2,8,768]{2,1,0:T(8,128)S(1)} %fusion.codes_ref, bf16[768,128]{1,0:T(8,128)(2,1)S(1)} %feat_add.3.refs_2_.own_ref, bf16[768,128]{1,0:T(8,128)(2,1)S(1)} %collective-permute-done.7.other_ref, bf16[4,256,128]{2,1,0:T(8,128)(2,1)S(1)} %hist_send.3.after_ref), custom_call_target="tpu_custom_call" | custom-call | tf_op jit(solution)/shard_map/hist_keep/pallas_call | solution.py:195
  43.8 1.6 %collective-permute-start.8 = (bf16[2,256,128]{2,1,0:T(8,128)(2,1)S(1)}, bf16[2,256,128]{2,1,0:T(8,128)(2,1)S(1)}, u32[]{:S(2)}, u32[]{:S(2)}) collective-permute-start(bf16[2,256,128]{2,1,0:T(8,128)(2,1)S(1)} %get-tuple-element.28), channel_id=1, source_target_pairs={{0,8},{4,12},{8,0},{12,4},{16,24},{20,28},{24,16},{28,20},{1,9},{5... | collective-permute-start | bytes 393224 | tf_op jit(solution)/shard_map/ppermute | solution.py:33
  45.4 2.7 %collective-permute-done.9.refs_1_ = bf16[64,1024]{1,0:T(8,128)(2,1)S(1)} collective-permute-done((bf16[64,1024]{1,0:T(8,128)(2,1)S(1)}, bf16[64,1024]{1,0:T(8,128)(2,1)S(1)}, u32[]{:S(2)}, u32[]{:S(2)}) %collective-permute-start.9) | collective-permute-done | bytes 131104 | tf_op jit(solution)/shard_map/ppermute | solution.py:33
  48.2 1.4 %collective-permute-done.8.refs_1_ = bf16[2,256,128]{2,1,0:T(8,128)(2,1)S(1)} collective-permute-done((bf16[2,256,128]{2,1,0:T(8,128)(2,1)S(1)}, bf16[2,256,128]{2,1,0:T(8,128)(2,1)S(1)}, u32[]{:S(2)}, u32[]{:S(2)}) %collective-permute-start.8) | collective-permute-done | bytes 131104 | tf_op jit(solution)/shard_map/ppermute | solution.py:33
  49.7 0.8 %collective-permute-start.12 = (bf16[2,256,128]{2,1,0:T(8,128)(2,1)S(1)}, bf16[2,256,128]{2,1,0:T(8,128)(2,1)S(1)}, u32[]{:S(2)}, u32[]{:S(2)}) collective-permute-start(bf16[2,256,128]{2,1,0:T(8,128)(2,1)S(1)} %get-tuple-element.32), channel_id=1, source_target_pairs={{0,8},{4,12},{8,0},{12,4},{16,24},{20,28},{24,16},{28,20},{1,9},{5... | collective-permute-start | bytes 393224 | tf_op jit(solution)/shard_map/ppermute | solution.py:33
  50.6 1.3 %collective-permute-start.13 = (bf16[32,1024]{1,0:T(8,128)(2,1)S(1)}, bf16[32,1024]{1,0:T(8,128)(2,1)S(1)}, u32[]{:S(2)}, u32[]{:S(2)}) collective-permute-start(bf16[32,1024]{1,0:T(8,128)(2,1)S(1)} %leaf_value.1.refs_2_.own_ref), channel_id=1, source_target_pairs={{0,4},{4,0},{8,12},{12,8},{16,20},{20,16},{24,28},{28,24},{1,5},{5... | collective-permute-start | bytes 196616 | tf_op jit(solution)/shard_map/ppermute | solution.py:33
  51.9 3.0 %collective-permute-start.10 = (bf16[1,256,128]{2,1,0:T(8,128)(2,1)S(1)}, bf16[1,256,128]{2,1,0:T(8,128)(2,1)S(1)}, u32[]{:S(2)}, u32[]{:S(2)}) collective-permute-start(bf16[1,256,128]{2,1,0:T(8,128)(2,1)S(1)} %get-tuple-element.30), channel_id=1, source_target_pairs={{0,16},{4,20},{8,24},{12,28},{16,0},{20,4},{24,8},{28,12},{1,17},{... | collective-permute-start | bytes 196616 | tf_op jit(solution)/shard_map/ppermute | solution.py:33
  54.8 0.0 collective-permute-done.13.other_ref
  54.8 2.7 %update.1 = (bf16[1536,1024]{1,0:T(8,128)(2,1)}, f32[64,1024]{1,0:T(8,128)}, f32[8,128]{1,0:T(8,128)S(1)}) custom-call(s32[2]{0:T(128)S(1)} %pad_add_fusion.pos_ref, s32[12,128]{1,0:T(8,128)S(1)} %bitcast.8, bf16[32,1024]{1,0:T(8,128)(2,1)S(1)} %leaf_value.1.refs_2_.own_ref, bf16[32,1024]{1,0:T(8,128)(2,1)S(1)} %collective-permute-done.13.other_ref, ...), custom_call_target="tpu_custom_call" | custom-call | tf_op jit(solution)/shard_map/update/pallas_call | solution.py:238
  57.6 2.9 %collective-permute-start.14 = (bf16[1,256,128]{2,1,0:T(8,128)(2,1)S(1)}, bf16[1,256,128]{2,1,0:T(8,128)(2,1)S(1)}, u32[]{:S(2)}, u32[]{:S(2)}) collective-permute-start(bf16[1,256,128]{2,1,0:T(8,128)(2,1)S(1)} %get-tuple-element.36), channel_id=1, source_target_pairs={{0,16},{4,20},{8,24},{12,28},{16,0},{20,4},{24,8},{28,12},{1,17},{... | collective-permute-start | bytes 196616 | tf_op jit(solution)/shard_map/ppermute | solution.py:33
  60.5 2.3 %collective-permute-done.14.refs_3_ = bf16[1,256,128]{2,1,0:T(8,128)(2,1)S(1)} collective-permute-done((bf16[1,256,128]{2,1,0:T(8,128)(2,1)S(1)}, bf16[1,256,128]{2,1,0:T(8,128)(2,1)S(1)}, u32[]{:S(2)}, u32[]{:S(2)}) %collective-permute-start.14) | collective-permute-done | bytes 65568 | tf_op jit(solution)/shard_map/ppermute | solution.py:33
  62.8 0.7 %last_add.1 = f32[256,256]{1,0:T(8,128)} custom-call(f32[1,256,128]{2,1,0:T(8,128)S(1)} %get-tuple-element.29.refs_2_.refs_0_, bf16[1,256,128]{2,1,0:T(8,128)(2,1)S(1)} %collective-permute-done.10.refs_1_, f32[1,256,128]{2,1,0:T(8,128)S(1)} %get-tuple-element.35.refs_2_.refs_4_, bf16[1,256,128]{2,1,0:T(8,128)(2,1)S(1)} %collective-permute-done.14.refs_3_, ...), custom_call_target="tpu_custom_call" | custom-call | tf_op jit(solution)/shard_map/last_add/pallas_call | solution.py:41
  (18 shorter events, 0.3 us)
Async XLA Ops:
  7.0 0.7 %copy-start.2 = (f32[64,1024]{1,0:T(8,128)}, f32[64,1024]{1,0:T(8,128)S(1)}, u32[]{:S(2)}) copy-start(f32[64,1024]{1,0:T(8,128)S(1)} %get-tuple-element.23.refs_0_) | copy-start | bytes 786436
  7.7 0.7 %copy-start.4 = (f32[64,1024]{1,0:T(8,128)}, f32[64,1024]{1,0:T(8,128)S(1)}, u32[]{:S(2)}) copy-start(f32[64,1024]{1,0:T(8,128)S(1)} %get-tuple-element.24.refs_1_) | copy-start | bytes 786436
  8.4 2.1 %collective-permute-start = (bf16[768,256]{1,0:T(8,128)(2,1)}, bf16[768,256]{1,0:T(8,128)(2,1)}, u32[]{:S(2)}, u32[]{:S(2)}) collective-permute-start(bf16[768,256]{1,0:T(8,128)(2,1)} %get-tuple-element.22), channel_id=1, source_target_pairs={{0,1},{1,0},{2,3},{3,2},{4,5},{5,4},{6,7},{7,6},{8,9},{9,8},{10,11... | collective-permute-start | bytes 1179656 | tf_op jit(solution)/shard_map/ppermute | solution.py:33
  12.3 12.7 %collective-permute-start.1 = (bf16[768,128]{1,0:T(8,128)(2,1)}, bf16[768,128]{1,0:T(8,128)(2,1)}, u32[]{:S(2)}, u32[]{:S(2)}) collective-permute-start(bf16[768,128]{1,0:T(8,128)(2,1)} %core_add.2.refs_2_.refs_0_), channel_id=1, source_target_pairs={{0,2},{1,3},{2,0},{3,1},{4,6},{5,7},{6,4},{7,5},{8,10},{9,11},{10,... | collective-permute-start | bytes 589832 | tf_op jit(solution)/shard_map/ppermute | solution.py:33
  15.2 0.9 %copy-start.3 = (f32[64,1024]{1,0:T(8,128)S(1)}, f32[64,1024]{1,0:T(8,128)}, u32[]{:S(2)}) copy-start(f32[64,1024]{1,0:T(8,128)} %copy-done.2) | copy-start | bytes 786436
  16.1 0.9 %copy-start.5 = (f32[64,1024]{1,0:T(8,128)S(1)}, f32[64,1024]{1,0:T(8,128)}, u32[]{:S(2)}) copy-start(f32[64,1024]{1,0:T(8,128)} %copy-done.4) | copy-start | bytes 786436
  17.7 0.7 %copy-start = (f32[64,1024]{1,0:T(8,128)}, f32[64,1024]{1,0:T(8,128)S(1)}, u32[]{:S(2)}) copy-start(f32[64,1024]{1,0:T(8,128)S(1)} %get-tuple-element.25.refs_2_.refs_0_) | copy-start | bytes 786436
  18.4 5.6 %collective-permute-start.2 = (bf16[64,1024]{1,0:T(8,128)(2,1)}, bf16[64,1024]{1,0:T(8,128)(2,1)}, u32[]{:S(2)}, u32[]{:S(2)}) collective-permute-start(bf16[64,1024]{1,0:T(8,128)(2,1)} %get-tuple-element.26), channel_id=1, source_target_pairs={{0,4},{4,0},{8,12},{12,8},{16,20},{20,16},{24,28},{28,24},{1,5},{5... | collective-permute-start | bytes 393224 | tf_op jit(solution)/shard_map/ppermute | solution.py:33
  21.4 0.9 %copy-start.1 = (f32[64,1024]{1,0:T(8,128)S(1)}, f32[64,1024]{1,0:T(8,128)}, u32[]{:S(2)}) copy-start(f32[64,1024]{1,0:T(8,128)} %copy-done) | copy-start | bytes 786436
  23.3 6.4 %collective-permute-start.5 = (bf16[768,128]{1,0:T(8,128)(2,1)S(1)}, bf16[768,128]{1,0:T(8,128)(2,1)S(1)}, u32[]{:S(2)}, u32[]{:S(2)}) collective-permute-start(bf16[768,128]{1,0:T(8,128)(2,1)S(1)} %core_add.3.refs_2_.refs_0_), channel_id=1, source_target_pairs={{0,2},{1,3},{2,0},{3,1},{4,6},{5,7},{6,4},{7,5},{8,10},{9,11},{10,... | collective-permute-start | bytes 589832 | tf_op jit(solution)/shard_map/ppermute | solution.py:33
  26.1 1.5 %collective-permute-start.3 = (bf16[768,128]{1,0:T(8,128)(2,1)S(1)}, bf16[768,128]{1,0:T(8,128)(2,1)S(1)}, u32[]{:S(2)}, u32[]{:S(2)}) collective-permute-start(bf16[768,128]{1,0:T(8,128)(2,1)S(1)} %feat_add.2.own_ref.after_ref), channel_id=1, source_target_pairs={{0,1},{1,0},{2,3},{3,2},{4,5},{5,4},{6,7},{7,6},{8,9},{9,8},{10,11... | collective-permute-start | bytes 589832 | tf_op jit(solution)/shard_map/ppermute | solution.py:33
  29.8 7.5 %collective-permute-start.7 = (bf16[768,128]{1,0:T(8,128)(2,1)S(1)}, bf16[768,128]{1,0:T(8,128)(2,1)S(1)}, u32[]{:S(2)}, u32[]{:S(2)}) collective-permute-start(bf16[768,128]{1,0:T(8,128)(2,1)S(1)} %feat_add.3.refs_2_.own_ref), channel_id=1, source_target_pairs={{0,1},{1,0},{2,3},{3,2},{4,5},{5,4},{6,7},{7,6},{8,9},{9,8},{10,11... | collective-permute-start | bytes 589832 | tf_op jit(solution)/shard_map/ppermute | solution.py:33
  29.9 5.9 %collective-permute-start.4 = (bf16[64,1024]{1,0:T(8,128)(2,1)S(1)}, bf16[64,1024]{1,0:T(8,128)(2,1)S(1)}, u32[]{:S(2)}, u32[]{:S(2)}) collective-permute-start(bf16[64,1024]{1,0:T(8,128)(2,1)S(1)} %leaf_add.2.refs_2_.refs_0_), channel_id=1, source_target_pairs={{0,8},{4,12},{8,0},{12,4},{16,24},{20,28},{24,16},{28,20},{1,9},{5... | collective-permute-start | bytes 393224 | tf_op jit(solution)/shard_map/ppermute | solution.py:33
  31.6 12.2 %collective-permute-start.6 = (bf16[4,256,128]{2,1,0:T(8,128)(2,1)S(1)}, bf16[4,256,128]{2,1,0:T(8,128)(2,1)S(1)}, u32[]{:S(2)}, u32[]{:S(2)}) collective-permute-start(bf16[4,256,128]{2,1,0:T(8,128)(2,1)S(1)} %hist_send.2.refs_2_), channel_id=1, source_target_pairs={{0,4},{4,0},{8,12},{12,8},{16,20},{20,16},{24,28},{28,24},{1,5},{5... | collective-permute-start | bytes 786440 | tf_op jit(solution)/shard_map/ppermute | solution.py:33
  37.4 17.5 %copy-start.6 = (s32[1536]{0:T(1024)S(1)}, s32[1536]{0:T(1024)}, u32[]{:S(2)}) copy-start(s32[1536]{0:T(1024)} %param.8) | copy-start | bytes 18436
  38.9 10.8 %collective-permute-start.11 = (bf16[4,256,128]{2,1,0:T(8,128)(2,1)S(1)}, bf16[4,256,128]{2,1,0:T(8,128)(2,1)S(1)}, u32[]{:S(2)}, u32[]{:S(2)}) collective-permute-start(bf16[4,256,128]{2,1,0:T(8,128)(2,1)S(1)} %hist_send.3.after_ref), channel_id=1, source_target_pairs={{0,4},{4,0},{8,12},{12,8},{16,20},{20,16},{24,28},{28,24},{1,5},{5... | collective-permute-start | bytes 786440 | tf_op jit(solution)/shard_map/ppermute | solution.py:33
  39.7 8.5 %collective-permute-start.9 = (bf16[64,1024]{1,0:T(8,128)(2,1)S(1)}, bf16[64,1024]{1,0:T(8,128)(2,1)S(1)}, u32[]{:S(2)}, u32[]{:S(2)}) collective-permute-start(bf16[64,1024]{1,0:T(8,128)(2,1)S(1)} %leaf_add.3.after_ref.refs_0_), channel_id=1, source_target_pairs={{0,16},{4,20},{8,24},{12,28},{16,0},{20,4},{24,8},{28,12},{1,17},{... | collective-permute-start | bytes 393224 | tf_op jit(solution)/shard_map/ppermute | solution.py:33
  43.8 5.8 %collective-permute-start.8 = (bf16[2,256,128]{2,1,0:T(8,128)(2,1)S(1)}, bf16[2,256,128]{2,1,0:T(8,128)(2,1)S(1)}, u32[]{:S(2)}, u32[]{:S(2)}) collective-permute-start(bf16[2,256,128]{2,1,0:T(8,128)(2,1)S(1)} %get-tuple-element.28), channel_id=1, source_target_pairs={{0,8},{4,12},{8,0},{12,4},{16,24},{20,28},{24,16},{28,20},{1,9},{5... | collective-permute-start | bytes 393224 | tf_op jit(solution)/shard_map/ppermute | solution.py:33
  49.7 7.8 %collective-permute-start.12 = (bf16[2,256,128]{2,1,0:T(8,128)(2,1)S(1)}, bf16[2,256,128]{2,1,0:T(8,128)(2,1)S(1)}, u32[]{:S(2)}, u32[]{:S(2)}) collective-permute-start(bf16[2,256,128]{2,1,0:T(8,128)(2,1)S(1)} %get-tuple-element.32), channel_id=1, source_target_pairs={{0,8},{4,12},{8,0},{12,4},{16,24},{20,28},{24,16},{28,20},{1,9},{5... | collective-permute-start | bytes 393224 | tf_op jit(solution)/shard_map/ppermute | solution.py:33
  50.6 4.3 %collective-permute-start.13 = (bf16[32,1024]{1,0:T(8,128)(2,1)S(1)}, bf16[32,1024]{1,0:T(8,128)(2,1)S(1)}, u32[]{:S(2)}, u32[]{:S(2)}) collective-permute-start(bf16[32,1024]{1,0:T(8,128)(2,1)S(1)} %leaf_value.1.refs_2_.own_ref), channel_id=1, source_target_pairs={{0,4},{4,0},{8,12},{12,8},{16,20},{20,16},{24,28},{28,24},{1,5},{5... | collective-permute-start | bytes 196616 | tf_op jit(solution)/shard_map/ppermute | solution.py:33
  51.9 8.6 %collective-permute-start.10 = (bf16[1,256,128]{2,1,0:T(8,128)(2,1)S(1)}, bf16[1,256,128]{2,1,0:T(8,128)(2,1)S(1)}, u32[]{:S(2)}, u32[]{:S(2)}) collective-permute-start(bf16[1,256,128]{2,1,0:T(8,128)(2,1)S(1)} %get-tuple-element.30), channel_id=1, source_target_pairs={{0,16},{4,20},{8,24},{12,28},{16,0},{20,4},{24,8},{28,12},{1,17},{... | collective-permute-start | bytes 196616 | tf_op jit(solution)/shard_map/ppermute | solution.py:33
  57.6 5.2 %collective-permute-start.14 = (bf16[1,256,128]{2,1,0:T(8,128)(2,1)S(1)}, bf16[1,256,128]{2,1,0:T(8,128)(2,1)S(1)}, u32[]{:S(2)}, u32[]{:S(2)}) collective-permute-start(bf16[1,256,128]{2,1,0:T(8,128)(2,1)S(1)} %get-tuple-element.36), channel_id=1, source_target_pairs={{0,16},{4,20},{8,24},{12,28},{16,0},{20,4},{24,8},{28,12},{1,17},{... | collective-permute-start | bytes 196616 | tf_op jit(solution)/shard_map/ppermute | solution.py:33

commit v6 on v5

--- a/solution.py
+++ b/solution.py
@@ -27,6 +27,10 @@
 
 
 PARAMS = pltpu.CompilerParams(vmem_limit_bytes=VMEM_LIMIT)
+
+
+def pin(x):
+    return pltpu.with_memory_space_constraint(x, pltpu.VMEM)
 
 
 def swap(x, axis, size, by):
@@ -46,7 +50,7 @@
         out_shape=out_shape,
         compiler_params=PARAMS,
         name=name,
-    )(*args, after)
+    )(*[pin(a) for a in args], after)
 
 
 def leaf_hot(leaf_ref, chunk, blk, flip, scale):
@@ -114,9 +118,9 @@
         rows_kernel,
         in_specs=[pl.BlockSpec(memory_space=pltpu.SMEM), hbm, hbm, hbm, hbm],
         out_specs=[vmem] * 5,
-        out_shape=[jax.ShapeDtypeStruct((rows // 2, w.shape[1]), bf16)] * 2
-        + [jax.ShapeDtypeStruct((LEAVES, cols), f32)] * 2
-        + [jax.ShapeDtypeStruct((chunks, blk, cols), bf16)],
+        out_shape=[pltpu.VMEM((rows // 2, w.shape[1]), bf16)] * 2
+        + [pltpu.VMEM((LEAVES, cols), f32)] * 2
+        + [pltpu.VMEM((chunks, blk, cols), bf16)],
         scratch_shapes=[
             pltpu.VMEM(leaf.shape, jnp.int32),
             pltpu.VMEM((chunks, blk, cols), bf16),
@@ -197,10 +201,10 @@
         grid=(blocks,),
         in_specs=[whole(codes), whole(own), whole(other), pl.BlockSpec(memory_space=pl.ANY)],
         out_specs=pl.BlockSpec((1, per * feats, width), lambda i: (i, 0, 0)),
-        out_shape=jax.ShapeDtypeStruct((blocks, per * feats, width), dtype),
+        out_shape=pltpu.VMEM((blocks, per * feats, width), dtype),
         compiler_params=PARAMS,
         name="hist_send" if odd else "hist_keep",
-    )(codes, own, other, after)
+    )(pin(codes), pin(own), pin(other), after)
 
 
 def update_kernel(pos_ref, leaf_ref, own_ref, other_ref, pred_ref, after_ref, new_hbm, values_hbm, done_ref,
@@ -240,9 +244,9 @@
         in_specs=[pl.BlockSpec(memory_space=pltpu.SMEM), vmem, vmem, vmem, vmem, hbm],
         out_specs=[pl.BlockSpec(memory_space=pltpu.HBM)] * 2 + [vmem],
         out_shape=[
-            jax.ShapeDtypeStruct((chunks * blk, cols), bf16),
-            jax.ShapeDtypeStruct((LEAVES, cols), f32),
-            jax.ShapeDtypeStruct((8, 128), f32),
+            pltpu.HBM((chunks * blk, cols), bf16),
+            pltpu.HBM((LEAVES, cols), f32),
+            pltpu.VMEM((8, 128), f32),
         ],
         scratch_shapes=[
             pltpu.VMEM((chunks, blk, cols), bf16),
@@ -252,7 +256,7 @@
         ],
         compiler_params=PARAMS,
         name="update",
-    )(pos, leaf, own, other, pred, after)
+    )(pos, leaf, pin(own), pin(other), pin(pred), after)
 
 
 def local(n, nf, predictions, labels, feature_codes, leaf_index, sketch_weight):
@@ -273,9 +277,9 @@
     pred = pltpu.with_memory_space_constraint(predictions, pltpu.HBM)
     lab = pltpu.with_memory_space_constraint(labels, pltpu.HBM)
     weight = pltpu.with_memory_space_constraint(sketch_weight, pltpu.HBM)
-    sketch16 = jax.ShapeDtypeStruct((half, width), bf16)
-    sums16 = jax.ShapeDtypeStruct((LEAVES, cols), bf16)
-    sums32 = jax.ShapeDtypeStruct((LEAVES, cols), f32)
+    sketch16 = pltpu.VMEM((half, width), bf16)
+    sums16 = pltpu.VMEM((LEAVES, cols), bf16)
+    sums32 = pltpu.VMEM((LEAVES, cols), f32)
 
     send, keep, grad, hess, held = rows_pass(pos, pltpu.with_memory_space_constraint(leaf, pltpu.HBM), pred, lab, weight)
     got = swap(send, "feat", nf, 1)
@@ -295,7 +299,7 @@
             acc = ordered(add_kernel, sums16, [acc, got], after, "leaf_add")
             leaf_state = (acc, swap(acc, "rows", n, by), 2 * by)
         elif by == n:
-            values16 = jax.ShapeDtypeStruct((LEAVES // 2, cols), bf16)
+            values16 = pltpu.VMEM((LEAVES // 2, cols), bf16)
             acc = ordered(value_kernel, values16, [acc, got], after, "leaf_value")
             leaf_state = (acc, swap(acc, "rows", n, 1), 2 * by)
         else:
@@ -324,21 +328,19 @@
         for p in range(parts):
             level = slot - p
             if 0 <= level < levels:
-                if p == parts - 1 and level == levels - 1:
-                    while leaf_state[2] <= n:
-                        after = leaf_step(after)
-                    updated, leaf_values, after = update_pass(
-                        pos, leaf, leaf_state[0], leaf_state[1], held, after)
                 blocks = heres[p].shape[0] // 2
                 shape = (blocks,) + heres[p].shape[1:]
                 after, sent = ordered(
                     halving_kernel,
-                    [jax.ShapeDtypeStruct(shape, f32), jax.ShapeDtypeStruct(shape, bf16)],
+                    [pltpu.VMEM(shape, f32), pltpu.VMEM(shape, bf16)],
                     [heres[p], backs[p]], after, "hist_add")
                 heres[p] = after
                 backs[p] = swap(sent, "rows", n, 2 << level)
                 if slot == 0:
                     after = leaf_step(after)
+    while leaf_state[2] <= n:
+        after = leaf_step(after)
+    updated, leaf_values, after = update_pass(pos, leaf, leaf_state[0], leaf_state[1], held, after)
     histograms = ordered(
         last_kernel, jax.ShapeDtypeStruct((per * feats, width * parts), f32),
         [a for p in range(parts) for a in (heres[p], backs[p])], after, "last_add")

time: 64 us -> 62.6 us (0.978)
  starting transfers between devices: 21 us -> 19.8 us
    ppermute x15, starting transfers between devices: 21 us -> 19.8 us  [swap(): return lax.ppermute(x, axis, [(i, i ^ by) for i in range(size)])]
  transfers between devices with their start and end apart: 15 -> 15, of which waited for: 8 -> 9; matrix products, arithmetic and copies ran while one was open for 4% -> 4% of each run, Pallas kernels for 20% -> 20%
where the time goes in v6:
time: 62.6 us; the launch traced here: 62.2 us
  Pallas kernels  21.3 us (34%)
  starting transfers between devices  19.8 us (32%)
  waiting for transfers between devices  12.9 us (21%)
  local copies, waits for them, and re-layouts  4.96 us (8%)
  other arithmetic  2.38 us (4%)
  between operations  0.81 us (1%)
    ppermute x15, starting transfers between devices, swap(): return lax.ppermute(x, axis, [(i, i ^ by) for i in range(size)])  19.8 us
    ppermute x15, waiting for transfers between devices, swap(): return lax.ppermute(x, axis, [(i, i ^ by) for i in range(size)])  12.9 us
    pallas_call x13, Pallas kernels, ordered(): pl.pallas_call(body, in_specs=[pl.BlockSpec(memory_space=pltpu.VMEM)] * l...  6.46 us
    pallas_call x1, Pallas kernels, rows_pass(): pl.pallas_call(rows_kernel, in_specs=[pl.BlockSpec(memory_space=pltpu.SME...  6.28 us
    pallas_call x4, Pallas kernels, hist_pass(): pl.pallas_call(functools.partial(hist_kernel, per=per, odd=odd, bits=bloc...  5.89 us
    unnamed x14, local copies, waits for them, and re-layouts  4.96 us
    pallas_call x1, Pallas kernels, update_pass(): pl.pallas_call(update_kernel, in_specs=[pl.BlockSpec(memory_space=pltpu.S...  2.67 us
    xor x1, other arithmetic, local(): codes = (feature_codes ^ me * per).reshape(feats, 2, half)  1.42 us
  transfers between devices with their start and end apart: 15, of which 9 were waited for; matrix products, arithmetic and copies ran while one was open for 4% of the time, Pallas kernels for 20%

profile of v6, /device:TPU:0, one launch (start us, length us, event | category | flops | bytes accessed | tf_op | source)
XLA Modules:
  0.0 62.2 jit_solution(9705370590279744782)
XLA Ops:
  0.6 0.1 pad_add_fusion.pos_ref
  0.7 6.3 %rows.1 = (bf16[768,256]{1,0:T(8,128)(2,1)}, bf16[768,256]{1,0:T(8,128)(2,1)S(1)}, f32[64,1024]{1,0:T(8,128)S(1)}, f32[64,1024]{1,0:T(8,128)S(1)}, bf16[6,256,1024]{2,1,0:T(8,128)(2,1)S(1)}) custom-call(s32[2]{0:T(128)S(1)} %pad_add_fusion.pos_ref, s32[12,128]{1,0:T(8,128)} %bitcast.7, bf16[1536,1024]{1,0:T(8,128)(2,1)} %pred_hbm.1, ...), custom_call_target="tpu_custom_call" | custom-call | tf_op jit(solution)/shard_map/rows/pallas_call | solution.py:117
  7.0 0.0 copy-start.2
  7.0 0.7 %copy-done.2 = f32[64,1024]{1,0:T(8,128)} copy-done((f32[64,1024]{1,0:T(8,128)}, f32[64,1024]{1,0:T(8,128)S(1)}, u32[]{:S(2)}) %copy-start.2) | copy-done | bytes 262168
  7.7 0.7 %copy-done.4 = f32[64,1024]{1,0:T(8,128)} copy-done((f32[64,1024]{1,0:T(8,128)}, f32[64,1024]{1,0:T(8,128)S(1)}, u32[]{:S(2)}) %copy-start.4) | copy-done | bytes 262168
  8.4 0.5 collective-permute-start
  8.9 1.7 %collective-permute-done.refs_1_ = bf16[768,256]{1,0:T(8,128)(2,1)} collective-permute-done((bf16[768,256]{1,0:T(8,128)(2,1)}, bf16[768,256]{1,0:T(8,128)(2,1)}, u32[]{:S(2)}, u32[]{:S(2)}) %collective-permute-start) | collective-permute-done | bytes 393248 | tf_op jit(solution)/shard_map/ppermute | solution.py:37
  10.5 1.7 %core_add.2.refs_2_.refs_0_ = bf16[768,128]{1,0:T(8,128)(2,1)} custom-call(bf16[768,256]{1,0:T(8,128)(2,1)S(1)} %get-tuple-element.21.refs_0_.refs_2_, bf16[768,256]{1,0:T(8,128)(2,1)} %collective-permute-done.refs_1_, bf16[768,256]{1,0:T(8,128)(2,1)S(1)} %get-tuple-element.21.refs_0_.refs_2_), custom_call_target="tpu_custom_call" | custom-call | tf_op jit(solution)/shard_map/core_add/pallas_call | solution.py:45
  12.3 2.9 %collective-permute-start.1 = (bf16[768,128]{1,0:T(8,128)(2,1)}, bf16[768,128]{1,0:T(8,128)(2,1)}, u32[]{:S(2)}, u32[]{:S(2)}) collective-permute-start(bf16[768,128]{1,0:T(8,128)(2,1)} %core_add.2.refs_2_.refs_0_), channel_id=1, source_target_pairs={{0,2},{1,3},{2,0},{3,1},{4,6},{5,7},{6,4},{7,5},{8,10},{9,11},{10,... | collective-permute-start | bytes 589832 | tf_op jit(solution)/shard_map/ppermute | solution.py:37
  15.2 0.9 %copy-done.3 = f32[64,1024]{1,0:T(8,128)S(1)} copy-done((f32[64,1024]{1,0:T(8,128)S(1)}, f32[64,1024]{1,0:T(8,128)}, u32[]{:S(2)}) %copy-start.3) | copy-done | bytes 262168
  16.1 0.9 %copy-done.5 = f32[64,1024]{1,0:T(8,128)S(1)} copy-done((f32[64,1024]{1,0:T(8,128)S(1)}, f32[64,1024]{1,0:T(8,128)}, u32[]{:S(2)}) %copy-start.5) | copy-done | bytes 262168
  17.1 0.7 %leaf_pack.1 = (f32[64,1024]{1,0:T(8,128)S(1)}, bf16[64,1024]{1,0:T(8,128)(2,1)}) custom-call(f32[64,1024]{1,0:T(8,128)S(1)} %copy-done.3, f32[64,1024]{1,0:T(8,128)S(1)} %copy-done.5, bf16[768,128]{1,0:T(8,128)(2,1)} %core_add.2.refs_2_.refs_0_), custom_call_target="tpu_custom_call" | custom-call | tf_op jit(solution)/shard_map/leaf_pack/pallas_call | solution.py:45
  17.7 0.7 %copy-done = f32[64,1024]{1,0:T(8,128)} copy-done((f32[64,1024]{1,0:T(8,128)}, f32[64,1024]{1,0:T(8,128)S(1)}, u32[]{:S(2)}) %copy-start) | copy-done | bytes 262168
  18.4 1.5 %collective-permute-start.2 = (bf16[64,1024]{1,0:T(8,128)(2,1)}, bf16[64,1024]{1,0:T(8,128)(2,1)}, u32[]{:S(2)}, u32[]{:S(2)}) collective-permute-start(bf16[64,1024]{1,0:T(8,128)(2,1)} %get-tuple-element.26), channel_id=1, source_target_pairs={{0,4},{4,0},{8,12},{12,8},{16,20},{20,16},{24,28},{28,24},{1,5},{5... | collective-permute-start | bytes 393224 | tf_op jit(solution)/shard_map/ppermute | solution.py:37
  19.9 1.4 %broadcast_xor_fusion = s32[8,1536]{1,0:T(8,128)} fusion(s32[8,1536]{1,0:T(8,128)} %param.7, s32[]{:T(128)S(6)} %mul.3), kind=kLoop, calls=%fused_computation.2 | loop fusion | flops 12288 | bytes 98308 | tf_op jit(solution)/shard_map/xor | solution.py:272
  21.4 0.9 %copy-done.1 = f32[64,1024]{1,0:T(8,128)S(1)} copy-done((f32[64,1024]{1,0:T(8,128)S(1)}, f32[64,1024]{1,0:T(8,128)}, u32[]{:S(2)}) %copy-start.1) | copy-done | bytes 262168
  22.3 1.0 %core_add.3.refs_2_.refs_0_ = bf16[768,128]{1,0:T(8,128)(2,1)S(1)} custom-call(bf16[768,256]{1,0:T(8,128)(2,1)S(1)} %get-tuple-element.21.refs_0_.refs_2_, bf16[768,256]{1,0:T(8,128)(2,1)} %collective-permute-done.refs_1_, f32[64,1024]{1,0:T(8,128)S(1)} %copy-done.1), custom_call_target="tpu_custom_call" | custom-call | tf_op jit(solution)/shard_map/core_add/pallas_call | solution.py:45
  23.3 0.6 collective-permute-start.5
  23.9 0.1 collective-permute-done.2.refs_1_
  24.0 0.9 %leaf_add.2.refs_2_.refs_0_ = bf16[64,1024]{1,0:T(8,128)(2,1)S(1)} custom-call(f32[64,1024]{1,0:T(8,128)S(1)} %copy-done.1, bf16[64,1024]{1,0:T(8,128)(2,1)} %collective-permute-done.2.refs_1_, bf16[768,128]{1,0:T(8,128)(2,1)S(1)} %core_add.3.refs_2_.refs_0_), custom_call_target="tpu_custom_call" | custom-call | tf_op jit(solution)/shard_map/leaf_add/pallas_call | solution.py:45
  25.0 1.1 %feat_add.2.own_ref.after_ref = bf16[768,128]{1,0:T(8,128)(2,1)S(1)} custom-call(bf16[768,128]{1,0:T(8,128)(2,1)} %core_add.2.refs_2_.refs_0_, bf16[768,128]{1,0:T(8,128)(2,1)} %collective-permute-done.1.refs_1_, bf16[64,1024]{1,0:T(8,128)(2,1)S(1)} %leaf_add.2.refs_2_.refs_0_), custom_call_target="tpu_custom_call" | custom-call | tf_op jit(solution)/shard_map/feat_add/pallas_call | solution.py:45
  26.1 0.1 collective-permute-start.3
  26.1 0.9 %fusion.codes_ref = s32[2,8,768]{2,1,0:T(8,128)S(1)} fusion(s32[8,2,768]{2,0,1:T(8,128)} %bitcast.10, pred[]{:T(512)S(6)} %eq.3), kind=kLoop, calls=%fused_computation.1 | loop fusion | flops 12288 | bytes 98305 | tf_op jit(solution)/shard_map/transpose | solution.py:273
  27.0 0.5 collective-permute-done.3.other_ref
  27.6 1.5 %hist_send.2.refs_2_ = bf16[4,256,128]{2,1,0:T(8,128)(2,1)S(1)} custom-call(s32[2,8,768]{2,1,0:T(8,128)S(1)} %fusion.codes_ref, bf16[768,128]{1,0:T(8,128)(2,1)S(1)} %feat_add.2.own_ref.after_ref, bf16[768,128]{1,0:T(8,128)(2,1)S(1)} %collective-permute-done.3.other_ref, bf16[768,128]{1,0:T(8,128)(2,1)S(1)} %feat_add.2.own_ref.after_ref), custom_call_target="tpu_custom_call" | custom-call | tf_op jit(solution)/shard_map/hist_send/pallas_call | solution.py:199
  29.0 0.8 %collective-permute-done.5.refs_1_ = bf16[768,128]{1,0:T(8,128)(2,1)S(1)} collective-permute-done((bf16[768,128]{1,0:T(8,128)(2,1)S(1)}, bf16[768,128]{1,0:T(8,128)(2,1)S(1)}, u32[]{:S(2)}, u32[]{:S(2)}) %collective-permute-start.5) | collective-permute-done | bytes 196640 | tf_op jit(solution)/shard_map/ppermute | solution.py:37
  29.8 0.1 collective-permute-start.7
  29.9 1.6 %collective-permute-start.4 = (bf16[64,1024]{1,0:T(8,128)(2,1)S(1)}, bf16[64,1024]{1,0:T(8,128)(2,1)S(1)}, u32[]{:S(2)}, u32[]{:S(2)}) collective-permute-start(bf16[64,1024]{1,0:T(8,128)(2,1)S(1)} %leaf_add.2.refs_2_.refs_0_), channel_id=1, source_target_pairs={{0,8},{4,12},{8,0},{12,4},{16,24},{20,28},{24,16},{28,20},{1,9},{5... | collective-permute-start | bytes 393224 | tf_op jit(solution)/shard_map/ppermute | solution.py:37
  31.6 0.8 %collective-permute-start.6 = (bf16[4,256,128]{2,1,0:T(8,128)(2,1)S(1)}, bf16[4,256,128]{2,1,0:T(8,128)(2,1)S(1)}, u32[]{:S(2)}, u32[]{:S(2)}) collective-permute-start(bf16[4,256,128]{2,1,0:T(8,128)(2,1)S(1)} %hist_send.2.refs_2_), channel_id=1, source_target_pairs={{0,4},{4,0},{8,12},{12,8},{16,20},{20,16},{24,28},{28,24},{1,5},{5... | collective-permute-start | bytes 786440 | tf_op jit(solution)/shard_map/ppermute | solution.py:37
  32.4 3.5 %collective-permute-done.4.refs_1_ = bf16[64,1024]{1,0:T(8,128)(2,1)S(1)} collective-permute-done((bf16[64,1024]{1,0:T(8,128)(2,1)S(1)}, bf16[64,1024]{1,0:T(8,128)(2,1)S(1)}, u32[]{:S(2)}, u32[]{:S(2)}) %collective-permute-start.4) | collective-permute-done | bytes 131104 | tf_op jit(solution)/shard_map/ppermute | solution.py:37
  35.9 1.5 %hist_keep.2.after_ref.refs_0_ = f32[4,256,128]{2,1,0:T(8,128)S(1)} custom-call(s32[2,8,768]{2,1,0:T(8,128)S(1)} %fusion.codes_ref, bf16[768,128]{1,0:T(8,128)(2,1)S(1)} %feat_add.2.own_ref.after_ref, bf16[768,128]{1,0:T(8,128)(2,1)S(1)} %collective-permute-done.3.other_ref, bf16[64,1024]{1,0:T(8,128)(2,1)S(1)} %leaf_add.3.after_ref.refs_0_), custom_call_target="tpu_custom_call" | custom-call | tf_op jit(solution)/shard_map/hist_keep/pallas_call | solution.py:199
  37.4 0.0 copy-start.6
  37.4 0.0 collective-permute-done.7.other_ref
  37.4 1.5 %hist_send.3.after_ref = bf16[4,256,128]{2,1,0:T(8,128)(2,1)S(1)} custom-call(s32[2,8,768]{2,1,0:T(8,128)S(1)} %fusion.codes_ref, bf16[768,128]{1,0:T(8,128)(2,1)S(1)} %feat_add.3.refs_2_.own_ref, bf16[768,128]{1,0:T(8,128)(2,1)S(1)} %collective-permute-done.7.other_ref, f32[4,256,128]{2,1,0:T(8,128)S(1)} %hist_keep.2.after_ref.refs_0_), custom_call_target="tpu_custom_call" | custom-call | tf_op jit(solution)/shard_map/hist_send/pallas_call | solution.py:199
  38.9 0.8 %collective-permute-start.11 = (bf16[4,256,128]{2,1,0:T(8,128)(2,1)S(1)}, bf16[4,256,128]{2,1,0:T(8,128)(2,1)S(1)}, u32[]{:S(2)}, u32[]{:S(2)}) collective-permute-start(bf16[4,256,128]{2,1,0:T(8,128)(2,1)S(1)} %hist_send.3.after_ref), channel_id=1, source_target_pairs={{0,4},{4,0},{8,12},{12,8},{16,20},{20,16},{24,28},{28,24},{1,5},{5... | collective-permute-start | bytes 786440 | tf_op jit(solution)/shard_map/ppermute | solution.py:37
  39.7 2.6 %collective-permute-start.9 = (bf16[64,1024]{1,0:T(8,128)(2,1)S(1)}, bf16[64,1024]{1,0:T(8,128)(2,1)S(1)}, u32[]{:S(2)}, u32[]{:S(2)}) collective-permute-start(bf16[64,1024]{1,0:T(8,128)(2,1)S(1)} %leaf_add.3.after_ref.refs_0_), channel_id=1, source_target_pairs={{0,16},{4,20},{8,24},{12,28},{16,0},{20,4},{24,8},{28,12},{1,17},{... | collective-permute-start | bytes 393224 | tf_op jit(solution)/shard_map/ppermute | solution.py:37
  42.3 1.5 %hist_keep.3.refs_2_.refs_0_ = f32[4,256,128]{2,1,0:T(8,128)S(1)} custom-call(s32[2,8,768]{2,1,0:T(8,128)S(1)} %fusion.codes_ref, bf16[768,128]{1,0:T(8,128)(2,1)S(1)} %feat_add.3.refs_2_.own_ref, bf16[768,128]{1,0:T(8,128)(2,1)S(1)} %collective-permute-done.7.other_ref, bf16[4,256,128]{2,1,0:T(8,128)(2,1)S(1)} %hist_send.3.after_ref), custom_call_target="tpu_custom_call" | custom-call | tf_op jit(solution)/shard_map/hist_keep/pallas_call | solution.py:199
  43.8 1.6 %collective-permute-start.8 = (bf16[2,256,128]{2,1,0:T(8,128)(2,1)S(1)}, bf16[2,256,128]{2,1,0:T(8,128)(2,1)S(1)}, u32[]{:S(2)}, u32[]{:S(2)}) collective-permute-start(bf16[2,256,128]{2,1,0:T(8,128)(2,1)S(1)} %get-tuple-element.28), channel_id=1, source_target_pairs={{0,8},{4,12},{8,0},{12,4},{16,24},{20,28},{24,16},{28,20},{1,9},{5... | collective-permute-start | bytes 393224 | tf_op jit(solution)/shard_map/ppermute | solution.py:37
  45.4 2.7 %collective-permute-done.9.refs_1_ = bf16[64,1024]{1,0:T(8,128)(2,1)S(1)} collective-permute-done((bf16[64,1024]{1,0:T(8,128)(2,1)S(1)}, bf16[64,1024]{1,0:T(8,128)(2,1)S(1)}, u32[]{:S(2)}, u32[]{:S(2)}) %collective-permute-start.9) | collective-permute-done | bytes 131104 | tf_op jit(solution)/shard_map/ppermute | solution.py:37
  48.2 1.4 %collective-permute-done.8.refs_1_ = bf16[2,256,128]{2,1,0:T(8,128)(2,1)S(1)} collective-permute-done((bf16[2,256,128]{2,1,0:T(8,128)(2,1)S(1)}, bf16[2,256,128]{2,1,0:T(8,128)(2,1)S(1)}, u32[]{:S(2)}, u32[]{:S(2)}) %collective-permute-start.8) | collective-permute-done | bytes 131104 | tf_op jit(solution)/shard_map/ppermute | solution.py:37
  49.7 0.8 %collective-permute-start.12 = (bf16[2,256,128]{2,1,0:T(8,128)(2,1)S(1)}, bf16[2,256,128]{2,1,0:T(8,128)(2,1)S(1)}, u32[]{:S(2)}, u32[]{:S(2)}) collective-permute-start(bf16[2,256,128]{2,1,0:T(8,128)(2,1)S(1)} %get-tuple-element.32), channel_id=1, source_target_pairs={{0,8},{4,12},{8,0},{12,4},{16,24},{20,28},{24,16},{28,20},{1,9},{5... | collective-permute-start | bytes 393224 | tf_op jit(solution)/shard_map/ppermute | solution.py:37
  50.6 1.3 %collective-permute-start.14 = (bf16[32,1024]{1,0:T(8,128)(2,1)S(1)}, bf16[32,1024]{1,0:T(8,128)(2,1)S(1)}, u32[]{:S(2)}, u32[]{:S(2)}) collective-permute-start(bf16[32,1024]{1,0:T(8,128)(2,1)S(1)} %leaf_value.1.refs_2_.own_ref), channel_id=1, source_target_pairs={{0,4},{4,0},{8,12},{12,8},{16,20},{20,16},{24,28},{28,24},{1,5},{5... | collective-permute-start | bytes 196616 | tf_op jit(solution)/shard_map/ppermute | solution.py:37
  51.9 3.0 %collective-permute-start.10 = (bf16[1,256,128]{2,1,0:T(8,128)(2,1)S(1)}, bf16[1,256,128]{2,1,0:T(8,128)(2,1)S(1)}, u32[]{:S(2)}, u32[]{:S(2)}) collective-permute-start(bf16[1,256,128]{2,1,0:T(8,128)(2,1)S(1)} %get-tuple-element.30), channel_id=1, source_target_pairs={{0,16},{4,20},{8,24},{12,28},{16,0},{20,4},{24,8},{28,12},{1,17},{... | collective-permute-start | bytes 196616 | tf_op jit(solution)/shard_map/ppermute | solution.py:37
  54.8 0.6 %collective-permute-done.12.refs_1_ = bf16[2,256,128]{2,1,0:T(8,128)(2,1)S(1)} collective-permute-done((bf16[2,256,128]{2,1,0:T(8,128)(2,1)S(1)}, bf16[2,256,128]{2,1,0:T(8,128)(2,1)S(1)}, u32[]{:S(2)}, u32[]{:S(2)}) %collective-permute-start.12) | collective-permute-done | bytes 131104 | tf_op jit(solution)/shard_map/ppermute | solution.py:37
  55.5 1.7 %collective-permute-start.13 = (bf16[1,256,128]{2,1,0:T(8,128)(2,1)S(1)}, bf16[1,256,128]{2,1,0:T(8,128)(2,1)S(1)}, u32[]{:S(2)}, u32[]{:S(2)}) collective-permute-start(bf16[1,256,128]{2,1,0:T(8,128)(2,1)S(1)} %get-tuple-element.34), channel_id=1, source_target_pairs={{0,16},{4,20},{8,24},{12,28},{16,0},{20,4},{24,8},{28,12},{1,17},{... | collective-permute-start | bytes 196616 | tf_op jit(solution)/shard_map/ppermute | solution.py:37
  57.2 2.7 %update.1 = (bf16[1536,1024]{1,0:T(8,128)(2,1)}, f32[64,1024]{1,0:T(8,128)}, f32[8,128]{1,0:T(8,128)S(1)}) custom-call(s32[2]{0:T(128)S(1)} %pad_add_fusion.pos_ref, s32[12,128]{1,0:T(8,128)S(1)} %bitcast.8, bf16[32,1024]{1,0:T(8,128)(2,1)S(1)} %leaf_value.1.refs_2_.own_ref, bf16[32,1024]{1,0:T(8,128)(2,1)S(1)} %collective-permute-done.14.other_ref, ...), custom_call_target="tpu_custom_call" | custom-call | tf_op jit(solution)/shard_map/update/pallas_call | solution.py:242
  59.9 1.5 %collective-permute-done.13.refs_3_ = bf16[1,256,128]{2,1,0:T(8,128)(2,1)S(1)} collective-permute-done((bf16[1,256,128]{2,1,0:T(8,128)(2,1)S(1)}, bf16[1,256,128]{2,1,0:T(8,128)(2,1)S(1)}, u32[]{:S(2)}, u32[]{:S(2)}) %collective-permute-start.13) | collective-permute-done | bytes 65568 | tf_op jit(solution)/shard_map/ppermute | solution.py:37
  61.4 0.7 %last_add.1 = f32[256,256]{1,0:T(8,128)} custom-call(f32[1,256,128]{2,1,0:T(8,128)S(1)} %get-tuple-element.29.refs_2_.refs_0_, bf16[1,256,128]{2,1,0:T(8,128)(2,1)S(1)} %collective-permute-done.10.refs_1_, f32[1,256,128]{2,1,0:T(8,128)S(1)} %get-tuple-element.33.after_ref.refs_2_, bf16[1,256,128]{2,1,0:T(8,128)(2,1)S(1)} %collective-permute-done.13.refs_3_, ...), custom_call_target="tpu_custom_call" | custom-call | tf_op jit(solution)/shard_map/last_add/pallas_call | solution.py:45
  (18 shorter events, 0.3 us)
Async XLA Ops:
  7.0 0.7 %copy-start.2 = (f32[64,1024]{1,0:T(8,128)}, f32[64,1024]{1,0:T(8,128)S(1)}, u32[]{:S(2)}) copy-start(f32[64,1024]{1,0:T(8,128)S(1)} %get-tuple-element.23.refs_0_) | copy-start | bytes 786436
  7.7 0.7 %copy-start.4 = (f32[64,1024]{1,0:T(8,128)}, f32[64,1024]{1,0:T(8,128)S(1)}, u32[]{:S(2)}) copy-start(f32[64,1024]{1,0:T(8,128)S(1)} %get-tuple-element.24.refs_1_) | copy-start | bytes 786436
  8.4 2.1 %collective-permute-start = (bf16[768,256]{1,0:T(8,128)(2,1)}, bf16[768,256]{1,0:T(8,128)(2,1)}, u32[]{:S(2)}, u32[]{:S(2)}) collective-permute-start(bf16[768,256]{1,0:T(8,128)(2,1)} %get-tuple-element.22), channel_id=1, source_target_pairs={{0,1},{1,0},{2,3},{3,2},{4,5},{5,4},{6,7},{7,6},{8,9},{9,8},{10,11... | collective-permute-start | bytes 1179656 | tf_op jit(solution)/shard_map/ppermute | solution.py:37
  12.3 12.7 %collective-permute-start.1 = (bf16[768,128]{1,0:T(8,128)(2,1)}, bf16[768,128]{1,0:T(8,128)(2,1)}, u32[]{:S(2)}, u32[]{:S(2)}) collective-permute-start(bf16[768,128]{1,0:T(8,128)(2,1)} %core_add.2.refs_2_.refs_0_), channel_id=1, source_target_pairs={{0,2},{1,3},{2,0},{3,1},{4,6},{5,7},{6,4},{7,5},{8,10},{9,11},{10,... | collective-permute-start | bytes 589832 | tf_op jit(solution)/shard_map/ppermute | solution.py:37
  15.2 0.9 %copy-start.3 = (f32[64,1024]{1,0:T(8,128)S(1)}, f32[64,1024]{1,0:T(8,128)}, u32[]{:S(2)}) copy-start(f32[64,1024]{1,0:T(8,128)} %copy-done.2) | copy-start | bytes 786436
  16.1 0.9 %copy-start.5 = (f32[64,1024]{1,0:T(8,128)S(1)}, f32[64,1024]{1,0:T(8,128)}, u32[]{:S(2)}) copy-start(f32[64,1024]{1,0:T(8,128)} %copy-done.4) | copy-start | bytes 786436
  17.7 0.7 %copy-start = (f32[64,1024]{1,0:T(8,128)}, f32[64,1024]{1,0:T(8,128)S(1)}, u32[]{:S(2)}) copy-start(f32[64,1024]{1,0:T(8,128)S(1)} %get-tuple-element.25.refs_2_.refs_0_) | copy-start | bytes 786436
  18.4 5.6 %collective-permute-start.2 = (bf16[64,1024]{1,0:T(8,128)(2,1)}, bf16[64,1024]{1,0:T(8,128)(2,1)}, u32[]{:S(2)}, u32[]{:S(2)}) collective-permute-start(bf16[64,1024]{1,0:T(8,128)(2,1)} %get-tuple-element.26), channel_id=1, source_target_pairs={{0,4},{4,0},{8,12},{12,8},{16,20},{20,16},{24,28},{28,24},{1,5},{5... | collective-permute-start | bytes 393224 | tf_op jit(solution)/shard_map/ppermute | solution.py:37
  21.4 0.9 %copy-start.1 = (f32[64,1024]{1,0:T(8,128)S(1)}, f32[64,1024]{1,0:T(8,128)}, u32[]{:S(2)}) copy-start(f32[64,1024]{1,0:T(8,128)} %copy-done) | copy-start | bytes 786436
  23.3 6.4 %collective-permute-start.5 = (bf16[768,128]{1,0:T(8,128)(2,1)S(1)}, bf16[768,128]{1,0:T(8,128)(2,1)S(1)}, u32[]{:S(2)}, u32[]{:S(2)}) collective-permute-start(bf16[768,128]{1,0:T(8,128)(2,1)S(1)} %core_add.3.refs_2_.refs_0_), channel_id=1, source_target_pairs={{0,2},{1,3},{2,0},{3,1},{4,6},{5,7},{6,4},{7,5},{8,10},{9,11},{10,... | collective-permute-start | bytes 589832 | tf_op jit(solution)/shard_map/ppermute | solution.py:37
  26.1 1.5 %collective-permute-start.3 = (bf16[768,128]{1,0:T(8,128)(2,1)S(1)}, bf16[768,128]{1,0:T(8,128)(2,1)S(1)}, u32[]{:S(2)}, u32[]{:S(2)}) collective-permute-start(bf16[768,128]{1,0:T(8,128)(2,1)S(1)} %feat_add.2.own_ref.after_ref), channel_id=1, source_target_pairs={{0,1},{1,0},{2,3},{3,2},{4,5},{5,4},{6,7},{7,6},{8,9},{9,8},{10,11... | collective-permute-start | bytes 589832 | tf_op jit(solution)/shard_map/ppermute | solution.py:37
  29.8 7.5 %collective-permute-start.7 = (bf16[768,128]{1,0:T(8,128)(2,1)S(1)}, bf16[768,128]{1,0:T(8,128)(2,1)S(1)}, u32[]{:S(2)}, u32[]{:S(2)}) collective-permute-start(bf16[768,128]{1,0:T(8,128)(2,1)S(1)} %feat_add.3.refs_2_.own_ref), channel_id=1, source_target_pairs={{0,1},{1,0},{2,3},{3,2},{4,5},{5,4},{6,7},{7,6},{8,9},{9,8},{10,11... | collective-permute-start | bytes 589832 | tf_op jit(solution)/shard_map/ppermute | solution.py:37
  29.9 5.9 %collective-permute-start.4 = (bf16[64,1024]{1,0:T(8,128)(2,1)S(1)}, bf16[64,1024]{1,0:T(8,128)(2,1)S(1)}, u32[]{:S(2)}, u32[]{:S(2)}) collective-permute-start(bf16[64,1024]{1,0:T(8,128)(2,1)S(1)} %leaf_add.2.refs_2_.refs_0_), channel_id=1, source_target_pairs={{0,8},{4,12},{8,0},{12,4},{16,24},{20,28},{24,16},{28,20},{1,9},{5... | collective-permute-start | bytes 393224 | tf_op jit(solution)/shard_map/ppermute | solution.py:37
  31.6 12.2 %collective-permute-start.6 = (bf16[4,256,128]{2,1,0:T(8,128)(2,1)S(1)}, bf16[4,256,128]{2,1,0:T(8,128)(2,1)S(1)}, u32[]{:S(2)}, u32[]{:S(2)}) collective-permute-start(bf16[4,256,128]{2,1,0:T(8,128)(2,1)S(1)} %hist_send.2.refs_2_), channel_id=1, source_target_pairs={{0,4},{4,0},{8,12},{12,8},{16,20},{20,16},{24,28},{28,24},{1,5},{5... | collective-permute-start | bytes 786440 | tf_op jit(solution)/shard_map/ppermute | solution.py:37
  37.4 19.8 %copy-start.6 = (s32[1536]{0:T(1024)S(1)}, s32[1536]{0:T(1024)}, u32[]{:S(2)}) copy-start(s32[1536]{0:T(1024)} %param.8) | copy-start | bytes 18436
  38.9 10.8 %collective-permute-start.11 = (bf16[4,256,128]{2,1,0:T(8,128)(2,1)S(1)}, bf16[4,256,128]{2,1,0:T(8,128)(2,1)S(1)}, u32[]{:S(2)}, u32[]{:S(2)}) collective-permute-start(bf16[4,256,128]{2,1,0:T(8,128)(2,1)S(1)} %hist_send.3.after_ref), channel_id=1, source_target_pairs={{0,4},{4,0},{8,12},{12,8},{16,20},{20,16},{24,28},{28,24},{1,5},{5... | collective-permute-start | bytes 786440 | tf_op jit(solution)/shard_map/ppermute | solution.py:37
  39.7 8.5 %collective-permute-start.9 = (bf16[64,1024]{1,0:T(8,128)(2,1)S(1)}, bf16[64,1024]{1,0:T(8,128)(2,1)S(1)}, u32[]{:S(2)}, u32[]{:S(2)}) collective-permute-start(bf16[64,1024]{1,0:T(8,128)(2,1)S(1)} %leaf_add.3.after_ref.refs_0_), channel_id=1, source_target_pairs={{0,16},{4,20},{8,24},{12,28},{16,0},{20,4},{24,8},{28,12},{1,17},{... | collective-permute-start | bytes 393224 | tf_op jit(solution)/shard_map/ppermute | solution.py:37
  43.8 5.8 %collective-permute-start.8 = (bf16[2,256,128]{2,1,0:T(8,128)(2,1)S(1)}, bf16[2,256,128]{2,1,0:T(8,128)(2,1)S(1)}, u32[]{:S(2)}, u32[]{:S(2)}) collective-permute-start(bf16[2,256,128]{2,1,0:T(8,128)(2,1)S(1)} %get-tuple-element.28), channel_id=1, source_target_pairs={{0,8},{4,12},{8,0},{12,4},{16,24},{20,28},{24,16},{28,20},{1,9},{5... | collective-permute-start | bytes 393224 | tf_op jit(solution)/shard_map/ppermute | solution.py:37
  49.7 5.7 %collective-permute-start.12 = (bf16[2,256,128]{2,1,0:T(8,128)(2,1)S(1)}, bf16[2,256,128]{2,1,0:T(8,128)(2,1)S(1)}, u32[]{:S(2)}, u32[]{:S(2)}) collective-permute-start(bf16[2,256,128]{2,1,0:T(8,128)(2,1)S(1)} %get-tuple-element.32), channel_id=1, source_target_pairs={{0,8},{4,12},{8,0},{12,4},{16,24},{20,28},{24,16},{28,20},{1,9},{5... | collective-permute-start | bytes 393224 | tf_op jit(solution)/shard_map/ppermute | solution.py:37
  50.6 6.6 %collective-permute-start.14 = (bf16[32,1024]{1,0:T(8,128)(2,1)S(1)}, bf16[32,1024]{1,0:T(8,128)(2,1)S(1)}, u32[]{:S(2)}, u32[]{:S(2)}) collective-permute-start(bf16[32,1024]{1,0:T(8,128)(2,1)S(1)} %leaf_value.1.refs_2_.own_ref), channel_id=1, source_target_pairs={{0,4},{4,0},{8,12},{12,8},{16,20},{20,16},{24,28},{28,24},{1,5},{5... | collective-permute-start | bytes 196616 | tf_op jit(solution)/shard_map/ppermute | solution.py:37
  51.9 8.0 %collective-permute-start.10 = (bf16[1,256,128]{2,1,0:T(8,128)(2,1)S(1)}, bf16[1,256,128]{2,1,0:T(8,128)(2,1)S(1)}, u32[]{:S(2)}, u32[]{:S(2)}) collective-permute-start(bf16[1,256,128]{2,1,0:T(8,128)(2,1)S(1)} %get-tuple-element.30), channel_id=1, source_target_pairs={{0,16},{4,20},{8,24},{12,28},{16,0},{20,4},{24,8},{28,12},{1,17},{... | collective-permute-start | bytes 196616 | tf_op jit(solution)/shard_map/ppermute | solution.py:37
  55.5 5.9 %collective-permute-start.13 = (bf16[1,256,128]{2,1,0:T(8,128)(2,1)S(1)}, bf16[1,256,128]{2,1,0:T(8,128)(2,1)S(1)}, u32[]{:S(2)}, u32[]{:S(2)}) collective-permute-start(bf16[1,256,128]{2,1,0:T(8,128)(2,1)S(1)} %get-tuple-element.34), channel_id=1, source_target_pairs={{0,16},{4,20},{8,24},{12,28},{16,0},{20,4},{24,8},{28,12},{1,17},{... | collective-permute-start | bytes 196616 | tf_op jit(solution)/shard_map/ppermute | solution.py:37

commit v7 on v5

--- a/solution.py
+++ b/solution.py
@@ -63,8 +63,8 @@
     return half * per_half + i % per_half
 
 
-def rows_kernel(pos_ref, leaf_hbm, pred_hbm, lab_hbm, w_hbm, send_ref, keep_ref, g_ref, h_ref, pred_buf,
-                leaf_buf, lab_buf, w_buf, pred_sem, lab_sem, w_sem, leaf_sem):
+def rows_kernel(pos_ref, leaf_hbm, pred_hbm, lab_hbm, w_hbm, send_ref, keep_ref, g_ref, h_ref,
+                leaf_buf, pred_buf, lab_buf, w_buf, pred_sem, lab_sem, w_sem, leaf_sem):
     core, side = pos_ref[0], pos_ref[1]
     chunks, blk, _ = pred_buf.shape
     per_half = chunks // 2
@@ -77,11 +77,11 @@
     w_copy = pltpu.make_async_copy(w_hbm, w_buf, w_sem)
     leaf_copy = pltpu.make_async_copy(leaf_hbm, leaf_buf, leaf_sem)
     for i in range(chunks):
-        for j, copy in enumerate(copies(i)):
-            copy.start(priority=j)
+        for copy in copies(i):
+            copy.start()
         if i == 0:
             w_copy.start()
-            leaf_copy.start(priority=1)
+            leaf_copy.start()
     for i in range(chunks):
         for copy in copies(i):
             copy.wait()
@@ -113,12 +113,12 @@
     return pl.pallas_call(
         rows_kernel,
         in_specs=[pl.BlockSpec(memory_space=pltpu.SMEM), hbm, hbm, hbm, hbm],
-        out_specs=[vmem] * 5,
+        out_specs=[vmem] * 4,
         out_shape=[jax.ShapeDtypeStruct((rows // 2, w.shape[1]), bf16)] * 2
-        + [jax.ShapeDtypeStruct((LEAVES, cols), f32)] * 2
-        + [jax.ShapeDtypeStruct((chunks, blk, cols), bf16)],
+        + [jax.ShapeDtypeStruct((LEAVES, cols), f32)] * 2,
         scratch_shapes=[
             pltpu.VMEM(leaf.shape, jnp.int32),
+            pltpu.VMEM((chunks, blk, cols), bf16),
             pltpu.VMEM((chunks, blk, cols), bf16),
             pltpu.VMEM(w.shape, bf16),
             pltpu.SemaphoreType.DMA((chunks,)),
@@ -127,6 +127,7 @@
             pltpu.SemaphoreType.DMA,
         ],
         compiler_params=PARAMS,
+        cost_estimate=pl.CostEstimate(flops=int(1.38e+10), transcendentals=0, bytes_accessed=0),
         name="rows",
     )(pos, leaf, pred, lab, w)
 
@@ -199,60 +200,75 @@
         out_specs=pl.BlockSpec((1, per * feats, width), lambda i: (i, 0, 0)),
         out_shape=jax.ShapeDtypeStruct((blocks, per * feats, width), dtype),
         compiler_params=PARAMS,
+        cost_estimate=pl.CostEstimate(flops=int(3.45e+09), transcendentals=0, bytes_accessed=0),
         name="hist_send" if odd else "hist_keep",
     )(codes, own, other, after)
 
 
-def update_kernel(pos_ref, leaf_ref, own_ref, other_ref, pred_ref, after_ref, new_hbm, values_hbm, done_ref,
-                  new_buf, values_buf, new_sem, values_sem):
-    core, side = pos_ref[0], pos_ref[1]
-    chunks, blk, _ = pred_ref.shape
+def update_kernel(pos_ref, leaf_ref, own_ref, other_ref, pred_hbm, after_ref, *rest, first):
+    if first:
+        new_hbm, values_hbm, done_ref, pred_buf, new_buf, pred_sem, new_sem, values_buf, values_sem = rest
+    else:
+        _, new_hbm, done_ref, pred_buf, new_buf, pred_sem, new_sem = rest
+    side = pos_ref[1]
+    chunks, blk, _ = pred_buf.shape
+    start = 0 if first else chunks
     half = LEAVES // 2
 
+    def read(i):
+        return pltpu.make_async_copy(pred_hbm.at[pl.ds((start + i) * blk, blk)], pred_buf.at[i], pred_sem.at[i])
+
     def write(i):
-        at = pl.ds(pl.multiple_of(chunk_place(i, chunks, core) * blk, blk), blk)
-        return pltpu.make_async_copy(new_buf.at[i], new_hbm.at[at], new_sem.at[i])
-
+        return pltpu.make_async_copy(new_buf.at[i], new_hbm.at[pl.ds((start + i) * blk, blk)], new_sem.at[i])
+
+    for i in range(chunks):
+        read(i).start()
     own, other = own_ref[...], other_ref[...]
-    first = side == 0
-    values_buf[:half] = jnp.where(first, own.astype(f32), other.astype(f32))
-    values_buf[half:] = jnp.where(first, other.astype(f32), own.astype(f32))
-    values_copy = pltpu.make_async_copy(values_buf, values_hbm, values_sem)
-    values_copy.start(priority=1)
+    if first:
+        low = side == 0
+        values_buf[:half] = jnp.where(low, own.astype(f32), other.astype(f32))
+        values_buf[half:] = jnp.where(low, other.astype(f32), own.astype(f32))
+        values_copy = pltpu.make_async_copy(values_buf, values_hbm, values_sem)
+        values_copy.start()
     table = jnp.concatenate([own, other], axis=0)
     for i in range(chunks):
-        hot = leaf_hot(leaf_ref, chunk_place(i, chunks, core), blk, side * half, shrinkage)
+        hot = leaf_hot(leaf_ref, start + i, blk, side * half, shrinkage)
         found = lax.dot_general(hot, table, (((0,), (0,)), ((), ())), preferred_element_type=f32)
-        new_buf[i] = (pred_ref[i].astype(f32) + found).astype(bf16)
-        write(i).start(priority=i % 2)
+        read(i).wait()
+        new_buf[i] = (pred_buf[i].astype(f32) + found).astype(bf16)
+        write(i).start()
     done_ref[...] = jnp.zeros_like(done_ref)
-    values_copy.wait()
+    if first:
+        values_copy.wait()
     for i in range(chunks):
         write(i).wait()
 
 
-def update_pass(pos, leaf, own, other, pred, after):
-    chunks, blk, cols = pred.shape
+def update_pass(pos, leaf, own, other, pred, after, begun):
+    rows, cols = pred.shape
+    blk = block_rows(rows // 2)
+    chunks = rows // blk // 2
+    first = begun is None
     vmem = pl.BlockSpec(memory_space=pltpu.VMEM)
     hbm = pl.BlockSpec(memory_space=pl.ANY)
+    new = jax.ShapeDtypeStruct((rows, cols), bf16)
+    done = jax.ShapeDtypeStruct((8, 128), f32)
     return pl.pallas_call(
-        update_kernel,
-        in_specs=[pl.BlockSpec(memory_space=pltpu.SMEM), vmem, vmem, vmem, vmem, hbm],
-        out_specs=[pl.BlockSpec(memory_space=pltpu.HBM)] * 2 + [vmem],
-        out_shape=[
-            jax.ShapeDtypeStruct((chunks * blk, cols), bf16),
-            jax.ShapeDtypeStruct((LEAVES, cols), f32),
-            jax.ShapeDtypeStruct((8, 128), f32),
-        ],
+        functools.partial(update_kernel, first=first),
+        in_specs=[pl.BlockSpec(memory_space=pltpu.SMEM), vmem, vmem, vmem, hbm, hbm] + [hbm] * (not first),
+        out_specs=[hbm] * (1 + first) + [vmem],
+        out_shape=[new, jax.ShapeDtypeStruct((LEAVES, cols), f32), done] if first else [new, done],
         scratch_shapes=[
             pltpu.VMEM((chunks, blk, cols), bf16),
-            pltpu.VMEM((LEAVES, cols), f32),
+            pltpu.VMEM((chunks, blk, cols), bf16),
             pltpu.SemaphoreType.DMA((chunks,)),
-            pltpu.SemaphoreType.DMA,
-        ],
+            pltpu.SemaphoreType.DMA((chunks,)),
+        ] + ([pltpu.VMEM((LEAVES, cols), f32), pltpu.SemaphoreType.DMA] if first else []),
+        input_output_aliases={} if first else {6: 0},
         compiler_params=PARAMS,
-        name="update",
-    )(pos, leaf, own, other, pred, after)
+        cost_estimate=pl.CostEstimate(flops=int(6.44e+09), transcendentals=0, bytes_accessed=0),
+        name="update_first" if first else "update_second",
+    )(pos, leaf, own, other, pred, after, *([] if first else [begun]))
 
 
 def local(n, nf, predictions, labels, feature_codes, leaf_index, sketch_weight):
@@ -277,68 +293,92 @@
     sums16 = jax.ShapeDtypeStruct((LEAVES, cols), bf16)
     sums32 = jax.ShapeDtypeStruct((LEAVES, cols), f32)
 
-    send, keep, grad, hess, held = rows_pass(pos, pltpu.with_memory_space_constraint(leaf, pltpu.HBM), pred, lab, weight)
+    send, keep, grad, hess = rows_pass(pos, pltpu.with_memory_space_constraint(leaf, pltpu.HBM), pred, lab, weight)
     got = swap(send, "feat", nf, 1)
-    pair, crossed, after = [], [], keep
-    for p in range(parts):
-        after = ordered(part_add(p, parts), sketch16, [keep, got], after, "core_add")
-        pair.append(after)
-        crossed.append([swap(after, "feat", nf, t) for t in range(2, nf, 2)])
-        if p == 0:
-            after, sent = ordered(leaf_pack_kernel, [sums32, sums16], [grad, hess], after, "leaf_pack")
-            leaf_state = (after, swap(sent, "rows", n, 1), 2)
-
-    def leaf_step(after):
-        nonlocal leaf_state
-        acc, got, by = leaf_state
-        if by < n:
-            acc = ordered(add_kernel, sums16, [acc, got], after, "leaf_add")
-            leaf_state = (acc, swap(acc, "rows", n, by), 2 * by)
-        elif by == n:
-            values16 = jax.ShapeDtypeStruct((LEAVES // 2, cols), bf16)
-            acc = ordered(value_kernel, values16, [acc, got], after, "leaf_value")
-            leaf_state = (acc, swap(acc, "rows", n, 1), 2 * by)
-        else:
-            return after
-        return acc
-
-    owns, others, backs, heres = [], [], [], []
-    after = leaf_step(after)
-    for p in range(parts):
+    after = keep
+    pair, crossed, owns, others, backs, heres = ([None] * parts for _ in range(6))
+    leaf_state = None
+    updated = leaf_values = None
+    levels = (n // 2).bit_length() - 1
+
+    def core_add(p):
+        nonlocal after
+        after = pair[p] = ordered(part_add(p, parts), sketch16, [keep, got], after, "core_add")
+        crossed[p] = [swap(after, "feat", nf, t) for t in range(2, nf, 2)]
+
+    def feat_add(p):
+        nonlocal after
         own = pair[p]
         for recv in crossed[p]:
             after = own = ordered(add_kernel, sketch16, [own, recv], after, "feat_add")
-        owns.append(own)
-        others.append(swap(own, "feat", nf, 1))
-        if p > 0:
-            after = leaf_step(after)
-            after = hist_pass(codes, owns[p - 1], others[p - 1], per, n // 2, 0, f32, after)
-            heres.append(after)
-        after = hist_pass(codes, own, others[p], per, n // 2, 1, bf16, after)
-        backs.append(swap(after, "rows", n, 1))
-    after = hist_pass(codes, owns[-1], others[-1], per, n // 2, 0, f32, after)
-    heres.append(after)
-
-    levels = (n // 2).bit_length() - 1
-    for slot in range(levels + parts - 1):
-        for p in range(parts):
-            level = slot - p
-            if 0 <= level < levels:
-                if p == parts - 1 and level == levels - 1:
-                    while leaf_state[2] <= n:
-                        after = leaf_step(after)
-                    updated, leaf_values, after = update_pass(
-                        pos, leaf, leaf_state[0], leaf_state[1], held, after)
-                blocks = heres[p].shape[0] // 2
-                shape = (blocks,) + heres[p].shape[1:]
-                after, sent = ordered(
-                    halving_kernel,
-                    [jax.ShapeDtypeStruct(shape, f32), jax.ShapeDtypeStruct(shape, bf16)],
-                    [heres[p], backs[p]], after, "hist_add")
-                heres[p] = after
-                backs[p] = swap(sent, "rows", n, 2 << level)
-                if slot == 0:
-                    after = leaf_step(after)
+        owns[p] = own
+        others[p] = swap(own, "feat", nf, 1)
+
+    def leaf_pack():
+        nonlocal after, leaf_state
+        after, sent = ordered(leaf_pack_kernel, [sums32, sums16], [grad, hess], after, "leaf_pack")
+        leaf_state = (after, swap(sent, "rows", n, 1), 2)
+
+    def leaf_step():
+        nonlocal after, leaf_state
+        acc, recv, by = leaf_state
+        if by < n:
+            after = ordered(add_kernel, sums16, [acc, recv], after, "leaf_add")
+            leaf_state = (after, swap(after, "rows", n, by), 2 * by)
+        elif by == n:
+            values16 = jax.ShapeDtypeStruct((LEAVES // 2, cols), bf16)
+            after = ordered(value_kernel, values16, [acc, recv], after, "leaf_value")
+            leaf_state = (after, swap(after, "rows", n, 1), 2 * by)
+
+    def update():
+        nonlocal after, updated, leaf_values
+        while leaf_state[2] <= n:
+            leaf_step()
+        if updated is None:
+            updated, leaf_values, after = update_pass(pos, leaf, leaf_state[0], leaf_state[1], pred, after, None)
+        else:
+            updated, after = update_pass(pos, leaf, leaf_state[0], leaf_state[1], pred, after, updated)
+
+    def hist_send(p):
+        nonlocal after
+        after = hist_pass(codes, owns[p], others[p], per, n // 2, 1, bf16, after)
+        backs[p] = swap(after, "rows", n, 1)
+
+    def hist_keep(p):
+        nonlocal after
+        after = heres[p] = hist_pass(codes, owns[p], others[p], per, n // 2, 0, f32, after)
+
+    def hist_add(p, level):
+        nonlocal after
+        blocks = heres[p].shape[0] // 2
+        shape = (blocks,) + heres[p].shape[1:]
+        heres[p], sent = ordered(
+            halving_kernel,
+            [jax.ShapeDtypeStruct(shape, f32), jax.ShapeDtypeStruct(shape, bf16)],
+            [heres[p], backs[p]], after, "hist_add")
+        after = heres[p]
+        backs[p] = swap(sent, "rows", n, 2 << level)
+
+    core_add(0)
+    leaf_pack()
+    core_add(1)
+    leaf_step()
+    feat_add(0)
+    hist_send(0)
+    feat_add(1)
+    hist_keep(0)
+    leaf_step()
+    hist_send(1)
+    hist_keep(1)
+    for level in range(levels):
+        hist_add(0, level)
+        if level == 0:
+            leaf_step()
+        if level > 0:
+            hist_add(1, level - 1)
+    update()
+    hist_add(1, levels - 1)
+    update()
     histograms = ordered(
         last_kernel, jax.ShapeDtypeStruct((per * feats, width * parts), f32),
         [a for p in range(parts) for a in (heres[p], backs[p])], after, "last_add")

time: 64 us -> 53.9 us (0.84)
  local copies, waits for them, and re-layouts: 4.96 us -> 0.01 us
  waiting for transfers between devices: 13.1 us -> 10 us
  other arithmetic: 2.38 us -> 0.09 us
  starting transfers between devices: 21 us -> 22.4 us
  Pallas kernels: 21.3 us -> 20.4 us
    pallas_call x13, Pallas kernels: 6.47 us -> 1.23 us  [ordered(): pl.pallas_call(body, in_specs=[pl.BlockSpec(memory_space=pltpu.VMEM)] * l...]
    unnamed x14 -> x4, local copies, waits for them, and re-layouts: 4.96 us -> 0.01 us
    pallas_call x1 -> x2, Pallas kernels: 2.67 us -> 7.21 us  [update_pass(): pl.pallas_call(functools.partial(update_kernel, first=first), in_specs=[p...]
    ppermute x15, waiting for transfers between devices: 13.1 us -> 10 us  [swap(): return lax.ppermute(x, axis, [(i, i ^ by) for i in range(size)])]
    xor x1, other arithmetic: 1.42 us -> 0.01 us  [local(): codes = (feature_codes ^ me * per).reshape(feats, 2, half)]
    ppermute x15, starting transfers between devices: 21 us -> 22.4 us  [swap(): return lax.ppermute(x, axis, [(i, i ^ by) for i in range(size)])]
    transpose x1, other arithmetic: 0.89 us -> 0.01 us  [local(): codes = jnp.where(core == 0, codes, codes[:, ::-1]).swapaxes(0, 1)]
  transfers between devices with their start and end apart: 15 -> 15, of which waited for: 8 -> 7; matrix products, arithmetic and copies ran while one was open for 4% -> 0% of each run, Pallas kernels for 20% -> 25%
where the time goes in v7:
time: 53.9 us; the launch traced here: 53.7 us
  starting transfers between devices  22.4 us (42%)
  Pallas kernels  20.4 us (38%)
  waiting for transfers between devices  10 us (19%)
  between operations  0.83 us (2%)
    ppermute x15, starting transfers between devices, swap(): return lax.ppermute(x, axis, [(i, i ^ by) for i in range(size)])  22.4 us
    ppermute x15, waiting for transfers between devices, swap(): return lax.ppermute(x, axis, [(i, i ^ by) for i in range(size)])  10 us
    pallas_call x2, Pallas kernels, update_pass(): pl.pallas_call(functools.partial(update_kernel, first=first), in_specs=[p...  7.21 us
    pallas_call x1, Pallas kernels, rows_pass(): pl.pallas_call(rows_kernel, in_specs=[pl.BlockSpec(memory_space=pltpu.SME...  6.06 us
    pallas_call x4, Pallas kernels, hist_pass(): pl.pallas_call(functools.partial(hist_kernel, per=per, odd=odd, bits=bloc...  5.88 us
    pallas_call x13, Pallas kernels, ordered(): pl.pallas_call(body, in_specs=[pl.BlockSpec(memory_space=pltpu.VMEM)] * l...  1.23 us
  transfers between devices with their start and end apart: 15, of which 7 were waited for; matrix products, arithmetic and copies ran while one was open for 0% of the time, Pallas kernels for 25%

profile of v7, /device:TPU:0, one launch (start us, length us, event | category | flops | bytes accessed | tf_op | source)
XLA Modules:
  0.0 53.7 jit_solution(14454626637460988990)
XLA Ops:
  0.6 0.1 pad_add_fusion.pos_ref
  0.7 0.0 copy-start.1
  0.7 6.1 %rows.1 = (bf16[768,256]{1,0:T(8,128)(2,1)S(1)}, bf16[768,256]{1,0:T(8,128)(2,1)S(1)}, f32[64,1024]{1,0:T(8,128)S(1)}, f32[64,1024]{1,0:T(8,128)S(1)}) custom-call(s32[2]{0:T(128)S(1)} %pad_add_fusion.pos_ref, s32[12,128]{1,0:T(8,128)} %bitcast.7, bf16[1536,1024]{1,0:T(8,128)(2,1)} %pred_hbm.5, bf16[1536,1024]{1,0:T(8,128)(2,1)} %lab_hbm.1, ...), custom_call_target="tpu_custom_call" | custom-call | flops 13799999488 | tf_op jit(solution)/shard_map/rows/pallas_call | solution.py:113
  6.8 0.5 collective-permute-start
  7.3 1.3 %collective-permute-done.refs_1_ = bf16[768,256]{1,0:T(8,128)(2,1)S(1)} collective-permute-done((bf16[768,256]{1,0:T(8,128)(2,1)S(1)}, bf16[768,256]{1,0:T(8,128)(2,1)S(1)}, u32[]{:S(2)}, u32[]{:S(2)}) %collective-permute-start) | collective-permute-done | bytes 393248 | tf_op jit(solution)/shard_map/ppermute | solution.py:33
  8.7 3.0 %collective-permute-start.1 = (bf16[768,128]{1,0:T(8,128)(2,1)S(1)}, bf16[768,128]{1,0:T(8,128)(2,1)S(1)}, u32[]{:S(2)}, u32[]{:S(2)}) collective-permute-start(bf16[768,128]{1,0:T(8,128)(2,1)S(1)} %core_add.2.refs_2_.refs_0_), channel_id=1, source_target_pairs={{0,2},{1,3},{2,0},{3,1},{4,6},{5,7},{6,4},{7,5},{8,10},{9,11},{10,... | collective-permute-start | bytes 589832 | tf_op jit(solution)/shard_map/ppermute | solution.py:33
  11.7 1.6 %collective-permute-start.2 = (bf16[64,1024]{1,0:T(8,128)(2,1)S(1)}, bf16[64,1024]{1,0:T(8,128)(2,1)S(1)}, u32[]{:S(2)}, u32[]{:S(2)}) collective-permute-start(bf16[64,1024]{1,0:T(8,128)(2,1)S(1)} %get-tuple-element.27), channel_id=1, source_target_pairs={{0,4},{4,0},{8,12},{12,8},{16,20},{20,16},{24,28},{28,24},{1,5},{5... | collective-permute-start | bytes 393224 | tf_op jit(solution)/shard_map/ppermute | solution.py:33
  13.2 0.0 copy-done.1
  13.3 3.7 %collective-permute-done.2.refs_1_ = bf16[64,1024]{1,0:T(8,128)(2,1)S(1)} collective-permute-done((bf16[64,1024]{1,0:T(8,128)(2,1)S(1)}, bf16[64,1024]{1,0:T(8,128)(2,1)S(1)}, u32[]{:S(2)}, u32[]{:S(2)}) %collective-permute-start.2) | collective-permute-done | bytes 131104 | tf_op jit(solution)/shard_map/ppermute | solution.py:33
  17.0 0.0 collective-permute-done.1.refs_1_
  17.1 0.1 collective-permute-start.3
  17.2 1.6 %collective-permute-start.4 = (bf16[768,128]{1,0:T(8,128)(2,1)S(1)}, bf16[768,128]{1,0:T(8,128)(2,1)S(1)}, u32[]{:S(2)}, u32[]{:S(2)}) collective-permute-start(bf16[768,128]{1,0:T(8,128)(2,1)S(1)} %core_add.3.refs_2_.refs_0_), channel_id=1, source_target_pairs={{0,2},{1,3},{2,0},{3,1},{4,6},{5,7},{6,4},{7,5},{8,10},{9,11},{10,... | collective-permute-start | bytes 589832 | tf_op jit(solution)/shard_map/ppermute | solution.py:33
  18.8 1.6 %collective-permute-start.7 = (bf16[64,1024]{1,0:T(8,128)(2,1)S(1)}, bf16[64,1024]{1,0:T(8,128)(2,1)S(1)}, u32[]{:S(2)}, u32[]{:S(2)}) collective-permute-start(bf16[64,1024]{1,0:T(8,128)(2,1)S(1)} %leaf_add.2.refs_2_.refs_0_), channel_id=1, source_target_pairs={{0,8},{4,12},{8,0},{12,4},{16,24},{20,28},{24,16},{28,20},{1,9},{5... | collective-permute-start | bytes 393224 | tf_op jit(solution)/shard_map/ppermute | solution.py:33
  20.4 0.0 collective-permute-done.3.other_ref
  20.4 1.5 %hist_send.2.refs_2_ = bf16[4,256,128]{2,1,0:T(8,128)(2,1)S(1)} custom-call(s32[2,8,768]{2,1,0:T(8,128)S(1)} %fusion.codes_ref, bf16[768,128]{1,0:T(8,128)(2,1)S(1)} %feat_add.2.own_ref.after_ref, bf16[768,128]{1,0:T(8,128)(2,1)S(1)} %collective-permute-done.3.other_ref, bf16[768,128]{1,0:T(8,128)(2,1)S(1)} %feat_add.2.own_ref.after_ref), custom_call_target="tpu_custom_call" | custom-call | flops 3449999872 | tf_op jit(solution)/shard_map/hist_send/pallas_call | solution.py:196
  21.9 1.6 %collective-permute-start.5 = (bf16[4,256,128]{2,1,0:T(8,128)(2,1)S(1)}, bf16[4,256,128]{2,1,0:T(8,128)(2,1)S(1)}, u32[]{:S(2)}, u32[]{:S(2)}) collective-permute-start(bf16[4,256,128]{2,1,0:T(8,128)(2,1)S(1)} %hist_send.2.refs_2_), channel_id=1, source_target_pairs={{0,4},{4,0},{8,12},{12,8},{16,20},{20,16},{24,28},{28,24},{1,5},{5... | collective-permute-start | bytes 786440 | tf_op jit(solution)/shard_map/ppermute | solution.py:33
  23.4 1.1 %collective-permute-done.4.refs_1_ = bf16[768,128]{1,0:T(8,128)(2,1)S(1)} collective-permute-done((bf16[768,128]{1,0:T(8,128)(2,1)S(1)}, bf16[768,128]{1,0:T(8,128)(2,1)S(1)}, u32[]{:S(2)}, u32[]{:S(2)}) %collective-permute-start.4) | collective-permute-done | bytes 196640 | tf_op jit(solution)/shard_map/ppermute | solution.py:33
  24.6 0.1 collective-permute-start.6
  24.6 1.5 %hist_keep.2.refs_2_.refs_0_ = f32[4,256,128]{2,1,0:T(8,128)S(1)} custom-call(s32[2,8,768]{2,1,0:T(8,128)S(1)} %fusion.codes_ref, bf16[768,128]{1,0:T(8,128)(2,1)S(1)} %feat_add.2.own_ref.after_ref, bf16[768,128]{1,0:T(8,128)(2,1)S(1)} %collective-permute-done.3.other_ref, bf16[768,128]{1,0:T(8,128)(2,1)S(1)} %feat_add.3.after_ref.own_ref), custom_call_target="tpu_custom_call" | custom-call | flops 3449999872 | tf_op jit(solution)/shard_map/hist_keep/pallas_call | solution.py:196
  26.1 0.0 collective-permute-done.7.refs_1_
  26.2 2.7 %collective-permute-start.9 = (bf16[64,1024]{1,0:T(8,128)(2,1)S(1)}, bf16[64,1024]{1,0:T(8,128)(2,1)S(1)}, u32[]{:S(2)}, u32[]{:S(2)}) collective-permute-start(bf16[64,1024]{1,0:T(8,128)(2,1)S(1)} %leaf_add.3.after_ref.refs_0_), channel_id=1, source_target_pairs={{0,16},{4,20},{8,24},{12,28},{16,0},{20,4},{24,8},{28,12},{1,17},{... | collective-permute-start | bytes 393224 | tf_op jit(solution)/shard_map/ppermute | solution.py:33
  28.9 0.0 collective-permute-done.6.other_ref
  28.9 1.5 %hist_send.3.after_ref = bf16[4,256,128]{2,1,0:T(8,128)(2,1)S(1)} custom-call(s32[2,8,768]{2,1,0:T(8,128)S(1)} %fusion.codes_ref, bf16[768,128]{1,0:T(8,128)(2,1)S(1)} %feat_add.3.after_ref.own_ref, bf16[768,128]{1,0:T(8,128)(2,1)S(1)} %collective-permute-done.6.other_ref, bf16[64,1024]{1,0:T(8,128)(2,1)S(1)} %leaf_add.3.after_ref.refs_0_), custom_call_target="tpu_custom_call" | custom-call | flops 3449999872 | tf_op jit(solution)/shard_map/hist_send/pallas_call | solution.py:196
  30.3 1.6 %collective-permute-start.11 = (bf16[4,256,128]{2,1,0:T(8,128)(2,1)S(1)}, bf16[4,256,128]{2,1,0:T(8,128)(2,1)S(1)}, u32[]{:S(2)}, u32[]{:S(2)}) collective-permute-start(bf16[4,256,128]{2,1,0:T(8,128)(2,1)S(1)} %hist_send.3.after_ref), channel_id=1, source_target_pairs={{0,4},{4,0},{8,12},{12,8},{16,20},{20,16},{24,28},{28,24},{1,5},{5... | collective-permute-start | bytes 786440 | tf_op jit(solution)/shard_map/ppermute | solution.py:33
  31.9 1.5 %hist_keep.3.refs_2_.refs_0_ = f32[4,256,128]{2,1,0:T(8,128)S(1)} custom-call(s32[2,8,768]{2,1,0:T(8,128)S(1)} %fusion.codes_ref, bf16[768,128]{1,0:T(8,128)(2,1)S(1)} %feat_add.3.after_ref.own_ref, bf16[768,128]{1,0:T(8,128)(2,1)S(1)} %collective-permute-done.6.other_ref, bf16[4,256,128]{2,1,0:T(8,128)(2,1)S(1)} %hist_send.3.after_ref), custom_call_target="tpu_custom_call" | custom-call | flops 3449999872 | tf_op jit(solution)/shard_map/hist_keep/pallas_call | solution.py:196
  33.4 0.0 copy-start
  33.4 0.0 collective-permute-done.5.refs_1_
  33.5 1.6 %collective-permute-start.8 = (bf16[2,256,128]{2,1,0:T(8,128)(2,1)S(1)}, bf16[2,256,128]{2,1,0:T(8,128)(2,1)S(1)}, u32[]{:S(2)}, u32[]{:S(2)}) collective-permute-start(bf16[2,256,128]{2,1,0:T(8,128)(2,1)S(1)} %get-tuple-element.29), channel_id=1, source_target_pairs={{0,8},{4,12},{8,0},{12,4},{16,24},{20,28},{24,16},{28,20},{1,9},{5... | collective-permute-start | bytes 393224 | tf_op jit(solution)/shard_map/ppermute | solution.py:33
  35.1 0.8 %collective-permute-done.9.refs_1_ = bf16[64,1024]{1,0:T(8,128)(2,1)S(1)} collective-permute-done((bf16[64,1024]{1,0:T(8,128)(2,1)S(1)}, bf16[64,1024]{1,0:T(8,128)(2,1)S(1)}, u32[]{:S(2)}, u32[]{:S(2)}) %collective-permute-start.9) | collective-permute-done | bytes 131104 | tf_op jit(solution)/shard_map/ppermute | solution.py:33
  35.9 1.7 %collective-permute-start.13 = (bf16[32,1024]{1,0:T(8,128)(2,1)S(1)}, bf16[32,1024]{1,0:T(8,128)(2,1)S(1)}, u32[]{:S(2)}, u32[]{:S(2)}) collective-permute-start(bf16[32,1024]{1,0:T(8,128)(2,1)S(1)} %leaf_value.1.refs_2_.own_ref), channel_id=1, source_target_pairs={{0,4},{4,0},{8,12},{12,8},{16,20},{20,16},{24,28},{28,24},{1,5},{5... | collective-permute-start | bytes 196616 | tf_op jit(solution)/shard_map/ppermute | solution.py:33
  37.6 1.3 %collective-permute-done.8.refs_1_ = bf16[2,256,128]{2,1,0:T(8,128)(2,1)S(1)} collective-permute-done((bf16[2,256,128]{2,1,0:T(8,128)(2,1)S(1)}, bf16[2,256,128]{2,1,0:T(8,128)(2,1)S(1)}, u32[]{:S(2)}, u32[]{:S(2)}) %collective-permute-start.8) | collective-permute-done | bytes 131104 | tf_op jit(solution)/shard_map/ppermute | solution.py:33
  38.9 1.5 %collective-permute-start.10 = (bf16[1,256,128]{2,1,0:T(8,128)(2,1)S(1)}, bf16[1,256,128]{2,1,0:T(8,128)(2,1)S(1)}, u32[]{:S(2)}, u32[]{:S(2)}) collective-permute-start(bf16[1,256,128]{2,1,0:T(8,128)(2,1)S(1)} %get-tuple-element.31), channel_id=1, source_target_pairs={{0,16},{4,20},{8,24},{12,28},{16,0},{20,4},{24,8},{28,12},{1,17},{... | collective-permute-start | bytes 196616 | tf_op jit(solution)/shard_map/ppermute | solution.py:33
  40.3 0.0 collective-permute-done.11.refs_1_
  40.4 2.5 %collective-permute-start.12 = (bf16[2,256,128]{2,1,0:T(8,128)(2,1)S(1)}, bf16[2,256,128]{2,1,0:T(8,128)(2,1)S(1)}, u32[]{:S(2)}, u32[]{:S(2)}) collective-permute-start(bf16[2,256,128]{2,1,0:T(8,128)(2,1)S(1)} %get-tuple-element.33), channel_id=1, source_target_pairs={{0,8},{4,12},{8,0},{12,4},{16,24},{20,28},{24,16},{28,20},{1,9},{5... | collective-permute-start | bytes 393224 | tf_op jit(solution)/shard_map/ppermute | solution.py:33
  42.9 0.0 collective-permute-done.13.other_ref
  42.9 0.0 copy-done
  42.9 3.7 %update_first.1 = (bf16[1536,1024]{1,0:T(8,128)(2,1)}, f32[64,1024]{1,0:T(8,128)}, f32[8,128]{1,0:T(8,128)S(1)}) custom-call(s32[2]{0:T(128)S(1)} %pad_add_fusion.pos_ref, s32[12,128]{1,0:T(8,128)S(1)} %bitcast.8, bf16[32,1024]{1,0:T(8,128)(2,1)S(1)} %leaf_value.1.refs_2_.own_ref, bf16[32,1024]{1,0:T(8,128)(2,1)S(1)} %collective-permute-done.13.other_ref, ...), custom_call_target="tpu_custom_call" | custom-call | flops 6440000000 | tf_op jit(solution)/shard_map/update_first/pallas_call | solution.py:256
  46.6 0.4 collective-permute-done.12.refs_1_
  47.1 0.9 %collective-permute-start.14 = (bf16[1,256,128]{2,1,0:T(8,128)(2,1)S(1)}, bf16[1,256,128]{2,1,0:T(8,128)(2,1)S(1)}, u32[]{:S(2)}, u32[]{:S(2)}) collective-permute-start(bf16[1,256,128]{2,1,0:T(8,128)(2,1)S(1)} %get-tuple-element.36), channel_id=1, source_target_pairs={{0,16},{4,20},{8,24},{12,28},{16,0},{20,4},{24,8},{28,12},{1,17},{... | collective-permute-start | bytes 196616 | tf_op jit(solution)/shard_map/ppermute | solution.py:33
  48.0 3.5 %update_second.1 = (bf16[1536,1024]{1,0:T(8,128)(2,1)}, f32[8,128]{1,0:T(8,128)S(1)}) custom-call(s32[2]{0:T(128)S(1)} %pad_add_fusion.pos_ref, s32[12,128]{1,0:T(8,128)S(1)} %bitcast.9, bf16[32,1024]{1,0:T(8,128)(2,1)S(1)} %leaf_value.1.refs_2_.own_ref, bf16[32,1024]{1,0:T(8,128)(2,1)S(1)} %collective-permute-done.13.other_ref, ...), custom_call_target="tpu_custom_call", output_to_operand_aliasing={{0}: (6, {})} | custom-call | flops 6440000000 | tf_op jit(solution)/shard_map/update_second/pallas_call | solution.py:256
  51.6 0.0 collective-permute-done.10.refs_1_
  51.6 1.4 %collective-permute-done.14.refs_3_ = bf16[1,256,128]{2,1,0:T(8,128)(2,1)S(1)} collective-permute-done((bf16[1,256,128]{2,1,0:T(8,128)(2,1)S(1)}, bf16[1,256,128]{2,1,0:T(8,128)(2,1)S(1)}, u32[]{:S(2)}, u32[]{:S(2)}) %collective-permute-start.14) | collective-permute-done | bytes 65568 | tf_op jit(solution)/shard_map/ppermute | solution.py:33
  53.0 0.7 %last_add.1 = f32[256,256]{1,0:T(8,128)} custom-call(f32[1,256,128]{2,1,0:T(8,128)S(1)} %get-tuple-element.30.refs_2_.refs_0_, bf16[1,256,128]{2,1,0:T(8,128)(2,1)S(1)} %collective-permute-done.10.refs_1_, f32[1,256,128]{2,1,0:T(8,128)S(1)} %get-tuple-element.35.after_ref.refs_2_, bf16[1,256,128]{2,1,0:T(8,128)(2,1)S(1)} %collective-permute-done.14.refs_3_, ...), custom_call_target="tpu_custom_call" | custom-call | tf_op jit(solution)/shard_map/last_add/pallas_call | solution.py:41
  (14 shorter events, 0.5 us)
Async XLA Ops:
  0.7 12.5 %copy-start.1 = (s32[8,1536]{1,0:T(8,128)S(1)}, s32[8,1536]{1,0:T(8,128)}, u32[]{:S(2)}) copy-start(s32[8,1536]{1,0:T(8,128)} %param.7) | copy-start | bytes 147460
  6.8 1.9 %collective-permute-start = (bf16[768,256]{1,0:T(8,128)(2,1)S(1)}, bf16[768,256]{1,0:T(8,128)(2,1)S(1)}, u32[]{:S(2)}, u32[]{:S(2)}) collective-permute-start(bf16[768,256]{1,0:T(8,128)(2,1)S(1)} %get-tuple-element.23), channel_id=1, source_target_pairs={{0,1},{1,0},{2,3},{3,2},{4,5},{5,4},{6,7},{7,6},{8,9},{9,8},{10,11... | collective-permute-start | bytes 1179656 | tf_op jit(solution)/shard_map/ppermute | solution.py:33
  8.7 8.3 %collective-permute-start.1 = (bf16[768,128]{1,0:T(8,128)(2,1)S(1)}, bf16[768,128]{1,0:T(8,128)(2,1)S(1)}, u32[]{:S(2)}, u32[]{:S(2)}) collective-permute-start(bf16[768,128]{1,0:T(8,128)(2,1)S(1)} %core_add.2.refs_2_.refs_0_), channel_id=1, source_target_pairs={{0,2},{1,3},{2,0},{3,1},{4,6},{5,7},{6,4},{7,5},{8,10},{9,11},{10,... | collective-permute-start | bytes 589832 | tf_op jit(solution)/shard_map/ppermute | solution.py:33
  11.7 5.3 %collective-permute-start.2 = (bf16[64,1024]{1,0:T(8,128)(2,1)S(1)}, bf16[64,1024]{1,0:T(8,128)(2,1)S(1)}, u32[]{:S(2)}, u32[]{:S(2)}) collective-permute-start(bf16[64,1024]{1,0:T(8,128)(2,1)S(1)} %get-tuple-element.27), channel_id=1, source_target_pairs={{0,4},{4,0},{8,12},{12,8},{16,20},{20,16},{24,28},{28,24},{1,5},{5... | collective-permute-start | bytes 393224 | tf_op jit(solution)/shard_map/ppermute | solution.py:33
  17.1 3.3 %collective-permute-start.3 = (bf16[768,128]{1,0:T(8,128)(2,1)S(1)}, bf16[768,128]{1,0:T(8,128)(2,1)S(1)}, u32[]{:S(2)}, u32[]{:S(2)}) collective-permute-start(bf16[768,128]{1,0:T(8,128)(2,1)S(1)} %feat_add.2.own_ref.after_ref), channel_id=1, source_target_pairs={{0,1},{1,0},{2,3},{3,2},{4,5},{5,4},{6,7},{7,6},{8,9},{9,8},{10,11... | collective-permute-start | bytes 589832 | tf_op jit(solution)/shard_map/ppermute | solution.py:33
  17.2 7.3 %collective-permute-start.4 = (bf16[768,128]{1,0:T(8,128)(2,1)S(1)}, bf16[768,128]{1,0:T(8,128)(2,1)S(1)}, u32[]{:S(2)}, u32[]{:S(2)}) collective-permute-start(bf16[768,128]{1,0:T(8,128)(2,1)S(1)} %core_add.3.refs_2_.refs_0_), channel_id=1, source_target_pairs={{0,2},{1,3},{2,0},{3,1},{4,6},{5,7},{6,4},{7,5},{8,10},{9,11},{10,... | collective-permute-start | bytes 589832 | tf_op jit(solution)/shard_map/ppermute | solution.py:33
  18.8 7.3 %collective-permute-start.7 = (bf16[64,1024]{1,0:T(8,128)(2,1)S(1)}, bf16[64,1024]{1,0:T(8,128)(2,1)S(1)}, u32[]{:S(2)}, u32[]{:S(2)}) collective-permute-start(bf16[64,1024]{1,0:T(8,128)(2,1)S(1)} %leaf_add.2.refs_2_.refs_0_), channel_id=1, source_target_pairs={{0,8},{4,12},{8,0},{12,4},{16,24},{20,28},{24,16},{28,20},{1,9},{5... | collective-permute-start | bytes 393224 | tf_op jit(solution)/shard_map/ppermute | solution.py:33
  21.9 11.5 %collective-permute-start.5 = (bf16[4,256,128]{2,1,0:T(8,128)(2,1)S(1)}, bf16[4,256,128]{2,1,0:T(8,128)(2,1)S(1)}, u32[]{:S(2)}, u32[]{:S(2)}) collective-permute-start(bf16[4,256,128]{2,1,0:T(8,128)(2,1)S(1)} %hist_send.2.refs_2_), channel_id=1, source_target_pairs={{0,4},{4,0},{8,12},{12,8},{16,20},{20,16},{24,28},{28,24},{1,5},{5... | collective-permute-start | bytes 786440 | tf_op jit(solution)/shard_map/ppermute | solution.py:33
  24.6 4.3 %collective-permute-start.6 = (bf16[768,128]{1,0:T(8,128)(2,1)S(1)}, bf16[768,128]{1,0:T(8,128)(2,1)S(1)}, u32[]{:S(2)}, u32[]{:S(2)}) collective-permute-start(bf16[768,128]{1,0:T(8,128)(2,1)S(1)} %feat_add.3.after_ref.own_ref), channel_id=1, source_target_pairs={{0,1},{1,0},{2,3},{3,2},{4,5},{5,4},{6,7},{7,6},{8,9},{9,8},{10,11... | collective-permute-start | bytes 589832 | tf_op jit(solution)/shard_map/ppermute | solution.py:33
  26.2 9.7 %collective-permute-start.9 = (bf16[64,1024]{1,0:T(8,128)(2,1)S(1)}, bf16[64,1024]{1,0:T(8,128)(2,1)S(1)}, u32[]{:S(2)}, u32[]{:S(2)}) collective-permute-start(bf16[64,1024]{1,0:T(8,128)(2,1)S(1)} %leaf_add.3.after_ref.refs_0_), channel_id=1, source_target_pairs={{0,16},{4,20},{8,24},{12,28},{16,0},{20,4},{24,8},{28,12},{1,17},{... | collective-permute-start | bytes 393224 | tf_op jit(solution)/shard_map/ppermute | solution.py:33
  30.3 10.0 %collective-permute-start.11 = (bf16[4,256,128]{2,1,0:T(8,128)(2,1)S(1)}, bf16[4,256,128]{2,1,0:T(8,128)(2,1)S(1)}, u32[]{:S(2)}, u32[]{:S(2)}) collective-permute-start(bf16[4,256,128]{2,1,0:T(8,128)(2,1)S(1)} %hist_send.3.after_ref), channel_id=1, source_target_pairs={{0,4},{4,0},{8,12},{12,8},{16,20},{20,16},{24,28},{28,24},{1,5},{5... | collective-permute-start | bytes 786440 | tf_op jit(solution)/shard_map/ppermute | solution.py:33
  33.4 9.6 %copy-start = (s32[1536]{0:T(1024)S(1)}, s32[1536]{0:T(1024)}, u32[]{:S(2)}) copy-start(s32[1536]{0:T(1024)} %param.8) | copy-start | bytes 18436
  33.5 5.4 %collective-permute-start.8 = (bf16[2,256,128]{2,1,0:T(8,128)(2,1)S(1)}, bf16[2,256,128]{2,1,0:T(8,128)(2,1)S(1)}, u32[]{:S(2)}, u32[]{:S(2)}) collective-permute-start(bf16[2,256,128]{2,1,0:T(8,128)(2,1)S(1)} %get-tuple-element.29), channel_id=1, source_target_pairs={{0,8},{4,12},{8,0},{12,4},{16,24},{20,28},{24,16},{28,20},{1,9},{5... | collective-permute-start | bytes 393224 | tf_op jit(solution)/shard_map/ppermute | solution.py:33
  35.9 7.0 %collective-permute-start.13 = (bf16[32,1024]{1,0:T(8,128)(2,1)S(1)}, bf16[32,1024]{1,0:T(8,128)(2,1)S(1)}, u32[]{:S(2)}, u32[]{:S(2)}) collective-permute-start(bf16[32,1024]{1,0:T(8,128)(2,1)S(1)} %leaf_value.1.refs_2_.own_ref), channel_id=1, source_target_pairs={{0,4},{4,0},{8,12},{12,8},{16,20},{20,16},{24,28},{28,24},{1,5},{5... | collective-permute-start | bytes 196616 | tf_op jit(solution)/shard_map/ppermute | solution.py:33
  38.9 12.7 %collective-permute-start.10 = (bf16[1,256,128]{2,1,0:T(8,128)(2,1)S(1)}, bf16[1,256,128]{2,1,0:T(8,128)(2,1)S(1)}, u32[]{:S(2)}, u32[]{:S(2)}) collective-permute-start(bf16[1,256,128]{2,1,0:T(8,128)(2,1)S(1)} %get-tuple-element.31), channel_id=1, source_target_pairs={{0,16},{4,20},{8,24},{12,28},{16,0},{20,4},{24,8},{28,12},{1,17},{... | collective-permute-start | bytes 196616 | tf_op jit(solution)/shard_map/ppermute | solution.py:33
  40.4 6.6 %collective-permute-start.12 = (bf16[2,256,128]{2,1,0:T(8,128)(2,1)S(1)}, bf16[2,256,128]{2,1,0:T(8,128)(2,1)S(1)}, u32[]{:S(2)}, u32[]{:S(2)}) collective-permute-start(bf16[2,256,128]{2,1,0:T(8,128)(2,1)S(1)} %get-tuple-element.33), channel_id=1, source_target_pairs={{0,8},{4,12},{8,0},{12,4},{16,24},{20,28},{24,16},{28,20},{1,9},{5... | collective-permute-start | bytes 393224 | tf_op jit(solution)/shard_map/ppermute | solution.py:33
  47.1 5.9 %collective-permute-start.14 = (bf16[1,256,128]{2,1,0:T(8,128)(2,1)S(1)}, bf16[1,256,128]{2,1,0:T(8,128)(2,1)S(1)}, u32[]{:S(2)}, u32[]{:S(2)}) collective-permute-start(bf16[1,256,128]{2,1,0:T(8,128)(2,1)S(1)} %get-tuple-element.36), channel_id=1, source_target_pairs={{0,16},{4,20},{8,24},{12,28},{16,0},{20,4},{24,8},{28,12},{1,17},{... | collective-permute-start | bytes 196616 | tf_op jit(solution)/shard_map/ppermute | solution.py:33

commit v8 on v7

--- a/solution.py
+++ b/solution.py
@@ -127,7 +127,6 @@
             pltpu.SemaphoreType.DMA,
         ],
         compiler_params=PARAMS,
-        cost_estimate=pl.CostEstimate(flops=int(1.38e+10), transcendentals=0, bytes_accessed=0),
         name="rows",
     )(pos, leaf, pred, lab, w)
 
@@ -171,7 +170,8 @@
         out_ref[:, p * width:(p + 1) * width] = refs[2 * p][0] + refs[2 * p + 1][0].astype(f32)
 
 
-def hist_kernel(codes_ref, own_ref, other_ref, after_ref, out_ref, *, per, odd, bits):
+def hist_kernel(codes_ref, after_ref, *refs, per, odd, bits):
+    parts = len(refs) // 3
     feats = codes_ref.shape[1]
     half = codes_ref.shape[2]
     codes = codes_ref[...].astype(f32).astype(bf16)
@@ -182,47 +182,47 @@
     one = jnp.ones((), bf16)
     zero = jnp.zeros((), bf16)
     total = None
-    for part, ref in ((0, own_ref), (1, other_ref)):
-        hot = jnp.where(codes[part][None] == levels, one, zero).reshape(per * feats, half)
-        term = jnp.dot(hot, ref[...], preferred_element_type=f32)
+    for h in range(2):
+        hot = jnp.where(codes[h][None] == levels, one, zero).reshape(per * feats, half)
+        rows = refs[h * parts:(h + 1) * parts]
+        sketch = jnp.concatenate([r[...] for r in rows], axis=1) if parts > 1 else rows[0][...]
+        term = jnp.dot(hot, sketch, preferred_element_type=f32)
         total = term if total is None else total + term
-    out_ref[0] = total.astype(out_ref.dtype)
-
-
-def hist_pass(codes, own, other, per, blocks, odd, dtype, after):
+    width = refs[-1].shape[2]
+    for p in range(parts):
+        out = refs[2 * parts + p]
+        out[0] = total[:, p * width:(p + 1) * width].astype(out.dtype)
+
+
+def hist_pass(codes, owns, others, per, blocks, odd, dtype, after):
     feats = codes.shape[1]
-    width = own.shape[1]
+    width = owns[0].shape[1]
+    parts = len(owns)
     whole = lambda a: pl.BlockSpec(a.shape, lambda i: (0,) * a.ndim)
     return pl.pallas_call(
         functools.partial(hist_kernel, per=per, odd=odd, bits=blocks.bit_length() - 1),
         grid=(blocks,),
-        in_specs=[whole(codes), whole(own), whole(other), pl.BlockSpec(memory_space=pl.ANY)],
-        out_specs=pl.BlockSpec((1, per * feats, width), lambda i: (i, 0, 0)),
-        out_shape=jax.ShapeDtypeStruct((blocks, per * feats, width), dtype),
+        in_specs=[whole(codes), pl.BlockSpec(memory_space=pl.ANY)] + [whole(a) for a in owns + others],
+        out_specs=[pl.BlockSpec((1, per * feats, width), lambda i: (i, 0, 0))] * parts,
+        out_shape=[jax.ShapeDtypeStruct((blocks, per * feats, width), dtype)] * parts,
         compiler_params=PARAMS,
-        cost_estimate=pl.CostEstimate(flops=int(3.45e+09), transcendentals=0, bytes_accessed=0),
         name="hist_send" if odd else "hist_keep",
-    )(codes, own, other, after)
-
-
-def update_kernel(pos_ref, leaf_ref, own_ref, other_ref, pred_hbm, after_ref, *rest, first):
+    )(codes, after, *owns, *others)
+
+
+def update_kernel(pos_ref, leaf_ref, own_ref, other_ref, pred_ref, after_ref, *rest, first):
     if first:
-        new_hbm, values_hbm, done_ref, pred_buf, new_buf, pred_sem, new_sem, values_buf, values_sem = rest
+        new_hbm, values_hbm, done_ref, new_buf, new_sem, values_buf, values_sem = rest
     else:
-        _, new_hbm, done_ref, pred_buf, new_buf, pred_sem, new_sem = rest
+        _, new_hbm, done_ref, new_buf, new_sem = rest
     side = pos_ref[1]
-    chunks, blk, _ = pred_buf.shape
+    chunks, blk, _ = new_buf.shape
     start = 0 if first else chunks
     half = LEAVES // 2
 
-    def read(i):
-        return pltpu.make_async_copy(pred_hbm.at[pl.ds((start + i) * blk, blk)], pred_buf.at[i], pred_sem.at[i])
-
     def write(i):
         return pltpu.make_async_copy(new_buf.at[i], new_hbm.at[pl.ds((start + i) * blk, blk)], new_sem.at[i])
 
-    for i in range(chunks):
-        read(i).start()
     own, other = own_ref[...], other_ref[...]
     if first:
         low = side == 0
@@ -234,8 +234,8 @@
     for i in range(chunks):
         hot = leaf_hot(leaf_ref, start + i, blk, side * half, shrinkage)
         found = lax.dot_general(hot, table, (((0,), (0,)), ((), ())), preferred_element_type=f32)
-        read(i).wait()
-        new_buf[i] = (pred_buf[i].astype(f32) + found).astype(bf16)
+        pred = pred_ref[pl.ds((start + i) * blk, blk)]
+        new_buf[i] = (pred.astype(f32) + found).astype(bf16)
         write(i).start()
     done_ref[...] = jnp.zeros_like(done_ref)
     if first:
@@ -255,18 +255,15 @@
     done = jax.ShapeDtypeStruct((8, 128), f32)
     return pl.pallas_call(
         functools.partial(update_kernel, first=first),
-        in_specs=[pl.BlockSpec(memory_space=pltpu.SMEM), vmem, vmem, vmem, hbm, hbm] + [hbm] * (not first),
+        in_specs=[pl.BlockSpec(memory_space=pltpu.SMEM), vmem, vmem, vmem, vmem, hbm] + [hbm] * (not first),
         out_specs=[hbm] * (1 + first) + [vmem],
         out_shape=[new, jax.ShapeDtypeStruct((LEAVES, cols), f32), done] if first else [new, done],
         scratch_shapes=[
             pltpu.VMEM((chunks, blk, cols), bf16),
-            pltpu.VMEM((chunks, blk, cols), bf16),
-            pltpu.SemaphoreType.DMA((chunks,)),
             pltpu.SemaphoreType.DMA((chunks,)),
         ] + ([pltpu.VMEM((LEAVES, cols), f32), pltpu.SemaphoreType.DMA] if first else []),
         input_output_aliases={} if first else {6: 0},
         compiler_params=PARAMS,
-        cost_estimate=pl.CostEstimate(flops=int(6.44e+09), transcendentals=0, bytes_accessed=0),
         name="update_first" if first else "update_second",
     )(pos, leaf, own, other, pred, after, *([] if first else [begun]))
 
@@ -335,18 +332,19 @@
         while leaf_state[2] <= n:
             leaf_step()
         if updated is None:
-            updated, leaf_values, after = update_pass(pos, leaf, leaf_state[0], leaf_state[1], pred, after, None)
+            updated, leaf_values, after = update_pass(pos, leaf, leaf_state[0], leaf_state[1], predictions, after, None)
         else:
-            updated, after = update_pass(pos, leaf, leaf_state[0], leaf_state[1], pred, after, updated)
+            updated, after = update_pass(pos, leaf, leaf_state[0], leaf_state[1], predictions, after, updated)
 
     def hist_send(p):
         nonlocal after
-        after = hist_pass(codes, owns[p], others[p], per, n // 2, 1, bf16, after)
+        after, = hist_pass(codes, [owns[p]], [others[p]], per, n // 2, 1, bf16, after)
         backs[p] = swap(after, "rows", n, 1)
 
-    def hist_keep(p):
-        nonlocal after
-        after = heres[p] = hist_pass(codes, owns[p], others[p], per, n // 2, 0, f32, after)
+    def hist_keep():
+        nonlocal after
+        heres[:] = hist_pass(codes, owns, others, per, n // 2, 0, f32, after)
+        after = heres[-1]
 
     def hist_add(p, level):
         nonlocal after
@@ -366,18 +364,16 @@
     feat_add(0)
     hist_send(0)
     feat_add(1)
-    hist_keep(0)
+    hist_send(1)
+    hist_keep()
     leaf_step()
-    hist_send(1)
-    hist_keep(1)
     for level in range(levels):
         hist_add(0, level)
+        if level == levels - 1:
+            update()
+        hist_add(1, level)
         if level == 0:
             leaf_step()
-        if level > 0:
-            hist_add(1, level - 1)
-    update()
-    hist_add(1, levels - 1)
     update()
     histograms = ordered(
         last_kernel, jax.ShapeDtypeStruct((per * feats, width * parts), f32),

time: 53.9 us -> 52.8 us (0.980)
  waiting for transfers between devices: 10 us -> 16.6 us
  Pallas kernels: 20.4 us -> 15.8 us
  starting transfers between devices: 22.4 us -> 19.3 us
    ppermute x15, waiting for transfers between devices: 10 us -> 16.6 us  [swap(): return lax.ppermute(x, axis, [(i, i ^ by) for i in range(size)])]
    pallas_call x2, Pallas kernels: 7.21 us -> 4.07 us  [update_pass(): pl.pallas_call(functools.partial(update_kernel, first=first), in_specs=[p...]
    ppermute x15, starting transfers between devices: 22.4 us -> 19.3 us  [swap(): return lax.ppermute(x, axis, [(i, i ^ by) for i in range(size)])]
    pallas_call x4 -> x3, Pallas kernels: 5.88 us -> 4.45 us  [hist_pass(): pl.pallas_call(functools.partial(hist_kernel, per=per, odd=odd, bits=bloc...]
  transfers between devices with their start and end apart: 15 -> 15, of which waited for: 7 -> 10; matrix products, arithmetic and copies ran while one was open for 0% -> 0% of each run, Pallas kernels for 25% -> 17%
where the time goes in v8:
time: 52.8 us; the launch traced here: 52.6 us
  starting transfers between devices  19.3 us (37%)
  waiting for transfers between devices  16.6 us (31%)
  Pallas kernels  15.8 us (30%)
  between operations  0.8 us (2%)
    ppermute x15, starting transfers between devices, swap(): return lax.ppermute(x, axis, [(i, i ^ by) for i in range(size)])  19.3 us
    ppermute x15, waiting for transfers between devices, swap(): return lax.ppermute(x, axis, [(i, i ^ by) for i in range(size)])  16.6 us
    pallas_call x1, Pallas kernels, rows_pass(): pl.pallas_call(rows_kernel, in_specs=[pl.BlockSpec(memory_space=pltpu.SME...  6.06 us
    pallas_call x3, Pallas kernels, hist_pass(): pl.pallas_call(functools.partial(hist_kernel, per=per, odd=odd, bits=bloc...  4.45 us
    pallas_call x2, Pallas kernels, update_pass(): pl.pallas_call(functools.partial(update_kernel, first=first), in_specs=[p...  4.07 us
    pallas_call x13, Pallas kernels, ordered(): pl.pallas_call(body, in_specs=[pl.BlockSpec(memory_space=pltpu.VMEM)] * l...  1.22 us
  transfers between devices with their start and end apart: 15, of which 10 were waited for; matrix products, arithmetic and copies ran while one was open for 0% of the time, Pallas kernels for 17%

profile of v8, /device:TPU:0, one launch (start us, length us, event | category | flops | bytes accessed | tf_op | source)
XLA Modules:
  0.0 52.6 jit_solution(9738135881369822380)
XLA Ops:
  0.6 0.1 pad_add_fusion.pos_ref
  0.7 0.0 copy-start.2
  0.7 6.1 %rows.1 = (bf16[768,256]{1,0:T(8,128)(2,1)S(1)}, bf16[768,256]{1,0:T(8,128)(2,1)S(1)}, f32[64,1024]{1,0:T(8,128)S(1)}, f32[64,1024]{1,0:T(8,128)S(1)}) custom-call(s32[2]{0:T(128)S(1)} %pad_add_fusion.pos_ref, s32[12,128]{1,0:T(8,128)} %bitcast.7, bf16[1536,1024]{1,0:T(8,128)(2,1)} %pred_ref.3, bf16[1536,1024]{1,0:T(8,128)(2,1)} %lab_hbm.1, ...), custom_call_target="tpu_custom_call" | custom-call | tf_op jit(solution)/shard_map/rows/pallas_call | solution.py:113
  6.8 0.5 collective-permute-start
  7.3 1.3 %collective-permute-done.refs_1_ = bf16[768,256]{1,0:T(8,128)(2,1)S(1)} collective-permute-done((bf16[768,256]{1,0:T(8,128)(2,1)S(1)}, bf16[768,256]{1,0:T(8,128)(2,1)S(1)}, u32[]{:S(2)}, u32[]{:S(2)}) %collective-permute-start) | collective-permute-done | bytes 393248 | tf_op jit(solution)/shard_map/ppermute | solution.py:33
  8.7 3.0 %collective-permute-start.2 = (bf16[768,128]{1,0:T(8,128)(2,1)S(1)}, bf16[768,128]{1,0:T(8,128)(2,1)S(1)}, u32[]{:S(2)}, u32[]{:S(2)}) collective-permute-start(bf16[768,128]{1,0:T(8,128)(2,1)S(1)} %core_add.2.refs_2_.refs_0_), channel_id=1, source_target_pairs={{0,2},{1,3},{2,0},{3,1},{4,6},{5,7},{6,4},{7,5},{8,10},{9,11},{10,... | collective-permute-start | bytes 589832 | tf_op jit(solution)/shard_map/ppermute | solution.py:33
  11.7 1.6 %collective-permute-start.3 = (bf16[64,1024]{1,0:T(8,128)(2,1)S(1)}, bf16[64,1024]{1,0:T(8,128)(2,1)S(1)}, u32[]{:S(2)}, u32[]{:S(2)}) collective-permute-start(bf16[64,1024]{1,0:T(8,128)(2,1)S(1)} %get-tuple-element.29), channel_id=1, source_target_pairs={{0,4},{4,0},{8,12},{12,8},{16,20},{20,16},{24,28},{28,24},{1,5},{5... | collective-permute-start | bytes 393224 | tf_op jit(solution)/shard_map/ppermute | solution.py:33
  13.2 0.0 copy-done.2
  13.3 0.6 %collective-permute-start.1 = (bf16[768,128]{1,0:T(8,128)(2,1)S(1)}, bf16[768,128]{1,0:T(8,128)(2,1)S(1)}, u32[]{:S(2)}, u32[]{:S(2)}) collective-permute-start(bf16[768,128]{1,0:T(8,128)(2,1)S(1)} %core_add.3.refs_2_.refs_0_), channel_id=1, source_target_pairs={{0,2},{1,3},{2,0},{3,1},{4,6},{5,7},{6,4},{7,5},{8,10},{9,11},{10,... | collective-permute-start | bytes 589832 | tf_op jit(solution)/shard_map/ppermute | solution.py:33
  13.9 3.1 %collective-permute-done.3.refs_1_ = bf16[64,1024]{1,0:T(8,128)(2,1)S(1)} collective-permute-done((bf16[64,1024]{1,0:T(8,128)(2,1)S(1)}, bf16[64,1024]{1,0:T(8,128)(2,1)S(1)}, u32[]{:S(2)}, u32[]{:S(2)}) %collective-permute-start.3) | collective-permute-done | bytes 131104 | tf_op jit(solution)/shard_map/ppermute | solution.py:33
  17.0 0.3 collective-permute-done.2.refs_1_
  17.4 0.1 collective-permute-start.4
  17.5 1.4 %collective-permute-done.4.refs_1_.refs_2_ = bf16[768,128]{1,0:T(8,128)(2,1)S(1)} collective-permute-done((bf16[768,128]{1,0:T(8,128)(2,1)S(1)}, bf16[768,128]{1,0:T(8,128)(2,1)S(1)}, u32[]{:S(2)}, u32[]{:S(2)}) %collective-permute-start.4) | collective-permute-done | bytes 196640 | tf_op jit(solution)/shard_map/ppermute | solution.py:33
  18.9 1.5 %hist_send.2.refs_2_ = bf16[4,256,128]{2,1,0:T(8,128)(2,1)S(1)} custom-call(s32[2,8,768]{2,1,0:T(8,128)S(1)} %fusion.codes_ref, bf16[768,128]{1,0:T(8,128)(2,1)S(1)} %feat_add.2.after_ref.refs_0_, bf16[768,128]{1,0:T(8,128)(2,1)S(1)} %feat_add.2.after_ref.refs_0_, bf16[768,128]{1,0:T(8,128)(2,1)S(1)} %collective-permute-done.4.refs_1_.refs_2_), custom_call_target="tpu_custom_call" | custom-call | tf_op jit(solution)/shard_map/hist_send/pallas_call | solution.py:202
  20.4 0.7 %collective-permute-done.1.refs_1_ = bf16[768,128]{1,0:T(8,128)(2,1)S(1)} collective-permute-done((bf16[768,128]{1,0:T(8,128)(2,1)S(1)}, bf16[768,128]{1,0:T(8,128)(2,1)S(1)}, u32[]{:S(2)}, u32[]{:S(2)}) %collective-permute-start.1) | collective-permute-done | bytes 196640 | tf_op jit(solution)/shard_map/ppermute | solution.py:33
  21.1 0.0 copy-start
  21.1 0.0 copy-start.1
  21.1 0.1 collective-permute-start.5
  21.2 1.8 %collective-permute-start.6 = (bf16[4,256,128]{2,1,0:T(8,128)(2,1)S(1)}, bf16[4,256,128]{2,1,0:T(8,128)(2,1)S(1)}, u32[]{:S(2)}, u32[]{:S(2)}) collective-permute-start(bf16[4,256,128]{2,1,0:T(8,128)(2,1)S(1)} %hist_send.2.refs_2_), channel_id=1, source_target_pairs={{0,4},{4,0},{8,12},{12,8},{16,20},{20,16},{24,28},{28,24},{1,5},{5... | collective-permute-start | bytes 786440 | tf_op jit(solution)/shard_map/ppermute | solution.py:33
  23.0 0.0 collective-permute-done.5.refs_1_.refs_3_
  23.0 1.5 %hist_send.3.after_ref = bf16[4,256,128]{2,1,0:T(8,128)(2,1)S(1)} custom-call(s32[2,8,768]{2,1,0:T(8,128)S(1)} %fusion.codes_ref, bf16[768,128]{1,0:T(8,128)(2,1)S(1)} %feat_add.3.after_ref.refs_0_.refs_1_, bf16[768,128]{1,0:T(8,128)(2,1)S(1)} %feat_add.3.after_ref.refs_0_.refs_1_, bf16[768,128]{1,0:T(8,128)(2,1)S(1)} %collective-permute-done.5.refs_1_.refs_3_), custom_call_target="tpu_custom_call" | custom-call | tf_op jit(solution)/shard_map/hist_send/pallas_call | solution.py:202
  24.5 1.4 %collective-permute-start.10 = (bf16[4,256,128]{2,1,0:T(8,128)(2,1)S(1)}, bf16[4,256,128]{2,1,0:T(8,128)(2,1)S(1)}, u32[]{:S(2)}, u32[]{:S(2)}) collective-permute-start(bf16[4,256,128]{2,1,0:T(8,128)(2,1)S(1)} %hist_send.3.after_ref), channel_id=1, source_target_pairs={{0,4},{4,0},{8,12},{12,8},{16,20},{20,16},{24,28},{28,24},{1,5},{5... | collective-permute-start | bytes 786440 | tf_op jit(solution)/shard_map/ppermute | solution.py:33
  25.9 1.6 %collective-permute-start.7 = (bf16[64,1024]{1,0:T(8,128)(2,1)S(1)}, bf16[64,1024]{1,0:T(8,128)(2,1)S(1)}, u32[]{:S(2)}, u32[]{:S(2)}) collective-permute-start(bf16[64,1024]{1,0:T(8,128)(2,1)S(1)} %leaf_add.2.refs_2_.refs_0_), channel_id=1, source_target_pairs={{0,8},{4,12},{8,0},{12,4},{16,24},{20,28},{24,16},{28,20},{1,9},{5... | collective-permute-start | bytes 393224 | tf_op jit(solution)/shard_map/ppermute | solution.py:33
  27.5 1.5 %hist_keep.1 = (f32[4,256,128]{2,1,0:T(8,128)S(1)}, f32[4,256,128]{2,1,0:T(8,128)S(1)}) custom-call(s32[2,8,768]{2,1,0:T(8,128)S(1)} %fusion.codes_ref, bf16[4,256,128]{2,1,0:T(8,128)(2,1)S(1)} %hist_send.3.after_ref, bf16[768,128]{1,0:T(8,128)(2,1)S(1)} %feat_add.2.after_ref.refs_0_, bf16[768,128]{1,0:T(8,128)(2,1)S(1)} %feat_add.3.after_ref.refs_0_.refs_1_, ...), custom_call_target="tpu_custom_call" | custom-call | tf_op jit(solution)/shard_map/hist_keep/pallas_call | solution.py:202
  29.0 2.1 %collective-permute-done.7.refs_1_ = bf16[64,1024]{1,0:T(8,128)(2,1)S(1)} collective-permute-done((bf16[64,1024]{1,0:T(8,128)(2,1)S(1)}, bf16[64,1024]{1,0:T(8,128)(2,1)S(1)}, u32[]{:S(2)}, u32[]{:S(2)}) %collective-permute-start.7) | collective-permute-done | bytes 131104 | tf_op jit(solution)/shard_map/ppermute | solution.py:33
  31.2 2.7 %collective-permute-start.9 = (bf16[64,1024]{1,0:T(8,128)(2,1)S(1)}, bf16[64,1024]{1,0:T(8,128)(2,1)S(1)}, u32[]{:S(2)}, u32[]{:S(2)}) collective-permute-start(bf16[64,1024]{1,0:T(8,128)(2,1)S(1)} %leaf_add.3.refs_2_.refs_0_), channel_id=1, source_target_pairs={{0,16},{4,20},{8,24},{12,28},{16,0},{20,4},{24,8},{28,12},{1,17},{... | collective-permute-start | bytes 393224 | tf_op jit(solution)/shard_map/ppermute | solution.py:33
  33.9 0.0 collective-permute-done.6.refs_1_
  33.9 1.6 %collective-permute-start.8 = (bf16[2,256,128]{2,1,0:T(8,128)(2,1)S(1)}, bf16[2,256,128]{2,1,0:T(8,128)(2,1)S(1)}, u32[]{:S(2)}, u32[]{:S(2)}) collective-permute-start(bf16[2,256,128]{2,1,0:T(8,128)(2,1)S(1)} %get-tuple-element.33), channel_id=1, source_target_pairs={{0,8},{4,12},{8,0},{12,4},{16,24},{20,28},{24,16},{28,20},{1,9},{5... | collective-permute-start | bytes 393224 | tf_op jit(solution)/shard_map/ppermute | solution.py:33
  35.5 0.0 collective-permute-done.10.refs_1_
  35.6 1.9 %collective-permute-start.12 = (bf16[2,256,128]{2,1,0:T(8,128)(2,1)S(1)}, bf16[2,256,128]{2,1,0:T(8,128)(2,1)S(1)}, u32[]{:S(2)}, u32[]{:S(2)}) collective-permute-start(bf16[2,256,128]{2,1,0:T(8,128)(2,1)S(1)} %get-tuple-element.37), channel_id=1, source_target_pairs={{0,8},{4,12},{8,0},{12,4},{16,24},{20,28},{24,16},{28,20},{1,9},{5... | collective-permute-start | bytes 393224 | tf_op jit(solution)/shard_map/ppermute | solution.py:33
  37.5 2.0 %collective-permute-done.9.refs_1_ = bf16[64,1024]{1,0:T(8,128)(2,1)S(1)} collective-permute-done((bf16[64,1024]{1,0:T(8,128)(2,1)S(1)}, bf16[64,1024]{1,0:T(8,128)(2,1)S(1)}, u32[]{:S(2)}, u32[]{:S(2)}) %collective-permute-start.9) | collective-permute-done | bytes 131104 | tf_op jit(solution)/shard_map/ppermute | solution.py:33
  39.5 0.8 %collective-permute-start.13 = (bf16[32,1024]{1,0:T(8,128)(2,1)S(1)}, bf16[32,1024]{1,0:T(8,128)(2,1)S(1)}, u32[]{:S(2)}, u32[]{:S(2)}) collective-permute-start(bf16[32,1024]{1,0:T(8,128)(2,1)S(1)} %leaf_value.1.refs_2_.own_ref), channel_id=1, source_target_pairs={{0,4},{4,0},{8,12},{12,8},{16,20},{20,16},{24,28},{28,24},{1,5},{5... | collective-permute-start | bytes 196616 | tf_op jit(solution)/shard_map/ppermute | solution.py:33
  40.3 0.7 %collective-permute-done.8.refs_1_ = bf16[2,256,128]{2,1,0:T(8,128)(2,1)S(1)} collective-permute-done((bf16[2,256,128]{2,1,0:T(8,128)(2,1)S(1)}, bf16[2,256,128]{2,1,0:T(8,128)(2,1)S(1)}, u32[]{:S(2)}, u32[]{:S(2)}) %collective-permute-start.8) | collective-permute-done | bytes 131104 | tf_op jit(solution)/shard_map/ppermute | solution.py:33
  41.1 0.7 %collective-permute-start.11 = (bf16[1,256,128]{2,1,0:T(8,128)(2,1)S(1)}, bf16[1,256,128]{2,1,0:T(8,128)(2,1)S(1)}, u32[]{:S(2)}, u32[]{:S(2)}) collective-permute-start(bf16[1,256,128]{2,1,0:T(8,128)(2,1)S(1)} %get-tuple-element.36), channel_id=1, source_target_pairs={{0,16},{4,20},{8,24},{12,28},{16,0},{20,4},{24,8},{28,12},{1,17},{... | collective-permute-start | bytes 196616 | tf_op jit(solution)/shard_map/ppermute | solution.py:33
  41.8 2.1 %collective-permute-done.13.other_ref = bf16[32,1024]{1,0:T(8,128)(2,1)S(1)} collective-permute-done((bf16[32,1024]{1,0:T(8,128)(2,1)S(1)}, bf16[32,1024]{1,0:T(8,128)(2,1)S(1)}, u32[]{:S(2)}, u32[]{:S(2)}) %collective-permute-start.13) | collective-permute-done | bytes 65568 | tf_op jit(solution)/shard_map/ppermute | solution.py:33
  43.9 0.0 copy-done
  43.9 0.0 copy-done.1
  43.9 2.0 %update_first.1 = (bf16[1536,1024]{1,0:T(8,128)(2,1)}, f32[64,1024]{1,0:T(8,128)}, f32[8,128]{1,0:T(8,128)S(1)}) custom-call(s32[2]{0:T(128)S(1)} %pad_add_fusion.pos_ref, s32[12,128]{1,0:T(8,128)S(1)} %bitcast.8, bf16[32,1024]{1,0:T(8,128)(2,1)S(1)} %leaf_value.1.refs_2_.own_ref, bf16[32,1024]{1,0:T(8,128)(2,1)S(1)} %collective-permute-done.13.other_ref, ...), custom_call_target="tpu_custom_call" | custom-call | tf_op jit(solution)/shard_map/update_first/pallas_call | solution.py:256
  45.9 0.0 collective-permute-done.12.refs_1_
  46.0 1.1 %collective-permute-start.14 = (bf16[1,256,128]{2,1,0:T(8,128)(2,1)S(1)}, bf16[1,256,128]{2,1,0:T(8,128)(2,1)S(1)}, u32[]{:S(2)}, u32[]{:S(2)}) collective-permute-start(bf16[1,256,128]{2,1,0:T(8,128)(2,1)S(1)} %get-tuple-element.40), channel_id=1, source_target_pairs={{0,16},{4,20},{8,24},{12,28},{16,0},{20,4},{24,8},{28,12},{1,17},{... | collective-permute-start | bytes 196616 | tf_op jit(solution)/shard_map/ppermute | solution.py:33
  47.1 2.0 %update_second.1 = (bf16[1536,1024]{1,0:T(8,128)(2,1)}, f32[8,128]{1,0:T(8,128)S(1)}) custom-call(s32[2]{0:T(128)S(1)} %pad_add_fusion.pos_ref, s32[12,128]{1,0:T(8,128)S(1)} %bitcast.9, bf16[32,1024]{1,0:T(8,128)(2,1)S(1)} %leaf_value.1.refs_2_.own_ref, bf16[32,1024]{1,0:T(8,128)(2,1)S(1)} %collective-permute-done.13.other_ref, ...), custom_call_target="tpu_custom_call", output_to_operand_aliasing={{0}: (6, {})} | custom-call | tf_op jit(solution)/shard_map/update_second/pallas_call | solution.py:256
  49.1 0.0 collective-permute-done.11.refs_1_
  49.2 2.7 %collective-permute-done.14.refs_3_ = bf16[1,256,128]{2,1,0:T(8,128)(2,1)S(1)} collective-permute-done((bf16[1,256,128]{2,1,0:T(8,128)(2,1)S(1)}, bf16[1,256,128]{2,1,0:T(8,128)(2,1)S(1)}, u32[]{:S(2)}, u32[]{:S(2)}) %collective-permute-start.14) | collective-permute-done | bytes 65568 | tf_op jit(solution)/shard_map/ppermute | solution.py:33
  51.9 0.7 %last_add.1 = f32[256,256]{1,0:T(8,128)} custom-call(f32[1,256,128]{2,1,0:T(8,128)S(1)} %get-tuple-element.35.after_ref.refs_0_, bf16[1,256,128]{2,1,0:T(8,128)(2,1)S(1)} %collective-permute-done.11.refs_1_, f32[1,256,128]{2,1,0:T(8,128)S(1)} %get-tuple-element.39.after_ref.refs_2_, bf16[1,256,128]{2,1,0:T(8,128)(2,1)S(1)} %collective-permute-done.14.refs_3_, ...), custom_call_target="tpu_custom_call" | custom-call | tf_op jit(solution)/shard_map/last_add/pallas_call | solution.py:41
  (14 shorter events, 0.5 us)
Async XLA Ops:
  0.7 12.5 %copy-start.2 = (s32[8,1536]{1,0:T(8,128)S(1)}, s32[8,1536]{1,0:T(8,128)}, u32[]{:S(2)}) copy-start(s32[8,1536]{1,0:T(8,128)} %param.7) | copy-start | bytes 147460
  6.8 1.9 %collective-permute-start = (bf16[768,256]{1,0:T(8,128)(2,1)S(1)}, bf16[768,256]{1,0:T(8,128)(2,1)S(1)}, u32[]{:S(2)}, u32[]{:S(2)}) collective-permute-start(bf16[768,256]{1,0:T(8,128)(2,1)S(1)} %get-tuple-element.25), channel_id=1, source_target_pairs={{0,1},{1,0},{2,3},{3,2},{4,5},{5,4},{6,7},{7,6},{8,9},{9,8},{10,11... | collective-permute-start | bytes 1179656 | tf_op jit(solution)/shard_map/ppermute | solution.py:33
  8.7 8.6 %collective-permute-start.2 = (bf16[768,128]{1,0:T(8,128)(2,1)S(1)}, bf16[768,128]{1,0:T(8,128)(2,1)S(1)}, u32[]{:S(2)}, u32[]{:S(2)}) collective-permute-start(bf16[768,128]{1,0:T(8,128)(2,1)S(1)} %core_add.2.refs_2_.refs_0_), channel_id=1, source_target_pairs={{0,2},{1,3},{2,0},{3,1},{4,6},{5,7},{6,4},{7,5},{8,10},{9,11},{10,... | collective-permute-start | bytes 589832 | tf_op jit(solution)/shard_map/ppermute | solution.py:33
  11.7 5.3 %collective-permute-start.3 = (bf16[64,1024]{1,0:T(8,128)(2,1)S(1)}, bf16[64,1024]{1,0:T(8,128)(2,1)S(1)}, u32[]{:S(2)}, u32[]{:S(2)}) collective-permute-start(bf16[64,1024]{1,0:T(8,128)(2,1)S(1)} %get-tuple-element.29), channel_id=1, source_target_pairs={{0,4},{4,0},{8,12},{12,8},{16,20},{20,16},{24,28},{28,24},{1,5},{5... | collective-permute-start | bytes 393224 | tf_op jit(solution)/shard_map/ppermute | solution.py:33
  13.3 7.8 %collective-permute-start.1 = (bf16[768,128]{1,0:T(8,128)(2,1)S(1)}, bf16[768,128]{1,0:T(8,128)(2,1)S(1)}, u32[]{:S(2)}, u32[]{:S(2)}) collective-permute-start(bf16[768,128]{1,0:T(8,128)(2,1)S(1)} %core_add.3.refs_2_.refs_0_), channel_id=1, source_target_pairs={{0,2},{1,3},{2,0},{3,1},{4,6},{5,7},{6,4},{7,5},{8,10},{9,11},{10,... | collective-permute-start | bytes 589832 | tf_op jit(solution)/shard_map/ppermute | solution.py:33
  17.4 1.5 %collective-permute-start.4 = (bf16[768,128]{1,0:T(8,128)(2,1)S(1)}, bf16[768,128]{1,0:T(8,128)(2,1)S(1)}, u32[]{:S(2)}, u32[]{:S(2)}) collective-permute-start(bf16[768,128]{1,0:T(8,128)(2,1)S(1)} %feat_add.2.after_ref.refs_0_), channel_id=1, source_target_pairs={{0,1},{1,0},{2,3},{3,2},{4,5},{5,4},{6,7},{7,6},{8,9},{9,8},{10,11... | collective-permute-start | bytes 589832 | tf_op jit(solution)/shard_map/ppermute | solution.py:33
  21.1 22.7 %copy-start = (bf16[1536,1024]{1,0:T(8,128)(2,1)S(1)}, bf16[1536,1024]{1,0:T(8,128)(2,1)}, u32[]{:S(2)}) copy-start(bf16[1536,1024]{1,0:T(8,128)(2,1)} %pred_ref.3) | copy-start | bytes 9437188
  21.1 22.7 %copy-start.1 = (s32[1536]{0:T(1024)S(1)}, s32[1536]{0:T(1024)}, u32[]{:S(2)}) copy-start(s32[1536]{0:T(1024)} %param.8) | copy-start | bytes 18436
  21.1 1.9 %collective-permute-start.5 = (bf16[768,128]{1,0:T(8,128)(2,1)S(1)}, bf16[768,128]{1,0:T(8,128)(2,1)S(1)}, u32[]{:S(2)}, u32[]{:S(2)}) collective-permute-start(bf16[768,128]{1,0:T(8,128)(2,1)S(1)} %feat_add.3.after_ref.refs_0_.refs_1_), channel_id=1, source_target_pairs={{0,1},{1,0},{2,3},{3,2},{4,5},{5,4},{6,7},{7,6},{8,9},{9,8},{10,11... | collective-permute-start | bytes 589832 | tf_op jit(solution)/shard_map/ppermute | solution.py:33
  21.2 12.6 %collective-permute-start.6 = (bf16[4,256,128]{2,1,0:T(8,128)(2,1)S(1)}, bf16[4,256,128]{2,1,0:T(8,128)(2,1)S(1)}, u32[]{:S(2)}, u32[]{:S(2)}) collective-permute-start(bf16[4,256,128]{2,1,0:T(8,128)(2,1)S(1)} %hist_send.2.refs_2_), channel_id=1, source_target_pairs={{0,4},{4,0},{8,12},{12,8},{16,20},{20,16},{24,28},{28,24},{1,5},{5... | collective-permute-start | bytes 786440 | tf_op jit(solution)/shard_map/ppermute | solution.py:33
  24.5 11.1 %collective-permute-start.10 = (bf16[4,256,128]{2,1,0:T(8,128)(2,1)S(1)}, bf16[4,256,128]{2,1,0:T(8,128)(2,1)S(1)}, u32[]{:S(2)}, u32[]{:S(2)}) collective-permute-start(bf16[4,256,128]{2,1,0:T(8,128)(2,1)S(1)} %hist_send.3.after_ref), channel_id=1, source_target_pairs={{0,4},{4,0},{8,12},{12,8},{16,20},{20,16},{24,28},{28,24},{1,5},{5... | collective-permute-start | bytes 786440 | tf_op jit(solution)/shard_map/ppermute | solution.py:33
  25.9 5.3 %collective-permute-start.7 = (bf16[64,1024]{1,0:T(8,128)(2,1)S(1)}, bf16[64,1024]{1,0:T(8,128)(2,1)S(1)}, u32[]{:S(2)}, u32[]{:S(2)}) collective-permute-start(bf16[64,1024]{1,0:T(8,128)(2,1)S(1)} %leaf_add.2.refs_2_.refs_0_), channel_id=1, source_target_pairs={{0,8},{4,12},{8,0},{12,4},{16,24},{20,28},{24,16},{28,20},{1,9},{5... | collective-permute-start | bytes 393224 | tf_op jit(solution)/shard_map/ppermute | solution.py:33
  31.2 8.3 %collective-permute-start.9 = (bf16[64,1024]{1,0:T(8,128)(2,1)S(1)}, bf16[64,1024]{1,0:T(8,128)(2,1)S(1)}, u32[]{:S(2)}, u32[]{:S(2)}) collective-permute-start(bf16[64,1024]{1,0:T(8,128)(2,1)S(1)} %leaf_add.3.refs_2_.refs_0_), channel_id=1, source_target_pairs={{0,16},{4,20},{8,24},{12,28},{16,0},{20,4},{24,8},{28,12},{1,17},{... | collective-permute-start | bytes 393224 | tf_op jit(solution)/shard_map/ppermute | solution.py:33
  33.9 7.1 %collective-permute-start.8 = (bf16[2,256,128]{2,1,0:T(8,128)(2,1)S(1)}, bf16[2,256,128]{2,1,0:T(8,128)(2,1)S(1)}, u32[]{:S(2)}, u32[]{:S(2)}) collective-permute-start(bf16[2,256,128]{2,1,0:T(8,128)(2,1)S(1)} %get-tuple-element.33), channel_id=1, source_target_pairs={{0,8},{4,12},{8,0},{12,4},{16,24},{20,28},{24,16},{28,20},{1,9},{5... | collective-permute-start | bytes 393224 | tf_op jit(solution)/shard_map/ppermute | solution.py:33
  35.6 10.3 %collective-permute-start.12 = (bf16[2,256,128]{2,1,0:T(8,128)(2,1)S(1)}, bf16[2,256,128]{2,1,0:T(8,128)(2,1)S(1)}, u32[]{:S(2)}, u32[]{:S(2)}) collective-permute-start(bf16[2,256,128]{2,1,0:T(8,128)(2,1)S(1)} %get-tuple-element.37), channel_id=1, source_target_pairs={{0,8},{4,12},{8,0},{12,4},{16,24},{20,28},{24,16},{28,20},{1,9},{5... | collective-permute-start | bytes 393224 | tf_op jit(solution)/shard_map/ppermute | solution.py:33
  39.5 4.3 %collective-permute-start.13 = (bf16[32,1024]{1,0:T(8,128)(2,1)S(1)}, bf16[32,1024]{1,0:T(8,128)(2,1)S(1)}, u32[]{:S(2)}, u32[]{:S(2)}) collective-permute-start(bf16[32,1024]{1,0:T(8,128)(2,1)S(1)} %leaf_value.1.refs_2_.own_ref), channel_id=1, source_target_pairs={{0,4},{4,0},{8,12},{12,8},{16,20},{20,16},{24,28},{28,24},{1,5},{5... | collective-permute-start | bytes 196616 | tf_op jit(solution)/shard_map/ppermute | solution.py:33
  41.1 8.1 %collective-permute-start.11 = (bf16[1,256,128]{2,1,0:T(8,128)(2,1)S(1)}, bf16[1,256,128]{2,1,0:T(8,128)(2,1)S(1)}, u32[]{:S(2)}, u32[]{:S(2)}) collective-permute-start(bf16[1,256,128]{2,1,0:T(8,128)(2,1)S(1)} %get-tuple-element.36), channel_id=1, source_target_pairs={{0,16},{4,20},{8,24},{12,28},{16,0},{20,4},{24,8},{28,12},{1,17},{... | collective-permute-start | bytes 196616 | tf_op jit(solution)/shard_map/ppermute | solution.py:33
  46.0 5.9 %collective-permute-start.14 = (bf16[1,256,128]{2,1,0:T(8,128)(2,1)S(1)}, bf16[1,256,128]{2,1,0:T(8,128)(2,1)S(1)}, u32[]{:S(2)}, u32[]{:S(2)}) collective-permute-start(bf16[1,256,128]{2,1,0:T(8,128)(2,1)S(1)} %get-tuple-element.40), channel_id=1, source_target_pairs={{0,16},{4,20},{8,24},{12,28},{16,0},{20,4},{24,8},{28,12},{1,17},{... | collective-permute-start | bytes 196616 | tf_op jit(solution)/shard_map/ppermute | solution.py:33

commit v9 on v8

--- a/solution.py
+++ b/solution.py
@@ -26,6 +26,10 @@
     return rows
 
 
+def cost(gflop):
+    return pl.CostEstimate(flops=int(gflop * 1e9), transcendentals=0, bytes_accessed=0)
+
+
 PARAMS = pltpu.CompilerParams(vmem_limit_bytes=VMEM_LIMIT)
 
 
@@ -33,7 +37,7 @@
     return lax.ppermute(x, axis, [(i, i ^ by) for i in range(size)])
 
 
-def ordered(kernel, out_shape, args, after, name):
+def ordered(kernel, out_shape, args, after, name, gflop=0):
     def body(*refs):
         kernel(*refs[:len(args)], *refs[len(args) + 1:])
 
@@ -44,6 +48,7 @@
         out_specs=[pl.BlockSpec(memory_space=pltpu.VMEM)] * len(out_shape)
         if many else pl.BlockSpec(memory_space=pltpu.VMEM),
         out_shape=out_shape,
+        cost_estimate=cost(gflop),
         compiler_params=PARAMS,
         name=name,
     )(*args, after)
@@ -194,7 +199,7 @@
         out[0] = total[:, p * width:(p + 1) * width].astype(out.dtype)
 
 
-def hist_pass(codes, owns, others, per, blocks, odd, dtype, after):
+def hist_pass(codes, owns, others, per, blocks, odd, dtype, after, gflop):
     feats = codes.shape[1]
     width = owns[0].shape[1]
     parts = len(owns)
@@ -205,6 +210,7 @@
         in_specs=[whole(codes), pl.BlockSpec(memory_space=pl.ANY)] + [whole(a) for a in owns + others],
         out_specs=[pl.BlockSpec((1, per * feats, width), lambda i: (i, 0, 0))] * parts,
         out_shape=[jax.ShapeDtypeStruct((blocks, per * feats, width), dtype)] * parts,
+        cost_estimate=cost(gflop),
         compiler_params=PARAMS,
         name="hist_send" if odd else "hist_keep",
     )(codes, after, *owns, *others)
@@ -263,6 +269,7 @@
             pltpu.SemaphoreType.DMA((chunks,)),
         ] + ([pltpu.VMEM((LEAVES, cols), f32), pltpu.SemaphoreType.DMA] if first else []),
         input_output_aliases={} if first else {6: 0},
+        cost_estimate=cost(3.0),
         compiler_params=PARAMS,
         name="update_first" if first else "update_second",
     )(pos, leaf, own, other, pred, after, *([] if first else [begun]))
@@ -307,7 +314,7 @@
         nonlocal after
         own = pair[p]
         for recv in crossed[p]:
-            after = own = ordered(add_kernel, sketch16, [own, recv], after, "feat_add")
+            after = own = ordered(add_kernel, sketch16, [own, recv], after, "feat_add", (0, 0.0)[p])
         owns[p] = own
         others[p] = swap(own, "feat", nf, 1)
 
@@ -338,12 +345,12 @@
 
     def hist_send(p):
         nonlocal after
-        after, = hist_pass(codes, [owns[p]], [others[p]], per, n // 2, 1, bf16, after)
+        after, = hist_pass(codes, [owns[p]], [others[p]], per, n // 2, 1, bf16, after, (2.0, 0.0)[p])
         backs[p] = swap(after, "rows", n, 1)
 
     def hist_keep():
         nonlocal after
-        heres[:] = hist_pass(codes, owns, others, per, n // 2, 0, f32, after)
+        heres[:] = hist_pass(codes, owns, others, per, n // 2, 0, f32, after, 0.0)
         after = heres[-1]
 
     def hist_add(p, level):
@@ -363,17 +370,18 @@
     leaf_step()
     feat_add(0)
     hist_send(0)
+    leaf_step()
     feat_add(1)
     hist_send(1)
     hist_keep()
     leaf_step()
-    for level in range(levels):
+    hist_add(0, 0)
+    hist_add(1, 0)
+    for level in range(1, levels):
         hist_add(0, level)
         if level == levels - 1:
             update()
         hist_add(1, level)
-        if level == 0:
-            leaf_step()
     update()
     histograms = ordered(
         last_kernel, jax.ShapeDtypeStruct((per * feats, width * parts), f32),

time: 52.8 us -> 51.5 us (0.975)
  waiting for transfers between devices: 16.6 us -> 13.9 us
  starting transfers between devices: 19.3 us -> 20.8 us
    ppermute x15, waiting for transfers between devices: 16.6 us -> 13.9 us  [swap(): return lax.ppermute(x, axis, [(i, i ^ by) for i in range(size)])]
    ppermute x15, starting transfers between devices: 19.3 us -> 20.8 us  [swap(): return lax.ppermute(x, axis, [(i, i ^ by) for i in range(size)])]
  transfers between devices with their start and end apart: 15 -> 15, of which waited for: 10 -> 7; matrix products, arithmetic and copies ran while one was open for 0% -> 0% of each run, Pallas kernels for 17% -> 17%
where the time goes in v9:
time: 51.5 us; the launch traced here: 51.4 us
  starting transfers between devices  20.8 us (40%)
  Pallas kernels  15.8 us (31%)
  waiting for transfers between devices  13.9 us (27%)
  between operations  0.83 us (2%)
    ppermute x15, starting transfers between devices, swap(): return lax.ppermute(x, axis, [(i, i ^ by) for i in range(size)])  20.8 us
    ppermute x15, waiting for transfers between devices, swap(): return lax.ppermute(x, axis, [(i, i ^ by) for i in range(size)])  13.9 us
    pallas_call x1, Pallas kernels, rows_pass(): pl.pallas_call(rows_kernel, in_specs=[pl.BlockSpec(memory_space=pltpu.SME...  6.06 us
    pallas_call x3, Pallas kernels, hist_pass(): pl.pallas_call(functools.partial(hist_kernel, per=per, odd=odd, bits=bloc...  4.46 us
    pallas_call x2, Pallas kernels, update_pass(): pl.pallas_call(functools.partial(update_kernel, first=first), in_specs=[p...  4.07 us
    pallas_call x13, Pallas kernels, ordered(): pl.pallas_call(body, in_specs=[pl.BlockSpec(memory_space=pltpu.VMEM)] * l...  1.21 us
  transfers between devices with their start and end apart: 15, of which 7 were waited for; matrix products, arithmetic and copies ran while one was open for 0% of the time, Pallas kernels for 17%

profile of v9, /device:TPU:0, one launch (start us, length us, event | category | flops | bytes accessed | tf_op | source)
XLA Modules:
  0.0 51.4 jit_solution(6563202522761227126)
XLA Ops:
  0.6 0.1 pad_add_fusion.pos_ref
  0.7 0.0 copy-start.2
  0.7 6.1 %rows.1 = (bf16[768,256]{1,0:T(8,128)(2,1)S(1)}, bf16[768,256]{1,0:T(8,128)(2,1)S(1)}, f32[64,1024]{1,0:T(8,128)S(1)}, f32[64,1024]{1,0:T(8,128)S(1)}) custom-call(s32[2]{0:T(128)S(1)} %pad_add_fusion.pos_ref, s32[12,128]{1,0:T(8,128)} %bitcast.7, bf16[1536,1024]{1,0:T(8,128)(2,1)} %pred_ref.3, bf16[1536,1024]{1,0:T(8,128)(2,1)} %lab_hbm.1, ...), custom_call_target="tpu_custom_call" | custom-call | tf_op jit(solution)/shard_map/rows/pallas_call | solution.py:118
  6.8 0.5 %collective-permute-start = (bf16[768,256]{1,0:T(8,128)(2,1)S(1)}, bf16[768,256]{1,0:T(8,128)(2,1)S(1)}, u32[]{:S(2)}, u32[]{:S(2)}) collective-permute-start(bf16[768,256]{1,0:T(8,128)(2,1)S(1)} %get-tuple-element.25), channel_id=1, source_target_pairs={{0,1},{1,0},{2,3},{3,2},{4,5},{5,4},{6,7},{7,6},{8,9},{9,8},{10,11... | collective-permute-start | bytes 1179656 | tf_op jit(solution)/shard_map/ppermute | solution.py:37
  7.3 1.3 %collective-permute-done.refs_1_ = bf16[768,256]{1,0:T(8,128)(2,1)S(1)} collective-permute-done((bf16[768,256]{1,0:T(8,128)(2,1)S(1)}, bf16[768,256]{1,0:T(8,128)(2,1)S(1)}, u32[]{:S(2)}, u32[]{:S(2)}) %collective-permute-start) | collective-permute-done | bytes 393248 | tf_op jit(solution)/shard_map/ppermute | solution.py:37
  8.7 3.0 %collective-permute-start.4 = (bf16[768,128]{1,0:T(8,128)(2,1)S(1)}, bf16[768,128]{1,0:T(8,128)(2,1)S(1)}, u32[]{:S(2)}, u32[]{:S(2)}) collective-permute-start(bf16[768,128]{1,0:T(8,128)(2,1)S(1)} %core_add.2.refs_2_.refs_0_), channel_id=1, source_target_pairs={{0,2},{1,3},{2,0},{3,1},{4,6},{5,7},{6,4},{7,5},{8,10},{9,11},{10,... | collective-permute-start | bytes 589832 | tf_op jit(solution)/shard_map/ppermute | solution.py:37
  11.7 1.6 %collective-permute-start.2 = (bf16[64,1024]{1,0:T(8,128)(2,1)S(1)}, bf16[64,1024]{1,0:T(8,128)(2,1)S(1)}, u32[]{:S(2)}, u32[]{:S(2)}) collective-permute-start(bf16[64,1024]{1,0:T(8,128)(2,1)S(1)} %get-tuple-element.29), channel_id=1, source_target_pairs={{0,4},{4,0},{8,12},{12,8},{16,20},{20,16},{24,28},{28,24},{1,5},{5... | collective-permute-start | bytes 393224 | tf_op jit(solution)/shard_map/ppermute | solution.py:37
  13.2 0.0 copy-done.2
  13.3 0.6 %collective-permute-start.1 = (bf16[768,128]{1,0:T(8,128)(2,1)S(1)}, bf16[768,128]{1,0:T(8,128)(2,1)S(1)}, u32[]{:S(2)}, u32[]{:S(2)}) collective-permute-start(bf16[768,128]{1,0:T(8,128)(2,1)S(1)} %core_add.3.refs_2_.refs_0_), channel_id=1, source_target_pairs={{0,2},{1,3},{2,0},{3,1},{4,6},{5,7},{6,4},{7,5},{8,10},{9,11},{10,... | collective-permute-start | bytes 589832 | tf_op jit(solution)/shard_map/ppermute | solution.py:37
  13.9 3.1 %collective-permute-done.2.refs_1_ = bf16[64,1024]{1,0:T(8,128)(2,1)S(1)} collective-permute-done((bf16[64,1024]{1,0:T(8,128)(2,1)S(1)}, bf16[64,1024]{1,0:T(8,128)(2,1)S(1)}, u32[]{:S(2)}, u32[]{:S(2)}) %collective-permute-start.2) | collective-permute-done | bytes 131104 | tf_op jit(solution)/shard_map/ppermute | solution.py:37
  17.0 0.3 collective-permute-done.4.refs_1_
  17.4 0.1 collective-permute-start.5
  17.5 2.2 %collective-permute-start.3 = (bf16[64,1024]{1,0:T(8,128)(2,1)S(1)}, bf16[64,1024]{1,0:T(8,128)(2,1)S(1)}, u32[]{:S(2)}, u32[]{:S(2)}) collective-permute-start(bf16[64,1024]{1,0:T(8,128)(2,1)S(1)} %leaf_add.2.refs_2_.refs_0_), channel_id=1, source_target_pairs={{0,8},{4,12},{8,0},{12,4},{16,24},{20,28},{24,16},{28,20},{1,9},{5... | collective-permute-start | bytes 393224 | tf_op jit(solution)/shard_map/ppermute | solution.py:37
  19.7 0.0 collective-permute-done.5.refs_1_.refs_2_
  19.7 1.5 %hist_send.2.refs_2_ = bf16[4,256,128]{2,1,0:T(8,128)(2,1)S(1)} custom-call(s32[2,8,768]{2,1,0:T(8,128)S(1)} %fusion.codes_ref, bf16[768,128]{1,0:T(8,128)(2,1)S(1)} %feat_add.2.after_ref.refs_0_, bf16[768,128]{1,0:T(8,128)(2,1)S(1)} %feat_add.2.after_ref.refs_0_, bf16[768,128]{1,0:T(8,128)(2,1)S(1)} %collective-permute-done.5.refs_1_.refs_2_), custom_call_target="tpu_custom_call" | custom-call | flops 2000000000 | tf_op jit(solution)/shard_map/hist_send/pallas_call | solution.py:207
  21.1 2.6 %collective-permute-done.3.refs_1_ = bf16[64,1024]{1,0:T(8,128)(2,1)S(1)} collective-permute-done((bf16[64,1024]{1,0:T(8,128)(2,1)S(1)}, bf16[64,1024]{1,0:T(8,128)(2,1)S(1)}, u32[]{:S(2)}, u32[]{:S(2)}) %collective-permute-start.3) | collective-permute-done | bytes 131104 | tf_op jit(solution)/shard_map/ppermute | solution.py:37
  23.8 0.0 copy-start
  23.8 0.0 copy-start.1
  23.8 0.0 collective-permute-done.1.refs_1_
  23.9 0.1 collective-permute-start.6
  24.0 1.7 %collective-permute-start.7 = (bf16[4,256,128]{2,1,0:T(8,128)(2,1)S(1)}, bf16[4,256,128]{2,1,0:T(8,128)(2,1)S(1)}, u32[]{:S(2)}, u32[]{:S(2)}) collective-permute-start(bf16[4,256,128]{2,1,0:T(8,128)(2,1)S(1)} %hist_send.2.refs_2_), channel_id=1, source_target_pairs={{0,4},{4,0},{8,12},{12,8},{16,20},{20,16},{24,28},{28,24},{1,5},{5... | collective-permute-start | bytes 786440 | tf_op jit(solution)/shard_map/ppermute | solution.py:37
  25.7 2.6 %collective-permute-start.8 = (bf16[64,1024]{1,0:T(8,128)(2,1)S(1)}, bf16[64,1024]{1,0:T(8,128)(2,1)S(1)}, u32[]{:S(2)}, u32[]{:S(2)}) collective-permute-start(bf16[64,1024]{1,0:T(8,128)(2,1)S(1)} %leaf_add.3.refs_2_.refs_0_), channel_id=1, source_target_pairs={{0,16},{4,20},{8,24},{12,28},{16,0},{20,4},{24,8},{28,12},{1,17},{... | collective-permute-start | bytes 393224 | tf_op jit(solution)/shard_map/ppermute | solution.py:37
  28.3 0.0 collective-permute-done.6.refs_1_.refs_3_
  28.3 1.5 %hist_send.3.after_ref = bf16[4,256,128]{2,1,0:T(8,128)(2,1)S(1)} custom-call(s32[2,8,768]{2,1,0:T(8,128)S(1)} %fusion.codes_ref, bf16[768,128]{1,0:T(8,128)(2,1)S(1)} %feat_add.3.after_ref.refs_0_.refs_1_, bf16[768,128]{1,0:T(8,128)(2,1)S(1)} %feat_add.3.after_ref.refs_0_.refs_1_, bf16[768,128]{1,0:T(8,128)(2,1)S(1)} %collective-permute-done.6.refs_1_.refs_3_), custom_call_target="tpu_custom_call" | custom-call | tf_op jit(solution)/shard_map/hist_send/pallas_call | solution.py:207
  29.8 0.6 %collective-permute-start.10 = (bf16[4,256,128]{2,1,0:T(8,128)(2,1)S(1)}, bf16[4,256,128]{2,1,0:T(8,128)(2,1)S(1)}, u32[]{:S(2)}, u32[]{:S(2)}) collective-permute-start(bf16[4,256,128]{2,1,0:T(8,128)(2,1)S(1)} %hist_send.3.after_ref), channel_id=1, source_target_pairs={{0,4},{4,0},{8,12},{12,8},{16,20},{20,16},{24,28},{28,24},{1,5},{5... | collective-permute-start | bytes 786440 | tf_op jit(solution)/shard_map/ppermute | solution.py:37
  30.4 1.5 %hist_keep.1 = (f32[4,256,128]{2,1,0:T(8,128)S(1)}, f32[4,256,128]{2,1,0:T(8,128)S(1)}) custom-call(s32[2,8,768]{2,1,0:T(8,128)S(1)} %fusion.codes_ref, bf16[4,256,128]{2,1,0:T(8,128)(2,1)S(1)} %hist_send.3.after_ref, bf16[768,128]{1,0:T(8,128)(2,1)S(1)} %feat_add.2.after_ref.refs_0_, bf16[768,128]{1,0:T(8,128)(2,1)S(1)} %feat_add.3.after_ref.refs_0_.refs_1_, ...), custom_call_target="tpu_custom_call" | custom-call | tf_op jit(solution)/shard_map/hist_keep/pallas_call | solution.py:207
  31.9 3.1 %collective-permute-done.8.refs_1_ = bf16[64,1024]{1,0:T(8,128)(2,1)S(1)} collective-permute-done((bf16[64,1024]{1,0:T(8,128)(2,1)S(1)}, bf16[64,1024]{1,0:T(8,128)(2,1)S(1)}, u32[]{:S(2)}, u32[]{:S(2)}) %collective-permute-start.8) | collective-permute-done | bytes 131104 | tf_op jit(solution)/shard_map/ppermute | solution.py:37
  35.0 0.0 collective-permute-done.7.refs_1_
  35.1 0.8 %collective-permute-start.9 = (bf16[2,256,128]{2,1,0:T(8,128)(2,1)S(1)}, bf16[2,256,128]{2,1,0:T(8,128)(2,1)S(1)}, u32[]{:S(2)}, u32[]{:S(2)}) collective-permute-start(bf16[2,256,128]{2,1,0:T(8,128)(2,1)S(1)} %get-tuple-element.33), channel_id=1, source_target_pairs={{0,8},{4,12},{8,0},{12,4},{16,24},{20,28},{24,16},{28,20},{1,9},{5... | collective-permute-start | bytes 393224 | tf_op jit(solution)/shard_map/ppermute | solution.py:37
  35.8 0.7 %collective-permute-start.13 = (bf16[32,1024]{1,0:T(8,128)(2,1)S(1)}, bf16[32,1024]{1,0:T(8,128)(2,1)S(1)}, u32[]{:S(2)}, u32[]{:S(2)}) collective-permute-start(bf16[32,1024]{1,0:T(8,128)(2,1)S(1)} %leaf_value.1.refs_2_.own_ref), channel_id=1, source_target_pairs={{0,4},{4,0},{8,12},{12,8},{16,20},{20,16},{24,28},{28,24},{1,5},{5... | collective-permute-start | bytes 196616 | tf_op jit(solution)/shard_map/ppermute | solution.py:37
  36.5 1.8 %collective-permute-done.10.refs_1_ = bf16[4,256,128]{2,1,0:T(8,128)(2,1)S(1)} collective-permute-done((bf16[4,256,128]{2,1,0:T(8,128)(2,1)S(1)}, bf16[4,256,128]{2,1,0:T(8,128)(2,1)S(1)}, u32[]{:S(2)}, u32[]{:S(2)}) %collective-permute-start.10) | collective-permute-done | bytes 262176 | tf_op jit(solution)/shard_map/ppermute | solution.py:37
  38.4 2.4 %collective-permute-start.12 = (bf16[2,256,128]{2,1,0:T(8,128)(2,1)S(1)}, bf16[2,256,128]{2,1,0:T(8,128)(2,1)S(1)}, u32[]{:S(2)}, u32[]{:S(2)}) collective-permute-start(bf16[2,256,128]{2,1,0:T(8,128)(2,1)S(1)} %get-tuple-element.37), channel_id=1, source_target_pairs={{0,8},{4,12},{8,0},{12,4},{16,24},{20,28},{24,16},{28,20},{1,9},{5... | collective-permute-start | bytes 393224 | tf_op jit(solution)/shard_map/ppermute | solution.py:37
  40.8 0.0 collective-permute-done.9.refs_1_
  40.8 2.5 %collective-permute-start.11 = (bf16[1,256,128]{2,1,0:T(8,128)(2,1)S(1)}, bf16[1,256,128]{2,1,0:T(8,128)(2,1)S(1)}, u32[]{:S(2)}, u32[]{:S(2)}) collective-permute-start(bf16[1,256,128]{2,1,0:T(8,128)(2,1)S(1)} %get-tuple-element.36), channel_id=1, source_target_pairs={{0,16},{4,20},{8,24},{12,28},{16,0},{20,4},{24,8},{28,12},{1,17},{... | collective-permute-start | bytes 196616 | tf_op jit(solution)/shard_map/ppermute | solution.py:37
  43.3 0.0 collective-permute-done.13.other_ref
  43.3 0.0 copy-done
  43.3 0.0 copy-done.1
  43.3 2.0 %update_first.1 = (bf16[1536,1024]{1,0:T(8,128)(2,1)}, f32[64,1024]{1,0:T(8,128)}, f32[8,128]{1,0:T(8,128)S(1)}) custom-call(s32[2]{0:T(128)S(1)} %pad_add_fusion.pos_ref, s32[12,128]{1,0:T(8,128)S(1)} %bitcast.8, bf16[32,1024]{1,0:T(8,128)(2,1)S(1)} %leaf_value.1.refs_2_.own_ref, bf16[32,1024]{1,0:T(8,128)(2,1)S(1)} %collective-permute-done.13.other_ref, ...), custom_call_target="tpu_custom_call" | custom-call | flops 3000000000 | tf_op jit(solution)/shard_map/update_first/pallas_call | solution.py:262
  45.4 0.0 collective-permute-done.12.refs_1_
  45.4 1.6 %collective-permute-start.14 = (bf16[1,256,128]{2,1,0:T(8,128)(2,1)S(1)}, bf16[1,256,128]{2,1,0:T(8,128)(2,1)S(1)}, u32[]{:S(2)}, u32[]{:S(2)}) collective-permute-start(bf16[1,256,128]{2,1,0:T(8,128)(2,1)S(1)} %get-tuple-element.40), channel_id=1, source_target_pairs={{0,16},{4,20},{8,24},{12,28},{16,0},{20,4},{24,8},{28,12},{1,17},{... | collective-permute-start | bytes 196616 | tf_op jit(solution)/shard_map/ppermute | solution.py:37
  47.0 2.0 %update_second.1 = (bf16[1536,1024]{1,0:T(8,128)(2,1)}, f32[8,128]{1,0:T(8,128)S(1)}) custom-call(s32[2]{0:T(128)S(1)} %pad_add_fusion.pos_ref, s32[12,128]{1,0:T(8,128)S(1)} %bitcast.9, bf16[32,1024]{1,0:T(8,128)(2,1)S(1)} %leaf_value.1.refs_2_.own_ref, bf16[32,1024]{1,0:T(8,128)(2,1)S(1)} %collective-permute-done.13.other_ref, ...), custom_call_target="tpu_custom_call", output_to_operand_aliasing={{0}: (6, {})} | custom-call | flops 3000000000 | tf_op jit(solution)/shard_map/update_second/pallas_call | solution.py:262
  49.1 0.0 collective-permute-done.11.refs_1_
  49.1 1.6 %collective-permute-done.14.refs_3_ = bf16[1,256,128]{2,1,0:T(8,128)(2,1)S(1)} collective-permute-done((bf16[1,256,128]{2,1,0:T(8,128)(2,1)S(1)}, bf16[1,256,128]{2,1,0:T(8,128)(2,1)S(1)}, u32[]{:S(2)}, u32[]{:S(2)}) %collective-permute-start.14) | collective-permute-done | bytes 65568 | tf_op jit(solution)/shard_map/ppermute | solution.py:37
  50.6 0.7 %last_add.1 = f32[256,256]{1,0:T(8,128)} custom-call(f32[1,256,128]{2,1,0:T(8,128)S(1)} %get-tuple-element.35.after_ref.refs_0_, bf16[1,256,128]{2,1,0:T(8,128)(2,1)S(1)} %collective-permute-done.11.refs_1_, f32[1,256,128]{2,1,0:T(8,128)S(1)} %get-tuple-element.39.after_ref.refs_2_, bf16[1,256,128]{2,1,0:T(8,128)(2,1)S(1)} %collective-permute-done.14.refs_3_, ...), custom_call_target="tpu_custom_call" | custom-call | tf_op jit(solution)/shard_map/last_add/pallas_call | solution.py:45
  (14 shorter events, 0.5 us)
Async XLA Ops:
  0.7 12.5 %copy-start.2 = (s32[8,1536]{1,0:T(8,128)S(1)}, s32[8,1536]{1,0:T(8,128)}, u32[]{:S(2)}) copy-start(s32[8,1536]{1,0:T(8,128)} %param.7) | copy-start | bytes 147460
  6.8 1.9 %collective-permute-start = (bf16[768,256]{1,0:T(8,128)(2,1)S(1)}, bf16[768,256]{1,0:T(8,128)(2,1)S(1)}, u32[]{:S(2)}, u32[]{:S(2)}) collective-permute-start(bf16[768,256]{1,0:T(8,128)(2,1)S(1)} %get-tuple-element.25), channel_id=1, source_target_pairs={{0,1},{1,0},{2,3},{3,2},{4,5},{5,4},{6,7},{7,6},{8,9},{9,8},{10,11... | collective-permute-start | bytes 1179656 | tf_op jit(solution)/shard_map/ppermute | solution.py:37
  8.7 8.6 %collective-permute-start.4 = (bf16[768,128]{1,0:T(8,128)(2,1)S(1)}, bf16[768,128]{1,0:T(8,128)(2,1)S(1)}, u32[]{:S(2)}, u32[]{:S(2)}) collective-permute-start(bf16[768,128]{1,0:T(8,128)(2,1)S(1)} %core_add.2.refs_2_.refs_0_), channel_id=1, source_target_pairs={{0,2},{1,3},{2,0},{3,1},{4,6},{5,7},{6,4},{7,5},{8,10},{9,11},{10,... | collective-permute-start | bytes 589832 | tf_op jit(solution)/shard_map/ppermute | solution.py:37
  11.7 5.3 %collective-permute-start.2 = (bf16[64,1024]{1,0:T(8,128)(2,1)S(1)}, bf16[64,1024]{1,0:T(8,128)(2,1)S(1)}, u32[]{:S(2)}, u32[]{:S(2)}) collective-permute-start(bf16[64,1024]{1,0:T(8,128)(2,1)S(1)} %get-tuple-element.29), channel_id=1, source_target_pairs={{0,4},{4,0},{8,12},{12,8},{16,20},{20,16},{24,28},{28,24},{1,5},{5... | collective-permute-start | bytes 393224 | tf_op jit(solution)/shard_map/ppermute | solution.py:37
  13.3 10.5 %collective-permute-start.1 = (bf16[768,128]{1,0:T(8,128)(2,1)S(1)}, bf16[768,128]{1,0:T(8,128)(2,1)S(1)}, u32[]{:S(2)}, u32[]{:S(2)}) collective-permute-start(bf16[768,128]{1,0:T(8,128)(2,1)S(1)} %core_add.3.refs_2_.refs_0_), channel_id=1, source_target_pairs={{0,2},{1,3},{2,0},{3,1},{4,6},{5,7},{6,4},{7,5},{8,10},{9,11},{10,... | collective-permute-start | bytes 589832 | tf_op jit(solution)/shard_map/ppermute | solution.py:37
  17.4 2.3 %collective-permute-start.5 = (bf16[768,128]{1,0:T(8,128)(2,1)S(1)}, bf16[768,128]{1,0:T(8,128)(2,1)S(1)}, u32[]{:S(2)}, u32[]{:S(2)}) collective-permute-start(bf16[768,128]{1,0:T(8,128)(2,1)S(1)} %feat_add.2.after_ref.refs_0_), channel_id=1, source_target_pairs={{0,1},{1,0},{2,3},{3,2},{4,5},{5,4},{6,7},{7,6},{8,9},{9,8},{10,11... | collective-permute-start | bytes 589832 | tf_op jit(solution)/shard_map/ppermute | solution.py:37
  17.5 6.3 %collective-permute-start.3 = (bf16[64,1024]{1,0:T(8,128)(2,1)S(1)}, bf16[64,1024]{1,0:T(8,128)(2,1)S(1)}, u32[]{:S(2)}, u32[]{:S(2)}) collective-permute-start(bf16[64,1024]{1,0:T(8,128)(2,1)S(1)} %leaf_add.2.refs_2_.refs_0_), channel_id=1, source_target_pairs={{0,8},{4,12},{8,0},{12,4},{16,24},{20,28},{24,16},{28,20},{1,9},{5... | collective-permute-start | bytes 393224 | tf_op jit(solution)/shard_map/ppermute | solution.py:37
  23.8 19.5 %copy-start = (bf16[1536,1024]{1,0:T(8,128)(2,1)S(1)}, bf16[1536,1024]{1,0:T(8,128)(2,1)}, u32[]{:S(2)}) copy-start(bf16[1536,1024]{1,0:T(8,128)(2,1)} %pred_ref.3) | copy-start | bytes 9437188
  23.8 19.5 %copy-start.1 = (s32[1536]{0:T(1024)S(1)}, s32[1536]{0:T(1024)}, u32[]{:S(2)}) copy-start(s32[1536]{0:T(1024)} %param.8) | copy-start | bytes 18436
  23.9 4.4 %collective-permute-start.6 = (bf16[768,128]{1,0:T(8,128)(2,1)S(1)}, bf16[768,128]{1,0:T(8,128)(2,1)S(1)}, u32[]{:S(2)}, u32[]{:S(2)}) collective-permute-start(bf16[768,128]{1,0:T(8,128)(2,1)S(1)} %feat_add.3.after_ref.refs_0_.refs_1_), channel_id=1, source_target_pairs={{0,1},{1,0},{2,3},{3,2},{4,5},{5,4},{6,7},{7,6},{8,9},{9,8},{10,11... | collective-permute-start | bytes 589832 | tf_op jit(solution)/shard_map/ppermute | solution.py:37
  24.0 11.1 %collective-permute-start.7 = (bf16[4,256,128]{2,1,0:T(8,128)(2,1)S(1)}, bf16[4,256,128]{2,1,0:T(8,128)(2,1)S(1)}, u32[]{:S(2)}, u32[]{:S(2)}) collective-permute-start(bf16[4,256,128]{2,1,0:T(8,128)(2,1)S(1)} %hist_send.2.refs_2_), channel_id=1, source_target_pairs={{0,4},{4,0},{8,12},{12,8},{16,20},{20,16},{24,28},{28,24},{1,5},{5... | collective-permute-start | bytes 786440 | tf_op jit(solution)/shard_map/ppermute | solution.py:37
  25.7 9.3 %collective-permute-start.8 = (bf16[64,1024]{1,0:T(8,128)(2,1)S(1)}, bf16[64,1024]{1,0:T(8,128)(2,1)S(1)}, u32[]{:S(2)}, u32[]{:S(2)}) collective-permute-start(bf16[64,1024]{1,0:T(8,128)(2,1)S(1)} %leaf_add.3.refs_2_.refs_0_), channel_id=1, source_target_pairs={{0,16},{4,20},{8,24},{12,28},{16,0},{20,4},{24,8},{28,12},{1,17},{... | collective-permute-start | bytes 393224 | tf_op jit(solution)/shard_map/ppermute | solution.py:37
  29.8 8.6 %collective-permute-start.10 = (bf16[4,256,128]{2,1,0:T(8,128)(2,1)S(1)}, bf16[4,256,128]{2,1,0:T(8,128)(2,1)S(1)}, u32[]{:S(2)}, u32[]{:S(2)}) collective-permute-start(bf16[4,256,128]{2,1,0:T(8,128)(2,1)S(1)} %hist_send.3.after_ref), channel_id=1, source_target_pairs={{0,4},{4,0},{8,12},{12,8},{16,20},{20,16},{24,28},{28,24},{1,5},{5... | collective-permute-start | bytes 786440 | tf_op jit(solution)/shard_map/ppermute | solution.py:37
  35.1 5.7 %collective-permute-start.9 = (bf16[2,256,128]{2,1,0:T(8,128)(2,1)S(1)}, bf16[2,256,128]{2,1,0:T(8,128)(2,1)S(1)}, u32[]{:S(2)}, u32[]{:S(2)}) collective-permute-start(bf16[2,256,128]{2,1,0:T(8,128)(2,1)S(1)} %get-tuple-element.33), channel_id=1, source_target_pairs={{0,8},{4,12},{8,0},{12,4},{16,24},{20,28},{24,16},{28,20},{1,9},{5... | collective-permute-start | bytes 393224 | tf_op jit(solution)/shard_map/ppermute | solution.py:37
  35.8 7.5 %collective-permute-start.13 = (bf16[32,1024]{1,0:T(8,128)(2,1)S(1)}, bf16[32,1024]{1,0:T(8,128)(2,1)S(1)}, u32[]{:S(2)}, u32[]{:S(2)}) collective-permute-start(bf16[32,1024]{1,0:T(8,128)(2,1)S(1)} %leaf_value.1.refs_2_.own_ref), channel_id=1, source_target_pairs={{0,4},{4,0},{8,12},{12,8},{16,20},{20,16},{24,28},{28,24},{1,5},{5... | collective-permute-start | bytes 196616 | tf_op jit(solution)/shard_map/ppermute | solution.py:37
  38.4 7.0 %collective-permute-start.12 = (bf16[2,256,128]{2,1,0:T(8,128)(2,1)S(1)}, bf16[2,256,128]{2,1,0:T(8,128)(2,1)S(1)}, u32[]{:S(2)}, u32[]{:S(2)}) collective-permute-start(bf16[2,256,128]{2,1,0:T(8,128)(2,1)S(1)} %get-tuple-element.37), channel_id=1, source_target_pairs={{0,8},{4,12},{8,0},{12,4},{16,24},{20,28},{24,16},{28,20},{1,9},{5... | collective-permute-start | bytes 393224 | tf_op jit(solution)/shard_map/ppermute | solution.py:37
  40.8 8.3 %collective-permute-start.11 = (bf16[1,256,128]{2,1,0:T(8,128)(2,1)S(1)}, bf16[1,256,128]{2,1,0:T(8,128)(2,1)S(1)}, u32[]{:S(2)}, u32[]{:S(2)}) collective-permute-start(bf16[1,256,128]{2,1,0:T(8,128)(2,1)S(1)} %get-tuple-element.36), channel_id=1, source_target_pairs={{0,16},{4,20},{8,24},{12,28},{16,0},{20,4},{24,8},{28,12},{1,17},{... | collective-permute-start | bytes 196616 | tf_op jit(solution)/shard_map/ppermute | solution.py:37
  45.4 5.2 %collective-permute-start.14 = (bf16[1,256,128]{2,1,0:T(8,128)(2,1)S(1)}, bf16[1,256,128]{2,1,0:T(8,128)(2,1)S(1)}, u32[]{:S(2)}, u32[]{:S(2)}) collective-permute-start(bf16[1,256,128]{2,1,0:T(8,128)(2,1)S(1)} %get-tuple-element.40), channel_id=1, source_target_pairs={{0,16},{4,20},{8,24},{12,28},{16,0},{20,4},{24,8},{28,12},{1,17},{... | collective-permute-start | bytes 196616 | tf_op jit(solution)/shard_map/ppermute | solution.py:37

commit v10 on v9

--- a/solution.py
+++ b/solution.py
@@ -314,7 +314,7 @@
         nonlocal after
         own = pair[p]
         for recv in crossed[p]:
-            after = own = ordered(add_kernel, sketch16, [own, recv], after, "feat_add", (0, 0.0)[p])
+            after = own = ordered(add_kernel, sketch16, [own, recv], after, "feat_add")
         owns[p] = own
         others[p] = swap(own, "feat", nf, 1)
 
@@ -327,7 +327,7 @@
         nonlocal after, leaf_state
         acc, recv, by = leaf_state
         if by < n:
-            after = ordered(add_kernel, sums16, [acc, recv], after, "leaf_add")
+            after = ordered(add_kernel, sums16, [acc, recv], after, "leaf_add", 0 if by == 2 else 3.0)
             leaf_state = (after, swap(after, "rows", n, by), 2 * by)
         elif by == n:
             values16 = jax.ShapeDtypeStruct((LEAVES // 2, cols), bf16)
@@ -345,12 +345,12 @@
 
     def hist_send(p):
         nonlocal after
-        after, = hist_pass(codes, [owns[p]], [others[p]], per, n // 2, 1, bf16, after, (2.0, 0.0)[p])
+        after, = hist_pass(codes, [owns[p]], [others[p]], per, n // 2, 1, bf16, after, (2.0, 3.0)[p])
         backs[p] = swap(after, "rows", n, 1)
 
     def hist_keep():
         nonlocal after
-        heres[:] = hist_pass(codes, owns, others, per, n // 2, 0, f32, after, 0.0)
+        heres[:] = hist_pass(codes, owns, others, per, n // 2, 0, f32, after, 3.0)
         after = heres[-1]
 
     def hist_add(p, level):
@@ -370,12 +370,12 @@
     leaf_step()
     feat_add(0)
     hist_send(0)
+    feat_add(1)
     leaf_step()
-    feat_add(1)
     hist_send(1)
     hist_keep()
+    hist_add(0, 0)
     leaf_step()
-    hist_add(0, 0)
     hist_add(1, 0)
     for level in range(1, levels):
         hist_add(0, level)

time: 51.5 us -> 47.7 us (0.926)
  waiting for transfers between devices: 13.9 us -> 8.88 us
  starting transfers between devices: 20.8 us -> 21.9 us
    ppermute x15, waiting for transfers between devices: 13.9 us -> 8.88 us  [swap(): return lax.ppermute(x, axis, [(i, i ^ by) for i in range(size)])]
    ppermute x15, starting transfers between devices: 20.8 us -> 21.9 us  [swap(): return lax.ppermute(x, axis, [(i, i ^ by) for i in range(size)])]
  transfers between devices with their start and end apart: 15 -> 15, of which waited for: 7 -> 7; matrix products, arithmetic and copies ran while one was open for 0% -> 0% of each run, Pallas kernels for 17% -> 19%
where the time goes in v10:
time: 47.7 us; the launch traced here: 47.5 us
  starting transfers between devices  21.9 us (46%)
  Pallas kernels  15.8 us (33%)
  waiting for transfers between devices  8.88 us (19%)
  between operations  0.81 us (2%)
    ppermute x15, starting transfers between devices, swap(): return lax.ppermute(x, axis, [(i, i ^ by) for i in range(size)])  21.9 us
    ppermute x15, waiting for transfers between devices, swap(): return lax.ppermute(x, axis, [(i, i ^ by) for i in range(size)])  8.88 us
    pallas_call x1, Pallas kernels, rows_pass(): pl.pallas_call(rows_kernel, in_specs=[pl.BlockSpec(memory_space=pltpu.SME...  6.06 us
    pallas_call x3, Pallas kernels, hist_pass(): pl.pallas_call(functools.partial(hist_kernel, per=per, odd=odd, bits=bloc...  4.46 us
    pallas_call x2, Pallas kernels, update_pass(): pl.pallas_call(functools.partial(update_kernel, first=first), in_specs=[p...  4.07 us
    pallas_call x13, Pallas kernels, ordered(): pl.pallas_call(body, in_specs=[pl.BlockSpec(memory_space=pltpu.VMEM)] * l...  1.2 us
  transfers between devices with their start and end apart: 15, of which 7 were waited for; matrix products, arithmetic and copies ran while one was open for 0% of the time, Pallas kernels for 19%

profile of v10, /device:TPU:0, one launch (start us, length us, event | category | flops | bytes accessed | tf_op | source)
XLA Modules:
  0.0 47.5 jit_solution(13604151698254840051)
XLA Ops:
  0.6 0.1 pad_add_fusion.pos_ref
  0.7 0.0 copy-start.2
  0.7 6.1 %rows.1 = (bf16[768,256]{1,0:T(8,128)(2,1)S(1)}, bf16[768,256]{1,0:T(8,128)(2,1)S(1)}, f32[64,1024]{1,0:T(8,128)S(1)}, f32[64,1024]{1,0:T(8,128)S(1)}) custom-call(s32[2]{0:T(128)S(1)} %pad_add_fusion.pos_ref, s32[12,128]{1,0:T(8,128)} %bitcast.7, bf16[1536,1024]{1,0:T(8,128)(2,1)} %pred_ref.3, bf16[1536,1024]{1,0:T(8,128)(2,1)} %lab_hbm.1, ...), custom_call_target="tpu_custom_call" | custom-call | tf_op jit(solution)/shard_map/rows/pallas_call | solution.py:118
  6.8 0.5 %collective-permute-start = (bf16[768,256]{1,0:T(8,128)(2,1)S(1)}, bf16[768,256]{1,0:T(8,128)(2,1)S(1)}, u32[]{:S(2)}, u32[]{:S(2)}) collective-permute-start(bf16[768,256]{1,0:T(8,128)(2,1)S(1)} %get-tuple-element.27), channel_id=1, source_target_pairs={{0,1},{1,0},{2,3},{3,2},{4,5},{5,4},{6,7},{7,6},{8,9},{9,8},{10,11... | collective-permute-start | bytes 1179656 | tf_op jit(solution)/shard_map/ppermute | solution.py:37
  7.3 1.3 %collective-permute-done.refs_1_ = bf16[768,256]{1,0:T(8,128)(2,1)S(1)} collective-permute-done((bf16[768,256]{1,0:T(8,128)(2,1)S(1)}, bf16[768,256]{1,0:T(8,128)(2,1)S(1)}, u32[]{:S(2)}, u32[]{:S(2)}) %collective-permute-start) | collective-permute-done | bytes 393248 | tf_op jit(solution)/shard_map/ppermute | solution.py:37
  8.7 3.0 %collective-permute-start.4 = (bf16[768,128]{1,0:T(8,128)(2,1)S(1)}, bf16[768,128]{1,0:T(8,128)(2,1)S(1)}, u32[]{:S(2)}, u32[]{:S(2)}) collective-permute-start(bf16[768,128]{1,0:T(8,128)(2,1)S(1)} %core_add.2.refs_2_.refs_0_), channel_id=1, source_target_pairs={{0,2},{1,3},{2,0},{3,1},{4,6},{5,7},{6,4},{7,5},{8,10},{9,11},{10,... | collective-permute-start | bytes 589832 | tf_op jit(solution)/shard_map/ppermute | solution.py:37
  11.7 1.6 %collective-permute-start.1 = (bf16[64,1024]{1,0:T(8,128)(2,1)S(1)}, bf16[64,1024]{1,0:T(8,128)(2,1)S(1)}, u32[]{:S(2)}, u32[]{:S(2)}) collective-permute-start(bf16[64,1024]{1,0:T(8,128)(2,1)S(1)} %get-tuple-element.29), channel_id=1, source_target_pairs={{0,4},{4,0},{8,12},{12,8},{16,20},{20,16},{24,28},{28,24},{1,5},{5... | collective-permute-start | bytes 393224 | tf_op jit(solution)/shard_map/ppermute | solution.py:37
  13.2 0.0 copy-done.2
  13.3 0.6 %collective-permute-start.3 = (bf16[768,128]{1,0:T(8,128)(2,1)S(1)}, bf16[768,128]{1,0:T(8,128)(2,1)S(1)}, u32[]{:S(2)}, u32[]{:S(2)}) collective-permute-start(bf16[768,128]{1,0:T(8,128)(2,1)S(1)} %core_add.3.refs_2_.refs_0_), channel_id=1, source_target_pairs={{0,2},{1,3},{2,0},{3,1},{4,6},{5,7},{6,4},{7,5},{8,10},{9,11},{10,... | collective-permute-start | bytes 589832 | tf_op jit(solution)/shard_map/ppermute | solution.py:37
  13.9 3.1 %collective-permute-done.1.refs_1_ = bf16[64,1024]{1,0:T(8,128)(2,1)S(1)} collective-permute-done((bf16[64,1024]{1,0:T(8,128)(2,1)S(1)}, bf16[64,1024]{1,0:T(8,128)(2,1)S(1)}, u32[]{:S(2)}, u32[]{:S(2)}) %collective-permute-start.1) | collective-permute-done | bytes 131104 | tf_op jit(solution)/shard_map/ppermute | solution.py:37
  17.0 0.3 collective-permute-done.4.refs_1_
  17.4 0.1 collective-permute-start.5
  17.5 2.2 %collective-permute-start.2 = (bf16[64,1024]{1,0:T(8,128)(2,1)S(1)}, bf16[64,1024]{1,0:T(8,128)(2,1)S(1)}, u32[]{:S(2)}, u32[]{:S(2)}) collective-permute-start(bf16[64,1024]{1,0:T(8,128)(2,1)S(1)} %leaf_add.2.refs_2_.refs_0_), channel_id=1, source_target_pairs={{0,8},{4,12},{8,0},{12,4},{16,24},{20,28},{24,16},{28,20},{1,9},{5... | collective-permute-start | bytes 393224 | tf_op jit(solution)/shard_map/ppermute | solution.py:37
  19.7 0.0 collective-permute-done.5.refs_1_.refs_2_
  19.7 1.5 %hist_send.2.refs_2_ = bf16[4,256,128]{2,1,0:T(8,128)(2,1)S(1)} custom-call(s32[2,8,768]{2,1,0:T(8,128)S(1)} %fusion.codes_ref, bf16[768,128]{1,0:T(8,128)(2,1)S(1)} %feat_add.2.after_ref.refs_0_, bf16[768,128]{1,0:T(8,128)(2,1)S(1)} %feat_add.2.after_ref.refs_0_, bf16[768,128]{1,0:T(8,128)(2,1)S(1)} %collective-permute-done.5.refs_1_.refs_2_), custom_call_target="tpu_custom_call" | custom-call | flops 2000000000 | tf_op jit(solution)/shard_map/hist_send/pallas_call | solution.py:207
  21.1 1.6 %collective-permute-start.7 = (bf16[4,256,128]{2,1,0:T(8,128)(2,1)S(1)}, bf16[4,256,128]{2,1,0:T(8,128)(2,1)S(1)}, u32[]{:S(2)}, u32[]{:S(2)}) collective-permute-start(bf16[4,256,128]{2,1,0:T(8,128)(2,1)S(1)} %hist_send.2.refs_2_), channel_id=1, source_target_pairs={{0,4},{4,0},{8,12},{12,8},{16,20},{20,16},{24,28},{28,24},{1,5},{5... | collective-permute-start | bytes 786440 | tf_op jit(solution)/shard_map/ppermute | solution.py:37
  22.7 0.0 collective-permute-done.3.refs_1_
  22.8 0.1 collective-permute-start.6
  22.8 0.9 %collective-permute-done.2.refs_1_ = bf16[64,1024]{1,0:T(8,128)(2,1)S(1)} collective-permute-done((bf16[64,1024]{1,0:T(8,128)(2,1)S(1)}, bf16[64,1024]{1,0:T(8,128)(2,1)S(1)}, u32[]{:S(2)}, u32[]{:S(2)}) %collective-permute-start.2) | collective-permute-done | bytes 131104 | tf_op jit(solution)/shard_map/ppermute | solution.py:37
  23.8 2.8 %collective-permute-start.10 = (bf16[64,1024]{1,0:T(8,128)(2,1)S(1)}, bf16[64,1024]{1,0:T(8,128)(2,1)S(1)}, u32[]{:S(2)}, u32[]{:S(2)}) collective-permute-start(bf16[64,1024]{1,0:T(8,128)(2,1)S(1)} %leaf_add.3.after_ref.refs_0_), channel_id=1, source_target_pairs={{0,16},{4,20},{8,24},{12,28},{16,0},{20,4},{24,8},{28,12},{1,17},{... | collective-permute-start | bytes 393224 | tf_op jit(solution)/shard_map/ppermute | solution.py:37
  26.6 0.0 collective-permute-done.6.refs_1_.refs_3_
  26.6 1.5 %hist_send.3.after_ref = bf16[4,256,128]{2,1,0:T(8,128)(2,1)S(1)} custom-call(s32[2,8,768]{2,1,0:T(8,128)S(1)} %fusion.codes_ref, bf16[64,1024]{1,0:T(8,128)(2,1)S(1)} %leaf_add.3.after_ref.refs_0_, bf16[768,128]{1,0:T(8,128)(2,1)S(1)} %feat_add.3.refs_2_.refs_0_.refs_1_, bf16[768,128]{1,0:T(8,128)(2,1)S(1)} %collective-permute-done.6.refs_1_.refs_3_), custom_call_target="tpu_custom_call" | custom-call | flops 3000000000 | tf_op jit(solution)/shard_map/hist_send/pallas_call | solution.py:207
  28.1 1.6 %collective-permute-start.9 = (bf16[4,256,128]{2,1,0:T(8,128)(2,1)S(1)}, bf16[4,256,128]{2,1,0:T(8,128)(2,1)S(1)}, u32[]{:S(2)}, u32[]{:S(2)}) collective-permute-start(bf16[4,256,128]{2,1,0:T(8,128)(2,1)S(1)} %hist_send.3.after_ref), channel_id=1, source_target_pairs={{0,4},{4,0},{8,12},{12,8},{16,20},{20,16},{24,28},{28,24},{1,5},{5... | collective-permute-start | bytes 786440 | tf_op jit(solution)/shard_map/ppermute | solution.py:37
  29.7 1.5 %hist_keep.1 = (f32[4,256,128]{2,1,0:T(8,128)S(1)}, f32[4,256,128]{2,1,0:T(8,128)S(1)}) custom-call(s32[2,8,768]{2,1,0:T(8,128)S(1)} %fusion.codes_ref, bf16[4,256,128]{2,1,0:T(8,128)(2,1)S(1)} %hist_send.3.after_ref, bf16[768,128]{1,0:T(8,128)(2,1)S(1)} %feat_add.2.after_ref.refs_0_, bf16[768,128]{1,0:T(8,128)(2,1)S(1)} %feat_add.3.refs_2_.refs_0_.refs_1_, ...), custom_call_target="tpu_custom_call" | custom-call | flops 3000000000 | tf_op jit(solution)/shard_map/hist_keep/pallas_call | solution.py:207
  31.2 0.0 copy-start
  31.2 0.0 copy-start.1
  31.2 0.0 collective-permute-done.7.refs_1_
  31.3 1.6 %collective-permute-start.8 = (bf16[2,256,128]{2,1,0:T(8,128)(2,1)S(1)}, bf16[2,256,128]{2,1,0:T(8,128)(2,1)S(1)}, u32[]{:S(2)}, u32[]{:S(2)}) collective-permute-start(bf16[2,256,128]{2,1,0:T(8,128)(2,1)S(1)} %get-tuple-element.33), channel_id=1, source_target_pairs={{0,8},{4,12},{8,0},{12,4},{16,24},{20,28},{24,16},{28,20},{1,9},{5... | collective-permute-start | bytes 393224 | tf_op jit(solution)/shard_map/ppermute | solution.py:37
  32.9 0.0 collective-permute-done.10.refs_1_
  33.0 1.5 %collective-permute-start.13 = (bf16[32,1024]{1,0:T(8,128)(2,1)S(1)}, bf16[32,1024]{1,0:T(8,128)(2,1)S(1)}, u32[]{:S(2)}, u32[]{:S(2)}) collective-permute-start(bf16[32,1024]{1,0:T(8,128)(2,1)S(1)} %leaf_value.1.refs_2_.own_ref), channel_id=1, source_target_pairs={{0,4},{4,0},{8,12},{12,8},{16,20},{20,16},{24,28},{28,24},{1,5},{5... | collective-permute-start | bytes 196616 | tf_op jit(solution)/shard_map/ppermute | solution.py:37
  34.5 2.0 %collective-permute-done.9.refs_1_ = bf16[4,256,128]{2,1,0:T(8,128)(2,1)S(1)} collective-permute-done((bf16[4,256,128]{2,1,0:T(8,128)(2,1)S(1)}, bf16[4,256,128]{2,1,0:T(8,128)(2,1)S(1)}, u32[]{:S(2)}, u32[]{:S(2)}) %collective-permute-start.9) | collective-permute-done | bytes 262176 | tf_op jit(solution)/shard_map/ppermute | solution.py:37
  36.5 1.6 %collective-permute-start.12 = (bf16[2,256,128]{2,1,0:T(8,128)(2,1)S(1)}, bf16[2,256,128]{2,1,0:T(8,128)(2,1)S(1)}, u32[]{:S(2)}, u32[]{:S(2)}) collective-permute-start(bf16[2,256,128]{2,1,0:T(8,128)(2,1)S(1)} %get-tuple-element.37), channel_id=1, source_target_pairs={{0,8},{4,12},{8,0},{12,4},{16,24},{20,28},{24,16},{28,20},{1,9},{5... | collective-permute-start | bytes 393224 | tf_op jit(solution)/shard_map/ppermute | solution.py:37
  38.1 0.0 collective-permute-done.8.refs_1_
  38.2 1.2 %collective-permute-start.11 = (bf16[1,256,128]{2,1,0:T(8,128)(2,1)S(1)}, bf16[1,256,128]{2,1,0:T(8,128)(2,1)S(1)}, u32[]{:S(2)}, u32[]{:S(2)}) collective-permute-start(bf16[1,256,128]{2,1,0:T(8,128)(2,1)S(1)} %get-tuple-element.36), channel_id=1, source_target_pairs={{0,16},{4,20},{8,24},{12,28},{16,0},{20,4},{24,8},{28,12},{1,17},{... | collective-permute-start | bytes 196616 | tf_op jit(solution)/shard_map/ppermute | solution.py:37
  39.3 0.0 collective-permute-done.13.other_ref
  39.3 0.0 copy-done
  39.3 0.0 copy-done.1
  39.3 2.0 %update_first.1 = (bf16[1536,1024]{1,0:T(8,128)(2,1)}, f32[64,1024]{1,0:T(8,128)}, f32[8,128]{1,0:T(8,128)S(1)}) custom-call(s32[2]{0:T(128)S(1)} %pad_add_fusion.pos_ref, s32[12,128]{1,0:T(8,128)S(1)} %bitcast.8, bf16[32,1024]{1,0:T(8,128)(2,1)S(1)} %leaf_value.1.refs_2_.own_ref, bf16[32,1024]{1,0:T(8,128)(2,1)S(1)} %collective-permute-done.13.other_ref, ...), custom_call_target="tpu_custom_call" | custom-call | flops 3000000000 | tf_op jit(solution)/shard_map/update_first/pallas_call | solution.py:262
  41.4 0.1 collective-permute-done.12.refs_1_
  41.5 2.1 %collective-permute-start.14 = (bf16[1,256,128]{2,1,0:T(8,128)(2,1)S(1)}, bf16[1,256,128]{2,1,0:T(8,128)(2,1)S(1)}, u32[]{:S(2)}, u32[]{:S(2)}) collective-permute-start(bf16[1,256,128]{2,1,0:T(8,128)(2,1)S(1)} %get-tuple-element.40), channel_id=1, source_target_pairs={{0,16},{4,20},{8,24},{12,28},{16,0},{20,4},{24,8},{28,12},{1,17},{... | collective-permute-start | bytes 196616 | tf_op jit(solution)/shard_map/ppermute | solution.py:37
  43.7 2.0 %update_second.1 = (bf16[1536,1024]{1,0:T(8,128)(2,1)}, f32[8,128]{1,0:T(8,128)S(1)}) custom-call(s32[2]{0:T(128)S(1)} %pad_add_fusion.pos_ref, s32[12,128]{1,0:T(8,128)S(1)} %bitcast.9, bf16[32,1024]{1,0:T(8,128)(2,1)S(1)} %leaf_value.1.refs_2_.own_ref, bf16[32,1024]{1,0:T(8,128)(2,1)S(1)} %collective-permute-done.13.other_ref, ...), custom_call_target="tpu_custom_call", output_to_operand_aliasing={{0}: (6, {})} | custom-call | flops 3000000000 | tf_op jit(solution)/shard_map/update_second/pallas_call | solution.py:262
  45.7 0.0 collective-permute-done.11.refs_1_
  45.7 1.1 %collective-permute-done.14.refs_3_ = bf16[1,256,128]{2,1,0:T(8,128)(2,1)S(1)} collective-permute-done((bf16[1,256,128]{2,1,0:T(8,128)(2,1)S(1)}, bf16[1,256,128]{2,1,0:T(8,128)(2,1)S(1)}, u32[]{:S(2)}, u32[]{:S(2)}) %collective-permute-start.14) | collective-permute-done | bytes 65568 | tf_op jit(solution)/shard_map/ppermute | solution.py:37
  46.8 0.7 %last_add.1 = f32[256,256]{1,0:T(8,128)} custom-call(f32[1,256,128]{2,1,0:T(8,128)S(1)} %get-tuple-element.35.after_ref.refs_0_, bf16[1,256,128]{2,1,0:T(8,128)(2,1)S(1)} %collective-permute-done.11.refs_1_, f32[1,256,128]{2,1,0:T(8,128)S(1)} %get-tuple-element.39.after_ref.refs_2_, bf16[1,256,128]{2,1,0:T(8,128)(2,1)S(1)} %collective-permute-done.14.refs_3_, ...), custom_call_target="tpu_custom_call" | custom-call | tf_op jit(solution)/shard_map/last_add/pallas_call | solution.py:45
  (14 shorter events, 0.5 us)
Async XLA Ops:
  0.7 12.5 %copy-start.2 = (s32[8,1536]{1,0:T(8,128)S(1)}, s32[8,1536]{1,0:T(8,128)}, u32[]{:S(2)}) copy-start(s32[8,1536]{1,0:T(8,128)} %param.7) | copy-start | bytes 147460
  6.8 1.9 %collective-permute-start = (bf16[768,256]{1,0:T(8,128)(2,1)S(1)}, bf16[768,256]{1,0:T(8,128)(2,1)S(1)}, u32[]{:S(2)}, u32[]{:S(2)}) collective-permute-start(bf16[768,256]{1,0:T(8,128)(2,1)S(1)} %get-tuple-element.27), channel_id=1, source_target_pairs={{0,1},{1,0},{2,3},{3,2},{4,5},{5,4},{6,7},{7,6},{8,9},{9,8},{10,11... | collective-permute-start | bytes 1179656 | tf_op jit(solution)/shard_map/ppermute | solution.py:37
  8.7 8.6 %collective-permute-start.4 = (bf16[768,128]{1,0:T(8,128)(2,1)S(1)}, bf16[768,128]{1,0:T(8,128)(2,1)S(1)}, u32[]{:S(2)}, u32[]{:S(2)}) collective-permute-start(bf16[768,128]{1,0:T(8,128)(2,1)S(1)} %core_add.2.refs_2_.refs_0_), channel_id=1, source_target_pairs={{0,2},{1,3},{2,0},{3,1},{4,6},{5,7},{6,4},{7,5},{8,10},{9,11},{10,... | collective-permute-start | bytes 589832 | tf_op jit(solution)/shard_map/ppermute | solution.py:37
  11.7 5.3 %collective-permute-start.1 = (bf16[64,1024]{1,0:T(8,128)(2,1)S(1)}, bf16[64,1024]{1,0:T(8,128)(2,1)S(1)}, u32[]{:S(2)}, u32[]{:S(2)}) collective-permute-start(bf16[64,1024]{1,0:T(8,128)(2,1)S(1)} %get-tuple-element.29), channel_id=1, source_target_pairs={{0,4},{4,0},{8,12},{12,8},{16,20},{20,16},{24,28},{28,24},{1,5},{5... | collective-permute-start | bytes 393224 | tf_op jit(solution)/shard_map/ppermute | solution.py:37
  13.3 9.4 %collective-permute-start.3 = (bf16[768,128]{1,0:T(8,128)(2,1)S(1)}, bf16[768,128]{1,0:T(8,128)(2,1)S(1)}, u32[]{:S(2)}, u32[]{:S(2)}) collective-permute-start(bf16[768,128]{1,0:T(8,128)(2,1)S(1)} %core_add.3.refs_2_.refs_0_), channel_id=1, source_target_pairs={{0,2},{1,3},{2,0},{3,1},{4,6},{5,7},{6,4},{7,5},{8,10},{9,11},{10,... | collective-permute-start | bytes 589832 | tf_op jit(solution)/shard_map/ppermute | solution.py:37
  17.4 2.3 %collective-permute-start.5 = (bf16[768,128]{1,0:T(8,128)(2,1)S(1)}, bf16[768,128]{1,0:T(8,128)(2,1)S(1)}, u32[]{:S(2)}, u32[]{:S(2)}) collective-permute-start(bf16[768,128]{1,0:T(8,128)(2,1)S(1)} %feat_add.2.after_ref.refs_0_), channel_id=1, source_target_pairs={{0,1},{1,0},{2,3},{3,2},{4,5},{5,4},{6,7},{7,6},{8,9},{9,8},{10,11... | collective-permute-start | bytes 589832 | tf_op jit(solution)/shard_map/ppermute | solution.py:37
  17.5 6.3 %collective-permute-start.2 = (bf16[64,1024]{1,0:T(8,128)(2,1)S(1)}, bf16[64,1024]{1,0:T(8,128)(2,1)S(1)}, u32[]{:S(2)}, u32[]{:S(2)}) collective-permute-start(bf16[64,1024]{1,0:T(8,128)(2,1)S(1)} %leaf_add.2.refs_2_.refs_0_), channel_id=1, source_target_pairs={{0,8},{4,12},{8,0},{12,4},{16,24},{20,28},{24,16},{28,20},{1,9},{5... | collective-permute-start | bytes 393224 | tf_op jit(solution)/shard_map/ppermute | solution.py:37
  21.1 10.1 %collective-permute-start.7 = (bf16[4,256,128]{2,1,0:T(8,128)(2,1)S(1)}, bf16[4,256,128]{2,1,0:T(8,128)(2,1)S(1)}, u32[]{:S(2)}, u32[]{:S(2)}) collective-permute-start(bf16[4,256,128]{2,1,0:T(8,128)(2,1)S(1)} %hist_send.2.refs_2_), channel_id=1, source_target_pairs={{0,4},{4,0},{8,12},{12,8},{16,20},{20,16},{24,28},{28,24},{1,5},{5... | collective-permute-start | bytes 786440 | tf_op jit(solution)/shard_map/ppermute | solution.py:37
  22.8 3.9 %collective-permute-start.6 = (bf16[768,128]{1,0:T(8,128)(2,1)S(1)}, bf16[768,128]{1,0:T(8,128)(2,1)S(1)}, u32[]{:S(2)}, u32[]{:S(2)}) collective-permute-start(bf16[768,128]{1,0:T(8,128)(2,1)S(1)} %feat_add.3.refs_2_.refs_0_.refs_1_), channel_id=1, source_target_pairs={{0,1},{1,0},{2,3},{3,2},{4,5},{5,4},{6,7},{7,6},{8,9},{9,8},{10,11... | collective-permute-start | bytes 589832 | tf_op jit(solution)/shard_map/ppermute | solution.py:37
  23.8 9.1 %collective-permute-start.10 = (bf16[64,1024]{1,0:T(8,128)(2,1)S(1)}, bf16[64,1024]{1,0:T(8,128)(2,1)S(1)}, u32[]{:S(2)}, u32[]{:S(2)}) collective-permute-start(bf16[64,1024]{1,0:T(8,128)(2,1)S(1)} %leaf_add.3.after_ref.refs_0_), channel_id=1, source_target_pairs={{0,16},{4,20},{8,24},{12,28},{16,0},{20,4},{24,8},{28,12},{1,17},{... | collective-permute-start | bytes 393224 | tf_op jit(solution)/shard_map/ppermute | solution.py:37
  28.1 8.3 %collective-permute-start.9 = (bf16[4,256,128]{2,1,0:T(8,128)(2,1)S(1)}, bf16[4,256,128]{2,1,0:T(8,128)(2,1)S(1)}, u32[]{:S(2)}, u32[]{:S(2)}) collective-permute-start(bf16[4,256,128]{2,1,0:T(8,128)(2,1)S(1)} %hist_send.3.after_ref), channel_id=1, source_target_pairs={{0,4},{4,0},{8,12},{12,8},{16,20},{20,16},{24,28},{28,24},{1,5},{5... | collective-permute-start | bytes 786440 | tf_op jit(solution)/shard_map/ppermute | solution.py:37
  31.2 8.1 %copy-start = (bf16[1536,1024]{1,0:T(8,128)(2,1)S(1)}, bf16[1536,1024]{1,0:T(8,128)(2,1)}, u32[]{:S(2)}) copy-start(bf16[1536,1024]{1,0:T(8,128)(2,1)} %pred_ref.3) | copy-start | bytes 9437188
  31.2 8.1 %copy-start.1 = (s32[1536]{0:T(1024)S(1)}, s32[1536]{0:T(1024)}, u32[]{:S(2)}) copy-start(s32[1536]{0:T(1024)} %param.8) | copy-start | bytes 18436
  31.3 6.8 %collective-permute-start.8 = (bf16[2,256,128]{2,1,0:T(8,128)(2,1)S(1)}, bf16[2,256,128]{2,1,0:T(8,128)(2,1)S(1)}, u32[]{:S(2)}, u32[]{:S(2)}) collective-permute-start(bf16[2,256,128]{2,1,0:T(8,128)(2,1)S(1)} %get-tuple-element.33), channel_id=1, source_target_pairs={{0,8},{4,12},{8,0},{12,4},{16,24},{20,28},{24,16},{28,20},{1,9},{5... | collective-permute-start | bytes 393224 | tf_op jit(solution)/shard_map/ppermute | solution.py:37
  33.0 6.4 %collective-permute-start.13 = (bf16[32,1024]{1,0:T(8,128)(2,1)S(1)}, bf16[32,1024]{1,0:T(8,128)(2,1)S(1)}, u32[]{:S(2)}, u32[]{:S(2)}) collective-permute-start(bf16[32,1024]{1,0:T(8,128)(2,1)S(1)} %leaf_value.1.refs_2_.own_ref), channel_id=1, source_target_pairs={{0,4},{4,0},{8,12},{12,8},{16,20},{20,16},{24,28},{28,24},{1,5},{5... | collective-permute-start | bytes 196616 | tf_op jit(solution)/shard_map/ppermute | solution.py:37
  36.5 5.0 %collective-permute-start.12 = (bf16[2,256,128]{2,1,0:T(8,128)(2,1)S(1)}, bf16[2,256,128]{2,1,0:T(8,128)(2,1)S(1)}, u32[]{:S(2)}, u32[]{:S(2)}) collective-permute-start(bf16[2,256,128]{2,1,0:T(8,128)(2,1)S(1)} %get-tuple-element.37), channel_id=1, source_target_pairs={{0,8},{4,12},{8,0},{12,4},{16,24},{20,28},{24,16},{28,20},{1,9},{5... | collective-permute-start | bytes 393224 | tf_op jit(solution)/shard_map/ppermute | solution.py:37
  38.2 7.5 %collective-permute-start.11 = (bf16[1,256,128]{2,1,0:T(8,128)(2,1)S(1)}, bf16[1,256,128]{2,1,0:T(8,128)(2,1)S(1)}, u32[]{:S(2)}, u32[]{:S(2)}) collective-permute-start(bf16[1,256,128]{2,1,0:T(8,128)(2,1)S(1)} %get-tuple-element.36), channel_id=1, source_target_pairs={{0,16},{4,20},{8,24},{12,28},{16,0},{20,4},{24,8},{28,12},{1,17},{... | collective-permute-start | bytes 196616 | tf_op jit(solution)/shard_map/ppermute | solution.py:37
  41.5 5.2 %collective-permute-start.14 = (bf16[1,256,128]{2,1,0:T(8,128)(2,1)S(1)}, bf16[1,256,128]{2,1,0:T(8,128)(2,1)S(1)}, u32[]{:S(2)}, u32[]{:S(2)}) collective-permute-start(bf16[1,256,128]{2,1,0:T(8,128)(2,1)S(1)} %get-tuple-element.40), channel_id=1, source_target_pairs={{0,16},{4,20},{8,24},{12,28},{16,0},{20,4},{24,8},{28,12},{1,17},{... | collective-permute-start | bytes 196616 | tf_op jit(solution)/shard_map/ppermute | solution.py:37

commit v11 on v10

--- a/solution.py
+++ b/solution.py
@@ -345,12 +345,12 @@
 
     def hist_send(p):
         nonlocal after
-        after, = hist_pass(codes, [owns[p]], [others[p]], per, n // 2, 1, bf16, after, (2.0, 3.0)[p])
+        after, = hist_pass(codes, [owns[p]], [others[p]], per, n // 2, 1, bf16, after, (2.0, 0.0)[p])
         backs[p] = swap(after, "rows", n, 1)
 
     def hist_keep():
         nonlocal after
-        heres[:] = hist_pass(codes, owns, others, per, n // 2, 0, f32, after, 3.0)
+        heres[:] = hist_pass(codes, owns, others, per, n // 2, 0, f32, after, 0.0)
         after = heres[-1]
 
     def hist_add(p, level):
@@ -367,21 +367,19 @@
     core_add(0)
     leaf_pack()
     core_add(1)
+    feat_add(0)
     leaf_step()
-    feat_add(0)
     hist_send(0)
     feat_add(1)
     leaf_step()
     hist_send(1)
     hist_keep()
-    hist_add(0, 0)
-    leaf_step()
-    hist_add(1, 0)
-    for level in range(1, levels):
+    for level in range(levels):
         hist_add(0, level)
-        if level == levels - 1:
-            update()
         hist_add(1, level)
+        if level == 0:
+            leaf_step()
+    update()
     update()
     histograms = ordered(
         last_kernel, jax.ShapeDtypeStruct((per * feats, width * parts), f32),

time: 47.7 us -> 48.6 us (1.019)
  starting transfers between devices: 21.9 us -> 23.2 us
    ppermute x15, starting transfers between devices: 21.9 us -> 23.2 us  [swap(): return lax.ppermute(x, axis, [(i, i ^ by) for i in range(size)])]
  transfers between devices with their start and end apart: 15 -> 15, of which waited for: 7 -> 5; matrix products, arithmetic and copies ran while one was open for 0% -> 0% of each run, Pallas kernels for 19% -> 19%
where the time goes in v11:
time: 48.6 us; the launch traced here: 48.5 us
  starting transfers between devices  23.2 us (48%)
  Pallas kernels  15.8 us (33%)
  waiting for transfers between devices  8.51 us (18%)
  between operations  0.83 us (2%)
    ppermute x15, starting transfers between devices, swap(): return lax.ppermute(x, axis, [(i, i ^ by) for i in range(size)])  23.2 us
    ppermute x15, waiting for transfers between devices, swap(): return lax.ppermute(x, axis, [(i, i ^ by) for i in range(size)])  8.51 us
    pallas_call x1, Pallas kernels, rows_pass(): pl.pallas_call(rows_kernel, in_specs=[pl.BlockSpec(memory_space=pltpu.SME...  6.06 us
    pallas_call x3, Pallas kernels, hist_pass(): pl.pallas_call(functools.partial(hist_kernel, per=per, odd=odd, bits=bloc...  4.47 us
    pallas_call x2, Pallas kernels, update_pass(): pl.pallas_call(functools.partial(update_kernel, first=first), in_specs=[p...  4.07 us
    pallas_call x13, Pallas kernels, ordered(): pl.pallas_call(body, in_specs=[pl.BlockSpec(memory_space=pltpu.VMEM)] * l...  1.21 us
  transfers between devices with their start and end apart: 15, of which 5 were waited for; matrix products, arithmetic and copies ran while one was open for 0% of the time, Pallas kernels for 19%

profile of v11, /device:TPU:0, one launch (start us, length us, event | category | flops | bytes accessed | tf_op | source)
XLA Modules:
  0.0 48.5 jit_solution(15003766666390430657)
XLA Ops:
  0.6 0.1 pad_add_fusion.pos_ref
  0.7 0.0 copy-start.2
  0.7 6.1 %rows.1 = (bf16[768,256]{1,0:T(8,128)(2,1)S(1)}, bf16[768,256]{1,0:T(8,128)(2,1)S(1)}, f32[64,1024]{1,0:T(8,128)S(1)}, f32[64,1024]{1,0:T(8,128)S(1)}) custom-call(s32[2]{0:T(128)S(1)} %pad_add_fusion.pos_ref, s32[12,128]{1,0:T(8,128)} %bitcast.7, bf16[1536,1024]{1,0:T(8,128)(2,1)} %pred_ref.3, bf16[1536,1024]{1,0:T(8,128)(2,1)} %lab_hbm.1, ...), custom_call_target="tpu_custom_call" | custom-call | tf_op jit(solution)/shard_map/rows/pallas_call | solution.py:118
  6.8 0.5 %collective-permute-start = (bf16[768,256]{1,0:T(8,128)(2,1)S(1)}, bf16[768,256]{1,0:T(8,128)(2,1)S(1)}, u32[]{:S(2)}, u32[]{:S(2)}) collective-permute-start(bf16[768,256]{1,0:T(8,128)(2,1)S(1)} %get-tuple-element.27), channel_id=1, source_target_pairs={{0,1},{1,0},{2,3},{3,2},{4,5},{5,4},{6,7},{7,6},{8,9},{9,8},{10,11... | collective-permute-start | bytes 1179656 | tf_op jit(solution)/shard_map/ppermute | solution.py:37
  7.3 1.3 %collective-permute-done.refs_1_ = bf16[768,256]{1,0:T(8,128)(2,1)S(1)} collective-permute-done((bf16[768,256]{1,0:T(8,128)(2,1)S(1)}, bf16[768,256]{1,0:T(8,128)(2,1)S(1)}, u32[]{:S(2)}, u32[]{:S(2)}) %collective-permute-start) | collective-permute-done | bytes 393248 | tf_op jit(solution)/shard_map/ppermute | solution.py:37
  8.7 3.0 %collective-permute-start.2 = (bf16[768,128]{1,0:T(8,128)(2,1)S(1)}, bf16[768,128]{1,0:T(8,128)(2,1)S(1)}, u32[]{:S(2)}, u32[]{:S(2)}) collective-permute-start(bf16[768,128]{1,0:T(8,128)(2,1)S(1)} %core_add.2.refs_2_.refs_0_), channel_id=1, source_target_pairs={{0,2},{1,3},{2,0},{3,1},{4,6},{5,7},{6,4},{7,5},{8,10},{9,11},{10,... | collective-permute-start | bytes 589832 | tf_op jit(solution)/shard_map/ppermute | solution.py:37
  11.7 0.0 copy-done.2
  11.7 1.6 %collective-permute-start.1 = (bf16[64,1024]{1,0:T(8,128)(2,1)S(1)}, bf16[64,1024]{1,0:T(8,128)(2,1)S(1)}, u32[]{:S(2)}, u32[]{:S(2)}) collective-permute-start(bf16[64,1024]{1,0:T(8,128)(2,1)S(1)} %get-tuple-element.29), channel_id=1, source_target_pairs={{0,4},{4,0},{8,12},{12,8},{16,20},{20,16},{24,28},{28,24},{1,5},{5... | collective-permute-start | bytes 393224 | tf_op jit(solution)/shard_map/ppermute | solution.py:37
  13.3 0.6 %collective-permute-start.4 = (bf16[768,128]{1,0:T(8,128)(2,1)S(1)}, bf16[768,128]{1,0:T(8,128)(2,1)S(1)}, u32[]{:S(2)}, u32[]{:S(2)}) collective-permute-start(bf16[768,128]{1,0:T(8,128)(2,1)S(1)} %core_add.3.refs_2_.refs_0_), channel_id=1, source_target_pairs={{0,2},{1,3},{2,0},{3,1},{4,6},{5,7},{6,4},{7,5},{8,10},{9,11},{10,... | collective-permute-start | bytes 589832 | tf_op jit(solution)/shard_map/ppermute | solution.py:37
  13.9 3.4 %collective-permute-done.2.refs_1_ = bf16[768,128]{1,0:T(8,128)(2,1)S(1)} collective-permute-done((bf16[768,128]{1,0:T(8,128)(2,1)S(1)}, bf16[768,128]{1,0:T(8,128)(2,1)S(1)}, u32[]{:S(2)}, u32[]{:S(2)}) %collective-permute-start.2) | collective-permute-done | bytes 196640 | tf_op jit(solution)/shard_map/ppermute | solution.py:37
  17.4 0.1 collective-permute-start.5
  17.5 0.0 collective-permute-done.1.refs_1_
  17.5 2.2 %collective-permute-start.3 = (bf16[64,1024]{1,0:T(8,128)(2,1)S(1)}, bf16[64,1024]{1,0:T(8,128)(2,1)S(1)}, u32[]{:S(2)}, u32[]{:S(2)}) collective-permute-start(bf16[64,1024]{1,0:T(8,128)(2,1)S(1)} %leaf_add.2.after_ref.refs_0_), channel_id=1, source_target_pairs={{0,8},{4,12},{8,0},{12,4},{16,24},{20,28},{24,16},{28,20},{1,9},{5... | collective-permute-start | bytes 393224 | tf_op jit(solution)/shard_map/ppermute | solution.py:37
  19.7 0.0 collective-permute-done.5.refs_1_.refs_2_
  19.7 1.5 %hist_send.2.refs_2_ = bf16[4,256,128]{2,1,0:T(8,128)(2,1)S(1)} custom-call(s32[2,8,768]{2,1,0:T(8,128)S(1)} %fusion.codes_ref, bf16[64,1024]{1,0:T(8,128)(2,1)S(1)} %leaf_add.2.after_ref.refs_0_, bf16[768,128]{1,0:T(8,128)(2,1)S(1)} %feat_add.2.refs_2_.refs_0_, bf16[768,128]{1,0:T(8,128)(2,1)S(1)} %collective-permute-done.5.refs_1_.refs_2_), custom_call_target="tpu_custom_call" | custom-call | flops 2000000000 | tf_op jit(solution)/shard_map/hist_send/pallas_call | solution.py:207
  21.2 1.6 %collective-permute-start.7 = (bf16[4,256,128]{2,1,0:T(8,128)(2,1)S(1)}, bf16[4,256,128]{2,1,0:T(8,128)(2,1)S(1)}, u32[]{:S(2)}, u32[]{:S(2)}) collective-permute-start(bf16[4,256,128]{2,1,0:T(8,128)(2,1)S(1)} %hist_send.2.refs_2_), channel_id=1, source_target_pairs={{0,4},{4,0},{8,12},{12,8},{16,20},{20,16},{24,28},{28,24},{1,5},{5... | collective-permute-start | bytes 786440 | tf_op jit(solution)/shard_map/ppermute | solution.py:37
  22.7 0.0 collective-permute-done.4.refs_1_
  22.8 0.1 collective-permute-start.6
  22.9 1.0 %collective-permute-done.3.refs_1_ = bf16[64,1024]{1,0:T(8,128)(2,1)S(1)} collective-permute-done((bf16[64,1024]{1,0:T(8,128)(2,1)S(1)}, bf16[64,1024]{1,0:T(8,128)(2,1)S(1)}, u32[]{:S(2)}, u32[]{:S(2)}) %collective-permute-start.3) | collective-permute-done | bytes 131104 | tf_op jit(solution)/shard_map/ppermute | solution.py:37
  23.9 0.0 copy-start
  23.9 0.0 copy-start.1
  23.9 0.4 collective-permute-done.6.refs_1_.refs_3_
  24.3 1.5 %hist_send.3.after_ref = bf16[4,256,128]{2,1,0:T(8,128)(2,1)S(1)} custom-call(s32[2,8,768]{2,1,0:T(8,128)S(1)} %fusion.codes_ref, bf16[64,1024]{1,0:T(8,128)(2,1)S(1)} %leaf_add.3.after_ref.refs_0_, bf16[768,128]{1,0:T(8,128)(2,1)S(1)} %feat_add.3.refs_2_.refs_0_.refs_1_, bf16[768,128]{1,0:T(8,128)(2,1)S(1)} %collective-permute-done.6.refs_1_.refs_3_), custom_call_target="tpu_custom_call" | custom-call | tf_op jit(solution)/shard_map/hist_send/pallas_call | solution.py:207
  25.8 1.4 %collective-permute-start.10 = (bf16[4,256,128]{2,1,0:T(8,128)(2,1)S(1)}, bf16[4,256,128]{2,1,0:T(8,128)(2,1)S(1)}, u32[]{:S(2)}, u32[]{:S(2)}) collective-permute-start(bf16[4,256,128]{2,1,0:T(8,128)(2,1)S(1)} %hist_send.3.after_ref), channel_id=1, source_target_pairs={{0,4},{4,0},{8,12},{12,8},{16,20},{20,16},{24,28},{28,24},{1,5},{5... | collective-permute-start | bytes 786440 | tf_op jit(solution)/shard_map/ppermute | solution.py:37
  27.1 2.6 %collective-permute-start.9 = (bf16[64,1024]{1,0:T(8,128)(2,1)S(1)}, bf16[64,1024]{1,0:T(8,128)(2,1)S(1)}, u32[]{:S(2)}, u32[]{:S(2)}) collective-permute-start(bf16[64,1024]{1,0:T(8,128)(2,1)S(1)} %leaf_add.3.after_ref.refs_0_), channel_id=1, source_target_pairs={{0,16},{4,20},{8,24},{12,28},{16,0},{20,4},{24,8},{28,12},{1,17},{... | collective-permute-start | bytes 393224 | tf_op jit(solution)/shard_map/ppermute | solution.py:37
  29.7 1.5 %hist_keep.1 = (f32[4,256,128]{2,1,0:T(8,128)S(1)}, f32[4,256,128]{2,1,0:T(8,128)S(1)}) custom-call(s32[2,8,768]{2,1,0:T(8,128)S(1)} %fusion.codes_ref, bf16[4,256,128]{2,1,0:T(8,128)(2,1)S(1)} %hist_send.3.after_ref, bf16[768,128]{1,0:T(8,128)(2,1)S(1)} %feat_add.2.refs_2_.refs_0_, bf16[768,128]{1,0:T(8,128)(2,1)S(1)} %feat_add.3.refs_2_.refs_0_.refs_1_, ...), custom_call_target="tpu_custom_call" | custom-call | tf_op jit(solution)/shard_map/hist_keep/pallas_call | solution.py:207
  31.3 0.0 collective-permute-done.7.refs_1_
  31.3 1.6 %collective-permute-start.8 = (bf16[2,256,128]{2,1,0:T(8,128)(2,1)S(1)}, bf16[2,256,128]{2,1,0:T(8,128)(2,1)S(1)}, u32[]{:S(2)}, u32[]{:S(2)}) collective-permute-start(bf16[2,256,128]{2,1,0:T(8,128)(2,1)S(1)} %get-tuple-element.33), channel_id=1, source_target_pairs={{0,8},{4,12},{8,0},{12,4},{16,24},{20,28},{24,16},{28,20},{1,9},{5... | collective-permute-start | bytes 393224 | tf_op jit(solution)/shard_map/ppermute | solution.py:37
  33.0 2.3 %collective-permute-done.10.refs_1_ = bf16[4,256,128]{2,1,0:T(8,128)(2,1)S(1)} collective-permute-done((bf16[4,256,128]{2,1,0:T(8,128)(2,1)S(1)}, bf16[4,256,128]{2,1,0:T(8,128)(2,1)S(1)}, u32[]{:S(2)}, u32[]{:S(2)}) %collective-permute-start.10) | collective-permute-done | bytes 262176 | tf_op jit(solution)/shard_map/ppermute | solution.py:37
  35.3 1.3 %collective-permute-start.12 = (bf16[2,256,128]{2,1,0:T(8,128)(2,1)S(1)}, bf16[2,256,128]{2,1,0:T(8,128)(2,1)S(1)}, u32[]{:S(2)}, u32[]{:S(2)}) collective-permute-start(bf16[2,256,128]{2,1,0:T(8,128)(2,1)S(1)} %get-tuple-element.37), channel_id=1, source_target_pairs={{0,8},{4,12},{8,0},{12,4},{16,24},{20,28},{24,16},{28,20},{1,9},{5... | collective-permute-start | bytes 393224 | tf_op jit(solution)/shard_map/ppermute | solution.py:37
  36.6 0.0 collective-permute-done.9.refs_1_
  36.7 1.6 %collective-permute-start.14 = (bf16[32,1024]{1,0:T(8,128)(2,1)S(1)}, bf16[32,1024]{1,0:T(8,128)(2,1)S(1)}, u32[]{:S(2)}, u32[]{:S(2)}) collective-permute-start(bf16[32,1024]{1,0:T(8,128)(2,1)S(1)} %leaf_value.1.refs_2_.own_ref), channel_id=1, source_target_pairs={{0,4},{4,0},{8,12},{12,8},{16,20},{20,16},{24,28},{28,24},{1,5},{5... | collective-permute-start | bytes 196616 | tf_op jit(solution)/shard_map/ppermute | solution.py:37
  38.2 0.0 collective-permute-done.8.refs_1_
  38.3 2.7 %collective-permute-start.11 = (bf16[1,256,128]{2,1,0:T(8,128)(2,1)S(1)}, bf16[1,256,128]{2,1,0:T(8,128)(2,1)S(1)}, u32[]{:S(2)}, u32[]{:S(2)}) collective-permute-start(bf16[1,256,128]{2,1,0:T(8,128)(2,1)S(1)} %get-tuple-element.36), channel_id=1, source_target_pairs={{0,16},{4,20},{8,24},{12,28},{16,0},{20,4},{24,8},{28,12},{1,17},{... | collective-permute-start | bytes 196616 | tf_op jit(solution)/shard_map/ppermute | solution.py:37
  40.9 0.0 collective-permute-done.12.refs_1_
  41.0 2.7 %collective-permute-start.13 = (bf16[1,256,128]{2,1,0:T(8,128)(2,1)S(1)}, bf16[1,256,128]{2,1,0:T(8,128)(2,1)S(1)}, u32[]{:S(2)}, u32[]{:S(2)}) collective-permute-start(bf16[1,256,128]{2,1,0:T(8,128)(2,1)S(1)} %get-tuple-element.39), channel_id=1, source_target_pairs={{0,16},{4,20},{8,24},{12,28},{16,0},{20,4},{24,8},{28,12},{1,17},{... | collective-permute-start | bytes 196616 | tf_op jit(solution)/shard_map/ppermute | solution.py:37
  43.6 0.0 collective-permute-done.14.other_ref
  43.6 0.0 copy-done
  43.6 0.0 copy-done.1
  43.7 2.0 %update_first.1 = (bf16[1536,1024]{1,0:T(8,128)(2,1)}, f32[64,1024]{1,0:T(8,128)}, f32[8,128]{1,0:T(8,128)S(1)}) custom-call(s32[2]{0:T(128)S(1)} %pad_add_fusion.pos_ref, s32[12,128]{1,0:T(8,128)S(1)} %bitcast.8, bf16[32,1024]{1,0:T(8,128)(2,1)S(1)} %leaf_value.1.refs_2_.own_ref, bf16[32,1024]{1,0:T(8,128)(2,1)S(1)} %collective-permute-done.14.other_ref, ...), custom_call_target="tpu_custom_call" | custom-call | flops 3000000000 | tf_op jit(solution)/shard_map/update_first/pallas_call | solution.py:262
  45.7 2.0 %update_second.1 = (bf16[1536,1024]{1,0:T(8,128)(2,1)}, f32[8,128]{1,0:T(8,128)S(1)}) custom-call(s32[2]{0:T(128)S(1)} %pad_add_fusion.pos_ref, s32[12,128]{1,0:T(8,128)S(1)} %bitcast.9, bf16[32,1024]{1,0:T(8,128)(2,1)S(1)} %leaf_value.1.refs_2_.own_ref, bf16[32,1024]{1,0:T(8,128)(2,1)S(1)} %collective-permute-done.14.other_ref, ...), custom_call_target="tpu_custom_call", output_to_operand_aliasing={{0}: (6, {})} | custom-call | flops 3000000000 | tf_op jit(solution)/shard_map/update_second/pallas_call | solution.py:262
  47.7 0.0 collective-permute-done.11.refs_1_
  47.8 0.0 collective-permute-done.13.refs_3_
  47.8 0.7 %last_add.1 = f32[256,256]{1,0:T(8,128)} custom-call(f32[1,256,128]{2,1,0:T(8,128)S(1)} %get-tuple-element.35.refs_2_.refs_0_, bf16[1,256,128]{2,1,0:T(8,128)(2,1)S(1)} %collective-permute-done.11.refs_1_, f32[1,256,128]{2,1,0:T(8,128)S(1)} %get-tuple-element.38.after_ref.refs_2_, bf16[1,256,128]{2,1,0:T(8,128)(2,1)S(1)} %collective-permute-done.13.refs_3_, ...), custom_call_target="tpu_custom_call" | custom-call | tf_op jit(solution)/shard_map/last_add/pallas_call | solution.py:45
  (14 shorter events, 0.5 us)
Async XLA Ops:
  0.7 10.9 %copy-start.2 = (s32[8,1536]{1,0:T(8,128)S(1)}, s32[8,1536]{1,0:T(8,128)}, u32[]{:S(2)}) copy-start(s32[8,1536]{1,0:T(8,128)} %param.7) | copy-start | bytes 147460
  6.8 1.9 %collective-permute-start = (bf16[768,256]{1,0:T(8,128)(2,1)S(1)}, bf16[768,256]{1,0:T(8,128)(2,1)S(1)}, u32[]{:S(2)}, u32[]{:S(2)}) collective-permute-start(bf16[768,256]{1,0:T(8,128)(2,1)S(1)} %get-tuple-element.27), channel_id=1, source_target_pairs={{0,1},{1,0},{2,3},{3,2},{4,5},{5,4},{6,7},{7,6},{8,9},{9,8},{10,11... | collective-permute-start | bytes 1179656 | tf_op jit(solution)/shard_map/ppermute | solution.py:37
  8.7 8.6 %collective-permute-start.2 = (bf16[768,128]{1,0:T(8,128)(2,1)S(1)}, bf16[768,128]{1,0:T(8,128)(2,1)S(1)}, u32[]{:S(2)}, u32[]{:S(2)}) collective-permute-start(bf16[768,128]{1,0:T(8,128)(2,1)S(1)} %core_add.2.refs_2_.refs_0_), channel_id=1, source_target_pairs={{0,2},{1,3},{2,0},{3,1},{4,6},{5,7},{6,4},{7,5},{8,10},{9,11},{10,... | collective-permute-start | bytes 589832 | tf_op jit(solution)/shard_map/ppermute | solution.py:37
  11.7 5.8 %collective-permute-start.1 = (bf16[64,1024]{1,0:T(8,128)(2,1)S(1)}, bf16[64,1024]{1,0:T(8,128)(2,1)S(1)}, u32[]{:S(2)}, u32[]{:S(2)}) collective-permute-start(bf16[64,1024]{1,0:T(8,128)(2,1)S(1)} %get-tuple-element.29), channel_id=1, source_target_pairs={{0,4},{4,0},{8,12},{12,8},{16,20},{20,16},{24,28},{28,24},{1,5},{5... | collective-permute-start | bytes 393224 | tf_op jit(solution)/shard_map/ppermute | solution.py:37
  13.3 9.4 %collective-permute-start.4 = (bf16[768,128]{1,0:T(8,128)(2,1)S(1)}, bf16[768,128]{1,0:T(8,128)(2,1)S(1)}, u32[]{:S(2)}, u32[]{:S(2)}) collective-permute-start(bf16[768,128]{1,0:T(8,128)(2,1)S(1)} %core_add.3.refs_2_.refs_0_), channel_id=1, source_target_pairs={{0,2},{1,3},{2,0},{3,1},{4,6},{5,7},{6,4},{7,5},{8,10},{9,11},{10,... | collective-permute-start | bytes 589832 | tf_op jit(solution)/shard_map/ppermute | solution.py:37
  17.4 2.3 %collective-permute-start.5 = (bf16[768,128]{1,0:T(8,128)(2,1)S(1)}, bf16[768,128]{1,0:T(8,128)(2,1)S(1)}, u32[]{:S(2)}, u32[]{:S(2)}) collective-permute-start(bf16[768,128]{1,0:T(8,128)(2,1)S(1)} %feat_add.2.refs_2_.refs_0_), channel_id=1, source_target_pairs={{0,1},{1,0},{2,3},{3,2},{4,5},{5,4},{6,7},{7,6},{8,9},{9,8},{10,11... | collective-permute-start | bytes 589832 | tf_op jit(solution)/shard_map/ppermute | solution.py:37
  17.5 6.3 %collective-permute-start.3 = (bf16[64,1024]{1,0:T(8,128)(2,1)S(1)}, bf16[64,1024]{1,0:T(8,128)(2,1)S(1)}, u32[]{:S(2)}, u32[]{:S(2)}) collective-permute-start(bf16[64,1024]{1,0:T(8,128)(2,1)S(1)} %leaf_add.2.after_ref.refs_0_), channel_id=1, source_target_pairs={{0,8},{4,12},{8,0},{12,4},{16,24},{20,28},{24,16},{28,20},{1,9},{5... | collective-permute-start | bytes 393224 | tf_op jit(solution)/shard_map/ppermute | solution.py:37
  21.2 10.1 %collective-permute-start.7 = (bf16[4,256,128]{2,1,0:T(8,128)(2,1)S(1)}, bf16[4,256,128]{2,1,0:T(8,128)(2,1)S(1)}, u32[]{:S(2)}, u32[]{:S(2)}) collective-permute-start(bf16[4,256,128]{2,1,0:T(8,128)(2,1)S(1)} %hist_send.2.refs_2_), channel_id=1, source_target_pairs={{0,4},{4,0},{8,12},{12,8},{16,20},{20,16},{24,28},{28,24},{1,5},{5... | collective-permute-start | bytes 786440 | tf_op jit(solution)/shard_map/ppermute | solution.py:37
  22.8 1.5 %collective-permute-start.6 = (bf16[768,128]{1,0:T(8,128)(2,1)S(1)}, bf16[768,128]{1,0:T(8,128)(2,1)S(1)}, u32[]{:S(2)}, u32[]{:S(2)}) collective-permute-start(bf16[768,128]{1,0:T(8,128)(2,1)S(1)} %feat_add.3.refs_2_.refs_0_.refs_1_), channel_id=1, source_target_pairs={{0,1},{1,0},{2,3},{3,2},{4,5},{5,4},{6,7},{7,6},{8,9},{9,8},{10,11... | collective-permute-start | bytes 589832 | tf_op jit(solution)/shard_map/ppermute | solution.py:37
  23.9 19.8 %copy-start = (bf16[1536,1024]{1,0:T(8,128)(2,1)S(1)}, bf16[1536,1024]{1,0:T(8,128)(2,1)}, u32[]{:S(2)}) copy-start(bf16[1536,1024]{1,0:T(8,128)(2,1)} %pred_ref.3) | copy-start | bytes 9437188
  23.9 19.7 %copy-start.1 = (s32[1536]{0:T(1024)S(1)}, s32[1536]{0:T(1024)}, u32[]{:S(2)}) copy-start(s32[1536]{0:T(1024)} %param.8) | copy-start | bytes 18436
  25.8 9.5 %collective-permute-start.10 = (bf16[4,256,128]{2,1,0:T(8,128)(2,1)S(1)}, bf16[4,256,128]{2,1,0:T(8,128)(2,1)S(1)}, u32[]{:S(2)}, u32[]{:S(2)}) collective-permute-start(bf16[4,256,128]{2,1,0:T(8,128)(2,1)S(1)} %hist_send.3.after_ref), channel_id=1, source_target_pairs={{0,4},{4,0},{8,12},{12,8},{16,20},{20,16},{24,28},{28,24},{1,5},{5... | collective-permute-start | bytes 786440 | tf_op jit(solution)/shard_map/ppermute | solution.py:37
  27.1 9.5 %collective-permute-start.9 = (bf16[64,1024]{1,0:T(8,128)(2,1)S(1)}, bf16[64,1024]{1,0:T(8,128)(2,1)S(1)}, u32[]{:S(2)}, u32[]{:S(2)}) collective-permute-start(bf16[64,1024]{1,0:T(8,128)(2,1)S(1)} %leaf_add.3.after_ref.refs_0_), channel_id=1, source_target_pairs={{0,16},{4,20},{8,24},{12,28},{16,0},{20,4},{24,8},{28,12},{1,17},{... | collective-permute-start | bytes 393224 | tf_op jit(solution)/shard_map/ppermute | solution.py:37
  31.3 6.9 %collective-permute-start.8 = (bf16[2,256,128]{2,1,0:T(8,128)(2,1)S(1)}, bf16[2,256,128]{2,1,0:T(8,128)(2,1)S(1)}, u32[]{:S(2)}, u32[]{:S(2)}) collective-permute-start(bf16[2,256,128]{2,1,0:T(8,128)(2,1)S(1)} %get-tuple-element.33), channel_id=1, source_target_pairs={{0,8},{4,12},{8,0},{12,4},{16,24},{20,28},{24,16},{28,20},{1,9},{5... | collective-permute-start | bytes 393224 | tf_op jit(solution)/shard_map/ppermute | solution.py:37
  35.3 5.6 %collective-permute-start.12 = (bf16[2,256,128]{2,1,0:T(8,128)(2,1)S(1)}, bf16[2,256,128]{2,1,0:T(8,128)(2,1)S(1)}, u32[]{:S(2)}, u32[]{:S(2)}) collective-permute-start(bf16[2,256,128]{2,1,0:T(8,128)(2,1)S(1)} %get-tuple-element.37), channel_id=1, source_target_pairs={{0,8},{4,12},{8,0},{12,4},{16,24},{20,28},{24,16},{28,20},{1,9},{5... | collective-permute-start | bytes 393224 | tf_op jit(solution)/shard_map/ppermute | solution.py:37
  36.7 7.0 %collective-permute-start.14 = (bf16[32,1024]{1,0:T(8,128)(2,1)S(1)}, bf16[32,1024]{1,0:T(8,128)(2,1)S(1)}, u32[]{:S(2)}, u32[]{:S(2)}) collective-permute-start(bf16[32,1024]{1,0:T(8,128)(2,1)S(1)} %leaf_value.1.refs_2_.own_ref), channel_id=1, source_target_pairs={{0,4},{4,0},{8,12},{12,8},{16,20},{20,16},{24,28},{28,24},{1,5},{5... | collective-permute-start | bytes 196616 | tf_op jit(solution)/shard_map/ppermute | solution.py:37
  38.3 9.5 %collective-permute-start.11 = (bf16[1,256,128]{2,1,0:T(8,128)(2,1)S(1)}, bf16[1,256,128]{2,1,0:T(8,128)(2,1)S(1)}, u32[]{:S(2)}, u32[]{:S(2)}) collective-permute-start(bf16[1,256,128]{2,1,0:T(8,128)(2,1)S(1)} %get-tuple-element.36), channel_id=1, source_target_pairs={{0,16},{4,20},{8,24},{12,28},{16,0},{20,4},{24,8},{28,12},{1,17},{... | collective-permute-start | bytes 196616 | tf_op jit(solution)/shard_map/ppermute | solution.py:37
  41.0 6.8 %collective-permute-start.13 = (bf16[1,256,128]{2,1,0:T(8,128)(2,1)S(1)}, bf16[1,256,128]{2,1,0:T(8,128)(2,1)S(1)}, u32[]{:S(2)}, u32[]{:S(2)}) collective-permute-start(bf16[1,256,128]{2,1,0:T(8,128)(2,1)S(1)} %get-tuple-element.39), channel_id=1, source_target_pairs={{0,16},{4,20},{8,24},{12,28},{16,0},{20,4},{24,8},{28,12},{1,17},{... | collective-permute-start | bytes 196616 | tf_op jit(solution)/shard_map/ppermute | solution.py:37

commit v12 on v10

--- a/solution.py
+++ b/solution.py
@@ -307,7 +307,7 @@
 
     def core_add(p):
         nonlocal after
-        after = pair[p] = ordered(part_add(p, parts), sketch16, [keep, got], after, "core_add")
+        after = pair[p] = ordered(part_add(p, parts), sketch16, [keep, got], after, "core_add", 1.0)
         crossed[p] = [swap(after, "feat", nf, t) for t in range(2, nf, 2)]
 
     def feat_add(p):
@@ -327,7 +327,7 @@
         nonlocal after, leaf_state
         acc, recv, by = leaf_state
         if by < n:
-            after = ordered(add_kernel, sums16, [acc, recv], after, "leaf_add", 0 if by == 2 else 3.0)
+            after = ordered(add_kernel, sums16, [acc, recv], after, "leaf_add", 1.0 if by == 2 else 3.0)
             leaf_state = (after, swap(after, "rows", n, by), 2 * by)
         elif by == n:
             values16 = jax.ShapeDtypeStruct((LEAVES // 2, cols), bf16)
@@ -345,7 +345,7 @@
 
     def hist_send(p):
         nonlocal after
-        after, = hist_pass(codes, [owns[p]], [others[p]], per, n // 2, 1, bf16, after, (2.0, 3.0)[p])
+        after, = hist_pass(codes, [owns[p]], [others[p]], per, n // 2, 1, bf16, after, (1.0, 3.0)[p])
         backs[p] = swap(after, "rows", n, 1)
 
     def hist_keep():
@@ -364,8 +364,8 @@
         after = heres[p]
         backs[p] = swap(sent, "rows", n, 2 << level)
 
+    leaf_pack()
     core_add(0)
-    leaf_pack()
     core_add(1)
     leaf_step()
     feat_add(0)

time: 47.7 us -> 47.7 us (level)
  waiting for transfers between devices: 8.88 us -> 10.7 us
  starting transfers between devices: 21.9 us -> 20.1 us
    ppermute x15, waiting for transfers between devices: 8.88 us -> 10.7 us  [swap(): return lax.ppermute(x, axis, [(i, i ^ by) for i in range(size)])]
    ppermute x15, starting transfers between devices: 21.9 us -> 20.1 us  [swap(): return lax.ppermute(x, axis, [(i, i ^ by) for i in range(size)])]
  transfers between devices with their start and end apart: 15 -> 15, of which waited for: 7 -> 8; matrix products, arithmetic and copies ran while one was open for 0% -> 0% of each run, Pallas kernels for 19% -> 19%
where the time goes in v12:
time: 47.7 us; the launch traced here: 47.5 us
  starting transfers between devices  20.1 us (42%)
  Pallas kernels  15.8 us (33%)
  waiting for transfers between devices  10.7 us (22%)
  between operations  0.82 us (2%)
    ppermute x15, starting transfers between devices, swap(): return lax.ppermute(x, axis, [(i, i ^ by) for i in range(size)])  20.1 us
    ppermute x15, waiting for transfers between devices, swap(): return lax.ppermute(x, axis, [(i, i ^ by) for i in range(size)])  10.7 us
    pallas_call x1, Pallas kernels, rows_pass(): pl.pallas_call(rows_kernel, in_specs=[pl.BlockSpec(memory_space=pltpu.SME...  6.06 us
    pallas_call x3, Pallas kernels, hist_pass(): pl.pallas_call(functools.partial(hist_kernel, per=per, odd=odd, bits=bloc...  4.45 us
    pallas_call x2, Pallas kernels, update_pass(): pl.pallas_call(functools.partial(update_kernel, first=first), in_specs=[p...  4.07 us
    pallas_call x13, Pallas kernels, ordered(): pl.pallas_call(body, in_specs=[pl.BlockSpec(memory_space=pltpu.VMEM)] * l...  1.21 us
  transfers between devices with their start and end apart: 15, of which 8 were waited for; matrix products, arithmetic and copies ran while one was open for 0% of the time, Pallas kernels for 19%

profile of v12, /device:TPU:0, one launch (start us, length us, event | category | flops | bytes accessed | tf_op | source)
XLA Modules:
  0.0 47.5 jit_solution(1998489329851153816)
XLA Ops:
  0.6 0.1 pad_add_fusion.pos_ref
  0.7 6.1 %rows.1 = (bf16[768,256]{1,0:T(8,128)(2,1)S(1)}, bf16[768,256]{1,0:T(8,128)(2,1)S(1)}, f32[64,1024]{1,0:T(8,128)S(1)}, f32[64,1024]{1,0:T(8,128)S(1)}) custom-call(s32[2]{0:T(128)S(1)} %pad_add_fusion.pos_ref, s32[12,128]{1,0:T(8,128)} %bitcast.7, bf16[1536,1024]{1,0:T(8,128)(2,1)} %pred_ref.3, bf16[1536,1024]{1,0:T(8,128)(2,1)} %lab_hbm.1, ...), custom_call_target="tpu_custom_call" | custom-call | tf_op jit(solution)/shard_map/rows/pallas_call | solution.py:118
  6.8 0.0 copy-start.2
  6.8 0.5 %collective-permute-start.1 = (bf16[768,256]{1,0:T(8,128)(2,1)S(1)}, bf16[768,256]{1,0:T(8,128)(2,1)S(1)}, u32[]{:S(2)}, u32[]{:S(2)}) collective-permute-start(bf16[768,256]{1,0:T(8,128)(2,1)S(1)} %get-tuple-element.29), channel_id=1, source_target_pairs={{0,1},{1,0},{2,3},{3,2},{4,5},{5,4},{6,7},{7,6},{8,9},{9,8},{10,11... | collective-permute-start | bytes 1179656 | tf_op jit(solution)/shard_map/ppermute | solution.py:37
  7.3 2.6 %collective-permute-start = (bf16[64,1024]{1,0:T(8,128)(2,1)S(1)}, bf16[64,1024]{1,0:T(8,128)(2,1)S(1)}, u32[]{:S(2)}, u32[]{:S(2)}) collective-permute-start(bf16[64,1024]{1,0:T(8,128)(2,1)S(1)} %get-tuple-element.28), channel_id=1, source_target_pairs={{0,4},{4,0},{8,12},{12,8},{16,20},{20,16},{24,28},{28,24},{1,5},{5... | collective-permute-start | bytes 393224 | tf_op jit(solution)/shard_map/ppermute | solution.py:37
  9.9 0.0 collective-permute-done.1.refs_1_
  9.9 0.1 core_add.2.refs_2_.refs_0_
  10.0 1.7 %collective-permute-start.4 = (bf16[768,128]{1,0:T(8,128)(2,1)S(1)}, bf16[768,128]{1,0:T(8,128)(2,1)S(1)}, u32[]{:S(2)}, u32[]{:S(2)}) collective-permute-start(bf16[768,128]{1,0:T(8,128)(2,1)S(1)} %core_add.2.refs_2_.refs_0_), channel_id=1, source_target_pairs={{0,2},{1,3},{2,0},{3,1},{4,6},{5,7},{6,4},{7,5},{8,10},{9,11},{10,... | collective-permute-start | bytes 589832 | tf_op jit(solution)/shard_map/ppermute | solution.py:37
  11.7 0.0 copy-done.2
  11.7 0.1 core_add.3.refs_2_.refs_0_
  11.7 0.5 collective-permute-start.3
  12.2 1.9 %collective-permute-done.refs_1_ = bf16[64,1024]{1,0:T(8,128)(2,1)S(1)} collective-permute-done((bf16[64,1024]{1,0:T(8,128)(2,1)S(1)}, bf16[64,1024]{1,0:T(8,128)(2,1)S(1)}, u32[]{:S(2)}, u32[]{:S(2)}) %collective-permute-start) | collective-permute-done | bytes 131104 | tf_op jit(solution)/shard_map/ppermute | solution.py:37
  14.1 1.9 %collective-permute-start.2 = (bf16[64,1024]{1,0:T(8,128)(2,1)S(1)}, bf16[64,1024]{1,0:T(8,128)(2,1)S(1)}, u32[]{:S(2)}, u32[]{:S(2)}) collective-permute-start(bf16[64,1024]{1,0:T(8,128)(2,1)S(1)} %leaf_add.2.refs_2_.refs_0_), channel_id=1, source_target_pairs={{0,8},{4,12},{8,0},{12,4},{16,24},{20,28},{24,16},{28,20},{1,9},{5... | collective-permute-start | bytes 393224 | tf_op jit(solution)/shard_map/ppermute | solution.py:37
  16.0 1.8 %collective-permute-done.4.refs_1_ = bf16[768,128]{1,0:T(8,128)(2,1)S(1)} collective-permute-done((bf16[768,128]{1,0:T(8,128)(2,1)S(1)}, bf16[768,128]{1,0:T(8,128)(2,1)S(1)}, u32[]{:S(2)}, u32[]{:S(2)}) %collective-permute-start.4) | collective-permute-done | bytes 196640 | tf_op jit(solution)/shard_map/ppermute | solution.py:37
  17.8 0.1 collective-permute-start.5
  17.9 1.4 %collective-permute-done.5.refs_1_.refs_2_ = bf16[768,128]{1,0:T(8,128)(2,1)S(1)} collective-permute-done((bf16[768,128]{1,0:T(8,128)(2,1)S(1)}, bf16[768,128]{1,0:T(8,128)(2,1)S(1)}, u32[]{:S(2)}, u32[]{:S(2)}) %collective-permute-start.5) | collective-permute-done | bytes 196640 | tf_op jit(solution)/shard_map/ppermute | solution.py:37
  19.3 1.5 %hist_send.2.refs_2_ = bf16[4,256,128]{2,1,0:T(8,128)(2,1)S(1)} custom-call(s32[2,8,768]{2,1,0:T(8,128)S(1)} %fusion.codes_ref, bf16[768,128]{1,0:T(8,128)(2,1)S(1)} %feat_add.2.after_ref.refs_0_, bf16[768,128]{1,0:T(8,128)(2,1)S(1)} %feat_add.2.after_ref.refs_0_, bf16[768,128]{1,0:T(8,128)(2,1)S(1)} %collective-permute-done.5.refs_1_.refs_2_), custom_call_target="tpu_custom_call" | custom-call | flops 1000000000 | tf_op jit(solution)/shard_map/hist_send/pallas_call | solution.py:207
  20.8 1.7 %collective-permute-start.7 = (bf16[4,256,128]{2,1,0:T(8,128)(2,1)S(1)}, bf16[4,256,128]{2,1,0:T(8,128)(2,1)S(1)}, u32[]{:S(2)}, u32[]{:S(2)}) collective-permute-start(bf16[4,256,128]{2,1,0:T(8,128)(2,1)S(1)} %hist_send.2.refs_2_), channel_id=1, source_target_pairs={{0,4},{4,0},{8,12},{12,8},{16,20},{20,16},{24,28},{28,24},{1,5},{5... | collective-permute-start | bytes 786440 | tf_op jit(solution)/shard_map/ppermute | solution.py:37
  22.5 0.0 collective-permute-done.3.refs_1_
  22.5 0.1 collective-permute-start.6
  22.6 0.0 collective-permute-done.2.refs_1_
  22.7 2.6 %collective-permute-start.10 = (bf16[64,1024]{1,0:T(8,128)(2,1)S(1)}, bf16[64,1024]{1,0:T(8,128)(2,1)S(1)}, u32[]{:S(2)}, u32[]{:S(2)}) collective-permute-start(bf16[64,1024]{1,0:T(8,128)(2,1)S(1)} %leaf_add.3.after_ref.refs_0_), channel_id=1, source_target_pairs={{0,16},{4,20},{8,24},{12,28},{16,0},{20,4},{24,8},{28,12},{1,17},{... | collective-permute-start | bytes 393224 | tf_op jit(solution)/shard_map/ppermute | solution.py:37
  25.3 0.0 collective-permute-done.6.refs_1_.refs_3_
  25.3 1.5 %hist_send.3.after_ref = bf16[4,256,128]{2,1,0:T(8,128)(2,1)S(1)} custom-call(s32[2,8,768]{2,1,0:T(8,128)S(1)} %fusion.codes_ref, bf16[64,1024]{1,0:T(8,128)(2,1)S(1)} %leaf_add.3.after_ref.refs_0_, bf16[768,128]{1,0:T(8,128)(2,1)S(1)} %feat_add.3.refs_2_.refs_0_.refs_1_, bf16[768,128]{1,0:T(8,128)(2,1)S(1)} %collective-permute-done.6.refs_1_.refs_3_), custom_call_target="tpu_custom_call" | custom-call | flops 3000000000 | tf_op jit(solution)/shard_map/hist_send/pallas_call | solution.py:207
  26.8 0.6 %collective-permute-start.9 = (bf16[4,256,128]{2,1,0:T(8,128)(2,1)S(1)}, bf16[4,256,128]{2,1,0:T(8,128)(2,1)S(1)}, u32[]{:S(2)}, u32[]{:S(2)}) collective-permute-start(bf16[4,256,128]{2,1,0:T(8,128)(2,1)S(1)} %hist_send.3.after_ref), channel_id=1, source_target_pairs={{0,4},{4,0},{8,12},{12,8},{16,20},{20,16},{24,28},{28,24},{1,5},{5... | collective-permute-start | bytes 786440 | tf_op jit(solution)/shard_map/ppermute | solution.py:37
  27.4 1.5 %hist_keep.1 = (f32[4,256,128]{2,1,0:T(8,128)S(1)}, f32[4,256,128]{2,1,0:T(8,128)S(1)}) custom-call(s32[2,8,768]{2,1,0:T(8,128)S(1)} %fusion.codes_ref, bf16[4,256,128]{2,1,0:T(8,128)(2,1)S(1)} %hist_send.3.after_ref, bf16[768,128]{1,0:T(8,128)(2,1)S(1)} %feat_add.2.after_ref.refs_0_, bf16[768,128]{1,0:T(8,128)(2,1)S(1)} %feat_add.3.refs_2_.refs_0_.refs_1_, ...), custom_call_target="tpu_custom_call" | custom-call | flops 3000000000 | tf_op jit(solution)/shard_map/hist_keep/pallas_call | solution.py:207
  28.9 0.0 copy-start
  28.9 0.0 copy-start.1
  29.0 0.3 collective-permute-done.7.refs_1_
  29.3 1.8 %collective-permute-start.8 = (bf16[2,256,128]{2,1,0:T(8,128)(2,1)S(1)}, bf16[2,256,128]{2,1,0:T(8,128)(2,1)S(1)}, u32[]{:S(2)}, u32[]{:S(2)}) collective-permute-start(bf16[2,256,128]{2,1,0:T(8,128)(2,1)S(1)} %get-tuple-element.33), channel_id=1, source_target_pairs={{0,8},{4,12},{8,0},{12,4},{16,24},{20,28},{24,16},{28,20},{1,9},{5... | collective-permute-start | bytes 393224 | tf_op jit(solution)/shard_map/ppermute | solution.py:37
  31.0 1.4 %collective-permute-done.10.refs_1_ = bf16[64,1024]{1,0:T(8,128)(2,1)S(1)} collective-permute-done((bf16[64,1024]{1,0:T(8,128)(2,1)S(1)}, bf16[64,1024]{1,0:T(8,128)(2,1)S(1)}, u32[]{:S(2)}, u32[]{:S(2)}) %collective-permute-start.10) | collective-permute-done | bytes 131104 | tf_op jit(solution)/shard_map/ppermute | solution.py:37
  32.5 0.7 %collective-permute-start.13 = (bf16[32,1024]{1,0:T(8,128)(2,1)S(1)}, bf16[32,1024]{1,0:T(8,128)(2,1)S(1)}, u32[]{:S(2)}, u32[]{:S(2)}) collective-permute-start(bf16[32,1024]{1,0:T(8,128)(2,1)S(1)} %leaf_value.1.refs_2_.own_ref), channel_id=1, source_target_pairs={{0,4},{4,0},{8,12},{12,8},{16,20},{20,16},{24,28},{28,24},{1,5},{5... | collective-permute-start | bytes 196616 | tf_op jit(solution)/shard_map/ppermute | solution.py:37
  33.2 2.5 %collective-permute-done.9.refs_1_ = bf16[4,256,128]{2,1,0:T(8,128)(2,1)S(1)} collective-permute-done((bf16[4,256,128]{2,1,0:T(8,128)(2,1)S(1)}, bf16[4,256,128]{2,1,0:T(8,128)(2,1)S(1)}, u32[]{:S(2)}, u32[]{:S(2)}) %collective-permute-start.9) | collective-permute-done | bytes 262176 | tf_op jit(solution)/shard_map/ppermute | solution.py:37
  35.8 1.9 %collective-permute-start.12 = (bf16[2,256,128]{2,1,0:T(8,128)(2,1)S(1)}, bf16[2,256,128]{2,1,0:T(8,128)(2,1)S(1)}, u32[]{:S(2)}, u32[]{:S(2)}) collective-permute-start(bf16[2,256,128]{2,1,0:T(8,128)(2,1)S(1)} %get-tuple-element.37), channel_id=1, source_target_pairs={{0,8},{4,12},{8,0},{12,4},{16,24},{20,28},{24,16},{28,20},{1,9},{5... | collective-permute-start | bytes 393224 | tf_op jit(solution)/shard_map/ppermute | solution.py:37
  37.7 0.0 collective-permute-done.8.refs_1_
  37.7 1.6 %collective-permute-start.11 = (bf16[1,256,128]{2,1,0:T(8,128)(2,1)S(1)}, bf16[1,256,128]{2,1,0:T(8,128)(2,1)S(1)}, u32[]{:S(2)}, u32[]{:S(2)}) collective-permute-start(bf16[1,256,128]{2,1,0:T(8,128)(2,1)S(1)} %get-tuple-element.36), channel_id=1, source_target_pairs={{0,16},{4,20},{8,24},{12,28},{16,0},{20,4},{24,8},{28,12},{1,17},{... | collective-permute-start | bytes 196616 | tf_op jit(solution)/shard_map/ppermute | solution.py:37
  39.3 0.0 collective-permute-done.13.other_ref
  39.3 0.0 copy-done
  39.3 0.0 copy-done.1
  39.3 2.0 %update_first.1 = (bf16[1536,1024]{1,0:T(8,128)(2,1)}, f32[64,1024]{1,0:T(8,128)}, f32[8,128]{1,0:T(8,128)S(1)}) custom-call(s32[2]{0:T(128)S(1)} %pad_add_fusion.pos_ref, s32[12,128]{1,0:T(8,128)S(1)} %bitcast.8, bf16[32,1024]{1,0:T(8,128)(2,1)S(1)} %leaf_value.1.refs_2_.own_ref, bf16[32,1024]{1,0:T(8,128)(2,1)S(1)} %collective-permute-done.13.other_ref, ...), custom_call_target="tpu_custom_call" | custom-call | flops 3000000000 | tf_op jit(solution)/shard_map/update_first/pallas_call | solution.py:262
  41.4 0.1 collective-permute-done.12.refs_1_
  41.6 1.9 %collective-permute-start.14 = (bf16[1,256,128]{2,1,0:T(8,128)(2,1)S(1)}, bf16[1,256,128]{2,1,0:T(8,128)(2,1)S(1)}, u32[]{:S(2)}, u32[]{:S(2)}) collective-permute-start(bf16[1,256,128]{2,1,0:T(8,128)(2,1)S(1)} %get-tuple-element.40), channel_id=1, source_target_pairs={{0,16},{4,20},{8,24},{12,28},{16,0},{20,4},{24,8},{28,12},{1,17},{... | collective-permute-start | bytes 196616 | tf_op jit(solution)/shard_map/ppermute | solution.py:37
  43.4 2.0 %update_second.1 = (bf16[1536,1024]{1,0:T(8,128)(2,1)}, f32[8,128]{1,0:T(8,128)S(1)}) custom-call(s32[2]{0:T(128)S(1)} %pad_add_fusion.pos_ref, s32[12,128]{1,0:T(8,128)S(1)} %bitcast.9, bf16[32,1024]{1,0:T(8,128)(2,1)S(1)} %leaf_value.1.refs_2_.own_ref, bf16[32,1024]{1,0:T(8,128)(2,1)S(1)} %collective-permute-done.13.other_ref, ...), custom_call_target="tpu_custom_call", output_to_operand_aliasing={{0}: (6, {})} | custom-call | flops 3000000000 | tf_op jit(solution)/shard_map/update_second/pallas_call | solution.py:262
  45.5 0.0 collective-permute-done.11.refs_1_
  45.5 1.3 %collective-permute-done.14.refs_3_ = bf16[1,256,128]{2,1,0:T(8,128)(2,1)S(1)} collective-permute-done((bf16[1,256,128]{2,1,0:T(8,128)(2,1)S(1)}, bf16[1,256,128]{2,1,0:T(8,128)(2,1)S(1)}, u32[]{:S(2)}, u32[]{:S(2)}) %collective-permute-start.14) | collective-permute-done | bytes 65568 | tf_op jit(solution)/shard_map/ppermute | solution.py:37
  46.8 0.7 %last_add.1 = f32[256,256]{1,0:T(8,128)} custom-call(f32[1,256,128]{2,1,0:T(8,128)S(1)} %get-tuple-element.35.after_ref.refs_0_, bf16[1,256,128]{2,1,0:T(8,128)(2,1)S(1)} %collective-permute-done.11.refs_1_, f32[1,256,128]{2,1,0:T(8,128)S(1)} %get-tuple-element.39.after_ref.refs_2_, bf16[1,256,128]{2,1,0:T(8,128)(2,1)S(1)} %collective-permute-done.14.refs_3_, ...), custom_call_target="tpu_custom_call" | custom-call | tf_op jit(solution)/shard_map/last_add/pallas_call | solution.py:45
  (12 shorter events, 0.4 us)
Async XLA Ops:
  6.8 4.9 %copy-start.2 = (s32[8,1536]{1,0:T(8,128)S(1)}, s32[8,1536]{1,0:T(8,128)}, u32[]{:S(2)}) copy-start(s32[8,1536]{1,0:T(8,128)} %param.7) | copy-start | bytes 147460
  6.8 3.1 %collective-permute-start.1 = (bf16[768,256]{1,0:T(8,128)(2,1)S(1)}, bf16[768,256]{1,0:T(8,128)(2,1)S(1)}, u32[]{:S(2)}, u32[]{:S(2)}) collective-permute-start(bf16[768,256]{1,0:T(8,128)(2,1)S(1)} %get-tuple-element.29), channel_id=1, source_target_pairs={{0,1},{1,0},{2,3},{3,2},{4,5},{5,4},{6,7},{7,6},{8,9},{9,8},{10,11... | collective-permute-start | bytes 1179656 | tf_op jit(solution)/shard_map/ppermute | solution.py:37
  7.3 6.7 %collective-permute-start = (bf16[64,1024]{1,0:T(8,128)(2,1)S(1)}, bf16[64,1024]{1,0:T(8,128)(2,1)S(1)}, u32[]{:S(2)}, u32[]{:S(2)}) collective-permute-start(bf16[64,1024]{1,0:T(8,128)(2,1)S(1)} %get-tuple-element.28), channel_id=1, source_target_pairs={{0,4},{4,0},{8,12},{12,8},{16,20},{20,16},{24,28},{28,24},{1,5},{5... | collective-permute-start | bytes 393224 | tf_op jit(solution)/shard_map/ppermute | solution.py:37
  10.0 7.8 %collective-permute-start.4 = (bf16[768,128]{1,0:T(8,128)(2,1)S(1)}, bf16[768,128]{1,0:T(8,128)(2,1)S(1)}, u32[]{:S(2)}, u32[]{:S(2)}) collective-permute-start(bf16[768,128]{1,0:T(8,128)(2,1)S(1)} %core_add.2.refs_2_.refs_0_), channel_id=1, source_target_pairs={{0,2},{1,3},{2,0},{3,1},{4,6},{5,7},{6,4},{7,5},{8,10},{9,11},{10,... | collective-permute-start | bytes 589832 | tf_op jit(solution)/shard_map/ppermute | solution.py:37
  11.7 10.7 %collective-permute-start.3 = (bf16[768,128]{1,0:T(8,128)(2,1)S(1)}, bf16[768,128]{1,0:T(8,128)(2,1)S(1)}, u32[]{:S(2)}, u32[]{:S(2)}) collective-permute-start(bf16[768,128]{1,0:T(8,128)(2,1)S(1)} %core_add.3.refs_2_.refs_0_), channel_id=1, source_target_pairs={{0,2},{1,3},{2,0},{3,1},{4,6},{5,7},{6,4},{7,5},{8,10},{9,11},{10,... | collective-permute-start | bytes 589832 | tf_op jit(solution)/shard_map/ppermute | solution.py:37
  14.1 8.5 %collective-permute-start.2 = (bf16[64,1024]{1,0:T(8,128)(2,1)S(1)}, bf16[64,1024]{1,0:T(8,128)(2,1)S(1)}, u32[]{:S(2)}, u32[]{:S(2)}) collective-permute-start(bf16[64,1024]{1,0:T(8,128)(2,1)S(1)} %leaf_add.2.refs_2_.refs_0_), channel_id=1, source_target_pairs={{0,8},{4,12},{8,0},{12,4},{16,24},{20,28},{24,16},{28,20},{1,9},{5... | collective-permute-start | bytes 393224 | tf_op jit(solution)/shard_map/ppermute | solution.py:37
  17.8 1.5 %collective-permute-start.5 = (bf16[768,128]{1,0:T(8,128)(2,1)S(1)}, bf16[768,128]{1,0:T(8,128)(2,1)S(1)}, u32[]{:S(2)}, u32[]{:S(2)}) collective-permute-start(bf16[768,128]{1,0:T(8,128)(2,1)S(1)} %feat_add.2.after_ref.refs_0_), channel_id=1, source_target_pairs={{0,1},{1,0},{2,3},{3,2},{4,5},{5,4},{6,7},{7,6},{8,9},{9,8},{10,11... | collective-permute-start | bytes 589832 | tf_op jit(solution)/shard_map/ppermute | solution.py:37
  20.8 8.4 %collective-permute-start.7 = (bf16[4,256,128]{2,1,0:T(8,128)(2,1)S(1)}, bf16[4,256,128]{2,1,0:T(8,128)(2,1)S(1)}, u32[]{:S(2)}, u32[]{:S(2)}) collective-permute-start(bf16[4,256,128]{2,1,0:T(8,128)(2,1)S(1)} %hist_send.2.refs_2_), channel_id=1, source_target_pairs={{0,4},{4,0},{8,12},{12,8},{16,20},{20,16},{24,28},{28,24},{1,5},{5... | collective-permute-start | bytes 786440 | tf_op jit(solution)/shard_map/ppermute | solution.py:37
  22.5 2.8 %collective-permute-start.6 = (bf16[768,128]{1,0:T(8,128)(2,1)S(1)}, bf16[768,128]{1,0:T(8,128)(2,1)S(1)}, u32[]{:S(2)}, u32[]{:S(2)}) collective-permute-start(bf16[768,128]{1,0:T(8,128)(2,1)S(1)} %feat_add.3.refs_2_.refs_0_.refs_1_), channel_id=1, source_target_pairs={{0,1},{1,0},{2,3},{3,2},{4,5},{5,4},{6,7},{7,6},{8,9},{9,8},{10,11... | collective-permute-start | bytes 589832 | tf_op jit(solution)/shard_map/ppermute | solution.py:37
  22.7 9.7 %collective-permute-start.10 = (bf16[64,1024]{1,0:T(8,128)(2,1)S(1)}, bf16[64,1024]{1,0:T(8,128)(2,1)S(1)}, u32[]{:S(2)}, u32[]{:S(2)}) collective-permute-start(bf16[64,1024]{1,0:T(8,128)(2,1)S(1)} %leaf_add.3.after_ref.refs_0_), channel_id=1, source_target_pairs={{0,16},{4,20},{8,24},{12,28},{16,0},{20,4},{24,8},{28,12},{1,17},{... | collective-permute-start | bytes 393224 | tf_op jit(solution)/shard_map/ppermute | solution.py:37
  26.8 8.9 %collective-permute-start.9 = (bf16[4,256,128]{2,1,0:T(8,128)(2,1)S(1)}, bf16[4,256,128]{2,1,0:T(8,128)(2,1)S(1)}, u32[]{:S(2)}, u32[]{:S(2)}) collective-permute-start(bf16[4,256,128]{2,1,0:T(8,128)(2,1)S(1)} %hist_send.3.after_ref), channel_id=1, source_target_pairs={{0,4},{4,0},{8,12},{12,8},{16,20},{20,16},{24,28},{28,24},{1,5},{5... | collective-permute-start | bytes 786440 | tf_op jit(solution)/shard_map/ppermute | solution.py:37
  28.9 10.4 %copy-start = (bf16[1536,1024]{1,0:T(8,128)(2,1)S(1)}, bf16[1536,1024]{1,0:T(8,128)(2,1)}, u32[]{:S(2)}) copy-start(bf16[1536,1024]{1,0:T(8,128)(2,1)} %pred_ref.3) | copy-start | bytes 9437188
  28.9 10.4 %copy-start.1 = (s32[1536]{0:T(1024)S(1)}, s32[1536]{0:T(1024)}, u32[]{:S(2)}) copy-start(s32[1536]{0:T(1024)} %param.8) | copy-start | bytes 18436
  29.3 8.4 %collective-permute-start.8 = (bf16[2,256,128]{2,1,0:T(8,128)(2,1)S(1)}, bf16[2,256,128]{2,1,0:T(8,128)(2,1)S(1)}, u32[]{:S(2)}, u32[]{:S(2)}) collective-permute-start(bf16[2,256,128]{2,1,0:T(8,128)(2,1)S(1)} %get-tuple-element.33), channel_id=1, source_target_pairs={{0,8},{4,12},{8,0},{12,4},{16,24},{20,28},{24,16},{28,20},{1,9},{5... | collective-permute-start | bytes 393224 | tf_op jit(solution)/shard_map/ppermute | solution.py:37
  32.5 6.9 %collective-permute-start.13 = (bf16[32,1024]{1,0:T(8,128)(2,1)S(1)}, bf16[32,1024]{1,0:T(8,128)(2,1)S(1)}, u32[]{:S(2)}, u32[]{:S(2)}) collective-permute-start(bf16[32,1024]{1,0:T(8,128)(2,1)S(1)} %leaf_value.1.refs_2_.own_ref), channel_id=1, source_target_pairs={{0,4},{4,0},{8,12},{12,8},{16,20},{20,16},{24,28},{28,24},{1,5},{5... | collective-permute-start | bytes 196616 | tf_op jit(solution)/shard_map/ppermute | solution.py:37
  35.8 5.7 %collective-permute-start.12 = (bf16[2,256,128]{2,1,0:T(8,128)(2,1)S(1)}, bf16[2,256,128]{2,1,0:T(8,128)(2,1)S(1)}, u32[]{:S(2)}, u32[]{:S(2)}) collective-permute-start(bf16[2,256,128]{2,1,0:T(8,128)(2,1)S(1)} %get-tuple-element.37), channel_id=1, source_target_pairs={{0,8},{4,12},{8,0},{12,4},{16,24},{20,28},{24,16},{28,20},{1,9},{5... | collective-permute-start | bytes 393224 | tf_op jit(solution)/shard_map/ppermute | solution.py:37
  37.7 7.8 %collective-permute-start.11 = (bf16[1,256,128]{2,1,0:T(8,128)(2,1)S(1)}, bf16[1,256,128]{2,1,0:T(8,128)(2,1)S(1)}, u32[]{:S(2)}, u32[]{:S(2)}) collective-permute-start(bf16[1,256,128]{2,1,0:T(8,128)(2,1)S(1)} %get-tuple-element.36), channel_id=1, source_target_pairs={{0,16},{4,20},{8,24},{12,28},{16,0},{20,4},{24,8},{28,12},{1,17},{... | collective-permute-start | bytes 196616 | tf_op jit(solution)/shard_map/ppermute | solution.py:37
  41.6 5.2 %collective-permute-start.14 = (bf16[1,256,128]{2,1,0:T(8,128)(2,1)S(1)}, bf16[1,256,128]{2,1,0:T(8,128)(2,1)S(1)}, u32[]{:S(2)}, u32[]{:S(2)}) collective-permute-start(bf16[1,256,128]{2,1,0:T(8,128)(2,1)S(1)} %get-tuple-element.40), channel_id=1, source_target_pairs={{0,16},{4,20},{8,24},{12,28},{16,0},{20,4},{24,8},{28,12},{1,17},{... | collective-permute-start | bytes 196616 | tf_op jit(solution)/shard_map/ppermute | solution.py:37

commit v13 on v12

--- a/solution.py
+++ b/solution.py
@@ -374,14 +374,13 @@
     leaf_step()
     hist_send(1)
     hist_keep()
-    hist_add(0, 0)
-    leaf_step()
-    hist_add(1, 0)
-    for level in range(1, levels):
+    for level in range(levels):
         hist_add(0, level)
         if level == levels - 1:
             update()
         hist_add(1, level)
+        if level == 0:
+            leaf_step()
     update()
     histograms = ordered(
         last_kernel, jax.ShapeDtypeStruct((per * feats, width * parts), f32),

time: 47.7 us -> 49.8 us (1.044)
  waiting for transfers between devices: 10.7 us -> 12 us
  starting transfers between devices: 20.1 us -> 20.9 us
    ppermute x15, waiting for transfers between devices: 10.7 us -> 12 us  [swap(): return lax.ppermute(x, axis, [(i, i ^ by) for i in range(size)])]
    ppermute x15, starting transfers between devices: 20.1 us -> 20.9 us  [swap(): return lax.ppermute(x, axis, [(i, i ^ by) for i in range(size)])]
  transfers between devices with their start and end apart: 15 -> 15, of which waited for: 8 -> 6; matrix products, arithmetic and copies ran while one was open for 0% -> 0% of each run, Pallas kernels for 19% -> 18%
where the time goes in v13:
time: 49.8 us; the launch traced here: 49.6 us
  starting transfers between devices  20.9 us (42%)
  Pallas kernels  15.8 us (32%)
  waiting for transfers between devices  12 us (24%)
  between operations  0.84 us (2%)
    ppermute x15, starting transfers between devices, swap(): return lax.ppermute(x, axis, [(i, i ^ by) for i in range(size)])  20.9 us
    ppermute x15, waiting for transfers between devices, swap(): return lax.ppermute(x, axis, [(i, i ^ by) for i in range(size)])  12 us
    pallas_call x1, Pallas kernels, rows_pass(): pl.pallas_call(rows_kernel, in_specs=[pl.BlockSpec(memory_space=pltpu.SME...  6.06 us
    pallas_call x3, Pallas kernels, hist_pass(): pl.pallas_call(functools.partial(hist_kernel, per=per, odd=odd, bits=bloc...  4.45 us
    pallas_call x2, Pallas kernels, update_pass(): pl.pallas_call(functools.partial(update_kernel, first=first), in_specs=[p...  4.07 us
    pallas_call x13, Pallas kernels, ordered(): pl.pallas_call(body, in_specs=[pl.BlockSpec(memory_space=pltpu.VMEM)] * l...  1.22 us
  transfers between devices with their start and end apart: 15, of which 6 were waited for; matrix products, arithmetic and copies ran while one was open for 0% of the time, Pallas kernels for 18%

profile of v13, /device:TPU:0, one launch (start us, length us, event | category | flops | bytes accessed | tf_op | source)
XLA Modules:
  0.0 49.6 jit_solution(1233835956080774123)
XLA Ops:
  0.6 0.1 pad_add_fusion.pos_ref
  0.7 6.1 %rows.1 = (bf16[768,256]{1,0:T(8,128)(2,1)S(1)}, bf16[768,256]{1,0:T(8,128)(2,1)S(1)}, f32[64,1024]{1,0:T(8,128)S(1)}, f32[64,1024]{1,0:T(8,128)S(1)}) custom-call(s32[2]{0:T(128)S(1)} %pad_add_fusion.pos_ref, s32[12,128]{1,0:T(8,128)} %bitcast.7, bf16[1536,1024]{1,0:T(8,128)(2,1)} %pred_ref.3, bf16[1536,1024]{1,0:T(8,128)(2,1)} %lab_hbm.1, ...), custom_call_target="tpu_custom_call" | custom-call | tf_op jit(solution)/shard_map/rows/pallas_call | solution.py:118
  6.8 0.0 copy-start.2
  6.8 0.5 %collective-permute-start.1 = (bf16[768,256]{1,0:T(8,128)(2,1)S(1)}, bf16[768,256]{1,0:T(8,128)(2,1)S(1)}, u32[]{:S(2)}, u32[]{:S(2)}) collective-permute-start(bf16[768,256]{1,0:T(8,128)(2,1)S(1)} %get-tuple-element.29), channel_id=1, source_target_pairs={{0,1},{1,0},{2,3},{3,2},{4,5},{5,4},{6,7},{7,6},{8,9},{9,8},{10,11... | collective-permute-start | bytes 1179656 | tf_op jit(solution)/shard_map/ppermute | solution.py:37
  7.3 2.6 %collective-permute-start = (bf16[64,1024]{1,0:T(8,128)(2,1)S(1)}, bf16[64,1024]{1,0:T(8,128)(2,1)S(1)}, u32[]{:S(2)}, u32[]{:S(2)}) collective-permute-start(bf16[64,1024]{1,0:T(8,128)(2,1)S(1)} %get-tuple-element.28), channel_id=1, source_target_pairs={{0,4},{4,0},{8,12},{12,8},{16,20},{20,16},{24,28},{28,24},{1,5},{5... | collective-permute-start | bytes 393224 | tf_op jit(solution)/shard_map/ppermute | solution.py:37
  9.9 0.0 collective-permute-done.1.refs_1_
  9.9 0.1 core_add.2.refs_2_.refs_0_
  10.0 1.7 %collective-permute-start.4 = (bf16[768,128]{1,0:T(8,128)(2,1)S(1)}, bf16[768,128]{1,0:T(8,128)(2,1)S(1)}, u32[]{:S(2)}, u32[]{:S(2)}) collective-permute-start(bf16[768,128]{1,0:T(8,128)(2,1)S(1)} %core_add.2.refs_2_.refs_0_), channel_id=1, source_target_pairs={{0,2},{1,3},{2,0},{3,1},{4,6},{5,7},{6,4},{7,5},{8,10},{9,11},{10,... | collective-permute-start | bytes 589832 | tf_op jit(solution)/shard_map/ppermute | solution.py:37
  11.7 0.0 copy-done.2
  11.7 0.1 core_add.3.refs_2_.refs_0_
  11.7 0.5 collective-permute-start.3
  12.2 1.9 %collective-permute-done.refs_1_ = bf16[64,1024]{1,0:T(8,128)(2,1)S(1)} collective-permute-done((bf16[64,1024]{1,0:T(8,128)(2,1)S(1)}, bf16[64,1024]{1,0:T(8,128)(2,1)S(1)}, u32[]{:S(2)}, u32[]{:S(2)}) %collective-permute-start) | collective-permute-done | bytes 131104 | tf_op jit(solution)/shard_map/ppermute | solution.py:37
  14.1 1.9 %collective-permute-start.2 = (bf16[64,1024]{1,0:T(8,128)(2,1)S(1)}, bf16[64,1024]{1,0:T(8,128)(2,1)S(1)}, u32[]{:S(2)}, u32[]{:S(2)}) collective-permute-start(bf16[64,1024]{1,0:T(8,128)(2,1)S(1)} %leaf_add.2.refs_2_.refs_0_), channel_id=1, source_target_pairs={{0,8},{4,12},{8,0},{12,4},{16,24},{20,28},{24,16},{28,20},{1,9},{5... | collective-permute-start | bytes 393224 | tf_op jit(solution)/shard_map/ppermute | solution.py:37
  16.0 1.8 %collective-permute-done.4.refs_1_ = bf16[768,128]{1,0:T(8,128)(2,1)S(1)} collective-permute-done((bf16[768,128]{1,0:T(8,128)(2,1)S(1)}, bf16[768,128]{1,0:T(8,128)(2,1)S(1)}, u32[]{:S(2)}, u32[]{:S(2)}) %collective-permute-start.4) | collective-permute-done | bytes 196640 | tf_op jit(solution)/shard_map/ppermute | solution.py:37
  17.8 0.1 collective-permute-start.5
  17.9 1.4 %collective-permute-done.5.refs_1_.refs_2_ = bf16[768,128]{1,0:T(8,128)(2,1)S(1)} collective-permute-done((bf16[768,128]{1,0:T(8,128)(2,1)S(1)}, bf16[768,128]{1,0:T(8,128)(2,1)S(1)}, u32[]{:S(2)}, u32[]{:S(2)}) %collective-permute-start.5) | collective-permute-done | bytes 196640 | tf_op jit(solution)/shard_map/ppermute | solution.py:37
  19.3 1.5 %hist_send.2.refs_2_ = bf16[4,256,128]{2,1,0:T(8,128)(2,1)S(1)} custom-call(s32[2,8,768]{2,1,0:T(8,128)S(1)} %fusion.codes_ref, bf16[768,128]{1,0:T(8,128)(2,1)S(1)} %feat_add.2.after_ref.refs_0_, bf16[768,128]{1,0:T(8,128)(2,1)S(1)} %feat_add.2.after_ref.refs_0_, bf16[768,128]{1,0:T(8,128)(2,1)S(1)} %collective-permute-done.5.refs_1_.refs_2_), custom_call_target="tpu_custom_call" | custom-call | flops 1000000000 | tf_op jit(solution)/shard_map/hist_send/pallas_call | solution.py:207
  20.8 1.7 %collective-permute-start.7 = (bf16[4,256,128]{2,1,0:T(8,128)(2,1)S(1)}, bf16[4,256,128]{2,1,0:T(8,128)(2,1)S(1)}, u32[]{:S(2)}, u32[]{:S(2)}) collective-permute-start(bf16[4,256,128]{2,1,0:T(8,128)(2,1)S(1)} %hist_send.2.refs_2_), channel_id=1, source_target_pairs={{0,4},{4,0},{8,12},{12,8},{16,20},{20,16},{24,28},{28,24},{1,5},{5... | collective-permute-start | bytes 786440 | tf_op jit(solution)/shard_map/ppermute | solution.py:37
  22.5 0.0 collective-permute-done.3.refs_1_
  22.5 0.1 collective-permute-start.6
  22.6 0.0 collective-permute-done.2.refs_1_
  22.7 2.6 %collective-permute-start.9 = (bf16[64,1024]{1,0:T(8,128)(2,1)S(1)}, bf16[64,1024]{1,0:T(8,128)(2,1)S(1)}, u32[]{:S(2)}, u32[]{:S(2)}) collective-permute-start(bf16[64,1024]{1,0:T(8,128)(2,1)S(1)} %leaf_add.3.after_ref.refs_0_), channel_id=1, source_target_pairs={{0,16},{4,20},{8,24},{12,28},{16,0},{20,4},{24,8},{28,12},{1,17},{... | collective-permute-start | bytes 393224 | tf_op jit(solution)/shard_map/ppermute | solution.py:37
  25.3 0.0 collective-permute-done.6.refs_1_.refs_3_
  25.3 1.5 %hist_send.3.after_ref = bf16[4,256,128]{2,1,0:T(8,128)(2,1)S(1)} custom-call(s32[2,8,768]{2,1,0:T(8,128)S(1)} %fusion.codes_ref, bf16[64,1024]{1,0:T(8,128)(2,1)S(1)} %leaf_add.3.after_ref.refs_0_, bf16[768,128]{1,0:T(8,128)(2,1)S(1)} %feat_add.3.refs_2_.refs_0_.refs_1_, bf16[768,128]{1,0:T(8,128)(2,1)S(1)} %collective-permute-done.6.refs_1_.refs_3_), custom_call_target="tpu_custom_call" | custom-call | flops 3000000000 | tf_op jit(solution)/shard_map/hist_send/pallas_call | solution.py:207
  26.8 0.6 %collective-permute-start.10 = (bf16[4,256,128]{2,1,0:T(8,128)(2,1)S(1)}, bf16[4,256,128]{2,1,0:T(8,128)(2,1)S(1)}, u32[]{:S(2)}, u32[]{:S(2)}) collective-permute-start(bf16[4,256,128]{2,1,0:T(8,128)(2,1)S(1)} %hist_send.3.after_ref), channel_id=1, source_target_pairs={{0,4},{4,0},{8,12},{12,8},{16,20},{20,16},{24,28},{28,24},{1,5},{5... | collective-permute-start | bytes 786440 | tf_op jit(solution)/shard_map/ppermute | solution.py:37
  27.4 1.5 %hist_keep.1 = (f32[4,256,128]{2,1,0:T(8,128)S(1)}, f32[4,256,128]{2,1,0:T(8,128)S(1)}) custom-call(s32[2,8,768]{2,1,0:T(8,128)S(1)} %fusion.codes_ref, bf16[4,256,128]{2,1,0:T(8,128)(2,1)S(1)} %hist_send.3.after_ref, bf16[768,128]{1,0:T(8,128)(2,1)S(1)} %feat_add.2.after_ref.refs_0_, bf16[768,128]{1,0:T(8,128)(2,1)S(1)} %feat_add.3.refs_2_.refs_0_.refs_1_, ...), custom_call_target="tpu_custom_call" | custom-call | flops 3000000000 | tf_op jit(solution)/shard_map/hist_keep/pallas_call | solution.py:207
  28.9 0.0 copy-start
  28.9 0.0 copy-start.1
  29.0 0.3 collective-permute-done.7.refs_1_
  29.3 1.8 %collective-permute-start.8 = (bf16[2,256,128]{2,1,0:T(8,128)(2,1)S(1)}, bf16[2,256,128]{2,1,0:T(8,128)(2,1)S(1)}, u32[]{:S(2)}, u32[]{:S(2)}) collective-permute-start(bf16[2,256,128]{2,1,0:T(8,128)(2,1)S(1)} %get-tuple-element.33), channel_id=1, source_target_pairs={{0,8},{4,12},{8,0},{12,4},{16,24},{20,28},{24,16},{28,20},{1,9},{5... | collective-permute-start | bytes 393224 | tf_op jit(solution)/shard_map/ppermute | solution.py:37
  31.0 4.3 %collective-permute-done.10.refs_1_ = bf16[4,256,128]{2,1,0:T(8,128)(2,1)S(1)} collective-permute-done((bf16[4,256,128]{2,1,0:T(8,128)(2,1)S(1)}, bf16[4,256,128]{2,1,0:T(8,128)(2,1)S(1)}, u32[]{:S(2)}, u32[]{:S(2)}) %collective-permute-start.10) | collective-permute-done | bytes 262176 | tf_op jit(solution)/shard_map/ppermute | solution.py:37
  35.3 0.0 collective-permute-done.9.refs_1_
  35.3 0.1 leaf_value.1.refs_2_.own_ref
  35.4 1.2 %collective-permute-start.13 = (bf16[32,1024]{1,0:T(8,128)(2,1)S(1)}, bf16[32,1024]{1,0:T(8,128)(2,1)S(1)}, u32[]{:S(2)}, u32[]{:S(2)}) collective-permute-start(bf16[32,1024]{1,0:T(8,128)(2,1)S(1)} %leaf_value.1.refs_2_.own_ref), channel_id=1, source_target_pairs={{0,4},{4,0},{8,12},{12,8},{16,20},{20,16},{24,28},{28,24},{1,5},{5... | collective-permute-start | bytes 196616 | tf_op jit(solution)/shard_map/ppermute | solution.py:37
  36.6 1.6 %collective-permute-start.12 = (bf16[2,256,128]{2,1,0:T(8,128)(2,1)S(1)}, bf16[2,256,128]{2,1,0:T(8,128)(2,1)S(1)}, u32[]{:S(2)}, u32[]{:S(2)}) collective-permute-start(bf16[2,256,128]{2,1,0:T(8,128)(2,1)S(1)} %get-tuple-element.37), channel_id=1, source_target_pairs={{0,8},{4,12},{8,0},{12,4},{16,24},{20,28},{24,16},{28,20},{1,9},{5... | collective-permute-start | bytes 393224 | tf_op jit(solution)/shard_map/ppermute | solution.py:37
  38.2 0.0 collective-permute-done.8.refs_1_
  38.2 2.6 %collective-permute-start.11 = (bf16[1,256,128]{2,1,0:T(8,128)(2,1)S(1)}, bf16[1,256,128]{2,1,0:T(8,128)(2,1)S(1)}, u32[]{:S(2)}, u32[]{:S(2)}) collective-permute-start(bf16[1,256,128]{2,1,0:T(8,128)(2,1)S(1)} %get-tuple-element.36), channel_id=1, source_target_pairs={{0,16},{4,20},{8,24},{12,28},{16,0},{20,4},{24,8},{28,12},{1,17},{... | collective-permute-start | bytes 196616 | tf_op jit(solution)/shard_map/ppermute | solution.py:37
  40.9 0.0 collective-permute-done.13.other_ref
  40.9 0.0 copy-done
  40.9 0.0 copy-done.1
  40.9 2.0 %update_first.1 = (bf16[1536,1024]{1,0:T(8,128)(2,1)}, f32[64,1024]{1,0:T(8,128)}, f32[8,128]{1,0:T(8,128)S(1)}) custom-call(s32[2]{0:T(128)S(1)} %pad_add_fusion.pos_ref, s32[12,128]{1,0:T(8,128)S(1)} %bitcast.8, bf16[32,1024]{1,0:T(8,128)(2,1)S(1)} %leaf_value.1.refs_2_.own_ref, bf16[32,1024]{1,0:T(8,128)(2,1)S(1)} %collective-permute-done.13.other_ref, ...), custom_call_target="tpu_custom_call" | custom-call | flops 3000000000 | tf_op jit(solution)/shard_map/update_first/pallas_call | solution.py:262
  42.9 0.0 collective-permute-done.12.refs_1_
  43.0 1.4 %collective-permute-start.14 = (bf16[1,256,128]{2,1,0:T(8,128)(2,1)S(1)}, bf16[1,256,128]{2,1,0:T(8,128)(2,1)S(1)}, u32[]{:S(2)}, u32[]{:S(2)}) collective-permute-start(bf16[1,256,128]{2,1,0:T(8,128)(2,1)S(1)} %get-tuple-element.40), channel_id=1, source_target_pairs={{0,16},{4,20},{8,24},{12,28},{16,0},{20,4},{24,8},{28,12},{1,17},{... | collective-permute-start | bytes 196616 | tf_op jit(solution)/shard_map/ppermute | solution.py:37
  44.4 2.0 %update_second.1 = (bf16[1536,1024]{1,0:T(8,128)(2,1)}, f32[8,128]{1,0:T(8,128)S(1)}) custom-call(s32[2]{0:T(128)S(1)} %pad_add_fusion.pos_ref, s32[12,128]{1,0:T(8,128)S(1)} %bitcast.9, bf16[32,1024]{1,0:T(8,128)(2,1)S(1)} %leaf_value.1.refs_2_.own_ref, bf16[32,1024]{1,0:T(8,128)(2,1)S(1)} %collective-permute-done.13.other_ref, ...), custom_call_target="tpu_custom_call", output_to_operand_aliasing={{0}: (6, {})} | custom-call | flops 3000000000 | tf_op jit(solution)/shard_map/update_second/pallas_call | solution.py:262
  46.5 0.0 collective-permute-done.11.refs_1_
  46.5 2.4 %collective-permute-done.14.refs_3_ = bf16[1,256,128]{2,1,0:T(8,128)(2,1)S(1)} collective-permute-done((bf16[1,256,128]{2,1,0:T(8,128)(2,1)S(1)}, bf16[1,256,128]{2,1,0:T(8,128)(2,1)S(1)}, u32[]{:S(2)}, u32[]{:S(2)}) %collective-permute-start.14) | collective-permute-done | bytes 65568 | tf_op jit(solution)/shard_map/ppermute | solution.py:37
  48.9 0.7 %last_add.1 = f32[256,256]{1,0:T(8,128)} custom-call(f32[1,256,128]{2,1,0:T(8,128)S(1)} %get-tuple-element.35.after_ref.refs_0_, bf16[1,256,128]{2,1,0:T(8,128)(2,1)S(1)} %collective-permute-done.11.refs_1_, f32[1,256,128]{2,1,0:T(8,128)S(1)} %get-tuple-element.39.after_ref.refs_2_, bf16[1,256,128]{2,1,0:T(8,128)(2,1)S(1)} %collective-permute-done.14.refs_3_, ...), custom_call_target="tpu_custom_call" | custom-call | tf_op jit(solution)/shard_map/last_add/pallas_call | solution.py:45
  (11 shorter events, 0.3 us)
Async XLA Ops:
  6.8 4.9 %copy-start.2 = (s32[8,1536]{1,0:T(8,128)S(1)}, s32[8,1536]{1,0:T(8,128)}, u32[]{:S(2)}) copy-start(s32[8,1536]{1,0:T(8,128)} %param.7) | copy-start | bytes 147460
  6.8 3.1 %collective-permute-start.1 = (bf16[768,256]{1,0:T(8,128)(2,1)S(1)}, bf16[768,256]{1,0:T(8,128)(2,1)S(1)}, u32[]{:S(2)}, u32[]{:S(2)}) collective-permute-start(bf16[768,256]{1,0:T(8,128)(2,1)S(1)} %get-tuple-element.29), channel_id=1, source_target_pairs={{0,1},{1,0},{2,3},{3,2},{4,5},{5,4},{6,7},{7,6},{8,9},{9,8},{10,11... | collective-permute-start | bytes 1179656 | tf_op jit(solution)/shard_map/ppermute | solution.py:37
  7.3 6.7 %collective-permute-start = (bf16[64,1024]{1,0:T(8,128)(2,1)S(1)}, bf16[64,1024]{1,0:T(8,128)(2,1)S(1)}, u32[]{:S(2)}, u32[]{:S(2)}) collective-permute-start(bf16[64,1024]{1,0:T(8,128)(2,1)S(1)} %get-tuple-element.28), channel_id=1, source_target_pairs={{0,4},{4,0},{8,12},{12,8},{16,20},{20,16},{24,28},{28,24},{1,5},{5... | collective-permute-start | bytes 393224 | tf_op jit(solution)/shard_map/ppermute | solution.py:37
  10.0 7.8 %collective-permute-start.4 = (bf16[768,128]{1,0:T(8,128)(2,1)S(1)}, bf16[768,128]{1,0:T(8,128)(2,1)S(1)}, u32[]{:S(2)}, u32[]{:S(2)}) collective-permute-start(bf16[768,128]{1,0:T(8,128)(2,1)S(1)} %core_add.2.refs_2_.refs_0_), channel_id=1, source_target_pairs={{0,2},{1,3},{2,0},{3,1},{4,6},{5,7},{6,4},{7,5},{8,10},{9,11},{10,... | collective-permute-start | bytes 589832 | tf_op jit(solution)/shard_map/ppermute | solution.py:37
  11.7 10.7 %collective-permute-start.3 = (bf16[768,128]{1,0:T(8,128)(2,1)S(1)}, bf16[768,128]{1,0:T(8,128)(2,1)S(1)}, u32[]{:S(2)}, u32[]{:S(2)}) collective-permute-start(bf16[768,128]{1,0:T(8,128)(2,1)S(1)} %core_add.3.refs_2_.refs_0_), channel_id=1, source_target_pairs={{0,2},{1,3},{2,0},{3,1},{4,6},{5,7},{6,4},{7,5},{8,10},{9,11},{10,... | collective-permute-start | bytes 589832 | tf_op jit(solution)/shard_map/ppermute | solution.py:37
  14.1 8.5 %collective-permute-start.2 = (bf16[64,1024]{1,0:T(8,128)(2,1)S(1)}, bf16[64,1024]{1,0:T(8,128)(2,1)S(1)}, u32[]{:S(2)}, u32[]{:S(2)}) collective-permute-start(bf16[64,1024]{1,0:T(8,128)(2,1)S(1)} %leaf_add.2.refs_2_.refs_0_), channel_id=1, source_target_pairs={{0,8},{4,12},{8,0},{12,4},{16,24},{20,28},{24,16},{28,20},{1,9},{5... | collective-permute-start | bytes 393224 | tf_op jit(solution)/shard_map/ppermute | solution.py:37
  17.8 1.5 %collective-permute-start.5 = (bf16[768,128]{1,0:T(8,128)(2,1)S(1)}, bf16[768,128]{1,0:T(8,128)(2,1)S(1)}, u32[]{:S(2)}, u32[]{:S(2)}) collective-permute-start(bf16[768,128]{1,0:T(8,128)(2,1)S(1)} %feat_add.2.after_ref.refs_0_), channel_id=1, source_target_pairs={{0,1},{1,0},{2,3},{3,2},{4,5},{5,4},{6,7},{7,6},{8,9},{9,8},{10,11... | collective-permute-start | bytes 589832 | tf_op jit(solution)/shard_map/ppermute | solution.py:37
  20.8 8.4 %collective-permute-start.7 = (bf16[4,256,128]{2,1,0:T(8,128)(2,1)S(1)}, bf16[4,256,128]{2,1,0:T(8,128)(2,1)S(1)}, u32[]{:S(2)}, u32[]{:S(2)}) collective-permute-start(bf16[4,256,128]{2,1,0:T(8,128)(2,1)S(1)} %hist_send.2.refs_2_), channel_id=1, source_target_pairs={{0,4},{4,0},{8,12},{12,8},{16,20},{20,16},{24,28},{28,24},{1,5},{5... | collective-permute-start | bytes 786440 | tf_op jit(solution)/shard_map/ppermute | solution.py:37
  22.5 2.8 %collective-permute-start.6 = (bf16[768,128]{1,0:T(8,128)(2,1)S(1)}, bf16[768,128]{1,0:T(8,128)(2,1)S(1)}, u32[]{:S(2)}, u32[]{:S(2)}) collective-permute-start(bf16[768,128]{1,0:T(8,128)(2,1)S(1)} %feat_add.3.refs_2_.refs_0_.refs_1_), channel_id=1, source_target_pairs={{0,1},{1,0},{2,3},{3,2},{4,5},{5,4},{6,7},{7,6},{8,9},{9,8},{10,11... | collective-permute-start | bytes 589832 | tf_op jit(solution)/shard_map/ppermute | solution.py:37
  22.7 12.7 %collective-permute-start.9 = (bf16[64,1024]{1,0:T(8,128)(2,1)S(1)}, bf16[64,1024]{1,0:T(8,128)(2,1)S(1)}, u32[]{:S(2)}, u32[]{:S(2)}) collective-permute-start(bf16[64,1024]{1,0:T(8,128)(2,1)S(1)} %leaf_add.3.after_ref.refs_0_), channel_id=1, source_target_pairs={{0,16},{4,20},{8,24},{12,28},{16,0},{20,4},{24,8},{28,12},{1,17},{... | collective-permute-start | bytes 393224 | tf_op jit(solution)/shard_map/ppermute | solution.py:37
  26.8 8.5 %collective-permute-start.10 = (bf16[4,256,128]{2,1,0:T(8,128)(2,1)S(1)}, bf16[4,256,128]{2,1,0:T(8,128)(2,1)S(1)}, u32[]{:S(2)}, u32[]{:S(2)}) collective-permute-start(bf16[4,256,128]{2,1,0:T(8,128)(2,1)S(1)} %hist_send.3.after_ref), channel_id=1, source_target_pairs={{0,4},{4,0},{8,12},{12,8},{16,20},{20,16},{24,28},{28,24},{1,5},{5... | collective-permute-start | bytes 786440 | tf_op jit(solution)/shard_map/ppermute | solution.py:37
  28.9 12.0 %copy-start = (bf16[1536,1024]{1,0:T(8,128)(2,1)S(1)}, bf16[1536,1024]{1,0:T(8,128)(2,1)}, u32[]{:S(2)}) copy-start(bf16[1536,1024]{1,0:T(8,128)(2,1)} %pred_ref.3) | copy-start | bytes 9437188
  28.9 12.0 %copy-start.1 = (s32[1536]{0:T(1024)S(1)}, s32[1536]{0:T(1024)}, u32[]{:S(2)}) copy-start(s32[1536]{0:T(1024)} %param.8) | copy-start | bytes 18436
  29.3 8.9 %collective-permute-start.8 = (bf16[2,256,128]{2,1,0:T(8,128)(2,1)S(1)}, bf16[2,256,128]{2,1,0:T(8,128)(2,1)S(1)}, u32[]{:S(2)}, u32[]{:S(2)}) collective-permute-start(bf16[2,256,128]{2,1,0:T(8,128)(2,1)S(1)} %get-tuple-element.33), channel_id=1, source_target_pairs={{0,8},{4,12},{8,0},{12,4},{16,24},{20,28},{24,16},{28,20},{1,9},{5... | collective-permute-start | bytes 393224 | tf_op jit(solution)/shard_map/ppermute | solution.py:37
  35.4 5.5 %collective-permute-start.13 = (bf16[32,1024]{1,0:T(8,128)(2,1)S(1)}, bf16[32,1024]{1,0:T(8,128)(2,1)S(1)}, u32[]{:S(2)}, u32[]{:S(2)}) collective-permute-start(bf16[32,1024]{1,0:T(8,128)(2,1)S(1)} %leaf_value.1.refs_2_.own_ref), channel_id=1, source_target_pairs={{0,4},{4,0},{8,12},{12,8},{16,20},{20,16},{24,28},{28,24},{1,5},{5... | collective-permute-start | bytes 196616 | tf_op jit(solution)/shard_map/ppermute | solution.py:37
  36.6 6.3 %collective-permute-start.12 = (bf16[2,256,128]{2,1,0:T(8,128)(2,1)S(1)}, bf16[2,256,128]{2,1,0:T(8,128)(2,1)S(1)}, u32[]{:S(2)}, u32[]{:S(2)}) collective-permute-start(bf16[2,256,128]{2,1,0:T(8,128)(2,1)S(1)} %get-tuple-element.37), channel_id=1, source_target_pairs={{0,8},{4,12},{8,0},{12,4},{16,24},{20,28},{24,16},{28,20},{1,9},{5... | collective-permute-start | bytes 393224 | tf_op jit(solution)/shard_map/ppermute | solution.py:37
  38.2 8.2 %collective-permute-start.11 = (bf16[1,256,128]{2,1,0:T(8,128)(2,1)S(1)}, bf16[1,256,128]{2,1,0:T(8,128)(2,1)S(1)}, u32[]{:S(2)}, u32[]{:S(2)}) collective-permute-start(bf16[1,256,128]{2,1,0:T(8,128)(2,1)S(1)} %get-tuple-element.36), channel_id=1, source_target_pairs={{0,16},{4,20},{8,24},{12,28},{16,0},{20,4},{24,8},{28,12},{1,17},{... | collective-permute-start | bytes 196616 | tf_op jit(solution)/shard_map/ppermute | solution.py:37
  43.0 5.9 %collective-permute-start.14 = (bf16[1,256,128]{2,1,0:T(8,128)(2,1)S(1)}, bf16[1,256,128]{2,1,0:T(8,128)(2,1)S(1)}, u32[]{:S(2)}, u32[]{:S(2)}) collective-permute-start(bf16[1,256,128]{2,1,0:T(8,128)(2,1)S(1)} %get-tuple-element.40), channel_id=1, source_target_pairs={{0,16},{4,20},{8,24},{12,28},{16,0},{20,4},{24,8},{28,12},{1,17},{... | collective-permute-start | bytes 196616 | tf_op jit(solution)/shard_map/ppermute | solution.py:37

commit v14 on v12

--- a/solution.py
+++ b/solution.py
@@ -345,7 +345,7 @@
 
     def hist_send(p):
         nonlocal after
-        after, = hist_pass(codes, [owns[p]], [others[p]], per, n // 2, 1, bf16, after, (1.0, 3.0)[p])
+        after, = hist_pass(codes, [owns[p]], [others[p]], per, n // 2, 1, bf16, after, (3.0, 3.0)[p])
         backs[p] = swap(after, "rows", n, 1)
 
     def hist_keep():

time: 47.7 us -> 51.1 us (1.071)
  waiting for transfers between devices: 10.7 us -> 14.8 us
  starting transfers between devices: 20.1 us -> 19.4 us
    ppermute x15, waiting for transfers between devices: 10.7 us -> 14.8 us  [swap(): return lax.ppermute(x, axis, [(i, i ^ by) for i in range(size)])]
    ppermute x15, starting transfers between devices: 20.1 us -> 19.4 us  [swap(): return lax.ppermute(x, axis, [(i, i ^ by) for i in range(size)])]
  transfers between devices with their start and end apart: 15 -> 15, of which waited for: 8 -> 7; matrix products, arithmetic and copies ran while one was open for 0% -> 0% of each run, Pallas kernels for 19% -> 18%
where the time goes in v14:
time: 51.1 us; the launch traced here: 50.9 us
  starting transfers between devices  19.4 us (38%)
  Pallas kernels  15.8 us (31%)
  waiting for transfers between devices  14.8 us (29%)
  between operations  0.83 us (2%)
    ppermute x15, starting transfers between devices, swap(): return lax.ppermute(x, axis, [(i, i ^ by) for i in range(size)])  19.4 us
    ppermute x15, waiting for transfers between devices, swap(): return lax.ppermute(x, axis, [(i, i ^ by) for i in range(size)])  14.8 us
    pallas_call x1, Pallas kernels, rows_pass(): pl.pallas_call(rows_kernel, in_specs=[pl.BlockSpec(memory_space=pltpu.SME...  6.06 us
    pallas_call x3, Pallas kernels, hist_pass(): pl.pallas_call(functools.partial(hist_kernel, per=per, odd=odd, bits=bloc...  4.44 us
    pallas_call x2, Pallas kernels, update_pass(): pl.pallas_call(functools.partial(update_kernel, first=first), in_specs=[p...  4.07 us
    pallas_call x13, Pallas kernels, ordered(): pl.pallas_call(body, in_specs=[pl.BlockSpec(memory_space=pltpu.VMEM)] * l...  1.21 us
  transfers between devices with their start and end apart: 15, of which 7 were waited for; matrix products, arithmetic and copies ran while one was open for 0% of the time, Pallas kernels for 18%

profile of v14, /device:TPU:0, one launch (start us, length us, event | category | flops | bytes accessed | tf_op | source)
XLA Modules:
  0.0 50.9 jit_solution(9307024557793811889)
XLA Ops:
  0.6 0.1 pad_add_fusion.pos_ref
  0.7 6.1 %rows.1 = (bf16[768,256]{1,0:T(8,128)(2,1)S(1)}, bf16[768,256]{1,0:T(8,128)(2,1)S(1)}, f32[64,1024]{1,0:T(8,128)S(1)}, f32[64,1024]{1,0:T(8,128)S(1)}) custom-call(s32[2]{0:T(128)S(1)} %pad_add_fusion.pos_ref, s32[12,128]{1,0:T(8,128)} %bitcast.7, bf16[1536,1024]{1,0:T(8,128)(2,1)} %pred_ref.3, bf16[1536,1024]{1,0:T(8,128)(2,1)} %lab_hbm.1, ...), custom_call_target="tpu_custom_call" | custom-call | tf_op jit(solution)/shard_map/rows/pallas_call | solution.py:118
  6.8 0.0 copy-start.2
  6.8 0.5 %collective-permute-start.1 = (bf16[768,256]{1,0:T(8,128)(2,1)S(1)}, bf16[768,256]{1,0:T(8,128)(2,1)S(1)}, u32[]{:S(2)}, u32[]{:S(2)}) collective-permute-start(bf16[768,256]{1,0:T(8,128)(2,1)S(1)} %get-tuple-element.29), channel_id=1, source_target_pairs={{0,1},{1,0},{2,3},{3,2},{4,5},{5,4},{6,7},{7,6},{8,9},{9,8},{10,11... | collective-permute-start | bytes 1179656 | tf_op jit(solution)/shard_map/ppermute | solution.py:37
  7.3 2.6 %collective-permute-start = (bf16[64,1024]{1,0:T(8,128)(2,1)S(1)}, bf16[64,1024]{1,0:T(8,128)(2,1)S(1)}, u32[]{:S(2)}, u32[]{:S(2)}) collective-permute-start(bf16[64,1024]{1,0:T(8,128)(2,1)S(1)} %get-tuple-element.28), channel_id=1, source_target_pairs={{0,4},{4,0},{8,12},{12,8},{16,20},{20,16},{24,28},{28,24},{1,5},{5... | collective-permute-start | bytes 393224 | tf_op jit(solution)/shard_map/ppermute | solution.py:37
  9.9 0.0 collective-permute-done.1.refs_1_
  9.9 0.1 core_add.2.refs_2_.refs_0_
  10.0 1.7 %collective-permute-start.4 = (bf16[768,128]{1,0:T(8,128)(2,1)S(1)}, bf16[768,128]{1,0:T(8,128)(2,1)S(1)}, u32[]{:S(2)}, u32[]{:S(2)}) collective-permute-start(bf16[768,128]{1,0:T(8,128)(2,1)S(1)} %core_add.2.refs_2_.refs_0_), channel_id=1, source_target_pairs={{0,2},{1,3},{2,0},{3,1},{4,6},{5,7},{6,4},{7,5},{8,10},{9,11},{10,... | collective-permute-start | bytes 589832 | tf_op jit(solution)/shard_map/ppermute | solution.py:37
  11.7 0.0 copy-done.2
  11.7 0.1 core_add.3.refs_2_.refs_0_
  11.7 2.3 %collective-permute-done.refs_1_ = bf16[64,1024]{1,0:T(8,128)(2,1)S(1)} collective-permute-done((bf16[64,1024]{1,0:T(8,128)(2,1)S(1)}, bf16[64,1024]{1,0:T(8,128)(2,1)S(1)}, u32[]{:S(2)}, u32[]{:S(2)}) %collective-permute-start) | collective-permute-done | bytes 131104 | tf_op jit(solution)/shard_map/ppermute | solution.py:37
  14.1 3.0 %collective-permute-done.4.refs_1_ = bf16[768,128]{1,0:T(8,128)(2,1)S(1)} collective-permute-done((bf16[768,128]{1,0:T(8,128)(2,1)S(1)}, bf16[768,128]{1,0:T(8,128)(2,1)S(1)}, u32[]{:S(2)}, u32[]{:S(2)}) %collective-permute-start.4) | collective-permute-done | bytes 196640 | tf_op jit(solution)/shard_map/ppermute | solution.py:37
  17.1 0.1 collective-permute-start.5
  17.2 1.7 %collective-permute-start.2 = (bf16[64,1024]{1,0:T(8,128)(2,1)S(1)}, bf16[64,1024]{1,0:T(8,128)(2,1)S(1)}, u32[]{:S(2)}, u32[]{:S(2)}) collective-permute-start(bf16[64,1024]{1,0:T(8,128)(2,1)S(1)} %leaf_add.2.refs_2_.refs_0_), channel_id=1, source_target_pairs={{0,8},{4,12},{8,0},{12,4},{16,24},{20,28},{24,16},{28,20},{1,9},{5... | collective-permute-start | bytes 393224 | tf_op jit(solution)/shard_map/ppermute | solution.py:37
  18.9 1.5 %collective-permute-start.3 = (bf16[768,128]{1,0:T(8,128)(2,1)S(1)}, bf16[768,128]{1,0:T(8,128)(2,1)S(1)}, u32[]{:S(2)}, u32[]{:S(2)}) collective-permute-start(bf16[768,128]{1,0:T(8,128)(2,1)S(1)} %core_add.3.refs_2_.refs_0_), channel_id=1, source_target_pairs={{0,2},{1,3},{2,0},{3,1},{4,6},{5,7},{6,4},{7,5},{8,10},{9,11},{10,... | collective-permute-start | bytes 589832 | tf_op jit(solution)/shard_map/ppermute | solution.py:37
  20.4 0.0 collective-permute-done.5.refs_1_.refs_2_
  20.4 1.5 %hist_send.2.refs_2_ = bf16[4,256,128]{2,1,0:T(8,128)(2,1)S(1)} custom-call(s32[2,8,768]{2,1,0:T(8,128)S(1)} %fusion.codes_ref, bf16[768,128]{1,0:T(8,128)(2,1)S(1)} %feat_add.2.after_ref.refs_0_, bf16[768,128]{1,0:T(8,128)(2,1)S(1)} %feat_add.2.after_ref.refs_0_, bf16[768,128]{1,0:T(8,128)(2,1)S(1)} %collective-permute-done.5.refs_1_.refs_2_), custom_call_target="tpu_custom_call" | custom-call | flops 3000000000 | tf_op jit(solution)/shard_map/hist_send/pallas_call | solution.py:207
  21.9 1.6 %collective-permute-start.7 = (bf16[4,256,128]{2,1,0:T(8,128)(2,1)S(1)}, bf16[4,256,128]{2,1,0:T(8,128)(2,1)S(1)}, u32[]{:S(2)}, u32[]{:S(2)}) collective-permute-start(bf16[4,256,128]{2,1,0:T(8,128)(2,1)S(1)} %hist_send.2.refs_2_), channel_id=1, source_target_pairs={{0,4},{4,0},{8,12},{12,8},{16,20},{20,16},{24,28},{28,24},{1,5},{5... | collective-permute-start | bytes 786440 | tf_op jit(solution)/shard_map/ppermute | solution.py:37
  23.4 2.4 %collective-permute-done.3.refs_1_ = bf16[768,128]{1,0:T(8,128)(2,1)S(1)} collective-permute-done((bf16[768,128]{1,0:T(8,128)(2,1)S(1)}, bf16[768,128]{1,0:T(8,128)(2,1)S(1)}, u32[]{:S(2)}, u32[]{:S(2)}) %collective-permute-start.3) | collective-permute-done | bytes 196640 | tf_op jit(solution)/shard_map/ppermute | solution.py:37
  25.9 0.1 collective-permute-start.6
  26.0 0.0 collective-permute-done.2.refs_1_
  26.0 2.7 %collective-permute-start.10 = (bf16[64,1024]{1,0:T(8,128)(2,1)S(1)}, bf16[64,1024]{1,0:T(8,128)(2,1)S(1)}, u32[]{:S(2)}, u32[]{:S(2)}) collective-permute-start(bf16[64,1024]{1,0:T(8,128)(2,1)S(1)} %leaf_add.3.after_ref.refs_0_), channel_id=1, source_target_pairs={{0,16},{4,20},{8,24},{12,28},{16,0},{20,4},{24,8},{28,12},{1,17},{... | collective-permute-start | bytes 393224 | tf_op jit(solution)/shard_map/ppermute | solution.py:37
  28.7 0.0 collective-permute-done.6.refs_1_.refs_3_
  28.7 1.5 %hist_send.3.after_ref = bf16[4,256,128]{2,1,0:T(8,128)(2,1)S(1)} custom-call(s32[2,8,768]{2,1,0:T(8,128)S(1)} %fusion.codes_ref, bf16[64,1024]{1,0:T(8,128)(2,1)S(1)} %leaf_add.3.after_ref.refs_0_, bf16[768,128]{1,0:T(8,128)(2,1)S(1)} %feat_add.3.refs_2_.refs_0_.refs_1_, bf16[768,128]{1,0:T(8,128)(2,1)S(1)} %collective-permute-done.6.refs_1_.refs_3_), custom_call_target="tpu_custom_call" | custom-call | flops 3000000000 | tf_op jit(solution)/shard_map/hist_send/pallas_call | solution.py:207
  30.2 1.6 %collective-permute-start.9 = (bf16[4,256,128]{2,1,0:T(8,128)(2,1)S(1)}, bf16[4,256,128]{2,1,0:T(8,128)(2,1)S(1)}, u32[]{:S(2)}, u32[]{:S(2)}) collective-permute-start(bf16[4,256,128]{2,1,0:T(8,128)(2,1)S(1)} %hist_send.3.after_ref), channel_id=1, source_target_pairs={{0,4},{4,0},{8,12},{12,8},{16,20},{20,16},{24,28},{28,24},{1,5},{5... | collective-permute-start | bytes 786440 | tf_op jit(solution)/shard_map/ppermute | solution.py:37
  31.7 1.5 %hist_keep.1 = (f32[4,256,128]{2,1,0:T(8,128)S(1)}, f32[4,256,128]{2,1,0:T(8,128)S(1)}) custom-call(s32[2,8,768]{2,1,0:T(8,128)S(1)} %fusion.codes_ref, bf16[4,256,128]{2,1,0:T(8,128)(2,1)S(1)} %hist_send.3.after_ref, bf16[768,128]{1,0:T(8,128)(2,1)S(1)} %feat_add.2.after_ref.refs_0_, bf16[768,128]{1,0:T(8,128)(2,1)S(1)} %feat_add.3.refs_2_.refs_0_.refs_1_, ...), custom_call_target="tpu_custom_call" | custom-call | flops 3000000000 | tf_op jit(solution)/shard_map/hist_keep/pallas_call | solution.py:207
  33.2 0.0 copy-start
  33.3 0.0 copy-start.1
  33.3 0.0 collective-permute-done.7.refs_1_
  33.3 0.5 %collective-permute-start.8 = (bf16[2,256,128]{2,1,0:T(8,128)(2,1)S(1)}, bf16[2,256,128]{2,1,0:T(8,128)(2,1)S(1)}, u32[]{:S(2)}, u32[]{:S(2)}) collective-permute-start(bf16[2,256,128]{2,1,0:T(8,128)(2,1)S(1)} %get-tuple-element.33), channel_id=1, source_target_pairs={{0,8},{4,12},{8,0},{12,4},{16,24},{20,28},{24,16},{28,20},{1,9},{5... | collective-permute-start | bytes 393224 | tf_op jit(solution)/shard_map/ppermute | solution.py:37
  33.8 1.7 %collective-permute-done.10.refs_1_ = bf16[64,1024]{1,0:T(8,128)(2,1)S(1)} collective-permute-done((bf16[64,1024]{1,0:T(8,128)(2,1)S(1)}, bf16[64,1024]{1,0:T(8,128)(2,1)S(1)}, u32[]{:S(2)}, u32[]{:S(2)}) %collective-permute-start.10) | collective-permute-done | bytes 131104 | tf_op jit(solution)/shard_map/ppermute | solution.py:37
  35.6 1.7 %collective-permute-start.13 = (bf16[32,1024]{1,0:T(8,128)(2,1)S(1)}, bf16[32,1024]{1,0:T(8,128)(2,1)S(1)}, u32[]{:S(2)}, u32[]{:S(2)}) collective-permute-start(bf16[32,1024]{1,0:T(8,128)(2,1)S(1)} %leaf_value.1.refs_2_.own_ref), channel_id=1, source_target_pairs={{0,4},{4,0},{8,12},{12,8},{16,20},{20,16},{24,28},{28,24},{1,5},{5... | collective-permute-start | bytes 196616 | tf_op jit(solution)/shard_map/ppermute | solution.py:37
  37.2 1.6 %collective-permute-done.9.refs_1_ = bf16[4,256,128]{2,1,0:T(8,128)(2,1)S(1)} collective-permute-done((bf16[4,256,128]{2,1,0:T(8,128)(2,1)S(1)}, bf16[4,256,128]{2,1,0:T(8,128)(2,1)S(1)}, u32[]{:S(2)}, u32[]{:S(2)}) %collective-permute-start.9) | collective-permute-done | bytes 262176 | tf_op jit(solution)/shard_map/ppermute | solution.py:37
  38.9 1.0 %collective-permute-start.12 = (bf16[2,256,128]{2,1,0:T(8,128)(2,1)S(1)}, bf16[2,256,128]{2,1,0:T(8,128)(2,1)S(1)}, u32[]{:S(2)}, u32[]{:S(2)}) collective-permute-start(bf16[2,256,128]{2,1,0:T(8,128)(2,1)S(1)} %get-tuple-element.37), channel_id=1, source_target_pairs={{0,8},{4,12},{8,0},{12,4},{16,24},{20,28},{24,16},{28,20},{1,9},{5... | collective-permute-start | bytes 393224 | tf_op jit(solution)/shard_map/ppermute | solution.py:37
  39.9 0.0 collective-permute-done.8.refs_1_
  39.9 0.9 %collective-permute-start.11 = (bf16[1,256,128]{2,1,0:T(8,128)(2,1)S(1)}, bf16[1,256,128]{2,1,0:T(8,128)(2,1)S(1)}, u32[]{:S(2)}, u32[]{:S(2)}) collective-permute-start(bf16[1,256,128]{2,1,0:T(8,128)(2,1)S(1)} %get-tuple-element.36), channel_id=1, source_target_pairs={{0,16},{4,20},{8,24},{12,28},{16,0},{20,4},{24,8},{28,12},{1,17},{... | collective-permute-start | bytes 196616 | tf_op jit(solution)/shard_map/ppermute | solution.py:37
  40.8 0.0 collective-permute-done.13.other_ref
  40.8 0.0 copy-done
  40.8 0.0 copy-done.1
  40.8 2.0 %update_first.1 = (bf16[1536,1024]{1,0:T(8,128)(2,1)}, f32[64,1024]{1,0:T(8,128)}, f32[8,128]{1,0:T(8,128)S(1)}) custom-call(s32[2]{0:T(128)S(1)} %pad_add_fusion.pos_ref, s32[12,128]{1,0:T(8,128)S(1)} %bitcast.8, bf16[32,1024]{1,0:T(8,128)(2,1)S(1)} %leaf_value.1.refs_2_.own_ref, bf16[32,1024]{1,0:T(8,128)(2,1)S(1)} %collective-permute-done.13.other_ref, ...), custom_call_target="tpu_custom_call" | custom-call | flops 3000000000 | tf_op jit(solution)/shard_map/update_first/pallas_call | solution.py:262
  42.9 1.4 %collective-permute-done.12.refs_1_ = bf16[2,256,128]{2,1,0:T(8,128)(2,1)S(1)} collective-permute-done((bf16[2,256,128]{2,1,0:T(8,128)(2,1)S(1)}, bf16[2,256,128]{2,1,0:T(8,128)(2,1)S(1)}, u32[]{:S(2)}, u32[]{:S(2)}) %collective-permute-start.12) | collective-permute-done | bytes 131104 | tf_op jit(solution)/shard_map/ppermute | solution.py:37
  44.3 1.5 %collective-permute-start.14 = (bf16[1,256,128]{2,1,0:T(8,128)(2,1)S(1)}, bf16[1,256,128]{2,1,0:T(8,128)(2,1)S(1)}, u32[]{:S(2)}, u32[]{:S(2)}) collective-permute-start(bf16[1,256,128]{2,1,0:T(8,128)(2,1)S(1)} %get-tuple-element.40), channel_id=1, source_target_pairs={{0,16},{4,20},{8,24},{12,28},{16,0},{20,4},{24,8},{28,12},{1,17},{... | collective-permute-start | bytes 196616 | tf_op jit(solution)/shard_map/ppermute | solution.py:37
  45.8 2.0 %update_second.1 = (bf16[1536,1024]{1,0:T(8,128)(2,1)}, f32[8,128]{1,0:T(8,128)S(1)}) custom-call(s32[2]{0:T(128)S(1)} %pad_add_fusion.pos_ref, s32[12,128]{1,0:T(8,128)S(1)} %bitcast.9, bf16[32,1024]{1,0:T(8,128)(2,1)S(1)} %leaf_value.1.refs_2_.own_ref, bf16[32,1024]{1,0:T(8,128)(2,1)S(1)} %collective-permute-done.13.other_ref, ...), custom_call_target="tpu_custom_call", output_to_operand_aliasing={{0}: (6, {})} | custom-call | flops 3000000000 | tf_op jit(solution)/shard_map/update_second/pallas_call | solution.py:262
  47.8 0.0 collective-permute-done.11.refs_1_
  47.8 2.4 %collective-permute-done.14.refs_3_ = bf16[1,256,128]{2,1,0:T(8,128)(2,1)S(1)} collective-permute-done((bf16[1,256,128]{2,1,0:T(8,128)(2,1)S(1)}, bf16[1,256,128]{2,1,0:T(8,128)(2,1)S(1)}, u32[]{:S(2)}, u32[]{:S(2)}) %collective-permute-start.14) | collective-permute-done | bytes 65568 | tf_op jit(solution)/shard_map/ppermute | solution.py:37
  50.2 0.7 %last_add.1 = f32[256,256]{1,0:T(8,128)} custom-call(f32[1,256,128]{2,1,0:T(8,128)S(1)} %get-tuple-element.35.after_ref.refs_0_, bf16[1,256,128]{2,1,0:T(8,128)(2,1)S(1)} %collective-permute-done.11.refs_1_, f32[1,256,128]{2,1,0:T(8,128)S(1)} %get-tuple-element.39.after_ref.refs_2_, bf16[1,256,128]{2,1,0:T(8,128)(2,1)S(1)} %collective-permute-done.14.refs_3_, ...), custom_call_target="tpu_custom_call" | custom-call | tf_op jit(solution)/shard_map/last_add/pallas_call | solution.py:45
  (12 shorter events, 0.4 us)
Async XLA Ops:
  6.8 4.9 %copy-start.2 = (s32[8,1536]{1,0:T(8,128)S(1)}, s32[8,1536]{1,0:T(8,128)}, u32[]{:S(2)}) copy-start(s32[8,1536]{1,0:T(8,128)} %param.7) | copy-start | bytes 147460
  6.8 3.1 %collective-permute-start.1 = (bf16[768,256]{1,0:T(8,128)(2,1)S(1)}, bf16[768,256]{1,0:T(8,128)(2,1)S(1)}, u32[]{:S(2)}, u32[]{:S(2)}) collective-permute-start(bf16[768,256]{1,0:T(8,128)(2,1)S(1)} %get-tuple-element.29), channel_id=1, source_target_pairs={{0,1},{1,0},{2,3},{3,2},{4,5},{5,4},{6,7},{7,6},{8,9},{9,8},{10,11... | collective-permute-start | bytes 1179656 | tf_op jit(solution)/shard_map/ppermute | solution.py:37
  7.3 6.7 %collective-permute-start = (bf16[64,1024]{1,0:T(8,128)(2,1)S(1)}, bf16[64,1024]{1,0:T(8,128)(2,1)S(1)}, u32[]{:S(2)}, u32[]{:S(2)}) collective-permute-start(bf16[64,1024]{1,0:T(8,128)(2,1)S(1)} %get-tuple-element.28), channel_id=1, source_target_pairs={{0,4},{4,0},{8,12},{12,8},{16,20},{20,16},{24,28},{28,24},{1,5},{5... | collective-permute-start | bytes 393224 | tf_op jit(solution)/shard_map/ppermute | solution.py:37
  10.0 7.1 %collective-permute-start.4 = (bf16[768,128]{1,0:T(8,128)(2,1)S(1)}, bf16[768,128]{1,0:T(8,128)(2,1)S(1)}, u32[]{:S(2)}, u32[]{:S(2)}) collective-permute-start(bf16[768,128]{1,0:T(8,128)(2,1)S(1)} %core_add.2.refs_2_.refs_0_), channel_id=1, source_target_pairs={{0,2},{1,3},{2,0},{3,1},{4,6},{5,7},{6,4},{7,5},{8,10},{9,11},{10,... | collective-permute-start | bytes 589832 | tf_op jit(solution)/shard_map/ppermute | solution.py:37
  17.1 3.3 %collective-permute-start.5 = (bf16[768,128]{1,0:T(8,128)(2,1)S(1)}, bf16[768,128]{1,0:T(8,128)(2,1)S(1)}, u32[]{:S(2)}, u32[]{:S(2)}) collective-permute-start(bf16[768,128]{1,0:T(8,128)(2,1)S(1)} %feat_add.2.after_ref.refs_0_), channel_id=1, source_target_pairs={{0,1},{1,0},{2,3},{3,2},{4,5},{5,4},{6,7},{7,6},{8,9},{9,8},{10,11... | collective-permute-start | bytes 589832 | tf_op jit(solution)/shard_map/ppermute | solution.py:37
  17.2 8.8 %collective-permute-start.2 = (bf16[64,1024]{1,0:T(8,128)(2,1)S(1)}, bf16[64,1024]{1,0:T(8,128)(2,1)S(1)}, u32[]{:S(2)}, u32[]{:S(2)}) collective-permute-start(bf16[64,1024]{1,0:T(8,128)(2,1)S(1)} %leaf_add.2.refs_2_.refs_0_), channel_id=1, source_target_pairs={{0,8},{4,12},{8,0},{12,4},{16,24},{20,28},{24,16},{28,20},{1,9},{5... | collective-permute-start | bytes 393224 | tf_op jit(solution)/shard_map/ppermute | solution.py:37
  18.9 7.0 %collective-permute-start.3 = (bf16[768,128]{1,0:T(8,128)(2,1)S(1)}, bf16[768,128]{1,0:T(8,128)(2,1)S(1)}, u32[]{:S(2)}, u32[]{:S(2)}) collective-permute-start(bf16[768,128]{1,0:T(8,128)(2,1)S(1)} %core_add.3.refs_2_.refs_0_), channel_id=1, source_target_pairs={{0,2},{1,3},{2,0},{3,1},{4,6},{5,7},{6,4},{7,5},{8,10},{9,11},{10,... | collective-permute-start | bytes 589832 | tf_op jit(solution)/shard_map/ppermute | solution.py:37
  21.9 11.4 %collective-permute-start.7 = (bf16[4,256,128]{2,1,0:T(8,128)(2,1)S(1)}, bf16[4,256,128]{2,1,0:T(8,128)(2,1)S(1)}, u32[]{:S(2)}, u32[]{:S(2)}) collective-permute-start(bf16[4,256,128]{2,1,0:T(8,128)(2,1)S(1)} %hist_send.2.refs_2_), channel_id=1, source_target_pairs={{0,4},{4,0},{8,12},{12,8},{16,20},{20,16},{24,28},{28,24},{1,5},{5... | collective-permute-start | bytes 786440 | tf_op jit(solution)/shard_map/ppermute | solution.py:37
  25.9 2.8 %collective-permute-start.6 = (bf16[768,128]{1,0:T(8,128)(2,1)S(1)}, bf16[768,128]{1,0:T(8,128)(2,1)S(1)}, u32[]{:S(2)}, u32[]{:S(2)}) collective-permute-start(bf16[768,128]{1,0:T(8,128)(2,1)S(1)} %feat_add.3.refs_2_.refs_0_.refs_1_), channel_id=1, source_target_pairs={{0,1},{1,0},{2,3},{3,2},{4,5},{5,4},{6,7},{7,6},{8,9},{9,8},{10,11... | collective-permute-start | bytes 589832 | tf_op jit(solution)/shard_map/ppermute | solution.py:37
  26.0 9.5 %collective-permute-start.10 = (bf16[64,1024]{1,0:T(8,128)(2,1)S(1)}, bf16[64,1024]{1,0:T(8,128)(2,1)S(1)}, u32[]{:S(2)}, u32[]{:S(2)}) collective-permute-start(bf16[64,1024]{1,0:T(8,128)(2,1)S(1)} %leaf_add.3.after_ref.refs_0_), channel_id=1, source_target_pairs={{0,16},{4,20},{8,24},{12,28},{16,0},{20,4},{24,8},{28,12},{1,17},{... | collective-permute-start | bytes 393224 | tf_op jit(solution)/shard_map/ppermute | solution.py:37
  30.2 8.7 %collective-permute-start.9 = (bf16[4,256,128]{2,1,0:T(8,128)(2,1)S(1)}, bf16[4,256,128]{2,1,0:T(8,128)(2,1)S(1)}, u32[]{:S(2)}, u32[]{:S(2)}) collective-permute-start(bf16[4,256,128]{2,1,0:T(8,128)(2,1)S(1)} %hist_send.3.after_ref), channel_id=1, source_target_pairs={{0,4},{4,0},{8,12},{12,8},{16,20},{20,16},{24,28},{28,24},{1,5},{5... | collective-permute-start | bytes 786440 | tf_op jit(solution)/shard_map/ppermute | solution.py:37
  33.2 7.6 %copy-start = (bf16[1536,1024]{1,0:T(8,128)(2,1)S(1)}, bf16[1536,1024]{1,0:T(8,128)(2,1)}, u32[]{:S(2)}) copy-start(bf16[1536,1024]{1,0:T(8,128)(2,1)} %pred_ref.3) | copy-start | bytes 9437188
  33.3 7.6 %copy-start.1 = (s32[1536]{0:T(1024)S(1)}, s32[1536]{0:T(1024)}, u32[]{:S(2)}) copy-start(s32[1536]{0:T(1024)} %param.8) | copy-start | bytes 18436
  33.3 6.6 %collective-permute-start.8 = (bf16[2,256,128]{2,1,0:T(8,128)(2,1)S(1)}, bf16[2,256,128]{2,1,0:T(8,128)(2,1)S(1)}, u32[]{:S(2)}, u32[]{:S(2)}) collective-permute-start(bf16[2,256,128]{2,1,0:T(8,128)(2,1)S(1)} %get-tuple-element.33), channel_id=1, source_target_pairs={{0,8},{4,12},{8,0},{12,4},{16,24},{20,28},{24,16},{28,20},{1,9},{5... | collective-permute-start | bytes 393224 | tf_op jit(solution)/shard_map/ppermute | solution.py:37
  35.6 5.2 %collective-permute-start.13 = (bf16[32,1024]{1,0:T(8,128)(2,1)S(1)}, bf16[32,1024]{1,0:T(8,128)(2,1)S(1)}, u32[]{:S(2)}, u32[]{:S(2)}) collective-permute-start(bf16[32,1024]{1,0:T(8,128)(2,1)S(1)} %leaf_value.1.refs_2_.own_ref), channel_id=1, source_target_pairs={{0,4},{4,0},{8,12},{12,8},{16,20},{20,16},{24,28},{28,24},{1,5},{5... | collective-permute-start | bytes 196616 | tf_op jit(solution)/shard_map/ppermute | solution.py:37
  38.9 5.3 %collective-permute-start.12 = (bf16[2,256,128]{2,1,0:T(8,128)(2,1)S(1)}, bf16[2,256,128]{2,1,0:T(8,128)(2,1)S(1)}, u32[]{:S(2)}, u32[]{:S(2)}) collective-permute-start(bf16[2,256,128]{2,1,0:T(8,128)(2,1)S(1)} %get-tuple-element.37), channel_id=1, source_target_pairs={{0,8},{4,12},{8,0},{12,4},{16,24},{20,28},{24,16},{28,20},{1,9},{5... | collective-permute-start | bytes 393224 | tf_op jit(solution)/shard_map/ppermute | solution.py:37
  39.9 7.9 %collective-permute-start.11 = (bf16[1,256,128]{2,1,0:T(8,128)(2,1)S(1)}, bf16[1,256,128]{2,1,0:T(8,128)(2,1)S(1)}, u32[]{:S(2)}, u32[]{:S(2)}) collective-permute-start(bf16[1,256,128]{2,1,0:T(8,128)(2,1)S(1)} %get-tuple-element.36), channel_id=1, source_target_pairs={{0,16},{4,20},{8,24},{12,28},{16,0},{20,4},{24,8},{28,12},{1,17},{... | collective-permute-start | bytes 196616 | tf_op jit(solution)/shard_map/ppermute | solution.py:37
  44.3 5.9 %collective-permute-start.14 = (bf16[1,256,128]{2,1,0:T(8,128)(2,1)S(1)}, bf16[1,256,128]{2,1,0:T(8,128)(2,1)S(1)}, u32[]{:S(2)}, u32[]{:S(2)}) collective-permute-start(bf16[1,256,128]{2,1,0:T(8,128)(2,1)S(1)} %get-tuple-element.40), channel_id=1, source_target_pairs={{0,16},{4,20},{8,24},{12,28},{16,0},{20,4},{24,8},{28,12},{1,17},{... | collective-permute-start | bytes 196616 | tf_op jit(solution)/shard_map/ppermute | solution.py:37

commit v15 on v12

--- a/solution.py
+++ b/solution.py
@@ -111,7 +111,7 @@
 
 def rows_pass(pos, leaf, pred, lab, w):
     rows, cols = pred.shape
-    blk = block_rows(rows // 2)
+    blk = min(128, block_rows(rows // 2))
     chunks = rows // blk
     vmem = pl.BlockSpec(memory_space=pltpu.VMEM)
     hbm = pl.BlockSpec(memory_space=pl.ANY)

time: 47.7 us -> 48.7 us (1.021)
  Pallas kernels: 15.8 us -> 16.8 us
    pallas_call x1, Pallas kernels: 6.06 us -> 7.09 us  [rows_pass(): pl.pallas_call(rows_kernel, in_specs=[pl.BlockSpec(memory_space=pltpu.SME...]
where the time goes in v15:
time: 48.7 us; the launch traced here: 48.6 us
  starting transfers between devices  20.1 us (41%)
  Pallas kernels  16.8 us (34%)
  waiting for transfers between devices  10.7 us (22%)
  between operations  0.82 us (2%)
    ppermute x15, starting transfers between devices, swap(): return lax.ppermute(x, axis, [(i, i ^ by) for i in range(size)])  20.1 us
    ppermute x15, waiting for transfers between devices, swap(): return lax.ppermute(x, axis, [(i, i ^ by) for i in range(size)])  10.7 us
    pallas_call x1, Pallas kernels, rows_pass(): pl.pallas_call(rows_kernel, in_specs=[pl.BlockSpec(memory_space=pltpu.SME...  7.09 us
    pallas_call x3, Pallas kernels, hist_pass(): pl.pallas_call(functools.partial(hist_kernel, per=per, odd=odd, bits=bloc...  4.45 us
    pallas_call x2, Pallas kernels, update_pass(): pl.pallas_call(functools.partial(update_kernel, first=first), in_specs=[p...  4.06 us
    pallas_call x13, Pallas kernels, ordered(): pl.pallas_call(body, in_specs=[pl.BlockSpec(memory_space=pltpu.VMEM)] * l...  1.21 us
  transfers between devices with their start and end apart: 15, of which 8 were waited for; matrix products, arithmetic and copies ran while one was open for 0% of the time, Pallas kernels for 19%

profile of v15, /device:TPU:0, one launch (start us, length us, event | category | flops | bytes accessed | tf_op | source)
XLA Modules:
  0.0 48.6 jit_solution(9317144551929918402)
XLA Ops:
  0.6 0.1 pad_add_fusion.pos_ref
  0.7 7.1 %rows.1 = (bf16[768,256]{1,0:T(8,128)(2,1)S(1)}, bf16[768,256]{1,0:T(8,128)(2,1)S(1)}, f32[64,1024]{1,0:T(8,128)S(1)}, f32[64,1024]{1,0:T(8,128)S(1)}) custom-call(s32[2]{0:T(128)S(1)} %pad_add_fusion.pos_ref, s32[12,128]{1,0:T(8,128)} %bitcast.7, bf16[1536,1024]{1,0:T(8,128)(2,1)} %pred_ref.3, bf16[1536,1024]{1,0:T(8,128)(2,1)} %lab_hbm.1, ...), custom_call_target="tpu_custom_call" | custom-call | tf_op jit(solution)/shard_map/rows/pallas_call | solution.py:118
  7.8 0.0 copy-start.2
  7.8 0.5 %collective-permute-start.1 = (bf16[768,256]{1,0:T(8,128)(2,1)S(1)}, bf16[768,256]{1,0:T(8,128)(2,1)S(1)}, u32[]{:S(2)}, u32[]{:S(2)}) collective-permute-start(bf16[768,256]{1,0:T(8,128)(2,1)S(1)} %get-tuple-element.29), channel_id=1, source_target_pairs={{0,1},{1,0},{2,3},{3,2},{4,5},{5,4},{6,7},{7,6},{8,9},{9,8},{10,11... | collective-permute-start | bytes 1179656 | tf_op jit(solution)/shard_map/ppermute | solution.py:37
  8.4 2.6 %collective-permute-start = (bf16[64,1024]{1,0:T(8,128)(2,1)S(1)}, bf16[64,1024]{1,0:T(8,128)(2,1)S(1)}, u32[]{:S(2)}, u32[]{:S(2)}) collective-permute-start(bf16[64,1024]{1,0:T(8,128)(2,1)S(1)} %get-tuple-element.28), channel_id=1, source_target_pairs={{0,4},{4,0},{8,12},{12,8},{16,20},{20,16},{24,28},{28,24},{1,5},{5... | collective-permute-start | bytes 393224 | tf_op jit(solution)/shard_map/ppermute | solution.py:37
  10.9 0.0 collective-permute-done.1.refs_1_
  11.0 0.1 core_add.2.refs_2_.refs_0_
  11.0 1.7 %collective-permute-start.4 = (bf16[768,128]{1,0:T(8,128)(2,1)S(1)}, bf16[768,128]{1,0:T(8,128)(2,1)S(1)}, u32[]{:S(2)}, u32[]{:S(2)}) collective-permute-start(bf16[768,128]{1,0:T(8,128)(2,1)S(1)} %core_add.2.refs_2_.refs_0_), channel_id=1, source_target_pairs={{0,2},{1,3},{2,0},{3,1},{4,6},{5,7},{6,4},{7,5},{8,10},{9,11},{10,... | collective-permute-start | bytes 589832 | tf_op jit(solution)/shard_map/ppermute | solution.py:37
  12.7 0.0 copy-done.2
  12.7 0.1 core_add.3.refs_2_.refs_0_
  12.8 0.5 collective-permute-start.3
  13.2 1.9 %collective-permute-done.refs_1_ = bf16[64,1024]{1,0:T(8,128)(2,1)S(1)} collective-permute-done((bf16[64,1024]{1,0:T(8,128)(2,1)S(1)}, bf16[64,1024]{1,0:T(8,128)(2,1)S(1)}, u32[]{:S(2)}, u32[]{:S(2)}) %collective-permute-start) | collective-permute-done | bytes 131104 | tf_op jit(solution)/shard_map/ppermute | solution.py:37
  15.1 1.9 %collective-permute-start.2 = (bf16[64,1024]{1,0:T(8,128)(2,1)S(1)}, bf16[64,1024]{1,0:T(8,128)(2,1)S(1)}, u32[]{:S(2)}, u32[]{:S(2)}) collective-permute-start(bf16[64,1024]{1,0:T(8,128)(2,1)S(1)} %leaf_add.2.refs_2_.refs_0_), channel_id=1, source_target_pairs={{0,8},{4,12},{8,0},{12,4},{16,24},{20,28},{24,16},{28,20},{1,9},{5... | collective-permute-start | bytes 393224 | tf_op jit(solution)/shard_map/ppermute | solution.py:37
  17.0 1.8 %collective-permute-done.4.refs_1_ = bf16[768,128]{1,0:T(8,128)(2,1)S(1)} collective-permute-done((bf16[768,128]{1,0:T(8,128)(2,1)S(1)}, bf16[768,128]{1,0:T(8,128)(2,1)S(1)}, u32[]{:S(2)}, u32[]{:S(2)}) %collective-permute-start.4) | collective-permute-done | bytes 196640 | tf_op jit(solution)/shard_map/ppermute | solution.py:37
  18.9 0.1 collective-permute-start.5
  19.0 1.4 %collective-permute-done.5.refs_1_.refs_2_ = bf16[768,128]{1,0:T(8,128)(2,1)S(1)} collective-permute-done((bf16[768,128]{1,0:T(8,128)(2,1)S(1)}, bf16[768,128]{1,0:T(8,128)(2,1)S(1)}, u32[]{:S(2)}, u32[]{:S(2)}) %collective-permute-start.5) | collective-permute-done | bytes 196640 | tf_op jit(solution)/shard_map/ppermute | solution.py:37
  20.4 1.5 %hist_send.2.refs_2_ = bf16[4,256,128]{2,1,0:T(8,128)(2,1)S(1)} custom-call(s32[2,8,768]{2,1,0:T(8,128)S(1)} %fusion.codes_ref, bf16[768,128]{1,0:T(8,128)(2,1)S(1)} %feat_add.2.after_ref.refs_0_, bf16[768,128]{1,0:T(8,128)(2,1)S(1)} %feat_add.2.after_ref.refs_0_, bf16[768,128]{1,0:T(8,128)(2,1)S(1)} %collective-permute-done.5.refs_1_.refs_2_), custom_call_target="tpu_custom_call" | custom-call | flops 1000000000 | tf_op jit(solution)/shard_map/hist_send/pallas_call | solution.py:207
  21.8 1.7 %collective-permute-start.7 = (bf16[4,256,128]{2,1,0:T(8,128)(2,1)S(1)}, bf16[4,256,128]{2,1,0:T(8,128)(2,1)S(1)}, u32[]{:S(2)}, u32[]{:S(2)}) collective-permute-start(bf16[4,256,128]{2,1,0:T(8,128)(2,1)S(1)} %hist_send.2.refs_2_), channel_id=1, source_target_pairs={{0,4},{4,0},{8,12},{12,8},{16,20},{20,16},{24,28},{28,24},{1,5},{5... | collective-permute-start | bytes 786440 | tf_op jit(solution)/shard_map/ppermute | solution.py:37
  23.5 0.0 collective-permute-done.3.refs_1_
  23.6 0.1 collective-permute-start.6
  23.6 0.0 collective-permute-done.2.refs_1_
  23.7 2.7 %collective-permute-start.10 = (bf16[64,1024]{1,0:T(8,128)(2,1)S(1)}, bf16[64,1024]{1,0:T(8,128)(2,1)S(1)}, u32[]{:S(2)}, u32[]{:S(2)}) collective-permute-start(bf16[64,1024]{1,0:T(8,128)(2,1)S(1)} %leaf_add.3.after_ref.refs_0_), channel_id=1, source_target_pairs={{0,16},{4,20},{8,24},{12,28},{16,0},{20,4},{24,8},{28,12},{1,17},{... | collective-permute-start | bytes 393224 | tf_op jit(solution)/shard_map/ppermute | solution.py:37
  26.4 0.0 collective-permute-done.6.refs_1_.refs_3_
  26.4 1.5 %hist_send.3.after_ref = bf16[4,256,128]{2,1,0:T(8,128)(2,1)S(1)} custom-call(s32[2,8,768]{2,1,0:T(8,128)S(1)} %fusion.codes_ref, bf16[64,1024]{1,0:T(8,128)(2,1)S(1)} %leaf_add.3.after_ref.refs_0_, bf16[768,128]{1,0:T(8,128)(2,1)S(1)} %feat_add.3.refs_2_.refs_0_.refs_1_, bf16[768,128]{1,0:T(8,128)(2,1)S(1)} %collective-permute-done.6.refs_1_.refs_3_), custom_call_target="tpu_custom_call" | custom-call | flops 3000000000 | tf_op jit(solution)/shard_map/hist_send/pallas_call | solution.py:207
  27.8 0.6 %collective-permute-start.9 = (bf16[4,256,128]{2,1,0:T(8,128)(2,1)S(1)}, bf16[4,256,128]{2,1,0:T(8,128)(2,1)S(1)}, u32[]{:S(2)}, u32[]{:S(2)}) collective-permute-start(bf16[4,256,128]{2,1,0:T(8,128)(2,1)S(1)} %hist_send.3.after_ref), channel_id=1, source_target_pairs={{0,4},{4,0},{8,12},{12,8},{16,20},{20,16},{24,28},{28,24},{1,5},{5... | collective-permute-start | bytes 786440 | tf_op jit(solution)/shard_map/ppermute | solution.py:37
  28.4 1.5 %hist_keep.1 = (f32[4,256,128]{2,1,0:T(8,128)S(1)}, f32[4,256,128]{2,1,0:T(8,128)S(1)}) custom-call(s32[2,8,768]{2,1,0:T(8,128)S(1)} %fusion.codes_ref, bf16[4,256,128]{2,1,0:T(8,128)(2,1)S(1)} %hist_send.3.after_ref, bf16[768,128]{1,0:T(8,128)(2,1)S(1)} %feat_add.2.after_ref.refs_0_, bf16[768,128]{1,0:T(8,128)(2,1)S(1)} %feat_add.3.refs_2_.refs_0_.refs_1_, ...), custom_call_target="tpu_custom_call" | custom-call | flops 3000000000 | tf_op jit(solution)/shard_map/hist_keep/pallas_call | solution.py:207
  30.0 0.0 copy-start
  30.0 0.0 copy-start.1
  30.0 0.3 collective-permute-done.7.refs_1_
  30.3 1.8 %collective-permute-start.8 = (bf16[2,256,128]{2,1,0:T(8,128)(2,1)S(1)}, bf16[2,256,128]{2,1,0:T(8,128)(2,1)S(1)}, u32[]{:S(2)}, u32[]{:S(2)}) collective-permute-start(bf16[2,256,128]{2,1,0:T(8,128)(2,1)S(1)} %get-tuple-element.33), channel_id=1, source_target_pairs={{0,8},{4,12},{8,0},{12,4},{16,24},{20,28},{24,16},{28,20},{1,9},{5... | collective-permute-start | bytes 393224 | tf_op jit(solution)/shard_map/ppermute | solution.py:37
  32.1 1.4 %collective-permute-done.10.refs_1_ = bf16[64,1024]{1,0:T(8,128)(2,1)S(1)} collective-permute-done((bf16[64,1024]{1,0:T(8,128)(2,1)S(1)}, bf16[64,1024]{1,0:T(8,128)(2,1)S(1)}, u32[]{:S(2)}, u32[]{:S(2)}) %collective-permute-start.10) | collective-permute-done | bytes 131104 | tf_op jit(solution)/shard_map/ppermute | solution.py:37
  33.5 0.8 %collective-permute-start.13 = (bf16[32,1024]{1,0:T(8,128)(2,1)S(1)}, bf16[32,1024]{1,0:T(8,128)(2,1)S(1)}, u32[]{:S(2)}, u32[]{:S(2)}) collective-permute-start(bf16[32,1024]{1,0:T(8,128)(2,1)S(1)} %leaf_value.1.refs_2_.own_ref), channel_id=1, source_target_pairs={{0,4},{4,0},{8,12},{12,8},{16,20},{20,16},{24,28},{28,24},{1,5},{5... | collective-permute-start | bytes 196616 | tf_op jit(solution)/shard_map/ppermute | solution.py:37
  34.2 2.5 %collective-permute-done.9.refs_1_ = bf16[4,256,128]{2,1,0:T(8,128)(2,1)S(1)} collective-permute-done((bf16[4,256,128]{2,1,0:T(8,128)(2,1)S(1)}, bf16[4,256,128]{2,1,0:T(8,128)(2,1)S(1)}, u32[]{:S(2)}, u32[]{:S(2)}) %collective-permute-start.9) | collective-permute-done | bytes 262176 | tf_op jit(solution)/shard_map/ppermute | solution.py:37
  36.8 1.9 %collective-permute-start.12 = (bf16[2,256,128]{2,1,0:T(8,128)(2,1)S(1)}, bf16[2,256,128]{2,1,0:T(8,128)(2,1)S(1)}, u32[]{:S(2)}, u32[]{:S(2)}) collective-permute-start(bf16[2,256,128]{2,1,0:T(8,128)(2,1)S(1)} %get-tuple-element.37), channel_id=1, source_target_pairs={{0,8},{4,12},{8,0},{12,4},{16,24},{20,28},{24,16},{28,20},{1,9},{5... | collective-permute-start | bytes 393224 | tf_op jit(solution)/shard_map/ppermute | solution.py:37
  38.7 0.0 collective-permute-done.8.refs_1_
  38.7 1.6 %collective-permute-start.11 = (bf16[1,256,128]{2,1,0:T(8,128)(2,1)S(1)}, bf16[1,256,128]{2,1,0:T(8,128)(2,1)S(1)}, u32[]{:S(2)}, u32[]{:S(2)}) collective-permute-start(bf16[1,256,128]{2,1,0:T(8,128)(2,1)S(1)} %get-tuple-element.36), channel_id=1, source_target_pairs={{0,16},{4,20},{8,24},{12,28},{16,0},{20,4},{24,8},{28,12},{1,17},{... | collective-permute-start | bytes 196616 | tf_op jit(solution)/shard_map/ppermute | solution.py:37
  40.4 0.0 collective-permute-done.13.other_ref
  40.4 0.0 copy-done
  40.4 0.0 copy-done.1
  40.4 2.0 %update_first.1 = (bf16[1536,1024]{1,0:T(8,128)(2,1)}, f32[64,1024]{1,0:T(8,128)}, f32[8,128]{1,0:T(8,128)S(1)}) custom-call(s32[2]{0:T(128)S(1)} %pad_add_fusion.pos_ref, s32[12,128]{1,0:T(8,128)S(1)} %bitcast.8, bf16[32,1024]{1,0:T(8,128)(2,1)S(1)} %leaf_value.1.refs_2_.own_ref, bf16[32,1024]{1,0:T(8,128)(2,1)S(1)} %collective-permute-done.13.other_ref, ...), custom_call_target="tpu_custom_call" | custom-call | flops 3000000000 | tf_op jit(solution)/shard_map/update_first/pallas_call | solution.py:262
  42.4 0.1 collective-permute-done.12.refs_1_
  42.6 1.9 %collective-permute-start.14 = (bf16[1,256,128]{2,1,0:T(8,128)(2,1)S(1)}, bf16[1,256,128]{2,1,0:T(8,128)(2,1)S(1)}, u32[]{:S(2)}, u32[]{:S(2)}) collective-permute-start(bf16[1,256,128]{2,1,0:T(8,128)(2,1)S(1)} %get-tuple-element.40), channel_id=1, source_target_pairs={{0,16},{4,20},{8,24},{12,28},{16,0},{20,4},{24,8},{28,12},{1,17},{... | collective-permute-start | bytes 196616 | tf_op jit(solution)/shard_map/ppermute | solution.py:37
  44.5 2.0 %update_second.1 = (bf16[1536,1024]{1,0:T(8,128)(2,1)}, f32[8,128]{1,0:T(8,128)S(1)}) custom-call(s32[2]{0:T(128)S(1)} %pad_add_fusion.pos_ref, s32[12,128]{1,0:T(8,128)S(1)} %bitcast.9, bf16[32,1024]{1,0:T(8,128)(2,1)S(1)} %leaf_value.1.refs_2_.own_ref, bf16[32,1024]{1,0:T(8,128)(2,1)S(1)} %collective-permute-done.13.other_ref, ...), custom_call_target="tpu_custom_call", output_to_operand_aliasing={{0}: (6, {})} | custom-call | flops 3000000000 | tf_op jit(solution)/shard_map/update_second/pallas_call | solution.py:262
  46.5 0.0 collective-permute-done.11.refs_1_
  46.5 1.3 %collective-permute-done.14.refs_3_ = bf16[1,256,128]{2,1,0:T(8,128)(2,1)S(1)} collective-permute-done((bf16[1,256,128]{2,1,0:T(8,128)(2,1)S(1)}, bf16[1,256,128]{2,1,0:T(8,128)(2,1)S(1)}, u32[]{:S(2)}, u32[]{:S(2)}) %collective-permute-start.14) | collective-permute-done | bytes 65568 | tf_op jit(solution)/shard_map/ppermute | solution.py:37
  47.8 0.7 %last_add.1 = f32[256,256]{1,0:T(8,128)} custom-call(f32[1,256,128]{2,1,0:T(8,128)S(1)} %get-tuple-element.35.after_ref.refs_0_, bf16[1,256,128]{2,1,0:T(8,128)(2,1)S(1)} %collective-permute-done.11.refs_1_, f32[1,256,128]{2,1,0:T(8,128)S(1)} %get-tuple-element.39.after_ref.refs_2_, bf16[1,256,128]{2,1,0:T(8,128)(2,1)S(1)} %collective-permute-done.14.refs_3_, ...), custom_call_target="tpu_custom_call" | custom-call | tf_op jit(solution)/shard_map/last_add/pallas_call | solution.py:45
  (12 shorter events, 0.4 us)
Async XLA Ops:
  7.8 4.9 %copy-start.2 = (s32[8,1536]{1,0:T(8,128)S(1)}, s32[8,1536]{1,0:T(8,128)}, u32[]{:S(2)}) copy-start(s32[8,1536]{1,0:T(8,128)} %param.7) | copy-start | bytes 147460
  7.8 3.1 %collective-permute-start.1 = (bf16[768,256]{1,0:T(8,128)(2,1)S(1)}, bf16[768,256]{1,0:T(8,128)(2,1)S(1)}, u32[]{:S(2)}, u32[]{:S(2)}) collective-permute-start(bf16[768,256]{1,0:T(8,128)(2,1)S(1)} %get-tuple-element.29), channel_id=1, source_target_pairs={{0,1},{1,0},{2,3},{3,2},{4,5},{5,4},{6,7},{7,6},{8,9},{9,8},{10,11... | collective-permute-start | bytes 1179656 | tf_op jit(solution)/shard_map/ppermute | solution.py:37
  8.4 6.7 %collective-permute-start = (bf16[64,1024]{1,0:T(8,128)(2,1)S(1)}, bf16[64,1024]{1,0:T(8,128)(2,1)S(1)}, u32[]{:S(2)}, u32[]{:S(2)}) collective-permute-start(bf16[64,1024]{1,0:T(8,128)(2,1)S(1)} %get-tuple-element.28), channel_id=1, source_target_pairs={{0,4},{4,0},{8,12},{12,8},{16,20},{20,16},{24,28},{28,24},{1,5},{5... | collective-permute-start | bytes 393224 | tf_op jit(solution)/shard_map/ppermute | solution.py:37
  11.0 7.8 %collective-permute-start.4 = (bf16[768,128]{1,0:T(8,128)(2,1)S(1)}, bf16[768,128]{1,0:T(8,128)(2,1)S(1)}, u32[]{:S(2)}, u32[]{:S(2)}) collective-permute-start(bf16[768,128]{1,0:T(8,128)(2,1)S(1)} %core_add.2.refs_2_.refs_0_), channel_id=1, source_target_pairs={{0,2},{1,3},{2,0},{3,1},{4,6},{5,7},{6,4},{7,5},{8,10},{9,11},{10,... | collective-permute-start | bytes 589832 | tf_op jit(solution)/shard_map/ppermute | solution.py:37
  12.8 10.7 %collective-permute-start.3 = (bf16[768,128]{1,0:T(8,128)(2,1)S(1)}, bf16[768,128]{1,0:T(8,128)(2,1)S(1)}, u32[]{:S(2)}, u32[]{:S(2)}) collective-permute-start(bf16[768,128]{1,0:T(8,128)(2,1)S(1)} %core_add.3.refs_2_.refs_0_), channel_id=1, source_target_pairs={{0,2},{1,3},{2,0},{3,1},{4,6},{5,7},{6,4},{7,5},{8,10},{9,11},{10,... | collective-permute-start | bytes 589832 | tf_op jit(solution)/shard_map/ppermute | solution.py:37
  15.1 8.5 %collective-permute-start.2 = (bf16[64,1024]{1,0:T(8,128)(2,1)S(1)}, bf16[64,1024]{1,0:T(8,128)(2,1)S(1)}, u32[]{:S(2)}, u32[]{:S(2)}) collective-permute-start(bf16[64,1024]{1,0:T(8,128)(2,1)S(1)} %leaf_add.2.refs_2_.refs_0_), channel_id=1, source_target_pairs={{0,8},{4,12},{8,0},{12,4},{16,24},{20,28},{24,16},{28,20},{1,9},{5... | collective-permute-start | bytes 393224 | tf_op jit(solution)/shard_map/ppermute | solution.py:37
  18.9 1.5 %collective-permute-start.5 = (bf16[768,128]{1,0:T(8,128)(2,1)S(1)}, bf16[768,128]{1,0:T(8,128)(2,1)S(1)}, u32[]{:S(2)}, u32[]{:S(2)}) collective-permute-start(bf16[768,128]{1,0:T(8,128)(2,1)S(1)} %feat_add.2.after_ref.refs_0_), channel_id=1, source_target_pairs={{0,1},{1,0},{2,3},{3,2},{4,5},{5,4},{6,7},{7,6},{8,9},{9,8},{10,11... | collective-permute-start | bytes 589832 | tf_op jit(solution)/shard_map/ppermute | solution.py:37
  21.8 8.4 %collective-permute-start.7 = (bf16[4,256,128]{2,1,0:T(8,128)(2,1)S(1)}, bf16[4,256,128]{2,1,0:T(8,128)(2,1)S(1)}, u32[]{:S(2)}, u32[]{:S(2)}) collective-permute-start(bf16[4,256,128]{2,1,0:T(8,128)(2,1)S(1)} %hist_send.2.refs_2_), channel_id=1, source_target_pairs={{0,4},{4,0},{8,12},{12,8},{16,20},{20,16},{24,28},{28,24},{1,5},{5... | collective-permute-start | bytes 786440 | tf_op jit(solution)/shard_map/ppermute | solution.py:37
  23.6 2.8 %collective-permute-start.6 = (bf16[768,128]{1,0:T(8,128)(2,1)S(1)}, bf16[768,128]{1,0:T(8,128)(2,1)S(1)}, u32[]{:S(2)}, u32[]{:S(2)}) collective-permute-start(bf16[768,128]{1,0:T(8,128)(2,1)S(1)} %feat_add.3.refs_2_.refs_0_.refs_1_), channel_id=1, source_target_pairs={{0,1},{1,0},{2,3},{3,2},{4,5},{5,4},{6,7},{7,6},{8,9},{9,8},{10,11... | collective-permute-start | bytes 589832 | tf_op jit(solution)/shard_map/ppermute | solution.py:37
  23.7 9.7 %collective-permute-start.10 = (bf16[64,1024]{1,0:T(8,128)(2,1)S(1)}, bf16[64,1024]{1,0:T(8,128)(2,1)S(1)}, u32[]{:S(2)}, u32[]{:S(2)}) collective-permute-start(bf16[64,1024]{1,0:T(8,128)(2,1)S(1)} %leaf_add.3.after_ref.refs_0_), channel_id=1, source_target_pairs={{0,16},{4,20},{8,24},{12,28},{16,0},{20,4},{24,8},{28,12},{1,17},{... | collective-permute-start | bytes 393224 | tf_op jit(solution)/shard_map/ppermute | solution.py:37
  27.8 9.0 %collective-permute-start.9 = (bf16[4,256,128]{2,1,0:T(8,128)(2,1)S(1)}, bf16[4,256,128]{2,1,0:T(8,128)(2,1)S(1)}, u32[]{:S(2)}, u32[]{:S(2)}) collective-permute-start(bf16[4,256,128]{2,1,0:T(8,128)(2,1)S(1)} %hist_send.3.after_ref), channel_id=1, source_target_pairs={{0,4},{4,0},{8,12},{12,8},{16,20},{20,16},{24,28},{28,24},{1,5},{5... | collective-permute-start | bytes 786440 | tf_op jit(solution)/shard_map/ppermute | solution.py:37
  30.0 10.4 %copy-start = (bf16[1536,1024]{1,0:T(8,128)(2,1)S(1)}, bf16[1536,1024]{1,0:T(8,128)(2,1)}, u32[]{:S(2)}) copy-start(bf16[1536,1024]{1,0:T(8,128)(2,1)} %pred_ref.3) | copy-start | bytes 9437188
  30.0 10.4 %copy-start.1 = (s32[1536]{0:T(1024)S(1)}, s32[1536]{0:T(1024)}, u32[]{:S(2)}) copy-start(s32[1536]{0:T(1024)} %param.8) | copy-start | bytes 18436
  30.3 8.4 %collective-permute-start.8 = (bf16[2,256,128]{2,1,0:T(8,128)(2,1)S(1)}, bf16[2,256,128]{2,1,0:T(8,128)(2,1)S(1)}, u32[]{:S(2)}, u32[]{:S(2)}) collective-permute-start(bf16[2,256,128]{2,1,0:T(8,128)(2,1)S(1)} %get-tuple-element.33), channel_id=1, source_target_pairs={{0,8},{4,12},{8,0},{12,4},{16,24},{20,28},{24,16},{28,20},{1,9},{5... | collective-permute-start | bytes 393224 | tf_op jit(solution)/shard_map/ppermute | solution.py:37
  33.5 6.9 %collective-permute-start.13 = (bf16[32,1024]{1,0:T(8,128)(2,1)S(1)}, bf16[32,1024]{1,0:T(8,128)(2,1)S(1)}, u32[]{:S(2)}, u32[]{:S(2)}) collective-permute-start(bf16[32,1024]{1,0:T(8,128)(2,1)S(1)} %leaf_value.1.refs_2_.own_ref), channel_id=1, source_target_pairs={{0,4},{4,0},{8,12},{12,8},{16,20},{20,16},{24,28},{28,24},{1,5},{5... | collective-permute-start | bytes 196616 | tf_op jit(solution)/shard_map/ppermute | solution.py:37
  36.8 5.7 %collective-permute-start.12 = (bf16[2,256,128]{2,1,0:T(8,128)(2,1)S(1)}, bf16[2,256,128]{2,1,0:T(8,128)(2,1)S(1)}, u32[]{:S(2)}, u32[]{:S(2)}) collective-permute-start(bf16[2,256,128]{2,1,0:T(8,128)(2,1)S(1)} %get-tuple-element.37), channel_id=1, source_target_pairs={{0,8},{4,12},{8,0},{12,4},{16,24},{20,28},{24,16},{28,20},{1,9},{5... | collective-permute-start | bytes 393224 | tf_op jit(solution)/shard_map/ppermute | solution.py:37
  38.7 7.8 %collective-permute-start.11 = (bf16[1,256,128]{2,1,0:T(8,128)(2,1)S(1)}, bf16[1,256,128]{2,1,0:T(8,128)(2,1)S(1)}, u32[]{:S(2)}, u32[]{:S(2)}) collective-permute-start(bf16[1,256,128]{2,1,0:T(8,128)(2,1)S(1)} %get-tuple-element.36), channel_id=1, source_target_pairs={{0,16},{4,20},{8,24},{12,28},{16,0},{20,4},{24,8},{28,12},{1,17},{... | collective-permute-start | bytes 196616 | tf_op jit(solution)/shard_map/ppermute | solution.py:37
  42.6 5.2 %collective-permute-start.14 = (bf16[1,256,128]{2,1,0:T(8,128)(2,1)S(1)}, bf16[1,256,128]{2,1,0:T(8,128)(2,1)S(1)}, u32[]{:S(2)}, u32[]{:S(2)}) collective-permute-start(bf16[1,256,128]{2,1,0:T(8,128)(2,1)S(1)} %get-tuple-element.40), channel_id=1, source_target_pairs={{0,16},{4,20},{8,24},{12,28},{16,0},{20,4},{24,8},{28,12},{1,17},{... | collective-permute-start | bytes 196616 | tf_op jit(solution)/shard_map/ppermute | solution.py:37

commit v16 on v12

--- a/solution.py
+++ b/solution.py
@@ -378,9 +378,9 @@
     leaf_step()
     hist_add(1, 0)
     for level in range(1, levels):
-        hist_add(0, level)
         if level == levels - 1:
             update()
+        hist_add(0, level)
         hist_add(1, level)
     update()
     histograms = ordered(

time: 47.7 us -> 48.1 us (level)
  waiting for transfers between devices: 10.7 us -> 12.3 us
  starting transfers between devices: 20.1 us -> 18.9 us
    ppermute x15, waiting for transfers between devices: 10.7 us -> 12.3 us  [swap(): return lax.ppermute(x, axis, [(i, i ^ by) for i in range(size)])]
    ppermute x15, starting transfers between devices: 20.1 us -> 18.9 us  [swap(): return lax.ppermute(x, axis, [(i, i ^ by) for i in range(size)])]
where the time goes in v16:
time: 48.1 us; the launch traced here: 48 us
  starting transfers between devices  18.9 us (39%)
  Pallas kernels  15.8 us (33%)
  waiting for transfers between devices  12.3 us (26%)
  between operations  0.81 us (2%)
    ppermute x15, starting transfers between devices, swap(): return lax.ppermute(x, axis, [(i, i ^ by) for i in range(size)])  18.9 us
    ppermute x15, waiting for transfers between devices, swap(): return lax.ppermute(x, axis, [(i, i ^ by) for i in range(size)])  12.3 us
    pallas_call x1, Pallas kernels, rows_pass(): pl.pallas_call(rows_kernel, in_specs=[pl.BlockSpec(memory_space=pltpu.SME...  6.06 us
    pallas_call x3, Pallas kernels, hist_pass(): pl.pallas_call(functools.partial(hist_kernel, per=per, odd=odd, bits=bloc...  4.45 us
    pallas_call x2, Pallas kernels, update_pass(): pl.pallas_call(functools.partial(update_kernel, first=first), in_specs=[p...  4.07 us
    pallas_call x13, Pallas kernels, ordered(): pl.pallas_call(body, in_specs=[pl.BlockSpec(memory_space=pltpu.VMEM)] * l...  1.23 us
  transfers between devices with their start and end apart: 15, of which 8 were waited for; matrix products, arithmetic and copies ran while one was open for 0% of the time, Pallas kernels for 19%

profile of v16, /device:TPU:0, one launch (start us, length us, event | category | flops | bytes accessed | tf_op | source)
XLA Modules:
  0.0 48.0 jit_solution(15743739342933343732)
XLA Ops:
  0.6 0.1 pad_add_fusion.pos_ref
  0.7 6.1 %rows.1 = (bf16[768,256]{1,0:T(8,128)(2,1)S(1)}, bf16[768,256]{1,0:T(8,128)(2,1)S(1)}, f32[64,1024]{1,0:T(8,128)S(1)}, f32[64,1024]{1,0:T(8,128)S(1)}) custom-call(s32[2]{0:T(128)S(1)} %pad_add_fusion.pos_ref, s32[12,128]{1,0:T(8,128)} %bitcast.7, bf16[1536,1024]{1,0:T(8,128)(2,1)} %pred_ref.3, bf16[1536,1024]{1,0:T(8,128)(2,1)} %lab_hbm.1, ...), custom_call_target="tpu_custom_call" | custom-call | tf_op jit(solution)/shard_map/rows/pallas_call | solution.py:118
  6.8 0.0 copy-start.2
  6.8 0.5 %collective-permute-start.1 = (bf16[768,256]{1,0:T(8,128)(2,1)S(1)}, bf16[768,256]{1,0:T(8,128)(2,1)S(1)}, u32[]{:S(2)}, u32[]{:S(2)}) collective-permute-start(bf16[768,256]{1,0:T(8,128)(2,1)S(1)} %get-tuple-element.29), channel_id=1, source_target_pairs={{0,1},{1,0},{2,3},{3,2},{4,5},{5,4},{6,7},{7,6},{8,9},{9,8},{10,11... | collective-permute-start | bytes 1179656 | tf_op jit(solution)/shard_map/ppermute | solution.py:37
  7.3 2.6 %collective-permute-start = (bf16[64,1024]{1,0:T(8,128)(2,1)S(1)}, bf16[64,1024]{1,0:T(8,128)(2,1)S(1)}, u32[]{:S(2)}, u32[]{:S(2)}) collective-permute-start(bf16[64,1024]{1,0:T(8,128)(2,1)S(1)} %get-tuple-element.28), channel_id=1, source_target_pairs={{0,4},{4,0},{8,12},{12,8},{16,20},{20,16},{24,28},{28,24},{1,5},{5... | collective-permute-start | bytes 393224 | tf_op jit(solution)/shard_map/ppermute | solution.py:37
  9.9 0.0 collective-permute-done.1.refs_1_
  9.9 0.1 core_add.2.refs_2_.refs_0_
  10.0 1.7 %collective-permute-start.4 = (bf16[768,128]{1,0:T(8,128)(2,1)S(1)}, bf16[768,128]{1,0:T(8,128)(2,1)S(1)}, u32[]{:S(2)}, u32[]{:S(2)}) collective-permute-start(bf16[768,128]{1,0:T(8,128)(2,1)S(1)} %core_add.2.refs_2_.refs_0_), channel_id=1, source_target_pairs={{0,2},{1,3},{2,0},{3,1},{4,6},{5,7},{6,4},{7,5},{8,10},{9,11},{10,... | collective-permute-start | bytes 589832 | tf_op jit(solution)/shard_map/ppermute | solution.py:37
  11.7 0.0 copy-done.2
  11.7 0.1 core_add.3.refs_2_.refs_0_
  11.7 0.5 collective-permute-start.3
  12.2 1.9 %collective-permute-done.refs_1_ = bf16[64,1024]{1,0:T(8,128)(2,1)S(1)} collective-permute-done((bf16[64,1024]{1,0:T(8,128)(2,1)S(1)}, bf16[64,1024]{1,0:T(8,128)(2,1)S(1)}, u32[]{:S(2)}, u32[]{:S(2)}) %collective-permute-start) | collective-permute-done | bytes 131104 | tf_op jit(solution)/shard_map/ppermute | solution.py:37
  14.1 1.9 %collective-permute-start.2 = (bf16[64,1024]{1,0:T(8,128)(2,1)S(1)}, bf16[64,1024]{1,0:T(8,128)(2,1)S(1)}, u32[]{:S(2)}, u32[]{:S(2)}) collective-permute-start(bf16[64,1024]{1,0:T(8,128)(2,1)S(1)} %leaf_add.2.refs_2_.refs_0_), channel_id=1, source_target_pairs={{0,8},{4,12},{8,0},{12,4},{16,24},{20,28},{24,16},{28,20},{1,9},{5... | collective-permute-start | bytes 393224 | tf_op jit(solution)/shard_map/ppermute | solution.py:37
  16.0 1.8 %collective-permute-done.4.refs_1_ = bf16[768,128]{1,0:T(8,128)(2,1)S(1)} collective-permute-done((bf16[768,128]{1,0:T(8,128)(2,1)S(1)}, bf16[768,128]{1,0:T(8,128)(2,1)S(1)}, u32[]{:S(2)}, u32[]{:S(2)}) %collective-permute-start.4) | collective-permute-done | bytes 196640 | tf_op jit(solution)/shard_map/ppermute | solution.py:37
  17.8 0.1 collective-permute-start.5
  17.9 1.4 %collective-permute-done.5.refs_1_.refs_2_ = bf16[768,128]{1,0:T(8,128)(2,1)S(1)} collective-permute-done((bf16[768,128]{1,0:T(8,128)(2,1)S(1)}, bf16[768,128]{1,0:T(8,128)(2,1)S(1)}, u32[]{:S(2)}, u32[]{:S(2)}) %collective-permute-start.5) | collective-permute-done | bytes 196640 | tf_op jit(solution)/shard_map/ppermute | solution.py:37
  19.3 1.5 %hist_send.2.refs_2_ = bf16[4,256,128]{2,1,0:T(8,128)(2,1)S(1)} custom-call(s32[2,8,768]{2,1,0:T(8,128)S(1)} %fusion.codes_ref, bf16[768,128]{1,0:T(8,128)(2,1)S(1)} %feat_add.2.after_ref.refs_0_, bf16[768,128]{1,0:T(8,128)(2,1)S(1)} %feat_add.2.after_ref.refs_0_, bf16[768,128]{1,0:T(8,128)(2,1)S(1)} %collective-permute-done.5.refs_1_.refs_2_), custom_call_target="tpu_custom_call" | custom-call | flops 1000000000 | tf_op jit(solution)/shard_map/hist_send/pallas_call | solution.py:207
  20.8 1.7 %collective-permute-start.7 = (bf16[4,256,128]{2,1,0:T(8,128)(2,1)S(1)}, bf16[4,256,128]{2,1,0:T(8,128)(2,1)S(1)}, u32[]{:S(2)}, u32[]{:S(2)}) collective-permute-start(bf16[4,256,128]{2,1,0:T(8,128)(2,1)S(1)} %hist_send.2.refs_2_), channel_id=1, source_target_pairs={{0,4},{4,0},{8,12},{12,8},{16,20},{20,16},{24,28},{28,24},{1,5},{5... | collective-permute-start | bytes 786440 | tf_op jit(solution)/shard_map/ppermute | solution.py:37
  22.5 0.0 collective-permute-done.3.refs_1_
  22.5 0.1 collective-permute-start.6
  22.6 0.0 collective-permute-done.2.refs_1_
  22.7 2.6 %collective-permute-start.9 = (bf16[64,1024]{1,0:T(8,128)(2,1)S(1)}, bf16[64,1024]{1,0:T(8,128)(2,1)S(1)}, u32[]{:S(2)}, u32[]{:S(2)}) collective-permute-start(bf16[64,1024]{1,0:T(8,128)(2,1)S(1)} %leaf_add.3.after_ref.refs_0_), channel_id=1, source_target_pairs={{0,16},{4,20},{8,24},{12,28},{16,0},{20,4},{24,8},{28,12},{1,17},{... | collective-permute-start | bytes 393224 | tf_op jit(solution)/shard_map/ppermute | solution.py:37
  25.3 0.0 collective-permute-done.6.refs_1_.refs_3_
  25.3 1.5 %hist_send.3.after_ref = bf16[4,256,128]{2,1,0:T(8,128)(2,1)S(1)} custom-call(s32[2,8,768]{2,1,0:T(8,128)S(1)} %fusion.codes_ref, bf16[64,1024]{1,0:T(8,128)(2,1)S(1)} %leaf_add.3.after_ref.refs_0_, bf16[768,128]{1,0:T(8,128)(2,1)S(1)} %feat_add.3.refs_2_.refs_0_.refs_1_, bf16[768,128]{1,0:T(8,128)(2,1)S(1)} %collective-permute-done.6.refs_1_.refs_3_), custom_call_target="tpu_custom_call" | custom-call | flops 3000000000 | tf_op jit(solution)/shard_map/hist_send/pallas_call | solution.py:207
  26.8 0.0 copy-start
  26.8 0.0 copy-start.1
  26.8 0.6 %collective-permute-start.11 = (bf16[4,256,128]{2,1,0:T(8,128)(2,1)S(1)}, bf16[4,256,128]{2,1,0:T(8,128)(2,1)S(1)}, u32[]{:S(2)}, u32[]{:S(2)}) collective-permute-start(bf16[4,256,128]{2,1,0:T(8,128)(2,1)S(1)} %hist_send.3.after_ref), channel_id=1, source_target_pairs={{0,4},{4,0},{8,12},{12,8},{16,20},{20,16},{24,28},{28,24},{1,5},{5... | collective-permute-start | bytes 786440 | tf_op jit(solution)/shard_map/ppermute | solution.py:37
  27.4 1.5 %hist_keep.1 = (f32[4,256,128]{2,1,0:T(8,128)S(1)}, f32[4,256,128]{2,1,0:T(8,128)S(1)}) custom-call(s32[2,8,768]{2,1,0:T(8,128)S(1)} %fusion.codes_ref, bf16[4,256,128]{2,1,0:T(8,128)(2,1)S(1)} %hist_send.3.after_ref, bf16[768,128]{1,0:T(8,128)(2,1)S(1)} %feat_add.2.after_ref.refs_0_, bf16[768,128]{1,0:T(8,128)(2,1)S(1)} %feat_add.3.refs_2_.refs_0_.refs_1_, ...), custom_call_target="tpu_custom_call" | custom-call | flops 3000000000 | tf_op jit(solution)/shard_map/hist_keep/pallas_call | solution.py:207
  29.0 0.3 collective-permute-done.7.refs_1_
  29.3 3.1 %collective-permute-done.9.refs_1_ = bf16[64,1024]{1,0:T(8,128)(2,1)S(1)} collective-permute-done((bf16[64,1024]{1,0:T(8,128)(2,1)S(1)}, bf16[64,1024]{1,0:T(8,128)(2,1)S(1)}, u32[]{:S(2)}, u32[]{:S(2)}) %collective-permute-start.9) | collective-permute-done | bytes 131104 | tf_op jit(solution)/shard_map/ppermute | solution.py:37
  32.4 0.5 %collective-permute-start.10 = (bf16[32,1024]{1,0:T(8,128)(2,1)S(1)}, bf16[32,1024]{1,0:T(8,128)(2,1)S(1)}, u32[]{:S(2)}, u32[]{:S(2)}) collective-permute-start(bf16[32,1024]{1,0:T(8,128)(2,1)S(1)} %leaf_value.1.refs_2_.own_ref), channel_id=1, source_target_pairs={{0,4},{4,0},{8,12},{12,8},{16,20},{20,16},{24,28},{28,24},{1,5},{5... | collective-permute-start | bytes 196616 | tf_op jit(solution)/shard_map/ppermute | solution.py:37
  32.9 0.7 %collective-permute-start.8 = (bf16[2,256,128]{2,1,0:T(8,128)(2,1)S(1)}, bf16[2,256,128]{2,1,0:T(8,128)(2,1)S(1)}, u32[]{:S(2)}, u32[]{:S(2)}) collective-permute-start(bf16[2,256,128]{2,1,0:T(8,128)(2,1)S(1)} %get-tuple-element.33), channel_id=1, source_target_pairs={{0,8},{4,12},{8,0},{12,4},{16,24},{20,28},{24,16},{28,20},{1,9},{5... | collective-permute-start | bytes 393224 | tf_op jit(solution)/shard_map/ppermute | solution.py:37
  33.7 2.1 %collective-permute-done.11.refs_1_ = bf16[4,256,128]{2,1,0:T(8,128)(2,1)S(1)} collective-permute-done((bf16[4,256,128]{2,1,0:T(8,128)(2,1)S(1)}, bf16[4,256,128]{2,1,0:T(8,128)(2,1)S(1)}, u32[]{:S(2)}, u32[]{:S(2)}) %collective-permute-start.11) | collective-permute-done | bytes 262176 | tf_op jit(solution)/shard_map/ppermute | solution.py:37
  35.8 1.9 %collective-permute-start.13 = (bf16[2,256,128]{2,1,0:T(8,128)(2,1)S(1)}, bf16[2,256,128]{2,1,0:T(8,128)(2,1)S(1)}, u32[]{:S(2)}, u32[]{:S(2)}) collective-permute-start(bf16[2,256,128]{2,1,0:T(8,128)(2,1)S(1)} %get-tuple-element.38), channel_id=1, source_target_pairs={{0,8},{4,12},{8,0},{12,4},{16,24},{20,28},{24,16},{28,20},{1,9},{5... | collective-permute-start | bytes 393224 | tf_op jit(solution)/shard_map/ppermute | solution.py:37
  37.7 0.0 collective-permute-done.10.other_ref
  37.7 0.0 copy-done
  37.7 0.0 copy-done.1
  37.7 2.0 %update_first.1 = (bf16[1536,1024]{1,0:T(8,128)(2,1)}, f32[64,1024]{1,0:T(8,128)}, f32[8,128]{1,0:T(8,128)S(1)}) custom-call(s32[2]{0:T(128)S(1)} %pad_add_fusion.pos_ref, s32[12,128]{1,0:T(8,128)S(1)} %bitcast.8, bf16[32,1024]{1,0:T(8,128)(2,1)S(1)} %leaf_value.1.refs_2_.own_ref, bf16[32,1024]{1,0:T(8,128)(2,1)S(1)} %collective-permute-done.10.other_ref, ...), custom_call_target="tpu_custom_call" | custom-call | flops 3000000000 | tf_op jit(solution)/shard_map/update_first/pallas_call | solution.py:262
  39.8 0.0 collective-permute-done.8.refs_1_
  39.8 1.7 %collective-permute-start.12 = (bf16[1,256,128]{2,1,0:T(8,128)(2,1)S(1)}, bf16[1,256,128]{2,1,0:T(8,128)(2,1)S(1)}, u32[]{:S(2)}, u32[]{:S(2)}) collective-permute-start(bf16[1,256,128]{2,1,0:T(8,128)(2,1)S(1)} %get-tuple-element.37), channel_id=1, source_target_pairs={{0,16},{4,20},{8,24},{12,28},{16,0},{20,4},{24,8},{28,12},{1,17},{... | collective-permute-start | bytes 196616 | tf_op jit(solution)/shard_map/ppermute | solution.py:37
  41.5 0.0 collective-permute-done.13.refs_1_
  41.5 1.9 %collective-permute-start.14 = (bf16[1,256,128]{2,1,0:T(8,128)(2,1)S(1)}, bf16[1,256,128]{2,1,0:T(8,128)(2,1)S(1)}, u32[]{:S(2)}, u32[]{:S(2)}) collective-permute-start(bf16[1,256,128]{2,1,0:T(8,128)(2,1)S(1)} %get-tuple-element.40), channel_id=1, source_target_pairs={{0,16},{4,20},{8,24},{12,28},{16,0},{20,4},{24,8},{28,12},{1,17},{... | collective-permute-start | bytes 196616 | tf_op jit(solution)/shard_map/ppermute | solution.py:37
  43.4 2.0 %update_second.1 = (bf16[1536,1024]{1,0:T(8,128)(2,1)}, f32[8,128]{1,0:T(8,128)S(1)}) custom-call(s32[2]{0:T(128)S(1)} %pad_add_fusion.pos_ref, s32[12,128]{1,0:T(8,128)S(1)} %bitcast.9, bf16[32,1024]{1,0:T(8,128)(2,1)S(1)} %leaf_value.1.refs_2_.own_ref, bf16[32,1024]{1,0:T(8,128)(2,1)S(1)} %collective-permute-done.10.other_ref, ...), custom_call_target="tpu_custom_call", output_to_operand_aliasing={{0}: (6, {})} | custom-call | flops 3000000000 | tf_op jit(solution)/shard_map/update_second/pallas_call | solution.py:262
  45.5 1.1 %collective-permute-done.12.refs_1_ = bf16[1,256,128]{2,1,0:T(8,128)(2,1)S(1)} collective-permute-done((bf16[1,256,128]{2,1,0:T(8,128)(2,1)S(1)}, bf16[1,256,128]{2,1,0:T(8,128)(2,1)S(1)}, u32[]{:S(2)}, u32[]{:S(2)}) %collective-permute-start.12) | collective-permute-done | bytes 65568 | tf_op jit(solution)/shard_map/ppermute | solution.py:37
  46.6 0.7 %collective-permute-done.14.refs_3_ = bf16[1,256,128]{2,1,0:T(8,128)(2,1)S(1)} collective-permute-done((bf16[1,256,128]{2,1,0:T(8,128)(2,1)S(1)}, bf16[1,256,128]{2,1,0:T(8,128)(2,1)S(1)}, u32[]{:S(2)}, u32[]{:S(2)}) %collective-permute-start.14) | collective-permute-done | bytes 65568 | tf_op jit(solution)/shard_map/ppermute | solution.py:37
  47.3 0.7 %last_add.1 = f32[256,256]{1,0:T(8,128)} custom-call(f32[1,256,128]{2,1,0:T(8,128)S(1)} %get-tuple-element.36.refs_2_.refs_0_, bf16[1,256,128]{2,1,0:T(8,128)(2,1)S(1)} %collective-permute-done.12.refs_1_, f32[1,256,128]{2,1,0:T(8,128)S(1)} %get-tuple-element.39.after_ref.refs_2_, bf16[1,256,128]{2,1,0:T(8,128)(2,1)S(1)} %collective-permute-done.14.refs_3_, ...), custom_call_target="tpu_custom_call" | custom-call | tf_op jit(solution)/shard_map/last_add/pallas_call | solution.py:45
  (12 shorter events, 0.4 us)
Async XLA Ops:
  6.8 4.9 %copy-start.2 = (s32[8,1536]{1,0:T(8,128)S(1)}, s32[8,1536]{1,0:T(8,128)}, u32[]{:S(2)}) copy-start(s32[8,1536]{1,0:T(8,128)} %param.7) | copy-start | bytes 147460
  6.8 3.1 %collective-permute-start.1 = (bf16[768,256]{1,0:T(8,128)(2,1)S(1)}, bf16[768,256]{1,0:T(8,128)(2,1)S(1)}, u32[]{:S(2)}, u32[]{:S(2)}) collective-permute-start(bf16[768,256]{1,0:T(8,128)(2,1)S(1)} %get-tuple-element.29), channel_id=1, source_target_pairs={{0,1},{1,0},{2,3},{3,2},{4,5},{5,4},{6,7},{7,6},{8,9},{9,8},{10,11... | collective-permute-start | bytes 1179656 | tf_op jit(solution)/shard_map/ppermute | solution.py:37
  7.3 6.7 %collective-permute-start = (bf16[64,1024]{1,0:T(8,128)(2,1)S(1)}, bf16[64,1024]{1,0:T(8,128)(2,1)S(1)}, u32[]{:S(2)}, u32[]{:S(2)}) collective-permute-start(bf16[64,1024]{1,0:T(8,128)(2,1)S(1)} %get-tuple-element.28), channel_id=1, source_target_pairs={{0,4},{4,0},{8,12},{12,8},{16,20},{20,16},{24,28},{28,24},{1,5},{5... | collective-permute-start | bytes 393224 | tf_op jit(solution)/shard_map/ppermute | solution.py:37
  10.0 7.8 %collective-permute-start.4 = (bf16[768,128]{1,0:T(8,128)(2,1)S(1)}, bf16[768,128]{1,0:T(8,128)(2,1)S(1)}, u32[]{:S(2)}, u32[]{:S(2)}) collective-permute-start(bf16[768,128]{1,0:T(8,128)(2,1)S(1)} %core_add.2.refs_2_.refs_0_), channel_id=1, source_target_pairs={{0,2},{1,3},{2,0},{3,1},{4,6},{5,7},{6,4},{7,5},{8,10},{9,11},{10,... | collective-permute-start | bytes 589832 | tf_op jit(solution)/shard_map/ppermute | solution.py:37
  11.7 10.7 %collective-permute-start.3 = (bf16[768,128]{1,0:T(8,128)(2,1)S(1)}, bf16[768,128]{1,0:T(8,128)(2,1)S(1)}, u32[]{:S(2)}, u32[]{:S(2)}) collective-permute-start(bf16[768,128]{1,0:T(8,128)(2,1)S(1)} %core_add.3.refs_2_.refs_0_), channel_id=1, source_target_pairs={{0,2},{1,3},{2,0},{3,1},{4,6},{5,7},{6,4},{7,5},{8,10},{9,11},{10,... | collective-permute-start | bytes 589832 | tf_op jit(solution)/shard_map/ppermute | solution.py:37
  14.1 8.5 %collective-permute-start.2 = (bf16[64,1024]{1,0:T(8,128)(2,1)S(1)}, bf16[64,1024]{1,0:T(8,128)(2,1)S(1)}, u32[]{:S(2)}, u32[]{:S(2)}) collective-permute-start(bf16[64,1024]{1,0:T(8,128)(2,1)S(1)} %leaf_add.2.refs_2_.refs_0_), channel_id=1, source_target_pairs={{0,8},{4,12},{8,0},{12,4},{16,24},{20,28},{24,16},{28,20},{1,9},{5... | collective-permute-start | bytes 393224 | tf_op jit(solution)/shard_map/ppermute | solution.py:37
  17.8 1.5 %collective-permute-start.5 = (bf16[768,128]{1,0:T(8,128)(2,1)S(1)}, bf16[768,128]{1,0:T(8,128)(2,1)S(1)}, u32[]{:S(2)}, u32[]{:S(2)}) collective-permute-start(bf16[768,128]{1,0:T(8,128)(2,1)S(1)} %feat_add.2.after_ref.refs_0_), channel_id=1, source_target_pairs={{0,1},{1,0},{2,3},{3,2},{4,5},{5,4},{6,7},{7,6},{8,9},{9,8},{10,11... | collective-permute-start | bytes 589832 | tf_op jit(solution)/shard_map/ppermute | solution.py:37
  20.8 8.4 %collective-permute-start.7 = (bf16[4,256,128]{2,1,0:T(8,128)(2,1)S(1)}, bf16[4,256,128]{2,1,0:T(8,128)(2,1)S(1)}, u32[]{:S(2)}, u32[]{:S(2)}) collective-permute-start(bf16[4,256,128]{2,1,0:T(8,128)(2,1)S(1)} %hist_send.2.refs_2_), channel_id=1, source_target_pairs={{0,4},{4,0},{8,12},{12,8},{16,20},{20,16},{24,28},{28,24},{1,5},{5... | collective-permute-start | bytes 786440 | tf_op jit(solution)/shard_map/ppermute | solution.py:37
  22.5 2.8 %collective-permute-start.6 = (bf16[768,128]{1,0:T(8,128)(2,1)S(1)}, bf16[768,128]{1,0:T(8,128)(2,1)S(1)}, u32[]{:S(2)}, u32[]{:S(2)}) collective-permute-start(bf16[768,128]{1,0:T(8,128)(2,1)S(1)} %feat_add.3.refs_2_.refs_0_.refs_1_), channel_id=1, source_target_pairs={{0,1},{1,0},{2,3},{3,2},{4,5},{5,4},{6,7},{7,6},{8,9},{9,8},{10,11... | collective-permute-start | bytes 589832 | tf_op jit(solution)/shard_map/ppermute | solution.py:37
  22.7 9.7 %collective-permute-start.9 = (bf16[64,1024]{1,0:T(8,128)(2,1)S(1)}, bf16[64,1024]{1,0:T(8,128)(2,1)S(1)}, u32[]{:S(2)}, u32[]{:S(2)}) collective-permute-start(bf16[64,1024]{1,0:T(8,128)(2,1)S(1)} %leaf_add.3.after_ref.refs_0_), channel_id=1, source_target_pairs={{0,16},{4,20},{8,24},{12,28},{16,0},{20,4},{24,8},{28,12},{1,17},{... | collective-permute-start | bytes 393224 | tf_op jit(solution)/shard_map/ppermute | solution.py:37
  26.8 10.9 %copy-start = (bf16[1536,1024]{1,0:T(8,128)(2,1)S(1)}, bf16[1536,1024]{1,0:T(8,128)(2,1)}, u32[]{:S(2)}) copy-start(bf16[1536,1024]{1,0:T(8,128)(2,1)} %pred_ref.3) | copy-start | bytes 9437188
  26.8 10.9 %copy-start.1 = (s32[1536]{0:T(1024)S(1)}, s32[1536]{0:T(1024)}, u32[]{:S(2)}) copy-start(s32[1536]{0:T(1024)} %param.8) | copy-start | bytes 18436
  26.8 9.0 %collective-permute-start.11 = (bf16[4,256,128]{2,1,0:T(8,128)(2,1)S(1)}, bf16[4,256,128]{2,1,0:T(8,128)(2,1)S(1)}, u32[]{:S(2)}, u32[]{:S(2)}) collective-permute-start(bf16[4,256,128]{2,1,0:T(8,128)(2,1)S(1)} %hist_send.3.after_ref), channel_id=1, source_target_pairs={{0,4},{4,0},{8,12},{12,8},{16,20},{20,16},{24,28},{28,24},{1,5},{5... | collective-permute-start | bytes 786440 | tf_op jit(solution)/shard_map/ppermute | solution.py:37
  32.4 5.3 %collective-permute-start.10 = (bf16[32,1024]{1,0:T(8,128)(2,1)S(1)}, bf16[32,1024]{1,0:T(8,128)(2,1)S(1)}, u32[]{:S(2)}, u32[]{:S(2)}) collective-permute-start(bf16[32,1024]{1,0:T(8,128)(2,1)S(1)} %leaf_value.1.refs_2_.own_ref), channel_id=1, source_target_pairs={{0,4},{4,0},{8,12},{12,8},{16,20},{20,16},{24,28},{28,24},{1,5},{5... | collective-permute-start | bytes 196616 | tf_op jit(solution)/shard_map/ppermute | solution.py:37
  32.9 6.8 %collective-permute-start.8 = (bf16[2,256,128]{2,1,0:T(8,128)(2,1)S(1)}, bf16[2,256,128]{2,1,0:T(8,128)(2,1)S(1)}, u32[]{:S(2)}, u32[]{:S(2)}) collective-permute-start(bf16[2,256,128]{2,1,0:T(8,128)(2,1)S(1)} %get-tuple-element.33), channel_id=1, source_target_pairs={{0,8},{4,12},{8,0},{12,4},{16,24},{20,28},{24,16},{28,20},{1,9},{5... | collective-permute-start | bytes 393224 | tf_op jit(solution)/shard_map/ppermute | solution.py:37
  35.8 5.6 %collective-permute-start.13 = (bf16[2,256,128]{2,1,0:T(8,128)(2,1)S(1)}, bf16[2,256,128]{2,1,0:T(8,128)(2,1)S(1)}, u32[]{:S(2)}, u32[]{:S(2)}) collective-permute-start(bf16[2,256,128]{2,1,0:T(8,128)(2,1)S(1)} %get-tuple-element.38), channel_id=1, source_target_pairs={{0,8},{4,12},{8,0},{12,4},{16,24},{20,28},{24,16},{28,20},{1,9},{5... | collective-permute-start | bytes 393224 | tf_op jit(solution)/shard_map/ppermute | solution.py:37
  39.8 6.8 %collective-permute-start.12 = (bf16[1,256,128]{2,1,0:T(8,128)(2,1)S(1)}, bf16[1,256,128]{2,1,0:T(8,128)(2,1)S(1)}, u32[]{:S(2)}, u32[]{:S(2)}) collective-permute-start(bf16[1,256,128]{2,1,0:T(8,128)(2,1)S(1)} %get-tuple-element.37), channel_id=1, source_target_pairs={{0,16},{4,20},{8,24},{12,28},{16,0},{20,4},{24,8},{28,12},{1,17},{... | collective-permute-start | bytes 196616 | tf_op jit(solution)/shard_map/ppermute | solution.py:37
  41.5 5.8 %collective-permute-start.14 = (bf16[1,256,128]{2,1,0:T(8,128)(2,1)S(1)}, bf16[1,256,128]{2,1,0:T(8,128)(2,1)S(1)}, u32[]{:S(2)}, u32[]{:S(2)}) collective-permute-start(bf16[1,256,128]{2,1,0:T(8,128)(2,1)S(1)} %get-tuple-element.40), channel_id=1, source_target_pairs={{0,16},{4,20},{8,24},{12,28},{16,0},{20,4},{24,8},{28,12},{1,17},{... | collective-permute-start | bytes 196616 | tf_op jit(solution)/shard_map/ppermute | solution.py:37
